TPU v7x, 512 devices: a whole 4x8x8 slice. The times are simulated.
512 devices in a mesh: layer: 2 (over x_hi), feat: 64 (over y, z), tok: 4 (over x_lo, core).
Axes of the slice: x: 4 (x_hi: 2, x_lo: 2; x = x_hi * 2 + x_lo), y: 8, z: 8, core: 2. Of those that a mesh axis runs over, the one named last changes fastest.
Arguments:
- resid: bfloat16 [2, 1024, 2304], P('layer', 'tok', 'feat'), may hold values from -6 to 6
- norm_gain: bfloat16 [2, 2304], P('layer', 'feat'), may hold values from 0.5 to 2
- prev_codes: bfloat16 [1024, 16384], P('tok', 'feat'), may hold values from 0 to 1.5
- feature_mask: int32 [2, 8, 128], P('layer', 'tok', 'feat'), may hold values 0 or 1
- w_gate: bfloat16 [2, 2304, 9216], P('layer', 'tok', 'feat'), may hold values from -0.125 to 0.125
- w_up: bfloat16 [2, 2304, 9216], P('layer', 'tok', 'feat'), may hold values from -0.125 to 0.125
- w_down: bfloat16 [2, 9216, 2304], P('layer', 'feat', 'tok'), may hold values from -0.0625 to 0.0625
- enc_weight: bfloat16 [2, 2304, 16384], P('layer', 'tok', 'feat'), may hold values from -0.125 to 0.125
- enc_bias: float32 [2, 16384], P('layer', 'feat'), may hold values from -3 to 3
- dec_own: bfloat16 [2, 16384, 2304], P('layer', 'feat', 'tok'), may hold values from -0.046875 to 0.046875
- dec_prev: bfloat16 [2, 16384, 2304], P('layer', 'feat', 'tok'), may hold values from -0.046875 to 0.046875
Outputs:
- grad_enc: float32 [2, 2304, 16384], P('layer', 'tok', 'feat')
- grad_bias: float32 [2, 16384], P('layer', 'feat')
- grad_own: float32 [2, 16384, 2304], P('layer', 'feat', 'tok')
- grad_prev: float32 [2, 16384, 2304], P('layer', 'feat', 'tok')
All inputs are finite; a program needn't handle non-finite values. No bound on the sum of `feature_mask` on one device may be relied on, other than what follows from the above.
Results may differ from a plain program's by a relative error of at most 0.0063.
Values may be sent and summed in bfloat16 or wider, within the bound.
No kernel may reach another device: no remote copies, remote signals or barrier semaphores. Data moves between devices by JAX's collectives and lax.ppermute only.
A program may use at most 64 MiB of HBM per device.

v0:
```python
import math

import jax
import jax.numpy as jnp
from jax import lax
from jax.sharding import Mesh
from jax.sharding import PartitionSpec as P

TILE = 128
TBLK = 128
TOK = ("tok_0", "tok_1")


def turned_gather(arrays, axis, dims):
    turned = [jnp.moveaxis(a, dim, 0) for a, dim in zip(arrays, dims)]
    widths = [t[0].size for t in turned]
    both = jnp.concatenate([t.reshape(-1, w) for t, w in zip(turned, widths)], axis=1)
    result = lax.all_gather(both, axis, axis=0, tiled=True)
    blocks = jnp.split(result, [sum(widths[:k]) for k in range(1, len(widths))], axis=1)
    return tuple(
        (
            jnp.moveaxis(b.reshape(-1, *t.shape[1:]), 0, dim)
            for b, t, dim in zip(blocks, turned, dims)
        )
    )


def from_everyone(array, axis):
    copies = jnp.broadcast_to(array, (lax.axis_size(axis), *array.shape))
    return lax.all_to_all(copies, axis, split_axis=0, concat_axis=0, tiled=True)


def in_order(blocks, dim):
    shape = list(blocks.shape[1:])
    shape[dim] *= blocks.shape[0]
    return jnp.moveaxis(blocks, 0, dim).reshape(shape)


def gather_axes(array, axes, dim):
    far, near = axes
    blocks = from_everyone(from_everyone(array, far), near)
    return in_order(blocks.swapaxes(0, 1).reshape(-1, *array.shape), dim)


def side_by_side(arrays, axis, dim, along):
    both = jnp.concatenate(arrays, axis=along)
    result, at, finished = (gather_axes(both, axis, dim), 0, [])
    for a in arrays:
        finished.append(lax.slice_in_dim(result, at, at + a.shape[along], axis=along))
        at += a.shape[along]
    return tuple(finished)


def passed_along(value, axis, steps):
    count = lax.axis_size(axis)
    leading, last = (max(0, -steps), min(count, count - steps))
    return lax.ppermute(value, axis, [(source, source + steps) for source in range(leading, last)])


def collect(array, axis, dim):
    blocks = from_everyone(array, axis)
    return in_order(blocks, dim)


def filled_up(lines, peers):
    spare = -lines.shape[0] % peers
    if not spare:
        return lines
    return jnp.concatenate([lines, jnp.zeros((spare, *lines.shape[1:]), lines.dtype)])


def cut_along(array, dim, peers):
    before, after = (array.shape[:dim], array.shape[dim + 1 :])
    return jnp.moveaxis(array.reshape(*before, peers, -1, *after), dim, 0)


def sent_and_summed(array, axis, dim):
    blocks = cut_along(array, dim, lax.axis_size(axis))
    arrived = lax.all_to_all(blocks, axis, split_axis=0, concat_axis=0, tiled=True)
    return arrived.astype(jnp.float32).sum(axis=0)


def nested_sum(array, axes):
    lines = array.reshape(-1, array.shape[-1])
    padded = filled_up(lines, lax.axis_size(axes))
    whole = collect(sent_and_summed(padded, axes, 0).astype(jnp.bfloat16), axes, 0)
    return lax.slice_in_dim(whole, 0, len(lines)).reshape(array.shape).astype(jnp.float32)


def sent_together(arrays, axis, dim, along):
    widths = [a.shape[along] for a in arrays]
    both = jnp.concatenate(arrays, axis=along)
    result = lax.all_gather(both, axis, axis=dim, tiled=True)
    return tuple(jnp.split(result, [sum(widths[:k]) for k in range(1, len(widths))], axis=along))


def block_keep(block_mask, height, breadth):
    blocks = block_mask.astype(jnp.float32)
    spread = jnp.broadcast_to(
        blocks[:, None, :, None], (blocks.shape[0], TBLK, blocks.shape[1], TILE)
    )
    return spread.reshape(height, breadth)


def local(
    resid,
    norm_gain,
    prev_codes,
    feature_mask,
    w_gate,
    w_up,
    w_down,
    enc_weight,
    enc_bias,
    dec_own,
    dec_prev,
):
    gathered, gains = turned_gather((resid[0], norm_gain), "feat", (1, 1))
    stream = gathered.astype(jnp.float32)
    normed = (
        stream
        * lax.rsqrt(jnp.mean(stream * stream, axis=1, keepdims=True) + 1e-06)
        * gains[0].astype(jnp.float32)
    ).astype(jnp.bfloat16)
    height = normed.shape[0]
    feat_local = enc_weight.shape[2]
    segments = side_by_side((w_gate[0], w_up[0], enc_weight[0]), ("tok_0", "tok_1"), 0, 1)
    gate_sum, up_sum, enc_sum = tuple(
        (jnp.dot(normed, segment, preferred_element_type=jnp.float32) for segment in segments)
    )
    hidden = (jax.nn.gelu(gate_sum, approximate=True) * up_sum).astype(jnp.bfloat16)
    preact = enc_sum + enc_bias[0]
    active = jnp.maximum(preact, 0.0)
    keeper = block_keep(feature_mask[0], height, feat_local)
    codes = (active * active * keeper).astype(jnp.bfloat16)
    shifted = passed_along(codes, "layer", 1)
    source = jnp.where(lax.axis_index("layer") == 0, prev_codes, shifted)
    own_full, prev_full = side_by_side((dec_own[0], dec_prev[0]), ("tok_0", "tok_1"), 1, 0)
    partial_value = (
        jnp.dot(codes, own_full, preferred_element_type=jnp.float32)
        + jnp.dot(source, prev_full, preferred_element_type=jnp.float32)
        - jnp.dot(hidden, collect(w_down[0], TOK, 1), preferred_element_type=jnp.float32)
    )
    error = nested_sum(partial_value.astype(jnp.bfloat16), "feat").astype(jnp.bfloat16)
    own_back = jnp.dot(error, own_full.T, preferred_element_type=jnp.float32)
    prev_back = jnp.dot(error, prev_full.T, preferred_element_type=jnp.float32)
    later = passed_along(prev_back.astype(jnp.bfloat16), "layer", -1).astype(prev_back.dtype)
    back = own_back + later
    factor = 1.0 / math.sqrt(height * lax.axis_size(TOK))
    pregrad = (back * keeper * (2.0 * active) * factor).astype(jnp.bfloat16)
    normed_cols = lax.all_to_all(normed, TOK, split_axis=1, concat_axis=0, tiled=True)
    error_cols = lax.all_to_all(error, TOK, split_axis=1, concat_axis=0, tiled=True)
    codes_all, source_all = sent_together((codes, source), TOK, 0, 1)
    pregrad_all = collect(pregrad, TOK, 0)
    grad_enc = jnp.dot(normed_cols.T, pregrad_all, preferred_element_type=jnp.float32)
    grad_bias = jnp.sum(pregrad_all.astype(jnp.float32), axis=0)
    grad_own = jnp.dot(codes_all.T, error_cols, preferred_element_type=jnp.float32) * factor
    grad_prev = jnp.dot(source_all.T, error_cols, preferred_element_type=jnp.float32) * factor
    return (grad_enc[None], grad_bias[None], grad_own[None], grad_prev[None])


def solution(mesh):
    split = Mesh(
        mesh.devices.reshape(mesh.shape["layer"], mesh.shape["feat"], 2, 2),
        ("layer", "feat", "tok_0", "tok_1"),
    )
    placed = (
        P("layer", TOK, "feat"),
        P("layer", "feat"),
        P(TOK, "feat"),
        P("layer", TOK, "feat"),
        P("layer", TOK, "feat"),
        P("layer", TOK, "feat"),
        P("layer", "feat", TOK),
        P("layer", TOK, "feat"),
        P("layer", "feat"),
        P("layer", "feat", TOK),
        P("layer", "feat", TOK),
    )
    return jax.shard_map(
        local,
        mesh=split,
        in_specs=placed,
        out_specs=(
            P("layer", TOK, "feat"),
            P("layer", "feat"),
            P("layer", "feat", TOK),
            P("layer", "feat", TOK),
        ),
        check_vma=False,
    )
```

profile of v0, /device:TPU:1, one launch (start us, length us, event | category | flops | bytes accessed | tf_op | source)
XLA Modules:
  0.0 276.7 jit_solution(6228047758705159638)
XLA Ops:
  7.2 0.8 copy.34
  8.0 1.3 maximum_bitcast_fusion
  9.4 1.9 broadcast_in_dim.46
  11.3 10.3 %all-to-all-start.5 = ((bf16[4,144,576]{2,1,0:T(8,128)(2,1)}), bf16[4,144,576]{2,1,0:T(8,128)(2,1)S(1)}, u32[]{:S(2)}, u32[]{:S(2)}) async-start(bf16[4,144,576]{2,1,0:T(8,128)(2,1)} %broadcast_in_dim.46), calls=%async_computation.5 | async-start | bytes 1474560 | tf_op jit(solution)/shard_map/all_to_all | solution.py:30
  21.7 10.2 %all-to-all-done.5 = bf16[4,144,576]{2,1,0:T(8,128)(2,1)S(1)} async-done(((bf16[4,144,576]{2,1,0:T(8,128)(2,1)}), bf16[4,144,576]{2,1,0:T(8,128)(2,1)S(1)}, u32[]{:S(2)}, u32[]{:S(2)}) %all-to-all-start.5) | async-done | bytes 663584 | tf_op jit(solution)/shard_map/all_to_all | solution.py:30
  31.9 1.1 broadcast_in_dim.44
  33.0 3.7 %all-to-all-start.3 = ((bf16[2,512,576]{1,2,0:T(8,128)(2,1)}), bf16[2,512,576]{1,2,0:T(8,128)(2,1)S(1)}, u32[]{:S(2)}, u32[]{:S(2)}) async-start(bf16[2,512,576]{1,2,0:T(8,128)(2,1)} %broadcast_in_dim.44), calls=%async_computation.3 | async-start | bytes 2359296 | tf_op jit(solution)/shard_map/all_to_all | solution.py:30
  37.1 1.4 pad_maximum_fusion
  38.5 1.1 copy.37
  39.6 11.3 %all-to-all-done.3 = bf16[2,512,576]{1,2,0:T(8,128)(2,1)S(1)} async-done(((bf16[2,512,576]{1,2,0:T(8,128)(2,1)}), bf16[2,512,576]{1,2,0:T(8,128)(2,1)S(1)}, u32[]{:S(2)}, u32[]{:S(2)}) %all-to-all-start.3) | async-done | bytes 1179680 | tf_op jit(solution)/shard_map/all_to_all | solution.py:30
  51.1 7.2 %all_to_all.75 = bf16[2,2,512,576]{2,3,1,0:T(8,128)(2,1)S(1)} all-to-all(bf16[2,2,512,576]{2,3,1,0:T(8,128)(2,1)S(1)} %broadcast_in_dim.45), channel_id=1, replica_groups=mesh['layer'=2,'feat'=64,'tok_0'=2,'tok_1'=2] {'tok_1'}, dimensions={0} | all-to-all | bytes 4718592 | tf_op jit(solution)/shard_map/all_to_all | solution.py:30
  58.3 1.2 broadcast_in_dim.41
  59.5 4.7 %all-to-all-start.1 = ((bf16[2,576,544]{1,2,0:T(8,128)(2,1)}), bf16[2,576,544]{1,2,0:T(8,128)(2,1)}, u32[]{:S(2)}, u32[]{:S(2)}) async-start(bf16[2,576,544]{1,2,0:T(8,128)(2,1)} %broadcast_in_dim.41), calls=%async_computation.1 | async-start | bytes 2785280 | tf_op jit(solution)/shard_map/all_to_all | solution.py:30
  64.4 1.1 copy.43
  65.6 2.5 reshape.57
  68.3 1.6 fusion.35
  69.8 11.5 %all-to-all-done.1 = bf16[2,576,544]{1,2,0:T(8,128)(2,1)} async-done(((bf16[2,576,544]{1,2,0:T(8,128)(2,1)}), bf16[2,576,544]{1,2,0:T(8,128)(2,1)}, u32[]{:S(2)}, u32[]{:S(2)}) %all-to-all-start.1) | async-done | bytes 1253408 | tf_op jit(solution)/shard_map/all_to_all | solution.py:30
  81.3 2.4 copy.38
  83.7 1.4 broadcast_in_dim.42
  85.2 6.9 %all_to_all.76 = bf16[2,2,576,544]{2,1,3,0:T(2,128)(2,1)S(1)} all-to-all(bf16[2,2,576,544]{2,1,3,0:T(2,128)(2,1)S(1)} %broadcast_in_dim.42), channel_id=1, replica_groups=mesh['layer'=2,'feat'=64,'tok_0'=2,'tok_1'=2] {'tok_1'}, dimensions={0} | all-to-all | bytes 5013504 | tf_op jit(solution)/shard_map/all_to_all | solution.py:30
  92.0 4.3 %copy.39 = bf16[2,2,576,544]{2,1,0,3:T(2,128)(2,1)S(1)} copy(bf16[2,2,576,544]{2,0,3,1:T(2,128)(2,1)S(1)} %bitcast.73) | data formatting | bytes 5013504 | tf_op jit(solution)/shard_map/transpose | solution.py:42
  96.3 3.1 %reshape_reshape.3 = bf16[2304,544]{0,1:T(8,128)(2,1)} reshape(bf16[2,2,576,544]{2,1,0,3:T(2,128)(2,1)S(1)} %copy.39) | data formatting | bytes 5013504 | tf_op jit(solution)/shard_map/reshape;reshape | solution.py:36
  99.5 2.8 reshape.62
  102.8 1.4 fusion.3
  105.0 2.5 fusion.22
  107.5 1.7 collective-permute-start
  109.8 2.4 fusion.32
  113.4 3.9 %fusion = bf16[256,2304]{1,0:T(8,128)(2,1)} fusion(f32[256,2304]{1,0:T(8,128)S(1)} %convolution_add_fusion, bf16[144,2304]{1,0:T(8,128)(2,1)} %reshape.57, f32[256,144]{0,1:T(8,128)} %fusion.32, bf16[2304,256]{1,0:T(8,128)(2,1)} %fusion.3, bf16[2304,544]{0,1:T(8,128)(2,1)} %reshape_reshape.3), kind=kOutput, calls=%fused_computation.2 | convolution fusion | flops 340992000 | bytes 6193152 | tf_op jit(solution)/shard_map/dot_general | solution.py:142
  117.3 2.4 reshape.58
  119.7 43.1 %all_to_all.77 = bf16[64,4,2304]{2,1,0:T(4,128)(2,1)S(1)} all-to-all(bf16[64,4,2304]{2,1,0:T(4,128)(2,1)S(1)} %reshape.58), channel_id=1, replica_groups=mesh['layer'=2,'feat'=64,'tok_0'=2,'tok_1'=2] {'feat'}, dimensions={0} | all-to-all | bytes 2359296 | tf_op jit(solution)/shard_map/all_to_all | solution.py:79
  163.7 38.2 %all_to_all.78 = bf16[64,4,2304]{2,1,0:T(4,128)(2,1)S(1)} all-to-all(bf16[64,4,2304]{2,1,0:T(4,128)(2,1)S(1)} %broadcast_in_dim.47), channel_id=1, replica_groups=mesh['layer'=2,'feat'=64,'tok_0'=2,'tok_1'=2] {'feat'}, dimensions={0} | all-to-all | bytes 2359296 | tf_op jit(solution)/shard_map/all_to_all | solution.py:30
  201.9 8.3 %all-to-all-start = ((bf16[256,4,576]{0,2,1:T(8,128)(2,1)}), bf16[256,4,576]{0,2,1:T(8,128)(2,1)}, u32[]{:S(2)}, u32[]{:S(2)}) async-start(bf16[256,4,576]{0,2,1:T(8,128)(2,1)} %bitcast.5), calls=%async_computation | async-start | bytes 2359296 | tf_op jit(solution)/shard_map/all_to_all | solution.py:151
  210.5 2.6 convolution_convert_fusion
  213.1 1.3 collective-permute-start.1
  214.4 0.7 pad_maximum_fusion.2
  215.2 15.1 %collective-permute-done.1 = bf16[256,256]{0,1:T(8,128)(2,1)} collective-permute-done((bf16[256,256]{0,1:T(8,128)(2,1)}, bf16[256,256]{0,1:T(8,128)(2,1)}, u32[]{:S(2)}, u32[]{:S(2)}) %collective-permute-start.1) | collective-permute-done | bytes 131104 | tf_op jit(solution)/shard_map/ppermute | solution.py:57
  230.3 2.3 fusion.25
  232.6 1.0 copy.46
  233.6 0.8 broadcast_in_dim.48
  234.5 4.0 %all-to-all-start.8 = ((bf16[4,256,256]{2,1,0:T(8,128)(2,1)}), bf16[4,256,256]{2,1,0:T(8,128)(2,1)S(1)}, u32[]{:S(2)}, u32[]{:S(2)}) async-start(bf16[4,256,256]{2,1,0:T(8,128)(2,1)} %broadcast_in_dim.48), calls=%async_computation.8 | async-start | bytes 1048576 | tf_op jit(solution)/shard_map/all_to_all | solution.py:30
  238.5 2.3 all_to_all.61
  240.9 3.4 %copy.47 = bf16[256,4,576]{0,2,1:T(8,128)(2,1)} copy(bf16[256,4,576]{2,1,0:T(4,128)(2,1)} %all_to_all.61) | data formatting | bytes 2359296 | tf_op jit(solution)/shard_map/all_to_all | solution.py:152
  244.3 2.2 all-to-all-done.8
  246.5 4.4 %all-to-all-start.9 = ((bf16[256,4,576]{0,2,1:T(8,128)(2,1)}), bf16[256,4,576]{0,2,1:T(8,128)(2,1)S(1)}, u32[]{:S(2)}, u32[]{:S(2)}) async-start(bf16[256,4,576]{0,2,1:T(8,128)(2,1)} %copy.47), calls=%async_computation.9 | async-start | bytes 2359296 | tf_op jit(solution)/shard_map/all_to_all | solution.py:152
  251.6 2.6 convolution_bitcast_fusion
  254.1 11.7 %all-to-all-done.9 = bf16[256,4,576]{0,2,1:T(8,128)(2,1)S(1)} async-done(((bf16[256,4,576]{0,2,1:T(8,128)(2,1)}), bf16[256,4,576]{0,2,1:T(8,128)(2,1)S(1)}, u32[]{:S(2)}, u32[]{:S(2)}) %all-to-all-start.9) | async-done | bytes 1179680 | tf_op jit(solution)/shard_map/all_to_all | solution.py:152
  266.1 2.5 fusion.5
  268.5 1.3 fusion.4
  (62 shorter events, 6.0 us)
Async XLA Ops:
  7.2 92.3 %all-gather.6.cloned.1.call-start = ((), (), s32[]{:S(2)}) async-start(), calls=%async_computation.11 | async-start | bytes 1996800 | tf_op jit(solution)/shard_map/all_gather | solution.py:18
  9.3 12.3 %copy-start.9 = (bf16[1,256,576]{1,2,0:T(8,128)(2,1)S(1)}, bf16[1,256,576]{1,2,0:T(8,128)(2,1)}, u32[]{:S(2)}) copy-start(bf16[1,256,576]{1,2,0:T(8,128)(2,1)} %param.21) | copy-start | bytes 884740
  9.4 12.3 %copy-start.10 = (bf16[1,256,576]{1,2,0:T(8,128)(2,1)S(1)}, bf16[1,256,576]{1,2,0:T(8,128)(2,1)}, u32[]{:S(2)}) copy-start(bf16[1,256,576]{1,2,0:T(8,128)(2,1)} %param.20) | copy-start | bytes 884740
  11.3 20.6 %all-to-all-start.5 = ((bf16[4,144,576]{2,1,0:T(8,128)(2,1)}), bf16[4,144,576]{2,1,0:T(8,128)(2,1)S(1)}, u32[]{:S(2)}, u32[]{:S(2)}) async-start(bf16[4,144,576]{2,1,0:T(8,128)(2,1)} %broadcast_in_dim.46), calls=%async_computation.5 | async-start | bytes 1474560 | tf_op jit(solution)/shard_map/all_to_all | solution.py:30
  33.0 3.7 %copy-start.11 = (bf16[1,576,144]{1,2,0:T(8,128)(2,1)S(1)}, bf16[1,576,144]{1,2,0:T(8,128)(2,1)}, u32[]{:S(2)}) copy-start(bf16[1,576,144]{1,2,0:T(8,128)(2,1)} %param.16) | copy-start | bytes 497668
  33.0 3.9 %copy-start.12 = (bf16[1,576,144]{1,2,0:T(8,128)(2,1)S(1)}, bf16[1,576,144]{1,2,0:T(8,128)(2,1)}, u32[]{:S(2)}) copy-start(bf16[1,576,144]{1,2,0:T(8,128)(2,1)} %param.15) | copy-start | bytes 497668
  33.0 17.9 %all-to-all-start.3 = ((bf16[2,512,576]{1,2,0:T(8,128)(2,1)}), bf16[2,512,576]{1,2,0:T(8,128)(2,1)S(1)}, u32[]{:S(2)}, u32[]{:S(2)}) async-start(bf16[2,512,576]{1,2,0:T(8,128)(2,1)} %broadcast_in_dim.44), calls=%async_computation.3 | async-start | bytes 2359296 | tf_op jit(solution)/shard_map/all_to_all | solution.py:30
  51.1 7.2 %copy-start.3 = (bf16[576,544]{0,1:T(8,128)(2,1)S(1)}, bf16[576,544]{0,1:T(8,128)(2,1)}, u32[]{:S(2)}) copy-start(bf16[576,544]{0,1:T(8,128)(2,1)} %copy.37) | copy-start | bytes 1880068
  59.5 4.7 %copy-start.14 = (s32[1,2,2]{2,1,0:T(2,128)S(1)}, s32[1,2,2]{2,1,0:T(2,128)}, u32[]{:S(2)}) copy-start(s32[1,2,2]{2,1,0:T(2,128)} %param.14) | copy-start | bytes 52
  59.5 4.8 %copy-start.13 = (bf16[256,256]{1,0:T(8,128)(2,1)S(1)}, bf16[256,256]{1,0:T(8,128)(2,1)}, u32[]{:S(2)}) copy-start(bf16[256,256]{1,0:T(8,128)(2,1)} %param.13) | copy-start | bytes 393220
  59.5 21.8 %all-to-all-start.1 = ((bf16[2,576,544]{1,2,0:T(8,128)(2,1)}), bf16[2,576,544]{1,2,0:T(8,128)(2,1)}, u32[]{:S(2)}, u32[]{:S(2)}) async-start(bf16[2,576,544]{1,2,0:T(8,128)(2,1)} %broadcast_in_dim.41), calls=%async_computation.1 | async-start | bytes 2785280 | tf_op jit(solution)/shard_map/all_to_all | solution.py:30
  102.8 2.1 copy-start.2
  102.8 2.1 copy-start.16
  104.4 3.1 %copy-start.6 = (f32[2,128,2,128]{1,0,3,2:T(2,128)}, f32[2,128,2,128]{1,0,3,2:T(2,128)S(1)}, u32[]{:S(2)}) copy-start(f32[2,128,2,128]{1,0,3,2:T(2,128)S(1)} %broadcast_in_dim.43) | copy-start | bytes 786436
  105.0 4.3 %copy-start = (bf16[256,4,576]{0,2,1:T(8,128)(2,1)S(1)}, bf16[256,4,576]{0,2,1:T(8,128)(2,1)}, u32[]{:S(2)}) copy-start(bf16[256,4,576]{0,2,1:T(8,128)(2,1)} %get-tuple-element.5) | copy-start | bytes 3538948
  107.5 2.3 copy-start.7
  107.5 4.7 %collective-permute-start = (bf16[256,256]{0,1:T(8,128)(2,1)S(1)}, bf16[256,256]{0,1:T(8,128)(2,1)S(1)}, u32[]{:S(2)}, u32[]{:S(2)}) collective-permute-start(bf16[256,256]{0,1:T(8,128)(2,1)S(1)} %get-tuple-element.6), channel_id=1, source_target_pairs={{0,256},{1,257},{2,258},{3,259},{4,260},{5,261},{6,262},{7,263},{8... | collective-permute-start | bytes 393224 | tf_op jit(solution)/shard_map/ppermute | solution.py:57
  109.8 3.1 %copy-start.1 = (bf16[256,4,576]{0,2,1:T(8,128)(2,1)S(1)}, bf16[256,4,576]{0,2,1:T(8,128)(2,1)}, u32[]{:S(2)}) copy-start(bf16[256,4,576]{0,2,1:T(8,128)(2,1)} %get-tuple-element.4) | copy-start | bytes 3538948
  112.2 0.6 copy-start.4
  201.9 31.7 %all-to-all-start = ((bf16[256,4,576]{0,2,1:T(8,128)(2,1)}), bf16[256,4,576]{0,2,1:T(8,128)(2,1)}, u32[]{:S(2)}, u32[]{:S(2)}) async-start(bf16[256,4,576]{0,2,1:T(8,128)(2,1)} %bitcast.5), calls=%async_computation | async-start | bytes 2359296 | tf_op jit(solution)/shard_map/all_to_all | solution.py:151
  210.2 55.8 %all-gather.4.cloned.1.call-start = ((), (), s32[]{:S(2)}) async-start(), calls=%async_computation.10 | async-start | bytes 1310720 | tf_op jit(solution)/shard_map/all_gather | solution.py:93
  210.5 3.9 %copy-start.5 = (bf16[256,256]{0,1:T(8,128)(2,1)S(1)}, bf16[256,256]{0,1:T(8,128)(2,1)}, u32[]{:S(2)}) copy-start(bf16[256,256]{0,1:T(8,128)(2,1)} %copy-done.4) | copy-start | bytes 393220
  210.5 3.9 %copy-start.8 = (bf16[256,256]{0,1:T(8,128)(2,1)S(1)}, bf16[256,256]{0,1:T(8,128)(2,1)}, u32[]{:S(2)}) copy-start(bf16[256,256]{0,1:T(8,128)(2,1)} %copy-done.7) | copy-start | bytes 393220
  213.1 17.2 %collective-permute-start.1 = (bf16[256,256]{0,1:T(8,128)(2,1)}, bf16[256,256]{0,1:T(8,128)(2,1)}, u32[]{:S(2)}, u32[]{:S(2)}) collective-permute-start(bf16[256,256]{0,1:T(8,128)(2,1)} %convolution_convert_fusion), channel_id=1, source_target_pairs={{256,0},{257,1},{258,2},{259,3},{260,4},{261,5},{262,6},{263,7},{2... | collective-permute-start | bytes 393224 | tf_op jit(solution)/shard_map/ppermute | solution.py:57
  234.5 12.0 %all-to-all-start.8 = ((bf16[4,256,256]{2,1,0:T(8,128)(2,1)}), bf16[4,256,256]{2,1,0:T(8,128)(2,1)S(1)}, u32[]{:S(2)}, u32[]{:S(2)}) async-start(bf16[4,256,256]{2,1,0:T(8,128)(2,1)} %broadcast_in_dim.48), calls=%async_computation.8 | async-start | bytes 1048576 | tf_op jit(solution)/shard_map/all_to_all | solution.py:30
  246.5 19.4 %all-to-all-start.9 = ((bf16[256,4,576]{0,2,1:T(8,128)(2,1)}), bf16[256,4,576]{0,2,1:T(8,128)(2,1)S(1)}, u32[]{:S(2)}, u32[]{:S(2)}) async-start(bf16[256,4,576]{0,2,1:T(8,128)(2,1)} %copy.47), calls=%async_computation.9 | async-start | bytes 2359296 | tf_op jit(solution)/shard_map/all_to_all | solution.py:152
  266.0 2.5 copy-start.15
Sparse Core Ops, SparseCore 0:
  11.6 84.8 all-gather.5
  215.3 22.8 all-gather.3
where the time goes:
time: 278 us; the launch traced here: 277 us
  blocking collectives  95.4 us (34%)
  waiting for transfers between devices  62.1 us (22%)
  starting transfers between devices  38.5 us (14%)
  local copies, waits for them, and re-layouts  38.5 us (14%)
  matrix products  21.1 us (8%)
  between operations  14.4 us (5%)
  other arithmetic  6.67 us (2%)
    all_to_all x3, blocking collectives, from_everyone(): return lax.all_to_all(copies, axis, split_axis=0, concat_axis=0, tiled=True)  52.2 us
    all_to_all x1, blocking collectives, sent_and_summed(): lax.all_to_all(blocks, axis, split_axis=0, concat_axis=0, tiled=True)  43.1 us
    all_to_all x4, waiting for transfers between devices, from_everyone(): return lax.all_to_all(copies, axis, split_axis=0, concat_axis=0, tiled=True)  35.2 us
    all_to_all x4, starting transfers between devices, from_everyone(): return lax.all_to_all(copies, axis, split_axis=0, concat_axis=0, tiled=True)  22.8 us
    ppermute x2, waiting for transfers between devices, passed_along(): lax.ppermute(value, axis, [(source, source + steps) for source in range(l...  15.1 us
    all_to_all x1, waiting for transfers between devices, local(): lax.all_to_all(error, TOK, split_axis=1, concat_axis=0, tiled=True)  11.7 us
    all_to_all x1, starting transfers between devices, local(): lax.all_to_all(normed, TOK, split_axis=1, concat_axis=0, tiled=True)  8.32 us
    broadcast_in_dim x7, local copies, waits for them, and re-layouts, from_everyone(): copies = jnp.broadcast_to(array, (lax.axis_size(axis), *array.shape))  7 us
  transfers between devices with their start and end apart: 10, of which 6 were waited for; matrix products, arithmetic and copies ran while one was open for 15% of the time, Pallas kernels for 0%

commit v1 on v0

v1 whole, which is shorter than its diff:
```python
import math

import jax
import jax.numpy as jnp
from jax import lax
from jax.experimental import pallas as pl
from jax.experimental.pallas import tpu as pltpu
from jax.sharding import Mesh
from jax.sharding import PartitionSpec as P

TILE = 128
TBLK = 128
BF = jnp.bfloat16
F32 = jnp.float32
TOK = ("tok_0", "tok_1")
PARAMS = pltpu.CompilerParams(vmem_limit_bytes=56 * 1024 * 1024)
VM = pl.BlockSpec(memory_space=pltpu.VMEM)
SM = pl.BlockSpec(memory_space=pltpu.SMEM)


def call(kernel, ins, outs, scratch=()):
    specs = [SM if a.dtype == jnp.int32 else VM for a in ins]
    return pl.pallas_call(
        kernel,
        out_shape=[jax.ShapeDtypeStruct(s, d) for s, d in outs],
        in_specs=specs,
        out_specs=[VM] * len(outs),
        scratch_shapes=list(scratch),
        compiler_params=PARAMS,
    )(*ins)


def dot(a, b, ca=1, cb=0):
    return lax.dot_general(a, b, (((ca,), (cb,)), ((), ())), preferred_element_type=F32)


def swap(x, axis):
    return lax.ppermute(x, axis, [(0, 1), (1, 0)])


def gather4(x):
    far = swap(x, "tok_0")
    near = swap(x, "tok_1")
    return [x, near, far, swap(far, "tok_1")]


def exchange(blocks, axis):
    return lax.all_to_all(blocks, axis, split_axis=0, concat_axis=0, tiled=True)


def spread_kernel(x_ref, o_ref):
    turned = x_ref[...].astype(F32).T
    half = turned.shape[1] // 2
    both = jnp.concatenate([turned[:, :half], turned[:, half:]], axis=0).astype(BF)
    o_ref[...] = jnp.broadcast_to(both[None], o_ref.shape)


def encode_kernel(
    t_ref, mask_ref, g_ref, gain_ref, w0, w1, w2, w3, bias_ref,
    nt_ref, codes_ref, slope_ref, hidden_ref, x_ref,
):
    feats, rows2, lanes = g_ref.shape
    rows = rows2 // 2
    for f in range(feats):
        for h in range(2):
            x_ref[pl.ds(f * rows, rows), pl.ds(h * lanes, lanes)] = g_ref[
                f, pl.ds(h * rows, rows), :
            ].astype(F32)
    depth = feats * rows
    block = depth // 4
    total = jnp.zeros((1, 2 * lanes), F32)
    for k in range(4):
        x = x_ref[pl.ds(k * block, block), :]
        total = total + jnp.sum(x * x, axis=0, keepdims=True)
    scale = lax.rsqrt(total / depth + 1e-06)
    for k in range(4):
        at = pl.ds(k * block, block)
        gain = gain_ref[at, :].astype(F32)
        for h in range(2):
            lane = pl.ds(h * lanes, lanes)
            value = x_ref[at, lane] * scale[:, h * lanes : (h + 1) * lanes] * gain
            nt_ref[k, :, lane] = value.astype(BF)
    t = t_ref[0]
    width = bias_ref.shape[1]
    sums = dot(nt_ref[t], w0[...], 0, 0)
    for k, w in ((1, w1), (2, w2), (3, w3)):
        sums += dot(nt_ref[jnp.bitwise_xor(t, k)], w[...], 0, 0)
    units = hidden_ref.shape[1]
    preact = sums[:, :width] + bias_ref[...]
    active = jnp.maximum(preact, 0.0)
    factor = 1.0 / math.sqrt(4 * codes_ref.shape[0])
    for i in range(codes_ref.shape[0] // TBLK):
        for j in range(width // TILE):
            keep = mask_ref[i, j].astype(F32)
            r, c = slice(i * TBLK, (i + 1) * TBLK), slice(j * TILE, (j + 1) * TILE)
            part = active[r, c]
            codes_ref[r, c] = (part * part * keep).astype(BF)
            slope_ref[r, c] = part * (keep * (2.0 * factor))
    gate, up = sums[:, width : width + units], sums[:, width + units :]
    hidden_ref[...] = (jax.nn.gelu(gate, approximate=True) * up).astype(BF)


def decode_kernel(t_ref, codes_ref, source_ref, hidden_ref, w0, w1, w2, w3, o_ref, s_ref):
    t = t_ref[0]
    n = codes_ref.shape[1]
    codes, source, hidden = codes_ref[...], source_ref[...], hidden_ref[...]
    for k, w in enumerate((w0, w1, w2, w3)):
        value = dot(codes, w[:n]) + dot(source, w[n : 2 * n]) - dot(hidden, w[2 * n :])
        s_ref[jnp.bitwise_xor(t, k)] = value
    peers, rows, cols = o_ref.shape
    for h in range(2):
        both = jnp.concatenate([s_ref[2 * h], s_ref[2 * h + 1]], axis=1)
        o_ref[pl.ds(h * peers // 2, peers // 2)] = both.reshape(peers // 2, rows, cols).astype(BF)


def total_kernel(x_ref, o_ref):
    total = jnp.sum(x_ref[...].astype(F32), axis=0).astype(BF)
    o_ref[...] = jnp.broadcast_to(total[None], o_ref.shape)


def back_kernel(t_ref, e_ref, w0, w1, w2, w3, own_ref, prev_ref, err_ref):
    t = t_ref[0]
    peers, rows, cols = e_ref.shape
    n = own_ref.shape[1]
    for h in range(2):
        e = e_ref[pl.ds(h * peers // 2, peers // 2)].astype(F32).reshape(peers // 2 * rows, cols)
        err_ref[2 * h] = e[:, : cols // 2].astype(BF)
        err_ref[2 * h + 1] = e[:, cols // 2 :].astype(BF)
    total = dot(err_ref[t], w0[: 2 * n], 1, 1)
    for k, w in ((1, w1), (2, w2), (3, w3)):
        total += dot(err_ref[jnp.bitwise_xor(t, k)], w[: 2 * n], 1, 1)
    own_ref[...] = total[:, :n]
    prev_ref[...] = total[:, n:].astype(BF)


def decoder_grads_kernel(t_ref, e_ref, c0, c1, c2, c3, own_ref, prev_ref):
    t = t_ref[0]
    n = own_ref.shape[0]
    factor = 1.0 / math.sqrt(4 * e_ref.shape[1])
    total = dot(c0[...], e_ref[t], 0, 0)
    for k, c in ((1, c1), (2, c2), (3, c3)):
        total += dot(c[...], e_ref[jnp.bitwise_xor(t, k)], 0, 0)
    own_ref[...] = total[:n] * factor
    prev_ref[...] = total[n:] * factor


def encoder_grads_kernel(t_ref, n_ref, p0, p1, p2, p3, grad_ref, bias_ref):
    t = t_ref[0]
    total = dot(n_ref[t], p0[...])
    bias = jnp.sum(p0[...].astype(F32), axis=0, keepdims=True)
    for k, p in ((1, p1), (2, p2), (3, p3)):
        total += dot(n_ref[jnp.bitwise_xor(t, k)], p[...])
        bias += jnp.sum(p[...].astype(F32), axis=0, keepdims=True)
    grad_ref[...] = total
    bias_ref[...] = bias


def local(
    resid,
    norm_gain,
    prev_codes,
    feature_mask,
    w_gate,
    w_up,
    w_down,
    enc_weight,
    enc_bias,
    dec_own,
    dec_prev,
):
    height, strip = resid.shape[1:]
    peers = lax.axis_size("feat")
    depth = strip * peers
    width = enc_weight.shape[2]
    units = w_gate.shape[2]
    block = depth // 4
    t = (2 * lax.axis_index("tok_0") + lax.axis_index("tok_1")).astype(jnp.int32).reshape(1)

    (copies,) = call(spread_kernel, (resid[0],), [((peers, 2 * strip, height // 2), BF)])
    gathered = exchange(copies, "feat")
    gains = exchange(jnp.broadcast_to(norm_gain[:, None], (peers, 1, strip)), "feat")
    gain_rows = jnp.broadcast_to(gains.reshape(depth, 1), (depth, 128))

    first = gather4(jnp.concatenate([enc_weight[0], w_gate[0], w_up[0]], axis=1))
    second = gather4(jnp.concatenate([dec_own[0], dec_prev[0], w_down[0]], axis=0))

    turned, codes, slope, hidden = call(
        encode_kernel,
        (t, feature_mask[0], gathered, gain_rows, *first, enc_bias),
        [
            ((4, block, height), BF),
            ((height, width), BF),
            ((height, width), F32),
            ((height, units), BF),
        ],
        [pltpu.VMEM((depth, height), F32)],
    )
    shifted = lax.ppermute(codes, "layer", [(0, 1)])
    source = jnp.where(lax.axis_index("layer") == 0, prev_codes, shifted)
    (parts,) = call(
        decode_kernel,
        (t, codes, source, hidden, *second),
        [((peers, height * 2 // peers, depth // 2), BF)],
        [pltpu.VMEM((4, height, block), F32)],
    )
    arrived = exchange(parts, "feat")
    turned_cols = exchange(turned, TOK)
    both_codes = gather4(jnp.concatenate([codes, source], axis=1))
    (copies,) = call(total_kernel, (arrived,), [(parts.shape, BF)])
    errors = exchange(copies, "feat")
    own_back, prev_back, err = call(
        back_kernel,
        (t, errors, *second),
        [((height, width), F32), ((height, width), BF), ((4, height, block), BF)],
    )
    later = lax.ppermute(prev_back, "layer", [(1, 0)]).astype(F32)
    err_cols = exchange(err, TOK)
    pregrad = gather4(((own_back + later) * slope).astype(BF))
    grad_own, grad_prev = call(
        decoder_grads_kernel,
        (t, err_cols, *both_codes),
        [((width, block), F32), ((width, block), F32)],
    )
    grad_enc, grad_bias = call(
        encoder_grads_kernel,
        (t, turned_cols, *pregrad),
        [((block, width), F32), ((1, width), F32)],
    )
    return (grad_enc[None], grad_bias, grad_own[None], grad_prev[None])


def solution(mesh):
    split = Mesh(
        mesh.devices.reshape(mesh.shape["layer"], mesh.shape["feat"], 2, 2),
        ("layer", "feat", "tok_0", "tok_1"),
    )
    placed = (
        P("layer", TOK, "feat"),
        P("layer", "feat"),
        P(TOK, "feat"),
        P("layer", TOK, "feat"),
        P("layer", TOK, "feat"),
        P("layer", TOK, "feat"),
        P("layer", "feat", TOK),
        P("layer", TOK, "feat"),
        P("layer", "feat"),
        P("layer", "feat", TOK),
        P("layer", "feat", TOK),
    )
    return jax.shard_map(
        local,
        mesh=split,
        in_specs=placed,
        out_specs=(
            P("layer", TOK, "feat"),
            P("layer", "feat"),
            P("layer", "feat", TOK),
            P("layer", "feat", TOK),
        ),
        check_vma=False,
    )
```

time: 278 us -> 264 us (0.950)
  starting transfers between devices: 38.5 us -> 78.1 us
  Pallas kernels: 0 us -> 25.6 us
  matrix products: 21.1 us -> 0 us
  local copies, waits for them, and re-layouts: 38.5 us -> 23.3 us
  blocking collectives: 95.4 us -> 80.3 us
  between operations: 14.4 us -> 1.07 us
  waiting for transfers between devices: 62.1 us -> 51.1 us
  other arithmetic: 6.67 us -> 3.38 us
    ppermute x2 -> x14, starting transfers between devices: 2.99 us -> 44 us  [the longest x12 38.1 us: swap(): return lax.ppermute(x, axis, [(0, 1), (1, 0)])]
    all_to_all x6 -> x4, waiting for transfers between devices: 46.9 us -> 15.1 us  [exchange(): return lax.all_to_all(blocks, axis, split_axis=0, concat_axis=0, tiled=True)]
    pallas_call x0 -> x7, Pallas kernels: none -> 25.6 us  [call(): pl.pallas_call(kernel, out_shape=[jax.ShapeDtypeStruct(s, d) for s, d in...]
    dot_general x10 -> x0, matrix products: 21.1 us -> none  [the longest x2 4.96 us: local(): jnp.dot(normed, segment, preferred_element_type=jnp.float32)]
    ppermute x2 -> x14, waiting for transfers between devices: 15.1 us -> 36 us  [the longest x12 17.2 us: swap(): return lax.ppermute(x, axis, [(0, 1), (1, 0)])]
    all_to_all x4 -> x2, blocking collectives: 95.4 us -> 80.3 us  [exchange(): return lax.all_to_all(blocks, axis, split_axis=0, concat_axis=0, tiled=True)]
    all_to_all x5 -> x1, local copies, waits for them, and re-layouts: 8.47 us -> 1.45 us  [exchange(): return lax.all_to_all(blocks, axis, split_axis=0, concat_axis=0, tiled=True)]
    transpose x3 -> x0, local copies, waits for them, and re-layouts: 6.21 us -> none  [the longest x1 4.3 us: gather_axes(): return in_order(blocks.swapaxes(0, 1).reshape(-1, *array.shape), dim)]
  transfers between devices with their start and end apart: 10 -> 18, of which waited for: 6 -> 7; matrix products, arithmetic and copies ran while one was open for 15% -> 8% of each run, Pallas kernels for 0% -> 6%
where the time goes in v1:
time: 264 us; the launch traced here: 263 us
  blocking collectives  80.3 us (30%)
  starting transfers between devices  78.1 us (30%)
  waiting for transfers between devices  51.1 us (19%)
  Pallas kernels  25.6 us (10%)
  local copies, waits for them, and re-layouts  23.3 us (9%)
  other arithmetic  3.38 us (1%)
    all_to_all x2, blocking collectives, exchange(): return lax.all_to_all(blocks, axis, split_axis=0, concat_axis=0, tiled=True)  80.3 us
    ppermute x12, starting transfers between devices, swap(): return lax.ppermute(x, axis, [(0, 1), (1, 0)])  38.1 us
    all_to_all x4, starting transfers between devices, exchange(): return lax.all_to_all(blocks, axis, split_axis=0, concat_axis=0, tiled=True)  34.1 us
    pallas_call x7, Pallas kernels, call(): pl.pallas_call(kernel, out_shape=[jax.ShapeDtypeStruct(s, d) for s, d in...  25.6 us
    ppermute x12, waiting for transfers between devices, swap(): return lax.ppermute(x, axis, [(0, 1), (1, 0)])  17.2 us
    ppermute x1, waiting for transfers between devices, local(): later = lax.ppermute(prev_back, 'layer', [(1, 0)]).astype(F32)  15.6 us
    all_to_all x4, waiting for transfers between devices, exchange(): return lax.all_to_all(blocks, axis, split_axis=0, concat_axis=0, tiled=True)  15.1 us
    unnamed x59, local copies, waits for them, and re-layouts  8.51 us
  transfers between devices with their start and end apart: 18, of which 7 were waited for; matrix products, arithmetic and copies ran while one was open for 8% of the time, Pallas kernels for 6%

profile of v1, /device:TPU:1, one launch (start us, length us, event | category | flops | bytes accessed | tf_op | source)
XLA Modules:
  0.0 262.9 jit_solution(2762867061646287487)
XLA Ops:
  0.6 1.3 broadcast_in_dim.25
  1.9 17.1 %all-to-all-start.1 = ((bf16[64,1,36]{2,1,0:T(2,128)(2,1)}), bf16[64,1,36]{2,1,0:T(2,128)(2,1)S(1)}, u32[]{:S(2)}, u32[]{:S(2)}) async-start(bf16[64,1,36]{2,1,0:T(2,128)(2,1)} %broadcast_in_dim.25), calls=%async_computation.1 | async-start | bytes 65536 | tf_op jit(solution)/shard_map/all_to_all | solution.py:48
  19.1 1.5 copy.29
  20.5 2.0 shard_map.138
  22.6 7.2 %all-to-all-done.1 = bf16[64,1,36]{2,1,0:T(2,128)(2,1)S(1)} async-done(((bf16[64,1,36]{2,1,0:T(2,128)(2,1)}), bf16[64,1,36]{2,1,0:T(2,128)(2,1)S(1)}, u32[]{:S(2)}, u32[]{:S(2)}) %all-to-all-start.1) | async-done | bytes 4640 | tf_op jit(solution)/shard_map/all_to_all | solution.py:48
  29.8 5.0 %all-to-all-start = ((bf16[64,72,128]{2,1,0:T(8,128)(2,1)}), bf16[64,72,128]{2,1,0:T(8,128)(2,1)S(1)}, u32[]{:S(2)}, u32[]{:S(2)}) async-start(bf16[64,72,128]{2,1,0:T(8,128)(2,1)} %shard_map.138), calls=%async_computation | async-start | bytes 2359296 | tf_op jit(solution)/shard_map/all_to_all | solution.py:48
  35.5 1.2 copy.32
  36.7 3.1 %collective-permute-start.1 = (bf16[576,544]{0,1:T(8,128)(2,1)}, bf16[576,544]{0,1:T(8,128)(2,1)S(1)}, u32[]{:S(2)}, u32[]{:S(2)}) collective-permute-start(bf16[576,544]{0,1:T(8,128)(2,1)} %copy.32), channel_id=1, source_target_pairs={{0,2},{2,0},{1,3},{3,1},{4,6},{6,4},{5,7},{7,5},{8,10},{10,8},{9,1... | collective-permute-start | bytes 1880072 | tf_op jit(solution)/shard_map/ppermute | solution.py:38
  40.0 1.2 copy.37
  41.3 2.2 collective-permute-start.5
  43.5 4.2 %collective-permute-start = (bf16[576,544]{0,1:T(8,128)(2,1)}, bf16[576,544]{0,1:T(8,128)(2,1)}, u32[]{:S(2)}, u32[]{:S(2)}) collective-permute-start(bf16[576,544]{0,1:T(8,128)(2,1)} %copy.32), channel_id=1, source_target_pairs={{0,1},{1,0},{2,3},{3,2},{4,5},{5,4},{6,7},{7,6},{8,9},{9,8},{10,11... | collective-permute-start | bytes 1880072 | tf_op jit(solution)/shard_map/ppermute | solution.py:38
  47.6 6.5 %collective-permute-done.1 = bf16[576,544]{0,1:T(8,128)(2,1)S(1)} collective-permute-done((bf16[576,544]{0,1:T(8,128)(2,1)}, bf16[576,544]{0,1:T(8,128)(2,1)S(1)}, u32[]{:S(2)}, u32[]{:S(2)}) %collective-permute-start.1) | collective-permute-done | bytes 626720 | tf_op jit(solution)/shard_map/ppermute | solution.py:38
  54.2 6.7 %collective-permute-start.2 = (bf16[576,544]{0,1:T(8,128)(2,1)S(1)}, bf16[576,544]{0,1:T(8,128)(2,1)}, u32[]{:S(2)}, u32[]{:S(2)}) collective-permute-start(bf16[576,544]{0,1:T(8,128)(2,1)S(1)} %collective-permute-done.1), channel_id=1, source_target_pairs={{0,1},{1,0},{2,3},{3,2},{4,5},{5,4},{6,7},{7,6},{8,9},{9,8},{10,11... | collective-permute-start | bytes 1880072 | tf_op jit(solution)/shard_map/ppermute | solution.py:38
  60.9 1.9 collective-permute-start.4
  62.9 9.3 %collective-permute-done.5.w2 = bf16[656,576]{1,0:T(8,128)(2,1)S(1)} collective-permute-done((bf16[656,576]{1,0:T(8,128)(2,1)S(1)}, bf16[656,576]{1,0:T(8,128)(2,1)S(1)}, u32[]{:S(2)}, u32[]{:S(2)}) %collective-permute-start.5) | collective-permute-done | bytes 755744 | tf_op jit(solution)/shard_map/ppermute | solution.py:38
  72.2 4.5 %collective-permute-start.6 = (bf16[656,576]{1,0:T(8,128)(2,1)S(1)}, bf16[656,576]{1,0:T(8,128)(2,1)}, u32[]{:S(2)}, u32[]{:S(2)}) collective-permute-start(bf16[656,576]{1,0:T(8,128)(2,1)S(1)} %collective-permute-done.5.w2), channel_id=1, source_target_pairs={{0,1},{1,0},{2,3},{3,2},{4,5},{5,4},{6,7},{7,6},{8,9},{9,8},{10,11... | collective-permute-start | bytes 2267144 | tf_op jit(solution)/shard_map/ppermute | solution.py:38
  76.7 1.5 reduce
  78.2 1.4 broadcast_in_dim.26
  79.6 1.2 copy.35.w2
  80.8 2.3 copy.34.w1
  83.2 2.3 copy.36.w3
  85.5 1.2 broadcast_in_dim.27.gain_ref
  86.7 5.2 %shard_map.139 = (bf16[4,576,256]{2,1,0:T(8,128)(2,1)}, bf16[256,256]{1,0:T(8,128)(2,1)}, f32[256,256]{1,0:T(8,128)}, bf16[256,144]{1,0:T(8,128)(2,1)}) custom-call(s32[1]{0:T(128)} %bitcast.t_ref, s32[2,2]{1,0:T(2,128)} %bitcast.22, bf16[64,72,128]{2,1,0:T(8,128)(2,1)} %copy-done.3, bf16[2304,128]{1,0:T(8,128)(2,1)} %broadcast_in_dim.27.gain_ref, ...), custom_call_target="tpu_custom_call" | custom-call | tf_op jit(solution)/shard_map/pallas_call | solution.py:23
  91.9 4.6 %collective-permute-start.3 = (bf16[256,256]{1,0:T(8,128)(2,1)}, bf16[256,256]{1,0:T(8,128)(2,1)S(1)}, u32[]{:S(2)}, u32[]{:S(2)}) collective-permute-start(bf16[256,256]{1,0:T(8,128)(2,1)} %get-tuple-element.16.codes_ref), channel_id=1, source_target_pairs={{0,256},{1,257},{2,258},{3,259},{4,260},{5,261},{6,262},{7,263},{8... | collective-permute-start | bytes 393224 | tf_op jit(solution)/shard_map/ppermute | solution.py:198
  96.6 3.2 %collective-permute-done.3 = bf16[256,256]{1,0:T(8,128)(2,1)S(1)} collective-permute-done((bf16[256,256]{1,0:T(8,128)(2,1)}, bf16[256,256]{1,0:T(8,128)(2,1)S(1)}, u32[]{:S(2)}, u32[]{:S(2)}) %collective-permute-start.3) | collective-permute-done | bytes 131104 | tf_op jit(solution)/shard_map/ppermute | solution.py:198
  100.4 4.8 %shard_map.140 = bf16[64,8,1152]{2,1,0:T(8,128)(2,1)} custom-call(s32[1]{0:T(128)} %bitcast.t_ref, bf16[256,256]{1,0:T(8,128)(2,1)} %get-tuple-element.16.codes_ref, bf16[256,256]{1,0:T(8,128)(2,1)} %broadcast_select_fusion.source_ref, bf16[256,144]{1,0:T(8,128)(2,1)} %get-tuple-element.17.hidden_ref, bf16[656,576]{1,0:T(8,128)(2,1)} %copy-done, ...), custom_call_target="tpu_custom_call" | custom-call | tf_op jit(solution)/shard_map/pallas_call | solution.py:23
  105.2 41.6 %all_to_all.30.x_ref = bf16[64,8,1152]{2,1,0:T(8,128)(2,1)} all-to-all(bf16[64,8,1152]{2,1,0:T(8,128)(2,1)} %shard_map.140), channel_id=1, replica_groups=mesh['layer'=2,'feat'=64,'tok_0'=2,'tok_1'=2] {'feat'}, dimensions={0} | all-to-all | bytes 2359296 | tf_op jit(solution)/shard_map/all_to_all | solution.py:48
  146.8 2.5 shard_map.141
  149.3 38.7 %all_to_all.31.e_ref = bf16[64,8,1152]{2,1,0:T(8,128)(2,1)} all-to-all(bf16[64,8,1152]{2,1,0:T(8,128)(2,1)} %shard_map.141), channel_id=1, replica_groups=mesh['layer'=2,'feat'=64,'tok_0'=2,'tok_1'=2] {'feat'}, dimensions={0} | all-to-all | bytes 2359296 | tf_op jit(solution)/shard_map/all_to_all | solution.py:48
  188.0 7.6 %all-to-all-start.2 = ((bf16[4,576,256]{2,1,0:T(8,128)(2,1)}), bf16[4,576,256]{2,1,0:T(8,128)(2,1)S(1)}, u32[]{:S(2)}, u32[]{:S(2)}) async-start(bf16[4,576,256]{2,1,0:T(8,128)(2,1)} %get-tuple-element.15), calls=%async_computation.2 | async-start | bytes 2359296 | tf_op jit(solution)/shard_map/all_to_all | solution.py:48
  195.6 4.7 %shard_map.142 = (f32[256,256]{1,0:T(8,128)}, bf16[256,256]{1,0:T(8,128)(2,1)}, bf16[4,256,576]{2,1,0:T(8,128)(2,1)}) custom-call(s32[1]{0:T(128)} %bitcast.t_ref, bf16[64,8,1152]{2,1,0:T(8,128)(2,1)} %all_to_all.31.e_ref, bf16[656,576]{1,0:T(8,128)(2,1)} %copy-done, bf16[656,576]{1,0:T(8,128)(2,1)} %collective-permute-done.4.w1, ...), custom_call_target="tpu_custom_call" | custom-call | tf_op jit(solution)/shard_map/pallas_call | solution.py:23
  200.3 2.4 copy.39
  202.7 7.9 %all-to-all-done.2.n_ref = bf16[4,576,256]{2,1,0:T(8,128)(2,1)S(1)} async-done(((bf16[4,576,256]{2,1,0:T(8,128)(2,1)}), bf16[4,576,256]{2,1,0:T(8,128)(2,1)S(1)}, u32[]{:S(2)}, u32[]{:S(2)}) %all-to-all-start.2) | async-done | bytes 1179680 | tf_op jit(solution)/shard_map/all_to_all | solution.py:48
  210.6 4.4 %all-to-all-start.5 = ((bf16[4,256,576]{1,2,0:T(8,128)(2,1)}), bf16[4,256,576]{1,2,0:T(8,128)(2,1)S(1)}, u32[]{:S(2)}, u32[]{:S(2)}) async-start(bf16[4,256,576]{1,2,0:T(8,128)(2,1)} %copy.39), calls=%async_computation.5 | async-start | bytes 2359296 | tf_op jit(solution)/shard_map/all_to_all | solution.py:48
  214.9 1.3 collective-permute-start.7
  216.3 3.3 %collective-permute-start.12 = (bf16[256,512]{1,0:T(8,128)(2,1)S(1)}, bf16[256,512]{1,0:T(8,128)(2,1)S(1)}, u32[]{:S(2)}, u32[]{:S(2)}) collective-permute-start(bf16[256,512]{1,0:T(8,128)(2,1)S(1)} %pad_maximum_fusion.2.c0), channel_id=1, source_target_pairs={{0,2},{2,0},{1,3},{3,1},{4,6},{6,4},{5,7},{7,5},{8,10},{10,8},{9,1... | collective-permute-start | bytes 786440 | tf_op jit(solution)/shard_map/ppermute | solution.py:38
  219.6 15.6 %collective-permute-done.7 = bf16[256,256]{1,0:T(8,128)(2,1)S(1)} collective-permute-done((bf16[256,256]{1,0:T(8,128)(2,1)S(1)}, bf16[256,256]{1,0:T(8,128)(2,1)S(1)}, u32[]{:S(2)}, u32[]{:S(2)}) %collective-permute-start.7) | collective-permute-done | bytes 131104 | tf_op jit(solution)/shard_map/ppermute | solution.py:216
  236.3 2.4 collective-permute-start.9
  238.7 3.5 %collective-permute-start.11 = (bf16[256,512]{1,0:T(8,128)(2,1)S(1)}, bf16[256,512]{1,0:T(8,128)(2,1)S(1)}, u32[]{:S(2)}, u32[]{:S(2)}) collective-permute-start(bf16[256,512]{1,0:T(8,128)(2,1)S(1)} %pad_maximum_fusion.2.c0), channel_id=1, source_target_pairs={{0,1},{1,0},{2,3},{3,2},{4,5},{5,4},{6,7},{7,6},{8,9},{9,8},{10,11... | collective-permute-start | bytes 786440 | tf_op jit(solution)/shard_map/ppermute | solution.py:38
  242.2 1.9 collective-permute-start.13
  244.2 2.4 collective-permute-start.8
  246.6 1.9 collective-permute-start.10
  248.6 1.3 collective-permute-done.10.p3
  250.5 2.7 %shard_map.143 = (f32[576,256]{1,0:T(8,128)}, f32[1,256]{1,0:T(1,128)}) custom-call(s32[1]{0:T(128)} %bitcast.t_ref, bf16[4,576,256]{2,1,0:T(8,128)(2,1)} %copy-done.2, bf16[256,256]{1,0:T(8,128)(2,1)} %copy-done.9, bf16[256,256]{1,0:T(8,128)(2,1)} %copy-done.20, bf16[256,256]{1,0:T(8,128)(2,1)} %copy-done.19, bf16[256,256]{1,0:T(8,128)(2,1)} %copy-done.21), custom_call_target="tpu_custom_call" | custom-call | tf_op jit(solution)/shard_map/pallas_call | solution.py:23
  253.2 1.4 copy.40.e_ref
  256.1 3.6 %shard_map.144 = (f32[256,576]{1,0:T(8,128)}, f32[256,576]{1,0:T(8,128)}) custom-call(s32[1]{0:T(128)} %bitcast.t_ref, bf16[4,256,576]{2,1,0:T(8,128)(2,1)} %copy.40.e_ref, bf16[256,512]{1,0:T(8,128)(2,1)} %copy-done.6, bf16[256,512]{1,0:T(8,128)(2,1)} %copy-done.14, bf16[256,512]{1,0:T(8,128)(2,1)} %copy-done.13, bf16[256,512]{1,0:T(8,128)(2,1)} %copy-done.15), custom_call_target="tpu_custom_call" | custom-call | tf_op jit(solution)/shard_map/pallas_call | solution.py:23
  259.7 2.2 copy.41
  261.9 1.0 copy.42
  (71 shorter events, 4.6 us)
Async XLA Ops:
  1.9 27.9 %all-to-all-start.1 = ((bf16[64,1,36]{2,1,0:T(2,128)(2,1)}), bf16[64,1,36]{2,1,0:T(2,128)(2,1)S(1)}, u32[]{:S(2)}, u32[]{:S(2)}) async-start(bf16[64,1,36]{2,1,0:T(2,128)(2,1)} %broadcast_in_dim.25), calls=%async_computation.1 | async-start | bytes 65536 | tf_op jit(solution)/shard_map/all_to_all | solution.py:48
  22.6 12.3 %copy-start.17 = (bf16[1,576,144]{1,2,0:T(8,128)(2,1)S(1)}, bf16[1,576,144]{1,2,0:T(8,128)(2,1)}, u32[]{:S(2)}) copy-start(bf16[1,576,144]{1,2,0:T(8,128)(2,1)} %param.16) | copy-start | bytes 497668
  22.6 12.5 %copy-start.18 = (bf16[1,576,144]{1,2,0:T(8,128)(2,1)S(1)}, bf16[1,576,144]{1,2,0:T(8,128)(2,1)}, u32[]{:S(2)}) copy-start(bf16[1,576,144]{1,2,0:T(8,128)(2,1)} %param.15) | copy-start | bytes 497668
  22.6 12.7 %copy-start.10 = (bf16[1,576,256]{2,1,0:T(8,128)(2,1)S(1)}, bf16[1,576,256]{2,1,0:T(8,128)(2,1)}, u32[]{:S(2)}) copy-start(bf16[1,576,256]{2,1,0:T(8,128)(2,1)} %param.18) | copy-start | bytes 884740
  29.8 5.1 %copy-start.23 = (bf16[64,1,36]{2,1,0:T(2,128)(2,1)}, bf16[64,1,36]{2,1,0:T(2,128)(2,1)S(1)}, u32[]{:S(2)}) copy-start(bf16[64,1,36]{2,1,0:T(2,128)(2,1)S(1)} %all-to-all-done.1) | copy-start | bytes 13828
  29.8 55.6 %all-to-all-start = ((bf16[64,72,128]{2,1,0:T(8,128)(2,1)}), bf16[64,72,128]{2,1,0:T(8,128)(2,1)S(1)}, u32[]{:S(2)}, u32[]{:S(2)}) async-start(bf16[64,72,128]{2,1,0:T(8,128)(2,1)} %shard_map.138), calls=%async_computation | async-start | bytes 2359296 | tf_op jit(solution)/shard_map/all_to_all | solution.py:48
  35.4 5.8 %copy-start.1 = (bf16[576,544]{1,0:T(8,128)(2,1)}, bf16[576,544]{1,0:T(8,128)(2,1)S(1)}, u32[]{:S(2)}) copy-start(bf16[576,544]{1,0:T(8,128)(2,1)S(1)} %pad_maximum_fusion.1.w0) | copy-start | bytes 1880068
  35.4 4.4 %copy-start.11 = (bf16[1,256,576]{1,2,0:T(8,128)(2,1)S(1)}, bf16[1,256,576]{1,2,0:T(8,128)(2,1)}, u32[]{:S(2)}) copy-start(bf16[1,256,576]{1,2,0:T(8,128)(2,1)} %param.21) | copy-start | bytes 884740
  35.5 5.7 %copy-start.16 = (bf16[1,144,576]{2,1,0:T(8,128)(2,1)S(1)}, bf16[1,144,576]{2,1,0:T(8,128)(2,1)}, u32[]{:S(2)}) copy-start(bf16[1,144,576]{2,1,0:T(8,128)(2,1)} %param.17) | copy-start | bytes 497668
  36.7 17.5 %collective-permute-start.1 = (bf16[576,544]{0,1:T(8,128)(2,1)}, bf16[576,544]{0,1:T(8,128)(2,1)S(1)}, u32[]{:S(2)}, u32[]{:S(2)}) collective-permute-start(bf16[576,544]{0,1:T(8,128)(2,1)} %copy.32), channel_id=1, source_target_pairs={{0,2},{2,0},{1,3},{3,1},{4,6},{6,4},{5,7},{7,5},{8,10},{10,8},{9,1... | collective-permute-start | bytes 1880072 | tf_op jit(solution)/shard_map/ppermute | solution.py:38
  41.3 41.9 %copy-start = (bf16[656,576]{1,0:T(8,128)(2,1)}, bf16[656,576]{1,0:T(8,128)(2,1)S(1)}, u32[]{:S(2)}) copy-start(bf16[656,576]{1,0:T(8,128)(2,1)S(1)} %pad_maximum_fusion.w0) | copy-start | bytes 2267140
  41.3 30.9 %collective-permute-start.5 = (bf16[656,576]{1,0:T(8,128)(2,1)S(1)}, bf16[656,576]{1,0:T(8,128)(2,1)S(1)}, u32[]{:S(2)}, u32[]{:S(2)}) collective-permute-start(bf16[656,576]{1,0:T(8,128)(2,1)S(1)} %pad_maximum_fusion.w0), channel_id=1, source_target_pairs={{0,2},{2,0},{1,3},{3,1},{4,6},{6,4},{5,7},{7,5},{8,10},{10,8},{9,1... | collective-permute-start | bytes 2267144 | tf_op jit(solution)/shard_map/ppermute | solution.py:38
  43.5 37.4 %collective-permute-start = (bf16[576,544]{0,1:T(8,128)(2,1)}, bf16[576,544]{0,1:T(8,128)(2,1)}, u32[]{:S(2)}, u32[]{:S(2)}) collective-permute-start(bf16[576,544]{0,1:T(8,128)(2,1)} %copy.32), channel_id=1, source_target_pairs={{0,1},{1,0},{2,3},{3,2},{4,5},{5,4},{6,7},{7,6},{8,9},{9,8},{10,11... | collective-permute-start | bytes 1880072 | tf_op jit(solution)/shard_map/ppermute | solution.py:38
  54.2 29.0 %collective-permute-start.2 = (bf16[576,544]{0,1:T(8,128)(2,1)S(1)}, bf16[576,544]{0,1:T(8,128)(2,1)}, u32[]{:S(2)}, u32[]{:S(2)}) collective-permute-start(bf16[576,544]{0,1:T(8,128)(2,1)S(1)} %collective-permute-done.1), channel_id=1, source_target_pairs={{0,1},{1,0},{2,3},{3,2},{4,5},{5,4},{6,7},{7,6},{8,9},{9,8},{10,11... | collective-permute-start | bytes 1880072 | tf_op jit(solution)/shard_map/ppermute | solution.py:38
  60.9 39.5 %collective-permute-start.4 = (bf16[656,576]{1,0:T(8,128)(2,1)S(1)}, bf16[656,576]{1,0:T(8,128)(2,1)}, u32[]{:S(2)}, u32[]{:S(2)}) collective-permute-start(bf16[656,576]{1,0:T(8,128)(2,1)S(1)} %pad_maximum_fusion.w0), channel_id=1, source_target_pairs={{0,1},{1,0},{2,3},{3,2},{4,5},{5,4},{6,7},{7,6},{8,9},{9,8},{10,11... | collective-permute-start | bytes 2267144 | tf_op jit(solution)/shard_map/ppermute | solution.py:38
  72.2 11.0 %copy-start.4 = (bf16[656,576]{1,0:T(8,128)(2,1)}, bf16[656,576]{1,0:T(8,128)(2,1)S(1)}, u32[]{:S(2)}) copy-start(bf16[656,576]{1,0:T(8,128)(2,1)S(1)} %collective-permute-done.5.w2) | copy-start | bytes 2267140
  72.2 28.3 %collective-permute-start.6 = (bf16[656,576]{1,0:T(8,128)(2,1)S(1)}, bf16[656,576]{1,0:T(8,128)(2,1)}, u32[]{:S(2)}, u32[]{:S(2)}) collective-permute-start(bf16[656,576]{1,0:T(8,128)(2,1)S(1)} %collective-permute-done.5.w2), channel_id=1, source_target_pairs={{0,1},{1,0},{2,3},{3,2},{4,5},{5,4},{6,7},{7,6},{8,9},{9,8},{10,11... | collective-permute-start | bytes 2267144 | tf_op jit(solution)/shard_map/ppermute | solution.py:38
  83.2 2.3 copy-start.24
  85.4 1.2 copy-start.3
  86.7 13.1 %copy-start.22 = (bf16[256,256]{1,0:T(8,128)(2,1)S(1)}, bf16[256,256]{1,0:T(8,128)(2,1)}, u32[]{:S(2)}) copy-start(bf16[256,256]{1,0:T(8,128)(2,1)} %param.13) | copy-start | bytes 393220
  91.9 7.9 %collective-permute-start.3 = (bf16[256,256]{1,0:T(8,128)(2,1)}, bf16[256,256]{1,0:T(8,128)(2,1)S(1)}, u32[]{:S(2)}, u32[]{:S(2)}) collective-permute-start(bf16[256,256]{1,0:T(8,128)(2,1)} %get-tuple-element.16.codes_ref), channel_id=1, source_target_pairs={{0,256},{1,257},{2,258},{3,259},{4,260},{5,261},{6,262},{7,263},{8... | collective-permute-start | bytes 393224 | tf_op jit(solution)/shard_map/ppermute | solution.py:198
  188.0 22.6 %all-to-all-start.2 = ((bf16[4,576,256]{2,1,0:T(8,128)(2,1)}), bf16[4,576,256]{2,1,0:T(8,128)(2,1)S(1)}, u32[]{:S(2)}, u32[]{:S(2)}) async-start(bf16[4,576,256]{2,1,0:T(8,128)(2,1)} %get-tuple-element.15), calls=%async_computation.2 | async-start | bytes 2359296 | tf_op jit(solution)/shard_map/all_to_all | solution.py:48
  202.7 12.3 %copy-start.25 = (bf16[256,256]{1,0:T(8,128)(2,1)S(1)}, bf16[256,256]{1,0:T(8,128)(2,1)}, u32[]{:S(2)}) copy-start(bf16[256,256]{1,0:T(8,128)(2,1)} %get-tuple-element.19) | copy-start | bytes 393220
  202.7 13.5 %copy-start.5 = (bf16[256,256]{1,0:T(8,128)(2,1)S(1)}, bf16[256,256]{1,0:T(8,128)(2,1)}, u32[]{:S(2)}) copy-start(bf16[256,256]{1,0:T(8,128)(2,1)} %broadcast_select_fusion.source_ref) | copy-start | bytes 393220
  202.7 13.6 %copy-start.8 = (bf16[256,256]{1,0:T(8,128)(2,1)S(1)}, bf16[256,256]{1,0:T(8,128)(2,1)}, u32[]{:S(2)}) copy-start(bf16[256,256]{1,0:T(8,128)(2,1)} %get-tuple-element.16.codes_ref) | copy-start | bytes 393220
  202.7 32.5 %copy-start.12 = (f32[256,256]{1,0:T(8,128)S(1)}, f32[256,256]{1,0:T(8,128)}, u32[]{:S(2)}) copy-start(f32[256,256]{1,0:T(8,128)} %get-tuple-element.20) | copy-start | bytes 786436
  210.6 5.7 %copy-start.2 = (bf16[4,576,256]{2,1,0:T(8,128)(2,1)}, bf16[4,576,256]{2,1,0:T(8,128)(2,1)S(1)}, u32[]{:S(2)}) copy-start(bf16[4,576,256]{2,1,0:T(8,128)(2,1)S(1)} %all-to-all-done.2.n_ref) | copy-start | bytes 3538948
  210.6 42.7 %all-to-all-start.5 = ((bf16[4,256,576]{1,2,0:T(8,128)(2,1)}), bf16[4,256,576]{1,2,0:T(8,128)(2,1)S(1)}, u32[]{:S(2)}, u32[]{:S(2)}) async-start(bf16[4,256,576]{1,2,0:T(8,128)(2,1)} %copy.39), calls=%async_computation.5 | async-start | bytes 2359296 | tf_op jit(solution)/shard_map/all_to_all | solution.py:48
  214.9 20.3 %collective-permute-start.7 = (bf16[256,256]{1,0:T(8,128)(2,1)S(1)}, bf16[256,256]{1,0:T(8,128)(2,1)S(1)}, u32[]{:S(2)}, u32[]{:S(2)}) collective-permute-start(bf16[256,256]{1,0:T(8,128)(2,1)S(1)} %copy-done.25), channel_id=1, source_target_pairs={{256,0},{257,1},{258,2},{259,3},{260,4},{261,5},{262,6},{263,7},{2... | collective-permute-start | bytes 393224 | tf_op jit(solution)/shard_map/ppermute | solution.py:216
  216.3 38.4 %copy-start.6 = (bf16[256,512]{1,0:T(8,128)(2,1)}, bf16[256,512]{1,0:T(8,128)(2,1)S(1)}, u32[]{:S(2)}) copy-start(bf16[256,512]{1,0:T(8,128)(2,1)S(1)} %pad_maximum_fusion.2.c0) | copy-start | bytes 786436
  216.3 25.9 %collective-permute-start.12 = (bf16[256,512]{1,0:T(8,128)(2,1)S(1)}, bf16[256,512]{1,0:T(8,128)(2,1)S(1)}, u32[]{:S(2)}, u32[]{:S(2)}) collective-permute-start(bf16[256,512]{1,0:T(8,128)(2,1)S(1)} %pad_maximum_fusion.2.c0), channel_id=1, source_target_pairs={{0,2},{2,0},{1,3},{3,1},{4,6},{6,4},{5,7},{7,5},{8,10},{10,8},{9,1... | collective-permute-start | bytes 786440 | tf_op jit(solution)/shard_map/ppermute | solution.py:38
  236.2 13.6 %copy-start.9 = (bf16[256,256]{1,0:T(8,128)(2,1)}, bf16[256,256]{1,0:T(8,128)(2,1)S(1)}, u32[]{:S(2)}) copy-start(bf16[256,256]{1,0:T(8,128)(2,1)S(1)} %multiply_convert_fusion.p0) | copy-start | bytes 393220
  236.3 10.3 %collective-permute-start.9 = (bf16[256,256]{1,0:T(8,128)(2,1)S(1)}, bf16[256,256]{1,0:T(8,128)(2,1)S(1)}, u32[]{:S(2)}, u32[]{:S(2)}) collective-permute-start(bf16[256,256]{1,0:T(8,128)(2,1)S(1)} %multiply_convert_fusion.p0), channel_id=1, source_target_pairs={{0,2},{2,0},{1,3},{3,1},{4,6},{6,4},{5,7},{7,5},{8,10},{10,8},{9,1... | collective-permute-start | bytes 393224 | tf_op jit(solution)/shard_map/ppermute | solution.py:38
  238.7 16.0 %collective-permute-start.11 = (bf16[256,512]{1,0:T(8,128)(2,1)S(1)}, bf16[256,512]{1,0:T(8,128)(2,1)S(1)}, u32[]{:S(2)}, u32[]{:S(2)}) collective-permute-start(bf16[256,512]{1,0:T(8,128)(2,1)S(1)} %pad_maximum_fusion.2.c0), channel_id=1, source_target_pairs={{0,1},{1,0},{2,3},{3,2},{4,5},{5,4},{6,7},{7,6},{8,9},{9,8},{10,11... | collective-permute-start | bytes 786440 | tf_op jit(solution)/shard_map/ppermute | solution.py:38
  242.2 12.5 %copy-start.13 = (bf16[256,512]{1,0:T(8,128)(2,1)}, bf16[256,512]{1,0:T(8,128)(2,1)S(1)}, u32[]{:S(2)}) copy-start(bf16[256,512]{1,0:T(8,128)(2,1)S(1)} %collective-permute-done.12.c2) | copy-start | bytes 786436
  242.2 12.5 %collective-permute-start.13 = (bf16[256,512]{1,0:T(8,128)(2,1)S(1)}, bf16[256,512]{1,0:T(8,128)(2,1)S(1)}, u32[]{:S(2)}, u32[]{:S(2)}) collective-permute-start(bf16[256,512]{1,0:T(8,128)(2,1)S(1)} %collective-permute-done.12.c2), channel_id=1, source_target_pairs={{0,1},{1,0},{2,3},{3,2},{4,5},{5,4},{6,7},{7,6},{8,9},{9,8},{10,11... | collective-permute-start | bytes 786440 | tf_op jit(solution)/shard_map/ppermute | solution.py:38
  244.2 4.4 %collective-permute-start.8 = (bf16[256,256]{1,0:T(8,128)(2,1)S(1)}, bf16[256,256]{1,0:T(8,128)(2,1)S(1)}, u32[]{:S(2)}, u32[]{:S(2)}) collective-permute-start(bf16[256,256]{1,0:T(8,128)(2,1)S(1)} %multiply_convert_fusion.p0), channel_id=1, source_target_pairs={{0,1},{1,0},{2,3},{3,2},{4,5},{5,4},{6,7},{7,6},{8,9},{9,8},{10,11... | collective-permute-start | bytes 393224 | tf_op jit(solution)/shard_map/ppermute | solution.py:38
  246.6 3.3 %copy-start.19 = (bf16[256,256]{1,0:T(8,128)(2,1)}, bf16[256,256]{1,0:T(8,128)(2,1)S(1)}, u32[]{:S(2)}) copy-start(bf16[256,256]{1,0:T(8,128)(2,1)S(1)} %collective-permute-done.9.p2) | copy-start | bytes 393220
  246.6 3.2 %collective-permute-start.10 = (bf16[256,256]{1,0:T(8,128)(2,1)S(1)}, bf16[256,256]{1,0:T(8,128)(2,1)S(1)}, u32[]{:S(2)}, u32[]{:S(2)}) collective-permute-start(bf16[256,256]{1,0:T(8,128)(2,1)S(1)} %collective-permute-done.9.p2), channel_id=1, source_target_pairs={{0,1},{1,0},{2,3},{3,2},{4,5},{5,4},{6,7},{7,6},{8,9},{9,8},{10,11... | collective-permute-start | bytes 393224 | tf_op jit(solution)/shard_map/ppermute | solution.py:38
  248.5 1.3 copy-start.20
  249.9 0.7 copy-start.21
  254.7 0.7 copy-start.14
  255.4 0.7 copy-start.15
  259.7 2.2 copy-start.7

commit v2 on v1

v2 whole, which is shorter than its diff:
```python
import math

import jax
import jax.numpy as jnp
from jax import lax
from jax.experimental import pallas as pl
from jax.experimental.pallas import tpu as pltpu
from jax.sharding import Mesh
from jax.sharding import PartitionSpec as P

TILE = 128
TBLK = 128
BF = jnp.bfloat16
F32 = jnp.float32
TOK = ("tok_0", "tok_1")
PARAMS = pltpu.CompilerParams(vmem_limit_bytes=56 * 1024 * 1024)
VM = pl.BlockSpec(memory_space=pltpu.VMEM)
SM = pl.BlockSpec(memory_space=pltpu.SMEM)


ANY = pl.BlockSpec(memory_space=pl.ANY)
PITCH = 40
ROWS = 72


def call(kernel, ins, outs, scratch=(), after=()):
    specs = [SM if a.dtype == jnp.int32 else VM for a in ins] + [ANY] * len(after)
    count = len(ins)

    def body(*refs):
        kernel(*refs[:count], *refs[count + len(after) :])

    return pl.pallas_call(
        body,
        out_shape=[jax.ShapeDtypeStruct(s, d) for s, d in outs],
        in_specs=specs,
        out_specs=[VM] * len(outs),
        scratch_shapes=list(scratch),
        compiler_params=PARAMS,
        name=kernel.__name__,
    )(*ins, *after)


def dot(a, b, ca=1, cb=0):
    return lax.dot_general(a, b, (((ca,), (cb,)), ((), ())), preferred_element_type=F32)


def toward(x, k):
    return lax.ppermute(x, TOK, [(i, i ^ k) for i in range(4)])


def gather4(x):
    far = toward(x, 2)
    return [x, toward(x, 1), far, toward(far, 1)]


def exchange4(blocks):
    return [blocks[0]] + [toward(blocks[k], k) for k in (1, 2, 3)]


def exchange(blocks):
    return lax.all_to_all(blocks, "feat", split_axis=0, concat_axis=0, tiled=True)


def spread_kernel(x_ref, gain_ref, o_ref):
    strip, height = x_ref.shape
    lanes = height // 2
    x = x_ref[...].astype(F32)
    gain = gain_ref[...].astype(F32)
    row = jnp.concatenate([gain, jnp.zeros((1, lanes - strip), F32)], axis=1)
    rest = jnp.zeros((PITCH - strip - 1, lanes), F32)
    parts = [x[:, :lanes], row, rest, x[:, lanes:], row, rest]
    o_ref[...] = jnp.broadcast_to(jnp.concatenate(parts, axis=0).astype(BF)[None], o_ref.shape)


def put_wide(o_ref, at, w):
    rows, cols = w.shape
    for c in range(0, cols, 128):
        wide = min(128, cols - c)
        o_ref[pl.ds(at, rows), pl.ds(0, wide)] = w[:, c : c + wide]
        at += rows
    return at


def get_wide(w_ref, at, rows, cols):
    pieces = [
        w_ref[pl.ds(at + rows * i, rows), : min(128, cols - 128 * i)] for i in range(-(-cols // 128))
    ]
    return jnp.concatenate(pieces, axis=1)


def pack_kernel(enc, gate, up, own, prev, down, before, first_ref, second_ref, before_ref):
    at = 0
    for w in (enc, gate, up):
        at = put_wide(first_ref, at, w[...])
    at = 0
    for w in (own, prev, down):
        at = put_wide(second_ref, at, w[...])
    before_ref[...] = before[...].astype(F32).T.astype(BF)


def encode_kernel(
    t_ref, mask_ref, g_ref, w0, w1, w2, w3, bias_ref,
    n0, n1, n2, n3, codes_ref, slope_ref, hidden_ref, x_ref,
):
    feats, _, lanes = g_ref.shape
    height = 2 * lanes
    block = n0.shape[0]
    strip = 4 * block // feats
    depth = feats * strip
    width = codes_ref.shape[0]
    units = hidden_ref.shape[0]
    gains = g_ref[:, strip, :].astype(F32).T
    total = jnp.zeros((8, height), F32)
    for f in range(feats):
        x = jnp.concatenate(
            [g_ref[f, pl.ds(0, strip), :], g_ref[f, pl.ds(PITCH, strip), :]], axis=1
        ).astype(F32)
        square = x * x
        for r in range(0, strip - 7, 8):
            total = total + square[r : r + 8]
        tail = square[strip // 8 * 8 :]
        total = total + jnp.concatenate([tail, jnp.zeros_like(tail)], axis=0)
        x_ref[pl.ds(f * strip, strip), :] = x * gains[:strip, f : f + 1]
    total = jnp.sum(total, axis=0, keepdims=True)
    scale = lax.rsqrt(total / depth + 1e-06)
    t = t_ref[0]
    sums = gate = up = 0.0
    for k, (n_ref, w) in enumerate(((n0, w0), (n1, w1), (n2, w2), (n3, w3))):
        at = pl.ds(pl.multiple_of(jnp.bitwise_xor(t, k) * block, 64), block)
        n = (x_ref[at, :] * scale).astype(BF)
        n_ref[...] = n
        sums += dot(get_wide(w, 0, block, width), n, 0, 0)
        base = block * width // 128
        gate += dot(get_wide(w, base, units, block), n)
        up += dot(get_wide(w, base + units * (-(-block // 128)), units, block), n)
    bias = jnp.broadcast_to(bias_ref[...], (128, width)).T
    factor = 1.0 / math.sqrt(4 * height)
    for j in range(width // TILE):
        for i in range(height // TBLK):
            keep = mask_ref[i, j].astype(F32)
            r, c = slice(j * TILE, (j + 1) * TILE), slice(i * TBLK, (i + 1) * TBLK)
            part = jnp.maximum(sums[r, c] + bias[r, :], 0.0)
            codes_ref[r, c] = (part * part * keep).astype(BF)
            slope_ref[r, c] = part * (keep * (2.0 * factor))
    hidden_ref[...] = (jax.nn.gelu(gate, approximate=True) * up).astype(BF)


def decode_kernel(
    t_ref, codes_ref, before_ref, shifted_ref, hidden_ref, w0, w1, w2, w3, o_ref, both_ref
):
    t, layer = t_ref[0], t_ref[1]
    n = codes_ref.shape[0]
    units = hidden_ref.shape[0]
    block = o_ref.shape[0] * ROWS // 8
    both_ref[:n] = codes_ref[...]

    @pl.when(layer == 0)
    def _():
        both_ref[n:] = before_ref[...]

    @pl.when(layer != 0)
    def _():
        both_ref[n:] = shifted_ref[...]

    both, hidden = both_ref[...], hidden_ref[...]
    peers, rows, lanes = o_ref.shape
    each = block // rows
    for k, w in enumerate((w0, w1, w2, w3)):
        decoder = jnp.concatenate(
            [get_wide(w, 0, block, n), get_wide(w, block * n // 128, block, n)], axis=1
        )
        down = get_wide(w, 2 * block * n // 128, units, block)
        value = dot(decoder, both) - dot(down, hidden, 0, 0)
        spot = jnp.bitwise_xor(t, k) * each
        for i in range(each):
            for h in range(2):
                o_ref[spot + (h * peers // 2 + i)] = value[
                    i * rows : (i + 1) * rows, h * lanes : (h + 1) * lanes
                ].astype(BF)


def total_kernel(x_ref, o_ref):
    total = jnp.sum(x_ref[...].astype(F32), axis=0).astype(BF)
    o_ref[...] = jnp.broadcast_to(total[None], o_ref.shape)


def back_kernel(t_ref, e_ref, w0, w1, w2, w3, own_ref, prev_ref, e0, e1, e2, e3):
    t = t_ref[0]
    peers, rows, lanes = e_ref.shape
    n = own_ref.shape[0]
    block = e0.shape[0]
    each = block // rows
    total = 0.0
    for k, (err_ref, w) in enumerate(((e0, w0), (e1, w1), (e2, w2), (e3, w3))):
        spot = jnp.bitwise_xor(t, k) * each
        half = [
            jnp.concatenate(
                [e_ref[spot + (h * peers // 2 + i)].astype(F32) for i in range(each)], axis=0
            ).astype(BF)
            for h in range(2)
        ]
        err = jnp.concatenate(half, axis=1)
        err_ref[...] = err
        decoder = jnp.concatenate(
            [get_wide(w, 0, block, n), get_wide(w, block * n // 128, block, n)], axis=1
        )
        total += dot(decoder, err, 0, 0)
    own_ref[...] = total[:n]
    prev_ref[...] = total[n:].astype(BF)


def decoder_grads_kernel(e0, e1, e2, e3, c0, c1, c2, c3, own_ref, prev_ref):
    n = own_ref.shape[1]
    factor = 1.0 / math.sqrt(4 * e0.shape[1])
    total = 0.0
    for e, c in ((e0, c0), (e1, c1), (e2, c2), (e3, c3)):
        total += dot(e[...], c[...], 1, 1)
    own_ref[...] = total[:, :n] * factor
    prev_ref[...] = total[:, n:] * factor


def encoder_grads_kernel(n0, n1, n2, n3, p0, p1, p2, p3, grad_ref, bias_ref):
    total = bias = 0.0
    ones = jnp.ones((8, p0.shape[1]), BF)
    for n, p in ((n0, p0), (n1, p1), (n2, p2), (n3, p3)):
        total += dot(n[...], p[...], 1, 1)
        bias += dot(ones, p[...], 1, 1)
    grad_ref[...] = total
    bias_ref[...] = bias[:1]


def local(
    resid,
    norm_gain,
    prev_codes,
    feature_mask,
    w_gate,
    w_up,
    w_down,
    enc_weight,
    enc_bias,
    dec_own,
    dec_prev,
):
    height, strip = resid.shape[1:]
    peers = lax.axis_size("feat")
    width = enc_weight.shape[2]
    units = w_gate.shape[2]
    block = strip * peers // 4
    spans = -(-block // 128)
    t = 2 * lax.axis_index("tok_0") + lax.axis_index("tok_1")
    place = jnp.stack([t, lax.axis_index("layer")]).astype(jnp.int32)
    flip = lambda a: jnp.swapaxes(a[0], 0, 1)

    (copies,) = call(
        spread_kernel, (flip(resid), norm_gain), [((peers, 2 * PITCH, height // 2), BF)]
    )
    gathered = exchange(copies)
    first, second, before = call(
        pack_kernel,
        (
            enc_weight[0], flip(w_gate), flip(w_up),
            flip(dec_own), flip(dec_prev), w_down[0], prev_codes,
        ),
        [
            ((block * width // 128 + 2 * units * spans, 128), BF),
            ((2 * block * width // 128 + units * spans, 128), BF),
            ((width, height), BF),
        ],
    )
    first = gather4(first)
    second = gather4(second)
    *normed, codes, slope, hidden = call(
        encode_kernel,
        (place, feature_mask[0], gathered, *first, enc_bias),
        [((block, height), BF)] * 4
        + [((width, height), BF), ((width, height), F32), ((units, height), BF)],
        [pltpu.VMEM((4 * block, height), F32)],
    )
    shifted = lax.ppermute(codes, "layer", [(0, 1)])
    parts, both = call(
        decode_kernel,
        (place, codes, before, shifted, hidden, *second),
        [((peers, ROWS, height // 2), BF), ((2 * width, height), BF)],
    )
    arrived = exchange(parts)
    normed = exchange4(normed)
    (copies,) = call(total_kernel, (arrived,), [(parts.shape, BF)], after=normed[1:])
    errors = exchange(copies)
    both = gather4(both)
    own_back, prev_back, *err = call(
        back_kernel,
        (place, errors, *second),
        [((width, height), F32), ((width, height), BF)] + [((block, height), BF)] * 4,
        after=both[1:],
    )
    later = lax.ppermute(prev_back, "layer", [(1, 0)]).astype(F32)
    err = exchange4(err)
    pregrad = gather4(((own_back + later) * slope).astype(BF))
    grad_own, grad_prev = call(
        decoder_grads_kernel, (*err, *both), [((block, width), F32)] * 2
    )
    grad_enc, grad_bias = call(
        encoder_grads_kernel,
        (*normed, *pregrad),
        [((block, width), F32), ((1, width), F32)],
    )
    return (grad_enc[None], grad_bias, grad_own.T[None], grad_prev.T[None])


def solution(mesh):
    split = Mesh(
        mesh.devices.reshape(mesh.shape["layer"], mesh.shape["feat"], 2, 2),
        ("layer", "feat", "tok_0", "tok_1"),
    )
    placed = (
        P("layer", TOK, "feat"),
        P("layer", "feat"),
        P(TOK, "feat"),
        P("layer", TOK, "feat"),
        P("layer", TOK, "feat"),
        P("layer", TOK, "feat"),
        P("layer", "feat", TOK),
        P("layer", TOK, "feat"),
        P("layer", "feat"),
        P("layer", "feat", TOK),
        P("layer", "feat", TOK),
    )
    return jax.shard_map(
        local,
        mesh=split,
        in_specs=placed,
        out_specs=(
            P("layer", TOK, "feat"),
            P("layer", "feat"),
            P("layer", "feat", TOK),
            P("layer", "feat", TOK),
        ),
        check_vma=False,
    )
```

time: 264 us -> 213 us (0.81)
  blocking collectives: 80.3 us -> 0 us
  waiting for transfers between devices: 51.1 us -> 77.7 us
  starting transfers between devices: 78.1 us -> 98.4 us
  local copies, waits for them, and re-layouts: 23.3 us -> 5.51 us
    all_to_all x2 -> x0, blocking collectives: 80.3 us -> none  [exchange(): return lax.all_to_all(blocks, axis, split_axis=0, concat_axis=0, tiled=True)]
    ppermute x12 -> x18, waiting for transfers between devices: 17.2 us -> 50 us  [toward(): return lax.ppermute(x, TOK, [(i, i ^ k) for i in range(4)])]
    ppermute x1, waiting for transfers between devices: 15.6 us -> 0.01 us  [local(): later = lax.ppermute(prev_back, 'layer', [(1, 0)]).astype(F32)]
    ppermute x12 -> x18, starting transfers between devices: 38.1 us -> 53.6 us  [toward(): return lax.ppermute(x, TOK, [(i, i ^ k) for i in range(4)])]
    all_to_all x4 -> x3, waiting for transfers between devices: 15.1 us -> 24.5 us  [exchange(): lax.all_to_all(blocks, 'feat', split_axis=0, concat_axis=0, tiled=True)]
    ppermute x3 -> x0, local copies, waits for them, and re-layouts: 5.82 us -> none  [swap(): return lax.ppermute(x, axis, [(0, 1), (1, 0)])]
    all_to_all x4 -> x3, starting transfers between devices: 34.1 us -> 38.9 us  [exchange(): lax.all_to_all(blocks, 'feat', split_axis=0, concat_axis=0, tiled=True)]
    broadcast_in_dim x3 -> x0, local copies, waits for them, and re-layouts: 3.91 us -> none  [the longest x2 2.62 us: local(): gain_rows = jnp.broadcast_to(gains.reshape(depth, 1), (depth, 128))]
  transfers between devices with their start and end apart: 18 -> 23, of which waited for: 7 -> 9; matrix products, arithmetic and copies ran while one was open for 8% -> 1% of each run, Pallas kernels for 6% -> 5%
where the time goes in v2:
time: 213 us; the launch traced here: 211 us
  starting transfers between devices  98.4 us (46%)
  waiting for transfers between devices  77.7 us (36%)
  Pallas kernels  26.2 us (12%)
  local copies, waits for them, and re-layouts  5.51 us (3%)
    ppermute x18, starting transfers between devices, toward(): return lax.ppermute(x, TOK, [(i, i ^ k) for i in range(4)])  53.6 us
    ppermute x18, waiting for transfers between devices, toward(): return lax.ppermute(x, TOK, [(i, i ^ k) for i in range(4)])  50 us
    all_to_all x3, starting transfers between devices, exchange(): lax.all_to_all(blocks, 'feat', split_axis=0, concat_axis=0, tiled=True)  38.9 us
    pallas_call x8, Pallas kernels, call(): pl.pallas_call(body, out_shape=[jax.ShapeDtypeStruct(s, d) for s, d in ou...  26.2 us
    all_to_all x3, waiting for transfers between devices, exchange(): lax.all_to_all(blocks, 'feat', split_axis=0, concat_axis=0, tiled=True)  24.5 us
    unnamed x50, local copies, waits for them, and re-layouts  5.51 us
    ppermute x1, starting transfers between devices, local(): shifted = lax.ppermute(codes, 'layer', [(0, 1)])  4.64 us
  transfers between devices with their start and end apart: 23, of which 9 were waited for; matrix products, arithmetic and copies ran while one was open for 1% of the time, Pallas kernels for 5%

profile of v2, /device:TPU:1, one launch (start us, length us, event | category | flops | bytes accessed | tf_op | source)
XLA Modules:
  0.0 210.6 jit_solution(9393162302832180035)
XLA Ops:
  0.6 2.0 spread_kernel.1
  2.6 17.1 %all-to-all-start = ((bf16[64,80,128]{2,1,0:T(8,128)(2,1)}), bf16[64,80,128]{2,1,0:T(8,128)(2,1)S(1)}, u32[]{:S(2)}, u32[]{:S(2)}) async-start(bf16[64,80,128]{2,1,0:T(8,128)(2,1)} %spread_kernel.1), calls=%async_computation | async-start | bytes 2621440 | tf_op jit(solution)/shard_map/all_to_all | solution.py:62
  19.8 2.7 %pack_kernel.1 = (bf16[2592,128]{1,0:T(8,128)(2,1)}, bf16[3024,128]{1,0:T(8,128)(2,1)}, bf16[256,256]{1,0:T(8,128)(2,1)}) custom-call(bf16[576,256]{1,0:T(8,128)(2,1)} %bitcast.27, bf16[144,576]{1,0:T(8,128)(2,1)} %bitcast.30, bf16[144,576]{1,0:T(8,128)(2,1)} %bitcast.31, bf16[576,256]{1,0:T(8,128)(2,1)} %bitcast.28, bf16[576,256]{1,0:T(8,128)(2,1)} %bitcast.29, ...), custom_call_target="tpu_custom_call" | custom-call | tf_op jit(solution)/shard_map/pack_kernel/pallas_call | solution.py:33
  22.5 3.1 %collective-permute-start.8 = (bf16[3024,128]{1,0:T(8,128)(2,1)}, bf16[3024,128]{1,0:T(8,128)(2,1)S(1)}, u32[]{:S(2)}, u32[]{:S(2)}) collective-permute-start(bf16[3024,128]{1,0:T(8,128)(2,1)} %get-tuple-element.34.refs_5_.refs_2_), channel_id=1, source_target_pairs={{0,2},{1,3},{2,0},{3,1},{4,6},{5,7},{6,4},{7,5},{8,10},{9,11},{10,... | collective-permute-start | bytes 2322440 | tf_op jit(solution)/shard_map/ppermute | solution.py:49
  25.6 2.2 %collective-permute-start.1 = (bf16[2592,128]{1,0:T(8,128)(2,1)}, bf16[2592,128]{1,0:T(8,128)(2,1)S(1)}, u32[]{:S(2)}, u32[]{:S(2)}) collective-permute-start(bf16[2592,128]{1,0:T(8,128)(2,1)} %get-tuple-element.26.refs_3_), channel_id=1, source_target_pairs={{0,2},{1,3},{2,0},{3,1},{4,6},{5,7},{6,4},{7,5},{8,10},{9,11},{10,... | collective-permute-start | bytes 1990664 | tf_op jit(solution)/shard_map/ppermute | solution.py:49
  27.7 3.4 %collective-permute-start = (bf16[2592,128]{1,0:T(8,128)(2,1)}, bf16[2592,128]{1,0:T(8,128)(2,1)}, u32[]{:S(2)}, u32[]{:S(2)}) collective-permute-start(bf16[2592,128]{1,0:T(8,128)(2,1)} %get-tuple-element.26.refs_3_), channel_id=1, source_target_pairs={{0,1},{1,0},{2,3},{3,2},{4,5},{5,4},{6,7},{7,6},{8,9},{9,8},{10,11... | collective-permute-start | bytes 1990664 | tf_op jit(solution)/shard_map/ppermute | solution.py:49
  31.2 25.4 %collective-permute-done.1.refs_5_ = bf16[2592,128]{1,0:T(8,128)(2,1)S(1)} collective-permute-done((bf16[2592,128]{1,0:T(8,128)(2,1)}, bf16[2592,128]{1,0:T(8,128)(2,1)S(1)}, u32[]{:S(2)}, u32[]{:S(2)}) %collective-permute-start.1) | collective-permute-done | bytes 663584 | tf_op jit(solution)/shard_map/ppermute | solution.py:49
  56.6 3.8 %collective-permute-start.2 = (bf16[2592,128]{1,0:T(8,128)(2,1)S(1)}, bf16[2592,128]{1,0:T(8,128)(2,1)}, u32[]{:S(2)}, u32[]{:S(2)}) collective-permute-start(bf16[2592,128]{1,0:T(8,128)(2,1)S(1)} %collective-permute-done.1.refs_5_), channel_id=1, source_target_pairs={{0,1},{1,0},{2,3},{3,2},{4,5},{5,4},{6,7},{7,6},{8,9},{9,8},{10,11... | collective-permute-start | bytes 1990664 | tf_op jit(solution)/shard_map/ppermute | solution.py:49
  60.4 1.9 collective-permute-start.7
  62.3 2.4 %collective-permute-start.9 = (bf16[3024,128]{1,0:T(8,128)(2,1)S(1)}, bf16[3024,128]{1,0:T(8,128)(2,1)}, u32[]{:S(2)}, u32[]{:S(2)}) collective-permute-start(bf16[3024,128]{1,0:T(8,128)(2,1)S(1)} %collective-permute-done.8.refs_7_.refs_4_), channel_id=1, source_target_pairs={{0,1},{1,0},{2,3},{3,2},{4,5},{5,4},{6,7},{7,6},{8,9},{9,8},{10,11... | collective-permute-start | bytes 2322440 | tf_op jit(solution)/shard_map/ppermute | solution.py:49
  64.7 0.6 pad_add_fusion.refs_0_
  65.4 1.1 copy-done
  66.5 4.6 %encode_kernel.1 = (bf16[576,256]{1,0:T(8,128)(2,1)}, bf16[576,256]{1,0:T(8,128)(2,1)}, bf16[576,256]{1,0:T(8,128)(2,1)}, bf16[576,256]{1,0:T(8,128)(2,1)}, bf16...) custom-call(s32[2]{0:T(128)} %pad_add_fusion.refs_0_, s32[2,2]{1,0:T(2,128)} %bitcast.34, ...), custom_call_target="tpu_custom_call" | custom-call | tf_op jit(solution)/shard_map/encode_kernel/pallas_call | solution.py:33
  71.1 4.6 %collective-permute-start.6 = (bf16[256,256]{1,0:T(8,128)(2,1)}, bf16[256,256]{1,0:T(8,128)(2,1)S(1)}, u32[]{:S(2)}, u32[]{:S(2)}) collective-permute-start(bf16[256,256]{1,0:T(8,128)(2,1)} %get-tuple-element.31.refs_1_), channel_id=1, source_target_pairs={{0,256},{1,257},{2,258},{3,259},{4,260},{5,261},{6,262},{7,263},{8... | collective-permute-start | bytes 393224 | tf_op jit(solution)/shard_map/ppermute | solution.py:281
  75.8 3.2 %collective-permute-done.6.refs_3_ = bf16[256,256]{1,0:T(8,128)(2,1)S(1)} collective-permute-done((bf16[256,256]{1,0:T(8,128)(2,1)}, bf16[256,256]{1,0:T(8,128)(2,1)S(1)}, u32[]{:S(2)}, u32[]{:S(2)}) %collective-permute-start.6) | collective-permute-done | bytes 131104 | tf_op jit(solution)/shard_map/ppermute | solution.py:281
  79.0 0.7 copy-done.21
  79.7 4.3 %decode_kernel.1 = (bf16[64,72,128]{2,1,0:T(8,128)(2,1)}, bf16[512,256]{1,0:T(8,128)(2,1)}) custom-call(s32[2]{0:T(128)} %pad_add_fusion.refs_0_, bf16[256,256]{1,0:T(8,128)(2,1)} %get-tuple-element.31.refs_1_, bf16[256,256]{1,0:T(8,128)(2,1)} %get-tuple-element.32.refs_2_, bf16[256,256]{1,0:T(8,128)(2,1)} %copy-done.21, ...), custom_call_target="tpu_custom_call" | custom-call | tf_op jit(solution)/shard_map/decode_kernel/pallas_call | solution.py:33
  83.9 12.3 %all-to-all-start.1 = ((bf16[64,72,128]{2,1,0:T(8,128)(2,1)}), bf16[64,72,128]{2,1,0:T(8,128)(2,1)S(1)}, u32[]{:S(2)}, u32[]{:S(2)}) async-start(bf16[64,72,128]{2,1,0:T(8,128)(2,1)} %get-tuple-element.35), calls=%async_computation.1 | async-start | bytes 2359296 | tf_op jit(solution)/shard_map/all_to_all | solution.py:62
  96.2 3.0 %collective-permute-start.3 = (bf16[576,256]{1,0:T(8,128)(2,1)S(1)}, bf16[576,256]{1,0:T(8,128)(2,1)S(1)}, u32[]{:S(2)}, u32[]{:S(2)}) collective-permute-start(bf16[576,256]{1,0:T(8,128)(2,1)S(1)} %copy-done.24), channel_id=1, source_target_pairs={{0,1},{1,0},{2,3},{3,2},{4,5},{5,4},{6,7},{7,6},{8,9},{9,8},{10,11... | collective-permute-start | bytes 884744 | tf_op jit(solution)/shard_map/ppermute | solution.py:49
  99.2 2.2 %collective-permute-start.4 = (bf16[576,256]{1,0:T(8,128)(2,1)S(1)}, bf16[576,256]{1,0:T(8,128)(2,1)S(1)}, u32[]{:S(2)}, u32[]{:S(2)}) collective-permute-start(bf16[576,256]{1,0:T(8,128)(2,1)S(1)} %copy-done.23), channel_id=1, source_target_pairs={{0,2},{1,3},{2,0},{3,1},{4,6},{5,7},{6,4},{7,5},{8,10},{9,11},{10,... | collective-permute-start | bytes 884744 | tf_op jit(solution)/shard_map/ppermute | solution.py:49
  101.5 3.2 %collective-permute-start.5 = (bf16[576,256]{1,0:T(8,128)(2,1)S(1)}, bf16[576,256]{1,0:T(8,128)(2,1)S(1)}, u32[]{:S(2)}, u32[]{:S(2)}) collective-permute-start(bf16[576,256]{1,0:T(8,128)(2,1)S(1)} %copy-done.22), channel_id=1, source_target_pairs={{0,3},{1,2},{2,1},{3,0},{4,7},{5,6},{6,5},{7,4},{8,11},{9,10},{10,... | collective-permute-start | bytes 884744 | tf_op jit(solution)/shard_map/ppermute | solution.py:49
  104.8 5.0 %collective-permute-done.4.refs_2_ = bf16[576,256]{1,0:T(8,128)(2,1)S(1)} collective-permute-done((bf16[576,256]{1,0:T(8,128)(2,1)S(1)}, bf16[576,256]{1,0:T(8,128)(2,1)S(1)}, u32[]{:S(2)}, u32[]{:S(2)}) %collective-permute-start.4) | collective-permute-done | bytes 294944 | tf_op jit(solution)/shard_map/ppermute | solution.py:49
  109.8 6.7 %collective-permute-done.5.refs_3_ = bf16[576,256]{1,0:T(8,128)(2,1)S(1)} collective-permute-done((bf16[576,256]{1,0:T(8,128)(2,1)S(1)}, bf16[576,256]{1,0:T(8,128)(2,1)S(1)}, u32[]{:S(2)}, u32[]{:S(2)}) %collective-permute-start.5) | collective-permute-done | bytes 294944 | tf_op jit(solution)/shard_map/ppermute | solution.py:49
  116.5 9.1 %all-to-all-done.1.refs_0_ = bf16[64,72,128]{2,1,0:T(8,128)(2,1)S(1)} async-done(((bf16[64,72,128]{2,1,0:T(8,128)(2,1)}), bf16[64,72,128]{2,1,0:T(8,128)(2,1)S(1)}, u32[]{:S(2)}, u32[]{:S(2)}) %all-to-all-start.1) | async-done | bytes 1179680 | tf_op jit(solution)/shard_map/all_to_all | solution.py:62
  125.6 1.0 copy-done.1
  126.6 2.6 %total_kernel.1 = bf16[64,72,128]{2,1,0:T(8,128)(2,1)} custom-call(bf16[64,72,128]{2,1,0:T(8,128)(2,1)} %copy-done.1, bf16[576,256]{1,0:T(8,128)(2,1)} %copy-done.5, bf16[576,256]{1,0:T(8,128)(2,1)} %copy-done.6, bf16[576,256]{1,0:T(8,128)(2,1)} %copy-done.7), custom_call_target="tpu_custom_call" | custom-call | tf_op jit(solution)/shard_map/total_kernel/pallas_call | solution.py:33
  129.2 9.4 %all-to-all-start.2 = ((bf16[64,72,128]{2,1,0:T(8,128)(2,1)}), bf16[64,72,128]{2,1,0:T(8,128)(2,1)S(1)}, u32[]{:S(2)}, u32[]{:S(2)}) async-start(bf16[64,72,128]{2,1,0:T(8,128)(2,1)} %total_kernel.1), calls=%async_computation.2 | async-start | bytes 2359296 | tf_op jit(solution)/shard_map/all_to_all | solution.py:62
  138.7 2.3 %collective-permute-start.11 = (bf16[512,256]{1,0:T(8,128)(2,1)S(1)}, bf16[512,256]{1,0:T(8,128)(2,1)S(1)}, u32[]{:S(2)}, u32[]{:S(2)}) collective-permute-start(bf16[512,256]{1,0:T(8,128)(2,1)S(1)} %copy-done.16), channel_id=1, source_target_pairs={{0,2},{1,3},{2,0},{3,1},{4,6},{5,7},{6,4},{7,5},{8,10},{9,11},{10,... | collective-permute-start | bytes 786440 | tf_op jit(solution)/shard_map/ppermute | solution.py:49
  141.0 3.4 %collective-permute-start.10 = (bf16[512,256]{1,0:T(8,128)(2,1)S(1)}, bf16[512,256]{1,0:T(8,128)(2,1)S(1)}, u32[]{:S(2)}, u32[]{:S(2)}) collective-permute-start(bf16[512,256]{1,0:T(8,128)(2,1)S(1)} %copy-done.16), channel_id=1, source_target_pairs={{0,1},{1,0},{2,3},{3,2},{4,5},{5,4},{6,7},{7,6},{8,9},{9,8},{10,11... | collective-permute-start | bytes 786440 | tf_op jit(solution)/shard_map/ppermute | solution.py:49
  144.4 3.0 %collective-permute-done.11.refs_7_.refs_6_ = bf16[512,256]{1,0:T(8,128)(2,1)S(1)} collective-permute-done((bf16[512,256]{1,0:T(8,128)(2,1)S(1)}, bf16[512,256]{1,0:T(8,128)(2,1)S(1)}, u32[]{:S(2)}, u32[]{:S(2)}) %collective-permute-start.11) | collective-permute-done | bytes 262176 | tf_op jit(solution)/shard_map/ppermute | solution.py:49
  147.3 4.0 %collective-permute-start.12 = (bf16[512,256]{1,0:T(8,128)(2,1)S(1)}, bf16[512,256]{1,0:T(8,128)(2,1)S(1)}, u32[]{:S(2)}, u32[]{:S(2)}) collective-permute-start(bf16[512,256]{1,0:T(8,128)(2,1)S(1)} %collective-permute-done.11.refs_7_.refs_6_), channel_id=1, source_target_pairs={{0,1},{1,0},{2,3},{3,2},{4,5},{5,4},{6,7},{7,6},{8,9},{9,8},{10,11... | collective-permute-start | bytes 786440 | tf_op jit(solution)/shard_map/ppermute | solution.py:49
  151.3 1.1 collective-permute-done.12.refs_8_.refs_7_
  152.5 15.4 %all-to-all-done.2.refs_1_ = bf16[64,72,128]{2,1,0:T(8,128)(2,1)S(1)} async-done(((bf16[64,72,128]{2,1,0:T(8,128)(2,1)}), bf16[64,72,128]{2,1,0:T(8,128)(2,1)S(1)}, u32[]{:S(2)}, u32[]{:S(2)}) %all-to-all-start.2) | async-done | bytes 1179680 | tf_op jit(solution)/shard_map/all_to_all | solution.py:62
  167.9 1.1 copy-done.2
  169.0 4.0 %back_kernel.1 = (f32[256,256]{1,0:T(8,128)}, bf16[256,256]{1,0:T(8,128)(2,1)}, bf16[576,256]{1,0:T(8,128)(2,1)}, bf16[576,256]{1,0:T(8,128)(2,1)}, bf16[576,256]{1,0:T(8,128)(2,1)}, /*index=5*/bf16[576,256]{1,0:T(8,128)(2,1)}) custom-call(s32[2]{0:T(128)} %pad_add_fusion.refs_0_, bf16[64,72,128]{2,1,0:T(8,128)(2,1)} %copy-done.2, ...), custom_call_target="tpu_custom_call" | custom-call | tf_op jit(solution)/shard_map/back_kernel/pallas_call | solution.py:33
  172.9 1.3 collective-permute-start.13
  174.2 6.0 %collective-permute-start.17 = (bf16[576,256]{1,0:T(8,128)(2,1)}, bf16[576,256]{1,0:T(8,128)(2,1)S(1)}, u32[]{:S(2)}, u32[]{:S(2)}) collective-permute-start(bf16[576,256]{1,0:T(8,128)(2,1)} %get-tuple-element.43), channel_id=1, source_target_pairs={{0,1},{1,0},{2,3},{3,2},{4,5},{5,4},{6,7},{7,6},{8,9},{9,8},{10,11... | collective-permute-start | bytes 884744 | tf_op jit(solution)/shard_map/ppermute | solution.py:49
  180.3 2.2 %collective-permute-start.18 = (bf16[576,256]{1,0:T(8,128)(2,1)}, bf16[576,256]{1,0:T(8,128)(2,1)S(1)}, u32[]{:S(2)}, u32[]{:S(2)}) collective-permute-start(bf16[576,256]{1,0:T(8,128)(2,1)} %get-tuple-element.44), channel_id=1, source_target_pairs={{0,2},{1,3},{2,0},{3,1},{4,6},{5,7},{6,4},{7,5},{8,10},{9,11},{10,... | collective-permute-start | bytes 884744 | tf_op jit(solution)/shard_map/ppermute | solution.py:49
  182.4 3.3 %collective-permute-start.19 = (bf16[576,256]{1,0:T(8,128)(2,1)}, bf16[576,256]{1,0:T(8,128)(2,1)S(1)}, u32[]{:S(2)}, u32[]{:S(2)}) collective-permute-start(bf16[576,256]{1,0:T(8,128)(2,1)} %get-tuple-element.45), channel_id=1, source_target_pairs={{0,3},{1,2},{2,1},{3,0},{4,7},{5,6},{6,5},{7,4},{8,11},{9,10},{10,... | collective-permute-start | bytes 884744 | tf_op jit(solution)/shard_map/ppermute | solution.py:49
  185.7 1.0 multiply_convert_fusion.refs_4_
  186.8 2.2 %collective-permute-start.15 = (bf16[256,256]{1,0:T(8,128)(2,1)S(1)}, bf16[256,256]{1,0:T(8,128)(2,1)S(1)}, u32[]{:S(2)}, u32[]{:S(2)}) collective-permute-start(bf16[256,256]{1,0:T(8,128)(2,1)S(1)} %multiply_convert_fusion.refs_4_), channel_id=1, source_target_pairs={{0,2},{1,3},{2,0},{3,1},{4,6},{5,7},{6,4},{7,5},{8,10},{9,11},{10,... | collective-permute-start | bytes 393224 | tf_op jit(solution)/shard_map/ppermute | solution.py:49
  188.9 2.4 %collective-permute-start.14 = (bf16[256,256]{1,0:T(8,128)(2,1)S(1)}, bf16[256,256]{1,0:T(8,128)(2,1)S(1)}, u32[]{:S(2)}, u32[]{:S(2)}) collective-permute-start(bf16[256,256]{1,0:T(8,128)(2,1)S(1)} %multiply_convert_fusion.refs_4_), channel_id=1, source_target_pairs={{0,1},{1,0},{2,3},{3,2},{4,5},{5,4},{6,7},{7,6},{8,9},{9,8},{10,11... | collective-permute-start | bytes 393224 | tf_op jit(solution)/shard_map/ppermute | solution.py:49
  191.4 8.8 %collective-permute-done.15.refs_6_ = bf16[256,256]{1,0:T(8,128)(2,1)S(1)} collective-permute-done((bf16[256,256]{1,0:T(8,128)(2,1)S(1)}, bf16[256,256]{1,0:T(8,128)(2,1)S(1)}, u32[]{:S(2)}, u32[]{:S(2)}) %collective-permute-start.15) | collective-permute-done | bytes 131104 | tf_op jit(solution)/shard_map/ppermute | solution.py:49
  200.1 2.7 %collective-permute-start.16 = (bf16[256,256]{1,0:T(8,128)(2,1)S(1)}, bf16[256,256]{1,0:T(8,128)(2,1)S(1)}, u32[]{:S(2)}, u32[]{:S(2)}) collective-permute-start(bf16[256,256]{1,0:T(8,128)(2,1)S(1)} %collective-permute-done.15.refs_6_), channel_id=1, source_target_pairs={{0,1},{1,0},{2,3},{3,2},{4,5},{5,4},{6,7},{7,6},{8,9},{9,8},{10,11... | collective-permute-start | bytes 393224 | tf_op jit(solution)/shard_map/ppermute | solution.py:49
  202.9 0.7 copy-done.13
  203.8 3.4 %decoder_grads_kernel.1 = (f32[576,256]{1,0:T(8,128)}, f32[576,256]{1,0:T(8,128)}) custom-call(bf16[576,256]{1,0:T(8,128)(2,1)} %get-tuple-element.42.refs_0_, bf16[576,256]{1,0:T(8,128)(2,1)} %copy-done.13, bf16[576,256]{1,0:T(8,128)(2,1)} %copy-done.14, bf16[576,256]{1,0:T(8,128)(2,1)} %copy-done.15, bf16[512,256]{1,0:T(8,128)(2,1)} %get-tuple-element.36.refs_4_, ...), custom_call_target="tpu_custom_call" | custom-call | tf_op jit(solution)/shard_map/decoder_grads_kernel/pallas_call | solution.py:33
  207.2 0.6 copy-done.19
  207.9 2.8 %encoder_grads_kernel.1 = (f32[576,256]{1,0:T(8,128)}, f32[1,256]{1,0:T(1,128)}) custom-call(bf16[576,256]{1,0:T(8,128)(2,1)} %get-tuple-element.27.refs_0_, bf16[576,256]{1,0:T(8,128)(2,1)} %copy-done.5, bf16[576,256]{1,0:T(8,128)(2,1)} %copy-done.6, bf16[576,256]{1,0:T(8,128)(2,1)} %copy-done.7, bf16[256,256]{1,0:T(8,128)(2,1)} %copy-done.12, ...), custom_call_target="tpu_custom_call" | custom-call | tf_op jit(solution)/shard_map/encoder_grads_kernel/pallas_call | solution.py:33
  (58 shorter events, 0.4 us)
Async XLA Ops:
  2.6 62.8 %all-to-all-start = ((bf16[64,80,128]{2,1,0:T(8,128)(2,1)}), bf16[64,80,128]{2,1,0:T(8,128)(2,1)S(1)}, u32[]{:S(2)}, u32[]{:S(2)}) async-start(bf16[64,80,128]{2,1,0:T(8,128)(2,1)} %spread_kernel.1), calls=%async_computation | async-start | bytes 2621440 | tf_op jit(solution)/shard_map/all_to_all | solution.py:62
  22.5 39.8 %collective-permute-start.8 = (bf16[3024,128]{1,0:T(8,128)(2,1)}, bf16[3024,128]{1,0:T(8,128)(2,1)S(1)}, u32[]{:S(2)}, u32[]{:S(2)}) collective-permute-start(bf16[3024,128]{1,0:T(8,128)(2,1)} %get-tuple-element.34.refs_5_.refs_2_), channel_id=1, source_target_pairs={{0,2},{1,3},{2,0},{3,1},{4,6},{5,7},{6,4},{7,5},{8,10},{9,11},{10,... | collective-permute-start | bytes 2322440 | tf_op jit(solution)/shard_map/ppermute | solution.py:49
  25.6 31.0 %collective-permute-start.1 = (bf16[2592,128]{1,0:T(8,128)(2,1)}, bf16[2592,128]{1,0:T(8,128)(2,1)S(1)}, u32[]{:S(2)}, u32[]{:S(2)}) collective-permute-start(bf16[2592,128]{1,0:T(8,128)(2,1)} %get-tuple-element.26.refs_3_), channel_id=1, source_target_pairs={{0,2},{1,3},{2,0},{3,1},{4,6},{5,7},{6,4},{7,5},{8,10},{9,11},{10,... | collective-permute-start | bytes 1990664 | tf_op jit(solution)/shard_map/ppermute | solution.py:49
  27.7 37.6 %collective-permute-start = (bf16[2592,128]{1,0:T(8,128)(2,1)}, bf16[2592,128]{1,0:T(8,128)(2,1)}, u32[]{:S(2)}, u32[]{:S(2)}) collective-permute-start(bf16[2592,128]{1,0:T(8,128)(2,1)} %get-tuple-element.26.refs_3_), channel_id=1, source_target_pairs={{0,1},{1,0},{2,3},{3,2},{4,5},{5,4},{6,7},{7,6},{8,9},{9,8},{10,11... | collective-permute-start | bytes 1990664 | tf_op jit(solution)/shard_map/ppermute | solution.py:49
  56.6 8.8 %copy-start.11 = (bf16[2592,128]{1,0:T(8,128)(2,1)}, bf16[2592,128]{1,0:T(8,128)(2,1)S(1)}, u32[]{:S(2)}) copy-start(bf16[2592,128]{1,0:T(8,128)(2,1)S(1)} %collective-permute-done.1.refs_5_) | copy-start | bytes 1990660
  56.6 8.8 %collective-permute-start.2 = (bf16[2592,128]{1,0:T(8,128)(2,1)S(1)}, bf16[2592,128]{1,0:T(8,128)(2,1)}, u32[]{:S(2)}, u32[]{:S(2)}) collective-permute-start(bf16[2592,128]{1,0:T(8,128)(2,1)S(1)} %collective-permute-done.1.refs_5_), channel_id=1, source_target_pairs={{0,1},{1,0},{2,3},{3,2},{4,5},{5,4},{6,7},{7,6},{8,9},{9,8},{10,11... | collective-permute-start | bytes 1990664 | tf_op jit(solution)/shard_map/ppermute | solution.py:49
  60.4 15.4 %collective-permute-start.7 = (bf16[3024,128]{1,0:T(8,128)(2,1)}, bf16[3024,128]{1,0:T(8,128)(2,1)S(1)}, u32[]{:S(2)}, u32[]{:S(2)}) collective-permute-start(bf16[3024,128]{1,0:T(8,128)(2,1)} %get-tuple-element.34.refs_5_.refs_2_), channel_id=1, source_target_pairs={{0,1},{1,0},{2,3},{3,2},{4,5},{5,4},{6,7},{7,6},{8,9},{9,8},{10,11... | collective-permute-start | bytes 2322440 | tf_op jit(solution)/shard_map/ppermute | solution.py:49
  62.3 16.7 %copy-start.3 = (bf16[3024,128]{1,0:T(8,128)(2,1)}, bf16[3024,128]{1,0:T(8,128)(2,1)S(1)}, u32[]{:S(2)}) copy-start(bf16[3024,128]{1,0:T(8,128)(2,1)S(1)} %collective-permute-done.8.refs_7_.refs_4_) | copy-start | bytes 2322436
  62.3 13.5 %collective-permute-start.9 = (bf16[3024,128]{1,0:T(8,128)(2,1)S(1)}, bf16[3024,128]{1,0:T(8,128)(2,1)}, u32[]{:S(2)}, u32[]{:S(2)}) collective-permute-start(bf16[3024,128]{1,0:T(8,128)(2,1)S(1)} %collective-permute-done.8.refs_7_.refs_4_), channel_id=1, source_target_pairs={{0,1},{1,0},{2,3},{3,2},{4,5},{5,4},{6,7},{7,6},{8,9},{9,8},{10,11... | collective-permute-start | bytes 2322440 | tf_op jit(solution)/shard_map/ppermute | solution.py:49
  65.4 1.1 copy-start
  71.1 7.8 %collective-permute-start.6 = (bf16[256,256]{1,0:T(8,128)(2,1)}, bf16[256,256]{1,0:T(8,128)(2,1)S(1)}, u32[]{:S(2)}, u32[]{:S(2)}) collective-permute-start(bf16[256,256]{1,0:T(8,128)(2,1)} %get-tuple-element.31.refs_1_), channel_id=1, source_target_pairs={{0,256},{1,257},{2,258},{3,259},{4,260},{5,261},{6,262},{7,263},{8... | collective-permute-start | bytes 393224 | tf_op jit(solution)/shard_map/ppermute | solution.py:281
  75.8 3.2 %copy-start.4 = (bf16[3024,128]{1,0:T(8,128)(2,1)}, bf16[3024,128]{1,0:T(8,128)(2,1)S(1)}, u32[]{:S(2)}) copy-start(bf16[3024,128]{1,0:T(8,128)(2,1)S(1)} %collective-permute-done.7.refs_6_.refs_3_) | copy-start | bytes 2322436
  79.0 0.7 copy-start.21
  83.9 12.3 %copy-start.24 = (bf16[576,256]{1,0:T(8,128)(2,1)S(1)}, bf16[576,256]{1,0:T(8,128)(2,1)}, u32[]{:S(2)}) copy-start(bf16[576,256]{1,0:T(8,128)(2,1)} %get-tuple-element.28) | copy-start | bytes 884740
  83.9 15.3 %copy-start.23 = (bf16[576,256]{1,0:T(8,128)(2,1)S(1)}, bf16[576,256]{1,0:T(8,128)(2,1)}, u32[]{:S(2)}) copy-start(bf16[576,256]{1,0:T(8,128)(2,1)} %get-tuple-element.29) | copy-start | bytes 884740
  83.9 17.5 %copy-start.22 = (bf16[576,256]{1,0:T(8,128)(2,1)S(1)}, bf16[576,256]{1,0:T(8,128)(2,1)}, u32[]{:S(2)}) copy-start(bf16[576,256]{1,0:T(8,128)(2,1)} %get-tuple-element.30) | copy-start | bytes 884740
  83.9 41.7 %all-to-all-start.1 = ((bf16[64,72,128]{2,1,0:T(8,128)(2,1)}), bf16[64,72,128]{2,1,0:T(8,128)(2,1)S(1)}, u32[]{:S(2)}, u32[]{:S(2)}) async-start(bf16[64,72,128]{2,1,0:T(8,128)(2,1)} %get-tuple-element.35), calls=%async_computation.1 | async-start | bytes 2359296 | tf_op jit(solution)/shard_map/all_to_all | solution.py:62
  96.2 8.5 %collective-permute-start.3 = (bf16[576,256]{1,0:T(8,128)(2,1)S(1)}, bf16[576,256]{1,0:T(8,128)(2,1)S(1)}, u32[]{:S(2)}, u32[]{:S(2)}) collective-permute-start(bf16[576,256]{1,0:T(8,128)(2,1)S(1)} %copy-done.24), channel_id=1, source_target_pairs={{0,1},{1,0},{2,3},{3,2},{4,5},{5,4},{6,7},{7,6},{8,9},{9,8},{10,11... | collective-permute-start | bytes 884744 | tf_op jit(solution)/shard_map/ppermute | solution.py:49
  99.2 10.5 %collective-permute-start.4 = (bf16[576,256]{1,0:T(8,128)(2,1)S(1)}, bf16[576,256]{1,0:T(8,128)(2,1)S(1)}, u32[]{:S(2)}, u32[]{:S(2)}) collective-permute-start(bf16[576,256]{1,0:T(8,128)(2,1)S(1)} %copy-done.23), channel_id=1, source_target_pairs={{0,2},{1,3},{2,0},{3,1},{4,6},{5,7},{6,4},{7,5},{8,10},{9,11},{10,... | collective-permute-start | bytes 884744 | tf_op jit(solution)/shard_map/ppermute | solution.py:49
  101.5 15.0 %collective-permute-start.5 = (bf16[576,256]{1,0:T(8,128)(2,1)S(1)}, bf16[576,256]{1,0:T(8,128)(2,1)S(1)}, u32[]{:S(2)}, u32[]{:S(2)}) collective-permute-start(bf16[576,256]{1,0:T(8,128)(2,1)S(1)} %copy-done.22), channel_id=1, source_target_pairs={{0,3},{1,2},{2,1},{3,0},{4,7},{5,6},{6,5},{7,4},{8,11},{9,10},{10,... | collective-permute-start | bytes 884744 | tf_op jit(solution)/shard_map/ppermute | solution.py:49
  104.7 20.9 %copy-start.5 = (bf16[576,256]{1,0:T(8,128)(2,1)}, bf16[576,256]{1,0:T(8,128)(2,1)S(1)}, u32[]{:S(2)}) copy-start(bf16[576,256]{1,0:T(8,128)(2,1)S(1)} %collective-permute-done.3.refs_1_) | copy-start | bytes 884740
  109.8 15.8 %copy-start.6 = (bf16[576,256]{1,0:T(8,128)(2,1)}, bf16[576,256]{1,0:T(8,128)(2,1)S(1)}, u32[]{:S(2)}) copy-start(bf16[576,256]{1,0:T(8,128)(2,1)S(1)} %collective-permute-done.4.refs_2_) | copy-start | bytes 884740
  116.5 9.1 %copy-start.7 = (bf16[576,256]{1,0:T(8,128)(2,1)}, bf16[576,256]{1,0:T(8,128)(2,1)S(1)}, u32[]{:S(2)}) copy-start(bf16[576,256]{1,0:T(8,128)(2,1)S(1)} %collective-permute-done.5.refs_3_) | copy-start | bytes 884740
  125.6 1.0 copy-start.1
  129.2 9.4 %copy-start.16 = (bf16[512,256]{1,0:T(8,128)(2,1)S(1)}, bf16[512,256]{1,0:T(8,128)(2,1)}, u32[]{:S(2)}) copy-start(bf16[512,256]{1,0:T(8,128)(2,1)} %get-tuple-element.36.refs_4_) | copy-start | bytes 786436
  129.2 38.7 %all-to-all-start.2 = ((bf16[64,72,128]{2,1,0:T(8,128)(2,1)}), bf16[64,72,128]{2,1,0:T(8,128)(2,1)S(1)}, u32[]{:S(2)}, u32[]{:S(2)}) async-start(bf16[64,72,128]{2,1,0:T(8,128)(2,1)} %total_kernel.1), calls=%async_computation.2 | async-start | bytes 2359296 | tf_op jit(solution)/shard_map/all_to_all | solution.py:62
  138.7 47.1 %copy-start.17 = (f32[256,256]{1,0:T(8,128)S(1)}, f32[256,256]{1,0:T(8,128)}, u32[]{:S(2)}) copy-start(f32[256,256]{1,0:T(8,128)} %get-tuple-element.39) | copy-start | bytes 786436
  138.7 8.7 %collective-permute-start.11 = (bf16[512,256]{1,0:T(8,128)(2,1)S(1)}, bf16[512,256]{1,0:T(8,128)(2,1)S(1)}, u32[]{:S(2)}, u32[]{:S(2)}) collective-permute-start(bf16[512,256]{1,0:T(8,128)(2,1)S(1)} %copy-done.16), channel_id=1, source_target_pairs={{0,2},{1,3},{2,0},{3,1},{4,6},{5,7},{6,4},{7,5},{8,10},{9,11},{10,... | collective-permute-start | bytes 786440 | tf_op jit(solution)/shard_map/ppermute | solution.py:49
  141.0 10.3 %collective-permute-start.10 = (bf16[512,256]{1,0:T(8,128)(2,1)S(1)}, bf16[512,256]{1,0:T(8,128)(2,1)S(1)}, u32[]{:S(2)}, u32[]{:S(2)}) collective-permute-start(bf16[512,256]{1,0:T(8,128)(2,1)S(1)} %copy-done.16), channel_id=1, source_target_pairs={{0,1},{1,0},{2,3},{3,2},{4,5},{5,4},{6,7},{7,6},{8,9},{9,8},{10,11... | collective-permute-start | bytes 786440 | tf_op jit(solution)/shard_map/ppermute | solution.py:49
  147.3 20.6 %copy-start.8 = (bf16[512,256]{1,0:T(8,128)(2,1)}, bf16[512,256]{1,0:T(8,128)(2,1)S(1)}, u32[]{:S(2)}) copy-start(bf16[512,256]{1,0:T(8,128)(2,1)S(1)} %collective-permute-done.11.refs_7_.refs_6_) | copy-start | bytes 786436
  147.3 5.1 %collective-permute-start.12 = (bf16[512,256]{1,0:T(8,128)(2,1)S(1)}, bf16[512,256]{1,0:T(8,128)(2,1)S(1)}, u32[]{:S(2)}, u32[]{:S(2)}) collective-permute-start(bf16[512,256]{1,0:T(8,128)(2,1)S(1)} %collective-permute-done.11.refs_7_.refs_6_), channel_id=1, source_target_pairs={{0,1},{1,0},{2,3},{3,2},{4,5},{5,4},{6,7},{7,6},{8,9},{9,8},{10,11... | collective-permute-start | bytes 786440 | tf_op jit(solution)/shard_map/ppermute | solution.py:49
  151.3 16.5 %copy-start.9 = (bf16[512,256]{1,0:T(8,128)(2,1)}, bf16[512,256]{1,0:T(8,128)(2,1)S(1)}, u32[]{:S(2)}) copy-start(bf16[512,256]{1,0:T(8,128)(2,1)S(1)} %collective-permute-done.10.refs_6_.refs_5_) | copy-start | bytes 786436
  152.5 15.4 %copy-start.10 = (bf16[512,256]{1,0:T(8,128)(2,1)}, bf16[512,256]{1,0:T(8,128)(2,1)S(1)}, u32[]{:S(2)}) copy-start(bf16[512,256]{1,0:T(8,128)(2,1)S(1)} %collective-permute-done.12.refs_8_.refs_7_) | copy-start | bytes 786436
  167.9 1.1 copy-start.2
  172.9 12.8 %collective-permute-start.13 = (bf16[256,256]{1,0:T(8,128)(2,1)}, bf16[256,256]{1,0:T(8,128)(2,1)S(1)}, u32[]{:S(2)}, u32[]{:S(2)}) collective-permute-start(bf16[256,256]{1,0:T(8,128)(2,1)} %get-tuple-element.38), channel_id=1, source_target_pairs={{256,0},{257,1},{258,2},{259,3},{260,4},{261,5},{262,6},{263,7},{2... | collective-permute-start | bytes 393224 | tf_op jit(solution)/shard_map/ppermute | solution.py:298
  174.2 28.6 %collective-permute-start.17 = (bf16[576,256]{1,0:T(8,128)(2,1)}, bf16[576,256]{1,0:T(8,128)(2,1)S(1)}, u32[]{:S(2)}, u32[]{:S(2)}) collective-permute-start(bf16[576,256]{1,0:T(8,128)(2,1)} %get-tuple-element.43), channel_id=1, source_target_pairs={{0,1},{1,0},{2,3},{3,2},{4,5},{5,4},{6,7},{7,6},{8,9},{9,8},{10,11... | collective-permute-start | bytes 884744 | tf_op jit(solution)/shard_map/ppermute | solution.py:49
  180.3 22.6 %collective-permute-start.18 = (bf16[576,256]{1,0:T(8,128)(2,1)}, bf16[576,256]{1,0:T(8,128)(2,1)S(1)}, u32[]{:S(2)}, u32[]{:S(2)}) collective-permute-start(bf16[576,256]{1,0:T(8,128)(2,1)} %get-tuple-element.44), channel_id=1, source_target_pairs={{0,2},{1,3},{2,0},{3,1},{4,6},{5,7},{6,4},{7,5},{8,10},{9,11},{10,... | collective-permute-start | bytes 884744 | tf_op jit(solution)/shard_map/ppermute | solution.py:49
  182.4 20.4 %collective-permute-start.19 = (bf16[576,256]{1,0:T(8,128)(2,1)}, bf16[576,256]{1,0:T(8,128)(2,1)S(1)}, u32[]{:S(2)}, u32[]{:S(2)}) collective-permute-start(bf16[576,256]{1,0:T(8,128)(2,1)} %get-tuple-element.45), channel_id=1, source_target_pairs={{0,3},{1,2},{2,1},{3,0},{4,7},{5,6},{6,5},{7,4},{8,11},{9,10},{10,... | collective-permute-start | bytes 884744 | tf_op jit(solution)/shard_map/ppermute | solution.py:49
  186.7 20.4 %copy-start.12 = (bf16[256,256]{1,0:T(8,128)(2,1)}, bf16[256,256]{1,0:T(8,128)(2,1)S(1)}, u32[]{:S(2)}) copy-start(bf16[256,256]{1,0:T(8,128)(2,1)S(1)} %multiply_convert_fusion.refs_4_) | copy-start | bytes 393220
  186.8 13.4 %collective-permute-start.15 = (bf16[256,256]{1,0:T(8,128)(2,1)S(1)}, bf16[256,256]{1,0:T(8,128)(2,1)S(1)}, u32[]{:S(2)}, u32[]{:S(2)}) collective-permute-start(bf16[256,256]{1,0:T(8,128)(2,1)S(1)} %multiply_convert_fusion.refs_4_), channel_id=1, source_target_pairs={{0,2},{1,3},{2,0},{3,1},{4,6},{5,7},{6,4},{7,5},{8,10},{9,11},{10,... | collective-permute-start | bytes 393224 | tf_op jit(solution)/shard_map/ppermute | solution.py:49
  188.9 18.2 %collective-permute-start.14 = (bf16[256,256]{1,0:T(8,128)(2,1)S(1)}, bf16[256,256]{1,0:T(8,128)(2,1)S(1)}, u32[]{:S(2)}, u32[]{:S(2)}) collective-permute-start(bf16[256,256]{1,0:T(8,128)(2,1)S(1)} %multiply_convert_fusion.refs_4_), channel_id=1, source_target_pairs={{0,1},{1,0},{2,3},{3,2},{4,5},{5,4},{6,7},{7,6},{8,9},{9,8},{10,11... | collective-permute-start | bytes 393224 | tf_op jit(solution)/shard_map/ppermute | solution.py:49
  200.1 7.1 %copy-start.18 = (bf16[256,256]{1,0:T(8,128)(2,1)}, bf16[256,256]{1,0:T(8,128)(2,1)S(1)}, u32[]{:S(2)}) copy-start(bf16[256,256]{1,0:T(8,128)(2,1)S(1)} %collective-permute-done.15.refs_6_) | copy-start | bytes 393220
  200.1 7.0 %collective-permute-start.16 = (bf16[256,256]{1,0:T(8,128)(2,1)S(1)}, bf16[256,256]{1,0:T(8,128)(2,1)S(1)}, u32[]{:S(2)}, u32[]{:S(2)}) collective-permute-start(bf16[256,256]{1,0:T(8,128)(2,1)S(1)} %collective-permute-done.15.refs_6_), channel_id=1, source_target_pairs={{0,1},{1,0},{2,3},{3,2},{4,5},{5,4},{6,7},{7,6},{8,9},{9,8},{10,11... | collective-permute-start | bytes 393224 | tf_op jit(solution)/shard_map/ppermute | solution.py:49
  202.8 0.7 copy-start.13
  202.8 0.8 copy-start.14
  202.9 0.9 copy-start.15
  207.1 0.7 copy-start.19
  207.2 0.7 copy-start.20

commit v3 on v2

v3 whole, which is shorter than its diff:
```python
import math

import jax
import jax.numpy as jnp
from jax import lax
from jax.experimental import pallas as pl
from jax.experimental.pallas import tpu as pltpu
from jax.sharding import Mesh
from jax.sharding import PartitionSpec as P

TILE = 128
TBLK = 128
BF = jnp.bfloat16
F32 = jnp.float32
TOK = ("tok_0", "tok_1")
PARAMS = pltpu.CompilerParams(vmem_limit_bytes=56 * 1024 * 1024)
VM = pl.BlockSpec(memory_space=pltpu.VMEM)
SM = pl.BlockSpec(memory_space=pltpu.SMEM)


ANY = pl.BlockSpec(memory_space=pl.ANY)
PITCH = 40
ROWS = 72


class Late:
    def __init__(self, array, low=0, high=None):
        self.array, self.low = array, low
        self.rows = (array.shape[0] if high is None else high) - low


class Coming:
    def __init__(self, source, held, sem, late):
        if late.rows != source.shape[0]:
            source = source.at[pl.ds(late.low, late.rows)]
        self.copy, self.held = pltpu.make_async_copy(source, held, sem), held

    def get(self):
        self.copy.wait()
        return self.held


def call(kernel, ins, outs, scratch=(), late=(), after=(), through=()):
    specs = [SM if a.dtype == jnp.int32 else VM for a in ins]
    specs += [ANY] * (len(late) + len(after) + len(through))
    n, m, p = len(ins), len(late), len(through)
    skip = n + m + len(after)

    def body(*refs):
        given, sources, rest = refs[:n], refs[n : n + m], refs[skip + p :]
        rest = (*rest[: len(outs)], *rest[len(outs) + p :])
        if m:
            held, sems, rest = rest[-m - 1 : -1], rest[-1], rest[: -m - 1]
        coming = [
            Coming(source, held[i], sems.at[i], late[i]) for i, source in enumerate(sources)
        ]
        for c in coming:
            c.copy.start()
        kernel(*given, *coming, *rest)

    held = [pltpu.VMEM((a.rows, *a.array.shape[1:]), a.array.dtype) for a in late]
    sems = [pltpu.SemaphoreType.DMA((m,))] if m else []
    return pl.pallas_call(
        body,
        out_shape=[jax.ShapeDtypeStruct(s, d) for s, d in outs]
        + [jax.ShapeDtypeStruct(a.shape, a.dtype) for a in through],
        in_specs=specs,
        out_specs=[VM] * len(outs) + [ANY] * p,
        input_output_aliases={skip + i: len(outs) + i for i in range(p)},
        scratch_shapes=[*scratch, *held, *sems],
        compiler_params=PARAMS,
        name=kernel.__name__,
    )(*ins, *(a.array for a in late), *after, *through)


def dot(a, b, ca=1, cb=0):
    return lax.dot_general(a, b, (((ca,), (cb,)), ((), ())), preferred_element_type=F32)


def toward(x, k):
    return lax.ppermute(x, TOK, [(i, i ^ k) for i in range(4)])


def gather4(x):
    far = toward(x, 2)
    return [x, toward(x, 1), far, toward(far, 1)]


def exchange4(blocks):
    return [blocks[0]] + [toward(blocks[k], k) for k in (1, 2, 3)]


def exchange(blocks, axis="feat"):
    return lax.all_to_all(blocks, axis, split_axis=0, concat_axis=0, tiled=True)


def spread_kernel(x_ref, gain_ref, o_ref):
    strip, height = x_ref.shape
    lanes = height // 2
    x = x_ref[...].astype(F32)
    gain = gain_ref[...].astype(F32)
    row = jnp.concatenate([gain, jnp.zeros((1, lanes - strip), F32)], axis=1)
    rest = jnp.zeros((PITCH - strip - 1, lanes), F32)
    parts = [x[:, :lanes], row, rest, x[:, lanes:], row, rest]
    o_ref[...] = jnp.broadcast_to(jnp.concatenate(parts, axis=0).astype(BF)[None], o_ref.shape)


def put_wide(o_ref, at, w):
    rows, cols = w.shape
    for c in range(0, cols, 128):
        wide = min(128, cols - c)
        o_ref[pl.ds(at, rows), pl.ds(0, wide)] = w[:, c : c + wide]
        at += rows
    return at


def get_wide(w_ref, at, rows, cols):
    pieces = [
        w_ref[pl.ds(at + rows * i, rows), : min(128, cols - 128 * i)] for i in range(-(-cols // 128))
    ]
    return jnp.concatenate(pieces, axis=1)


def pack_kernel(*refs):
    *ws, o_ref = refs
    at = 0
    for w in ws:
        at = put_wide(o_ref, at, w[...])


def pack_turn_kernel(*refs):
    *ws, x_ref, o_ref, turned_ref = refs
    pack_kernel(*ws, o_ref)
    turned_ref[...] = x_ref[...].astype(F32).T.astype(BF)


def turn_first_kernel(w0, w1, w2, w3, enc_ref, down_ref):
    _, width, block = enc_ref.shape
    units = down_ref.shape[2]
    base = block * width // 128 + 2 * units * (-(-block // 128))
    for k, late in enumerate((w0, w1, w2, w3)):
        w = late.get()
        enc_ref[k] = get_wide(w, 0, block, width).T
        down_ref[k] = get_wide(w, base, units, block).T


def turn_second_kernel(w0, w1, w2, w3, dec_ref):
    _, n, block = dec_ref.shape
    for k, late in enumerate((w0, w1, w2, w3)):
        dec_ref[k] = get_wide(late.get(), 0, block, n).T


def encode_kernel(
    t_ref, mask_ref, bias_ref, g_late, w_late,
    n0, n1, n2, n3, codes_ref, slope_ref, x_ref,
):
    g_ref = g_late.get()
    feats, _, lanes = g_ref.shape
    height = 2 * lanes
    block = n0.shape[0]
    strip = 4 * block // feats
    depth = feats * strip
    width = codes_ref.shape[0]
    gains = g_ref[:, strip, :].astype(F32).T
    total = jnp.zeros((8, height), F32)
    for f in range(feats):
        x = jnp.concatenate(
            [g_ref[f, pl.ds(0, strip), :], g_ref[f, pl.ds(PITCH, strip), :]], axis=1
        ).astype(F32)
        square = x * x
        for r in range(0, strip - 7, 8):
            total = total + square[r : r + 8]
        tail = square[strip // 8 * 8 :]
        total = total + jnp.concatenate([tail, jnp.zeros_like(tail)], axis=0)
        x_ref[pl.ds(f * strip, strip), :] = x * gains[:strip, f : f + 1]
    total = jnp.sum(total, axis=0, keepdims=True)
    scale = lax.rsqrt(total / depth + 1e-06)
    t = t_ref[0]
    sums = 0.0
    w_ref = w_late.get()
    for k, n_ref in enumerate((n0, n1, n2, n3)):
        at = pl.ds(pl.multiple_of(jnp.bitwise_xor(t, k) * block, 64), block)
        n = (x_ref[at, :] * scale).astype(BF)
        n_ref[...] = n
        sums += dot(w_ref[k], n)
    bias = jnp.broadcast_to(bias_ref[...], (128, width)).T
    factor = 1.0 / math.sqrt(4 * height)
    for j in range(width // TILE):
        for i in range(height // TBLK):
            keep = mask_ref[i, j].astype(F32)
            r, c = slice(j * TILE, (j + 1) * TILE), slice(i * TBLK, (i + 1) * TBLK)
            part = jnp.maximum(sums[r, c] + bias[r, :], 0.0)
            codes_ref[r, c] = (part * part * keep).astype(BF)
            slope_ref[r, c] = part * (keep * (2.0 * factor))


def hidden_kernel(n0, n1, n2, n3, w0, w1, w2, w3, hidden_ref):
    units = hidden_ref.shape[0]
    gate = up = 0.0
    for late, w in ((n0, w0), (n1, w1), (n2, w2), (n3, w3)):
        n, w_ref = late.get()[...], w.get()
        block = n.shape[0]
        gate += dot(get_wide(w_ref, 0, units, block), n)
        up += dot(get_wide(w_ref, units * (-(-block // 128)), units, block), n)
    hidden_ref[...] = (jax.nn.gelu(gate, approximate=True) * up).astype(BF)


def decode_kernel(
    t_ref, codes_ref, before_ref, shifted_ref, hidden_ref, d_late, w0, w1, w2, w3, o_ref, both_ref
):
    t, layer = t_ref[0], t_ref[1]
    n = codes_ref.shape[0]
    block = o_ref.shape[2]
    both_ref[:n] = codes_ref[...]

    @pl.when(layer == 0)
    def _():
        both_ref[n:] = before_ref[...]

    @pl.when(layer != 0)
    def _():
        both_ref[n:] = shifted_ref[...]

    both, hidden = both_ref[...], hidden_ref[...]
    down_ref = d_late.get()
    lanes = o_ref.shape[3]
    for k, late in enumerate((w0, w1, w2, w3)):
        w = late.get()
        value = dot(get_wide(w, 0, block, 2 * n), both) - dot(down_ref[k], hidden)
        spot = jnp.bitwise_xor(t, k)
        for h in range(2):
            o_ref[spot, h] = value[:, h * lanes : (h + 1) * lanes].astype(BF)


def copies_kernel(x_ref, o_ref):
    o_ref[...] = jnp.broadcast_to(x_ref[...][None], o_ref.shape)


def back_kernel(t_ref, e_late, w_late, own_ref, prev_ref):
    t = t_ref[0]
    e_ref, w_ref = e_late.get(), w_late.get()
    n = own_ref.shape[0]
    total = 0.0
    for k in range(4):
        spot = jnp.bitwise_xor(t, k)
        err = jnp.concatenate([e_ref[spot, h] for h in range(2)], axis=1)
        total += dot(w_ref[k], err)
    own_ref[...] = total[:n]
    prev_ref[...] = total[n:].astype(BF)


def decoder_grads_kernel(t_ref, e_ref, c0, c1, c2, c3, own_ref, prev_ref):
    t = t_ref[0]
    n = own_ref.shape[1]
    factor = 1.0 / math.sqrt(8 * e_ref.shape[3])
    total = 0.0
    for k, c in enumerate((c0, c1, c2, c3)):
        spot = jnp.bitwise_xor(t, k)
        err = jnp.concatenate([e_ref[spot, h] for h in range(2)], axis=1)
        total += dot(err, c[...], 1, 1)
    own_ref[...] = total[:, :n] * factor
    prev_ref[...] = total[:, n:] * factor


def encoder_grads_kernel(n0, n1, n2, n3, p0, p1, p2, p3, grad_ref, bias_ref):
    total = bias = 0.0
    ones = jnp.ones((8, p0.shape[1]), BF)
    for n, p in ((n0, p0), (n1, p1), (n2, p2), (n3, p3)):
        total += dot(n[...], p[...], 1, 1)
        bias += dot(ones, p[...], 1, 1)
    grad_ref[...] = total
    bias_ref[...] = bias[:1]


def local(
    resid,
    norm_gain,
    prev_codes,
    feature_mask,
    w_gate,
    w_up,
    w_down,
    enc_weight,
    enc_bias,
    dec_own,
    dec_prev,
):
    height, strip = resid.shape[1:]
    peers = lax.axis_size("feat")
    width = enc_weight.shape[2]
    units = w_gate.shape[2]
    block = strip * peers // 4
    spans = -(-block // 128)
    t = 2 * lax.axis_index("tok_0") + lax.axis_index("tok_1")
    place = jnp.stack([t, lax.axis_index("layer")]).astype(jnp.int32)
    flip = lambda a: jnp.swapaxes(a[0], 0, 1)

    (copies,) = call(
        spread_kernel, (flip(resid), norm_gain), [((peers, 2 * PITCH, height // 2), BF)]
    )
    gathered = exchange(copies)
    first, before = call(
        pack_turn_kernel,
        (enc_weight[0], flip(w_gate), flip(w_up), w_down[0], prev_codes),
        [
            ((block * width // 128 + 3 * units * spans, 128), BF),
            ((width, height), BF),
        ],
    )
    first = gather4(first)
    (own_second,) = call(
        pack_kernel,
        (flip(dec_own), flip(dec_prev)),
        [((2 * block * width // 128, 128), BF)],
        after=(before,),
    )
    far_second = toward(own_second, 2)
    near_second = toward(own_second, 1)
    enc_turned, down_turned = call(
        turn_first_kernel,
        (),
        [((4, width, block), BF), ((4, block, units), BF)],
        late=[Late(w) for w in first],
    )
    cutoff = block * width // 128
    *normed, codes, slope = call(
        encode_kernel,
        (place, feature_mask[0], enc_bias),
        [((block, height), BF)] * 4 + [((width, height), BF), ((width, height), F32)],
        [pltpu.VMEM((4 * block, height), F32)],
        late=(Late(gathered), Late(enc_turned)),
    )
    shifted = lax.ppermute(codes, "layer", [(0, 1)])
    hidden, far_second = call(
        hidden_kernel,
        (),
        [((units, height), BF)],
        late=(*(Late(n) for n in normed), *(Late(w, cutoff, cutoff + 2 * units * spans) for w in first)),
        through=(far_second,),
    )
    second = [own_second, near_second, far_second, toward(far_second, 1)]
    (dec_turned,) = call(
        turn_second_kernel, (), [((4, 2 * width, block), BF)], late=[Late(w) for w in second]
    )
    parts, both = call(
        decode_kernel,
        (place, codes, before, shifted, hidden),
        [((4, 2, block, height // 2), BF), ((2 * width, height), BF)],
        late=(Late(down_turned), *(Late(w) for w in second)),
    )
    arrived = exchange(parts.reshape(peers, ROWS, height // 2))
    total = jnp.sum(arrived.astype(F32), axis=0).astype(BF)
    normed = exchange4(normed)
    (copies,) = call(
        copies_kernel, (total,), [(arrived.shape, BF)], after=(dec_turned, *normed[1:])
    )
    errors = exchange(copies).reshape(parts.shape)
    both = gather4(both)
    own_back, prev_back = call(
        back_kernel,
        (place,),
        [((width, height), F32), ((width, height), BF)],
        late=(Late(errors), Late(dec_turned)),
        after=both[1:],
    )
    err = exchange(errors, TOK)
    later = lax.ppermute(prev_back, "layer", [(1, 0)]).astype(F32)
    pregrad = gather4(((own_back + later) * slope).astype(BF))
    grad_own, grad_prev = call(
        decoder_grads_kernel, (place, err, *both), [((block, width), F32)] * 2
    )
    grad_enc, grad_bias = call(
        encoder_grads_kernel,
        (*normed, *pregrad),
        [((block, width), F32), ((1, width), F32)],
    )
    return (grad_enc[None], grad_bias, grad_own.T[None], grad_prev.T[None])


def solution(mesh):
    split = Mesh(
        mesh.devices.reshape(mesh.shape["layer"], mesh.shape["feat"], 2, 2),
        ("layer", "feat", "tok_0", "tok_1"),
    )
    placed = (
        P("layer", TOK, "feat"),
        P("layer", "feat"),
        P(TOK, "feat"),
        P("layer", TOK, "feat"),
        P("layer", TOK, "feat"),
        P("layer", TOK, "feat"),
        P("layer", "feat", TOK),
        P("layer", TOK, "feat"),
        P("layer", "feat"),
        P("layer", "feat", TOK),
        P("layer", "feat", TOK),
    )
    return jax.shard_map(
        local,
        mesh=split,
        in_specs=placed,
        out_specs=(
            P("layer", TOK, "feat"),
            P("layer", "feat"),
            P("layer", "feat", TOK),
            P("layer", "feat", TOK),
        ),
        check_vma=False,
    )
```

time: 213 us -> 220 us (1.033)
  Pallas kernels: 26.2 us -> 38.2 us
  waiting for transfers between devices: 77.7 us -> 72.6 us
    ppermute x18 -> x15, waiting for transfers between devices: 50 us -> 22.5 us  [toward(): return lax.ppermute(x, TOK, [(i, i ^ k) for i in range(4)])]
    ppermute x1, waiting for transfers between devices: 0.01 us -> 13.3 us  [local(): later = lax.ppermute(prev_back, 'layer', [(1, 0)]).astype(F32)]
    pallas_call x8 -> x12, Pallas kernels: 26.2 us -> 38.2 us  [call(): pl.pallas_call(body, out_shape=[jax.ShapeDtypeStruct(s, d) for s, d in ou...]
    all_to_all x3 -> x4, waiting for transfers between devices: 24.5 us -> 33.9 us  [exchange(): return lax.all_to_all(blocks, axis, split_axis=0, concat_axis=0, tiled=True)]
    ppermute x18 -> x15, starting transfers between devices: 53.6 us -> 44.8 us  [toward(): return lax.ppermute(x, TOK, [(i, i ^ k) for i in range(4)])]
    all_to_all x3 -> x4, starting transfers between devices: 38.9 us -> 46.7 us  [exchange(): return lax.all_to_all(blocks, axis, split_axis=0, concat_axis=0, tiled=True)]
    unnamed x50 -> x46, local copies, waits for them, and re-layouts: 5.51 us -> 7.39 us
  transfers between devices with their start and end apart: 23 -> 21, of which waited for: 9 -> 9; matrix products, arithmetic and copies ran while one was open for 1% -> 1% of each run, Pallas kernels for 5% -> 12%
where the time goes in v3:
time: 220 us; the launch traced here: 219 us
  starting transfers between devices  97.4 us (44%)
  waiting for transfers between devices  72.6 us (33%)
  Pallas kernels  38.2 us (17%)
  local copies, waits for them, and re-layouts  7.39 us (3%)
  other arithmetic  2.4 us (1%)
    all_to_all x4, starting transfers between devices, exchange(): return lax.all_to_all(blocks, axis, split_axis=0, concat_axis=0, tiled=True)  46.7 us
    ppermute x15, starting transfers between devices, toward(): return lax.ppermute(x, TOK, [(i, i ^ k) for i in range(4)])  44.8 us
    pallas_call x12, Pallas kernels, call(): pl.pallas_call(body, out_shape=[jax.ShapeDtypeStruct(s, d) for s, d in ou...  38.2 us
    all_to_all x4, waiting for transfers between devices, exchange(): return lax.all_to_all(blocks, axis, split_axis=0, concat_axis=0, tiled=True)  33.9 us
    ppermute x15, waiting for transfers between devices, toward(): return lax.ppermute(x, TOK, [(i, i ^ k) for i in range(4)])  22.5 us
    ppermute x1, waiting for transfers between devices, local(): later = lax.ppermute(prev_back, 'layer', [(1, 0)]).astype(F32)  13.3 us
    unnamed x46, local copies, waits for them, and re-layouts  7.39 us
    ppermute x1, starting transfers between devices, local(): shifted = lax.ppermute(codes, 'layer', [(0, 1)])  4.66 us
  transfers between devices with their start and end apart: 21, of which 9 were waited for; matrix products, arithmetic and copies ran while one was open for 1% of the time, Pallas kernels for 12%

profile of v3, /device:TPU:1, one launch (start us, length us, event | category | flops | bytes accessed | tf_op | source)
XLA Modules:
  0.0 219.0 jit_solution(3542667131297324655)
XLA Ops:
  0.6 1.9 spread_kernel.1
  2.6 17.1 %all-to-all-start = ((bf16[64,80,128]{2,1,0:T(8,128)(2,1)}), bf16[64,80,128]{2,1,0:T(8,128)(2,1)S(1)}, u32[]{:S(2)}, u32[]{:S(2)}) async-start(bf16[64,80,128]{2,1,0:T(8,128)(2,1)} %spread_kernel.1), calls=%async_computation | async-start | bytes 2621440 | tf_op jit(solution)/shard_map/all_to_all | solution.py:94
  19.7 2.4 %pack_turn_kernel.1 = (bf16[3312,128]{1,0:T(8,128)(2,1)}, bf16[256,256]{1,0:T(8,128)(2,1)}) custom-call(bf16[576,256]{1,0:T(8,128)(2,1)} %bitcast.32, bf16[144,576]{1,0:T(8,128)(2,1)} %bitcast.33, bf16[144,576]{1,0:T(8,128)(2,1)} %bitcast.34, bf16[144,576]{1,0:T(8,128)(2,1)} %bitcast.35, bf16[256,256]{1,0:T(8,128)(2,1)} %refs_4_.1), custom_call_target="tpu_custom_call" | custom-call | tf_op jit(solution)/shard_map/pack_turn_kernel/pallas_call | solution.py:63
  22.1 3.1 %collective-permute-start.1 = (bf16[3312,128]{1,0:T(8,128)(2,1)}, bf16[3312,128]{1,0:T(8,128)(2,1)S(1)}, u32[]{:S(2)}, u32[]{:S(2)}) collective-permute-start(bf16[3312,128]{1,0:T(8,128)(2,1)} %get-tuple-element.24.refs_0_.refs_4_), channel_id=1, source_target_pairs={{0,2},{1,3},{2,0},{3,1},{4,6},{5,7},{6,4},{7,5},{8,10},{9,11},{10,... | collective-permute-start | bytes 2543624 | tf_op jit(solution)/shard_map/ppermute | solution.py:81
  25.2 3.1 %collective-permute-start = (bf16[3312,128]{1,0:T(8,128)(2,1)}, bf16[3312,128]{1,0:T(8,128)(2,1)}, u32[]{:S(2)}, u32[]{:S(2)}) collective-permute-start(bf16[3312,128]{1,0:T(8,128)(2,1)} %get-tuple-element.24.refs_0_.refs_4_), channel_id=1, source_target_pairs={{0,1},{1,0},{2,3},{3,2},{4,5},{5,4},{6,7},{7,6},{8,9},{9,8},{10,11... | collective-permute-start | bytes 2543624 | tf_op jit(solution)/shard_map/ppermute | solution.py:81
  28.3 15.2 %collective-permute-done.1.refs_2_.refs_6_ = bf16[3312,128]{1,0:T(8,128)(2,1)S(1)} collective-permute-done((bf16[3312,128]{1,0:T(8,128)(2,1)}, bf16[3312,128]{1,0:T(8,128)(2,1)S(1)}, u32[]{:S(2)}, u32[]{:S(2)}) %collective-permute-start.1) | collective-permute-done | bytes 847904 | tf_op jit(solution)/shard_map/ppermute | solution.py:81
  43.6 3.8 %collective-permute-start.2 = (bf16[3312,128]{1,0:T(8,128)(2,1)S(1)}, bf16[3312,128]{1,0:T(8,128)(2,1)}, u32[]{:S(2)}, u32[]{:S(2)}) collective-permute-start(bf16[3312,128]{1,0:T(8,128)(2,1)S(1)} %collective-permute-done.1.refs_2_.refs_6_), channel_id=1, source_target_pairs={{0,1},{1,0},{2,3},{3,2},{4,5},{5,4},{6,7},{7,6},{8,9},{9,8},{10,11... | collective-permute-start | bytes 2543624 | tf_op jit(solution)/shard_map/ppermute | solution.py:81
  47.3 1.9 pack_kernel.1.refs_6_.refs_0_
  49.3 3.1 %collective-permute-start.7 = (bf16[2304,128]{1,0:T(8,128)(2,1)}, bf16[2304,128]{1,0:T(8,128)(2,1)S(1)}, u32[]{:S(2)}, u32[]{:S(2)}) collective-permute-start(bf16[2304,128]{1,0:T(8,128)(2,1)} %pack_kernel.1.refs_6_.refs_0_), channel_id=1, source_target_pairs={{0,2},{1,3},{2,0},{3,1},{4,6},{5,7},{6,4},{7,5},{8,10},{9,11},{10,... | collective-permute-start | bytes 1769480 | tf_op jit(solution)/shard_map/ppermute | solution.py:81
  52.4 2.2 %collective-permute-start.8 = (bf16[2304,128]{1,0:T(8,128)(2,1)}, bf16[2304,128]{1,0:T(8,128)(2,1)S(1)}, u32[]{:S(2)}, u32[]{:S(2)}) collective-permute-start(bf16[2304,128]{1,0:T(8,128)(2,1)} %pack_kernel.1.refs_6_.refs_0_), channel_id=1, source_target_pairs={{0,1},{1,0},{2,3},{3,2},{4,5},{5,4},{6,7},{7,6},{8,9},{9,8},{10,11... | collective-permute-start | bytes 1769480 | tf_op jit(solution)/shard_map/ppermute | solution.py:81
  55.2 3.5 %turn_first_kernel.1 = (bf16[4,256,576]{2,1,0:T(8,128)(2,1)}, bf16[4,576,144]{2,1,0:T(8,128)(2,1)}) custom-call(bf16[3312,128]{1,0:T(8,128)(2,1)} %get-tuple-element.24.refs_0_.refs_4_, bf16[3312,128]{1,0:T(8,128)(2,1)} %collective-permute-done.refs_1_.refs_5_, bf16[3312,128]{1,0:T(8,128)(2,1)} %copy-done.3, ...), custom_call_target="tpu_custom_call" | custom-call | tf_op jit(solution)/shard_map/turn_first_kernel/pallas_call | solution.py:63
  58.8 1.0 copy-done.1
  59.8 4.0 %encode_kernel.1 = (bf16[576,256]{1,0:T(8,128)(2,1)}, bf16[576,256]{1,0:T(8,128)(2,1)}, bf16[576,256]{1,0:T(8,128)(2,1)}, bf16[576,256]{1,0:T(8,128)(2,1)}, bf16...) custom-call(s32[2]{0:T(128)} %pad_add_fusion.refs_0_, s32[2,2]{1,0:T(2,128)} %bitcast.37, f32[1,256]{1,0:T(1,128)} %refs_2_.1, ...), custom_call_target="tpu_custom_call" | custom-call | tf_op jit(solution)/shard_map/encode_kernel/pallas_call | solution.py:63
  63.9 2.5 %collective-permute-done.7.refs_8_ = bf16[2304,128]{1,0:T(8,128)(2,1)S(1)} collective-permute-done((bf16[2304,128]{1,0:T(8,128)(2,1)}, bf16[2304,128]{1,0:T(8,128)(2,1)S(1)}, u32[]{:S(2)}, u32[]{:S(2)}) %collective-permute-start.7) | collective-permute-done | bytes 589856 | tf_op jit(solution)/shard_map/ppermute | solution.py:81
  66.3 0.8 copy-done
  67.1 3.0 %hidden_kernel.1 = (bf16[144,256]{1,0:T(8,128)(2,1)}, bf16[2304,128]{1,0:T(8,128)(2,1)}) custom-call(bf16[576,256]{1,0:T(8,128)(2,1)} %get-tuple-element.26.refs_0_, bf16[576,256]{1,0:T(8,128)(2,1)} %get-tuple-element.27.refs_1_, bf16[576,256]{1,0:T(8,128)(2,1)} %get-tuple-element.28.refs_2_, ...), custom_call_target="tpu_custom_call", output_to_operand_aliasing={{1}: (8, {})} | custom-call | tf_op jit(solution)/shard_map/hidden_kernel/pallas_call | solution.py:63
  70.1 2.7 %collective-permute-start.9 = (bf16[2304,128]{1,0:T(8,128)(2,1)}, bf16[2304,128]{1,0:T(8,128)(2,1)S(1)}, u32[]{:S(2)}, u32[]{:S(2)}) collective-permute-start(bf16[2304,128]{1,0:T(8,128)(2,1)} %get-tuple-element.34.refs_8_.refs_2_), channel_id=1, source_target_pairs={{0,1},{1,0},{2,3},{3,2},{4,5},{5,4},{6,7},{7,6},{8,9},{9,8},{10,11... | collective-permute-start | bytes 1769480 | tf_op jit(solution)/shard_map/ppermute | solution.py:81
  72.8 4.7 %collective-permute-start.6 = (bf16[256,256]{1,0:T(8,128)(2,1)S(1)}, bf16[256,256]{1,0:T(8,128)(2,1)S(1)}, u32[]{:S(2)}, u32[]{:S(2)}) collective-permute-start(bf16[256,256]{1,0:T(8,128)(2,1)S(1)} %copy-done.18), channel_id=1, source_target_pairs={{0,256},{1,257},{2,258},{3,259},{4,260},{5,261},{6,262},{7,263},{8... | collective-permute-start | bytes 393224 | tf_op jit(solution)/shard_map/ppermute | solution.py:333
  77.5 2.9 %collective-permute-done.6.refs_3_ = bf16[256,256]{1,0:T(8,128)(2,1)S(1)} collective-permute-done((bf16[256,256]{1,0:T(8,128)(2,1)S(1)}, bf16[256,256]{1,0:T(8,128)(2,1)S(1)}, u32[]{:S(2)}, u32[]{:S(2)}) %collective-permute-start.6) | collective-permute-done | bytes 131104 | tf_op jit(solution)/shard_map/ppermute | solution.py:333
  81.3 5.5 %decode_kernel.1 = (bf16[4,2,576,128]{3,2,1,0:T(8,128)(2,1)}, bf16[512,256]{1,0:T(8,128)(2,1)}) custom-call(s32[2]{0:T(128)} %pad_add_fusion.refs_0_, bf16[256,256]{1,0:T(8,128)(2,1)} %get-tuple-element.30.refs_1_, bf16[256,256]{1,0:T(8,128)(2,1)} %get-tuple-element.31.refs_2_, bf16[256,256]{1,0:T(8,128)(2,1)} %copy-done.19, ...), custom_call_target="tpu_custom_call" | custom-call | tf_op jit(solution)/shard_map/decode_kernel/pallas_call | solution.py:63
  86.8 12.3 %all-to-all-start.1 = ((bf16[64,72,128]{2,1,0:T(8,128)(2,1)}), bf16[64,72,128]{2,1,0:T(8,128)(2,1)S(1)}, u32[]{:S(2)}, u32[]{:S(2)}) async-start(bf16[64,72,128]{2,1,0:T(8,128)(2,1)} %bitcast.29), calls=%async_computation.1 | async-start | bytes 2359296 | tf_op jit(solution)/shard_map/all_to_all | solution.py:94
  99.1 3.0 %collective-permute-start.3 = (bf16[576,256]{1,0:T(8,128)(2,1)S(1)}, bf16[576,256]{1,0:T(8,128)(2,1)S(1)}, u32[]{:S(2)}, u32[]{:S(2)}) collective-permute-start(bf16[576,256]{1,0:T(8,128)(2,1)S(1)} %copy-done.15), channel_id=1, source_target_pairs={{0,1},{1,0},{2,3},{3,2},{4,5},{5,4},{6,7},{7,6},{8,9},{9,8},{10,11... | collective-permute-start | bytes 884744 | tf_op jit(solution)/shard_map/ppermute | solution.py:81
  102.1 2.2 %collective-permute-start.4 = (bf16[576,256]{1,0:T(8,128)(2,1)S(1)}, bf16[576,256]{1,0:T(8,128)(2,1)S(1)}, u32[]{:S(2)}, u32[]{:S(2)}) collective-permute-start(bf16[576,256]{1,0:T(8,128)(2,1)S(1)} %copy-done.14), channel_id=1, source_target_pairs={{0,2},{1,3},{2,0},{3,1},{4,6},{5,7},{6,4},{7,5},{8,10},{9,11},{10,... | collective-permute-start | bytes 884744 | tf_op jit(solution)/shard_map/ppermute | solution.py:81
  104.3 3.2 %collective-permute-start.5 = (bf16[576,256]{1,0:T(8,128)(2,1)S(1)}, bf16[576,256]{1,0:T(8,128)(2,1)S(1)}, u32[]{:S(2)}, u32[]{:S(2)}) collective-permute-start(bf16[576,256]{1,0:T(8,128)(2,1)S(1)} %copy-done.13), channel_id=1, source_target_pairs={{0,3},{1,2},{2,1},{3,0},{4,7},{5,6},{6,5},{7,4},{8,11},{9,10},{10,... | collective-permute-start | bytes 884744 | tf_op jit(solution)/shard_map/ppermute | solution.py:81
  107.5 3.5 %turn_second_kernel.1.refs_1_.refs_2_ = bf16[4,512,576]{2,1,0:T(8,128)(2,1)} custom-call(bf16[2304,128]{1,0:T(8,128)(2,1)} %pack_kernel.1.refs_6_.refs_0_, bf16[2304,128]{1,0:T(8,128)(2,1)} %copy-done.4, bf16[2304,128]{1,0:T(8,128)(2,1)} %get-tuple-element.34.refs_8_.refs_2_, bf16[2304,128]{1,0:T(8,128)(2,1)} %copy-done.5), custom_call_target="tpu_custom_call" | custom-call | tf_op jit(solution)/shard_map/turn_second_kernel/pallas_call | solution.py:63
  111.0 17.3 %all-to-all-done.1 = bf16[64,72,128]{2,1,0:T(8,128)(2,1)S(1)} async-done(((bf16[64,72,128]{2,1,0:T(8,128)(2,1)}), bf16[64,72,128]{2,1,0:T(8,128)(2,1)S(1)}, u32[]{:S(2)}, u32[]{:S(2)}) %all-to-all-start.1) | async-done | bytes 1179680 | tf_op jit(solution)/shard_map/all_to_all | solution.py:94
  128.4 0.8 reduce_sum.12.refs_0_
  130.0 0.7 copy-done.8
  130.7 1.9 copies_kernel.1
  132.6 9.7 %all-to-all-start.2 = ((bf16[64,72,128]{2,1,0:T(8,128)(2,1)}), bf16[64,72,128]{2,1,0:T(8,128)(2,1)}, u32[]{:S(2)}, u32[]{:S(2)}) async-start(bf16[64,72,128]{2,1,0:T(8,128)(2,1)} %copies_kernel.1), calls=%async_computation.2 | async-start | bytes 2359296 | tf_op jit(solution)/shard_map/all_to_all | solution.py:94
  142.3 2.2 %collective-permute-start.11 = (bf16[512,256]{1,0:T(8,128)(2,1)S(1)}, bf16[512,256]{1,0:T(8,128)(2,1)S(1)}, u32[]{:S(2)}, u32[]{:S(2)}) collective-permute-start(bf16[512,256]{1,0:T(8,128)(2,1)S(1)} %copy-done.16), channel_id=1, source_target_pairs={{0,2},{1,3},{2,0},{3,1},{4,6},{5,7},{6,4},{7,5},{8,10},{9,11},{10,... | collective-permute-start | bytes 786440 | tf_op jit(solution)/shard_map/ppermute | solution.py:81
  144.6 3.4 %collective-permute-start.10 = (bf16[512,256]{1,0:T(8,128)(2,1)S(1)}, bf16[512,256]{1,0:T(8,128)(2,1)S(1)}, u32[]{:S(2)}, u32[]{:S(2)}) collective-permute-start(bf16[512,256]{1,0:T(8,128)(2,1)S(1)} %copy-done.16), channel_id=1, source_target_pairs={{0,1},{1,0},{2,3},{3,2},{4,5},{5,4},{6,7},{7,6},{8,9},{9,8},{10,11... | collective-permute-start | bytes 786440 | tf_op jit(solution)/shard_map/ppermute | solution.py:81
  147.9 3.0 %collective-permute-done.11.refs_4_ = bf16[512,256]{1,0:T(8,128)(2,1)S(1)} collective-permute-done((bf16[512,256]{1,0:T(8,128)(2,1)S(1)}, bf16[512,256]{1,0:T(8,128)(2,1)S(1)}, u32[]{:S(2)}, u32[]{:S(2)}) %collective-permute-start.11) | collective-permute-done | bytes 262176 | tf_op jit(solution)/shard_map/ppermute | solution.py:81
  150.9 3.9 %collective-permute-start.12 = (bf16[512,256]{1,0:T(8,128)(2,1)S(1)}, bf16[512,256]{1,0:T(8,128)(2,1)S(1)}, u32[]{:S(2)}, u32[]{:S(2)}) collective-permute-start(bf16[512,256]{1,0:T(8,128)(2,1)S(1)} %collective-permute-done.11.refs_4_), channel_id=1, source_target_pairs={{0,1},{1,0},{2,3},{3,2},{4,5},{5,4},{6,7},{7,6},{8,9},{9,8},{10,11... | collective-permute-start | bytes 786440 | tf_op jit(solution)/shard_map/ppermute | solution.py:81
  154.8 16.6 %all-to-all-done.2 = bf16[64,72,128]{2,1,0:T(8,128)(2,1)} async-done(((bf16[64,72,128]{2,1,0:T(8,128)(2,1)}), bf16[64,72,128]{2,1,0:T(8,128)(2,1)}, u32[]{:S(2)}, u32[]{:S(2)}) %all-to-all-start.2) | async-done | bytes 1179680 | tf_op jit(solution)/shard_map/all_to_all | solution.py:94
  171.4 7.6 %all-to-all-start.3 = ((bf16[4,2,576,128]{3,2,1,0:T(8,128)(2,1)}), bf16[4,2,576,128]{3,2,1,0:T(8,128)(2,1)S(1)}, u32[]{:S(2)}, u32[]{:S(2)}) async-start(bf16[4,2,576,128]{3,2,1,0:T(8,128)(2,1)} %bitcast.16.refs_1_), calls=%async_computation.3 | async-start | bytes 2359296 | tf_op jit(solution)/shard_map/all_to_all | solution.py:94
  180.4 4.4 %back_kernel.1 = (f32[256,256]{1,0:T(8,128)}, bf16[256,256]{1,0:T(8,128)(2,1)}) custom-call(s32[2]{0:T(128)} %pad_add_fusion.refs_0_, bf16[4,2,576,128]{3,2,1,0:T(8,128)(2,1)} %bitcast.16.refs_1_, bf16[4,512,576]{2,1,0:T(8,128)(2,1)} %turn_second_kernel.1.refs_1_.refs_2_, bf16[512,256]{1,0:T(8,128)(2,1)} %copy-done.10, bf16[512,256]{1,0:T(8,128)(2,1)} %copy-done.9, ...), custom_call_target="tpu_custom_call" | custom-call | tf_op jit(solution)/shard_map/back_kernel/pallas_call | solution.py:63
  184.8 1.3 collective-permute-start.13
  186.1 13.3 %collective-permute-done.13 = bf16[256,256]{1,0:T(8,128)(2,1)S(1)} collective-permute-done((bf16[256,256]{1,0:T(8,128)(2,1)}, bf16[256,256]{1,0:T(8,128)(2,1)S(1)}, u32[]{:S(2)}, u32[]{:S(2)}) %collective-permute-start.13) | collective-permute-done | bytes 131104 | tf_op jit(solution)/shard_map/ppermute | solution.py:367
  199.4 1.0 multiply_convert_fusion.refs_4_
  200.4 2.4 %collective-permute-start.15 = (bf16[256,256]{1,0:T(8,128)(2,1)S(1)}, bf16[256,256]{1,0:T(8,128)(2,1)S(1)}, u32[]{:S(2)}, u32[]{:S(2)}) collective-permute-start(bf16[256,256]{1,0:T(8,128)(2,1)S(1)} %multiply_convert_fusion.refs_4_), channel_id=1, source_target_pairs={{0,2},{1,3},{2,0},{3,1},{4,6},{5,7},{6,4},{7,5},{8,10},{9,11},{10,... | collective-permute-start | bytes 393224 | tf_op jit(solution)/shard_map/ppermute | solution.py:81
  202.8 3.1 %collective-permute-start.14 = (bf16[256,256]{1,0:T(8,128)(2,1)S(1)}, bf16[256,256]{1,0:T(8,128)(2,1)S(1)}, u32[]{:S(2)}, u32[]{:S(2)}) collective-permute-start(bf16[256,256]{1,0:T(8,128)(2,1)S(1)} %multiply_convert_fusion.refs_4_), channel_id=1, source_target_pairs={{0,1},{1,0},{2,3},{3,2},{4,5},{5,4},{6,7},{7,6},{8,9},{9,8},{10,11... | collective-permute-start | bytes 393224 | tf_op jit(solution)/shard_map/ppermute | solution.py:81
  205.9 0.8 collective-permute-done.15.refs_6_
  206.8 3.4 %collective-permute-start.16 = (bf16[256,256]{1,0:T(8,128)(2,1)S(1)}, bf16[256,256]{1,0:T(8,128)(2,1)S(1)}, u32[]{:S(2)}, u32[]{:S(2)}) collective-permute-start(bf16[256,256]{1,0:T(8,128)(2,1)S(1)} %collective-permute-done.15.refs_6_), channel_id=1, source_target_pairs={{0,1},{1,0},{2,3},{3,2},{4,5},{5,4},{6,7},{7,6},{8,9},{9,8},{10,11... | collective-permute-start | bytes 393224 | tf_op jit(solution)/shard_map/ppermute | solution.py:81
  210.2 0.9 collective-permute-done.16.refs_7_
  211.8 2.8 %encoder_grads_kernel.1 = (f32[576,256]{1,0:T(8,128)}, f32[1,256]{1,0:T(1,128)}) custom-call(bf16[576,256]{1,0:T(8,128)(2,1)} %get-tuple-element.26.refs_0_, bf16[576,256]{1,0:T(8,128)(2,1)} %copy-done.6, bf16[576,256]{1,0:T(8,128)(2,1)} %copy-done.7, bf16[576,256]{1,0:T(8,128)(2,1)} %copy-done.8, bf16[256,256]{1,0:T(8,128)(2,1)} %copy-done.12, ...), custom_call_target="tpu_custom_call" | custom-call | tf_op jit(solution)/shard_map/encoder_grads_kernel/pallas_call | solution.py:63
  214.5 1.1 copy-done.2
  215.6 3.4 %decoder_grads_kernel.1 = (f32[576,256]{1,0:T(8,128)}, f32[576,256]{1,0:T(8,128)}) custom-call(s32[2]{0:T(128)} %pad_add_fusion.refs_0_, bf16[4,2,576,128]{3,2,1,0:T(8,128)(2,1)} %copy-done.2, bf16[512,256]{1,0:T(8,128)(2,1)} %get-tuple-element.36.refs_2_, bf16[512,256]{1,0:T(8,128)(2,1)} %copy-done.10, bf16[512,256]{1,0:T(8,128)(2,1)} %copy-done.9, ...), custom_call_target="tpu_custom_call" | custom-call | tf_op jit(solution)/shard_map/decoder_grads_kernel/pallas_call | solution.py:63
  (55 shorter events, 4.4 us)
Async XLA Ops:
  2.6 56.2 %all-to-all-start = ((bf16[64,80,128]{2,1,0:T(8,128)(2,1)}), bf16[64,80,128]{2,1,0:T(8,128)(2,1)S(1)}, u32[]{:S(2)}, u32[]{:S(2)}) async-start(bf16[64,80,128]{2,1,0:T(8,128)(2,1)} %spread_kernel.1), calls=%async_computation | async-start | bytes 2621440 | tf_op jit(solution)/shard_map/all_to_all | solution.py:94
  22.1 21.5 %collective-permute-start.1 = (bf16[3312,128]{1,0:T(8,128)(2,1)}, bf16[3312,128]{1,0:T(8,128)(2,1)S(1)}, u32[]{:S(2)}, u32[]{:S(2)}) collective-permute-start(bf16[3312,128]{1,0:T(8,128)(2,1)} %get-tuple-element.24.refs_0_.refs_4_), channel_id=1, source_target_pairs={{0,2},{1,3},{2,0},{3,1},{4,6},{5,7},{6,4},{7,5},{8,10},{9,11},{10,... | collective-permute-start | bytes 2543624 | tf_op jit(solution)/shard_map/ppermute | solution.py:81
  25.2 30.1 %collective-permute-start = (bf16[3312,128]{1,0:T(8,128)(2,1)}, bf16[3312,128]{1,0:T(8,128)(2,1)}, u32[]{:S(2)}, u32[]{:S(2)}) collective-permute-start(bf16[3312,128]{1,0:T(8,128)(2,1)} %get-tuple-element.24.refs_0_.refs_4_), channel_id=1, source_target_pairs={{0,1},{1,0},{2,3},{3,2},{4,5},{5,4},{6,7},{7,6},{8,9},{9,8},{10,11... | collective-permute-start | bytes 2543624 | tf_op jit(solution)/shard_map/ppermute | solution.py:81
  43.6 11.7 %copy-start.3 = (bf16[3312,128]{1,0:T(8,128)(2,1)}, bf16[3312,128]{1,0:T(8,128)(2,1)S(1)}, u32[]{:S(2)}) copy-start(bf16[3312,128]{1,0:T(8,128)(2,1)S(1)} %collective-permute-done.1.refs_2_.refs_6_) | copy-start | bytes 2543620
  43.6 11.7 %collective-permute-start.2 = (bf16[3312,128]{1,0:T(8,128)(2,1)S(1)}, bf16[3312,128]{1,0:T(8,128)(2,1)}, u32[]{:S(2)}, u32[]{:S(2)}) collective-permute-start(bf16[3312,128]{1,0:T(8,128)(2,1)S(1)} %collective-permute-done.1.refs_2_.refs_6_), channel_id=1, source_target_pairs={{0,1},{1,0},{2,3},{3,2},{4,5},{5,4},{6,7},{7,6},{8,9},{9,8},{10,11... | collective-permute-start | bytes 2543624 | tf_op jit(solution)/shard_map/ppermute | solution.py:81
  49.3 17.0 %collective-permute-start.7 = (bf16[2304,128]{1,0:T(8,128)(2,1)}, bf16[2304,128]{1,0:T(8,128)(2,1)S(1)}, u32[]{:S(2)}, u32[]{:S(2)}) collective-permute-start(bf16[2304,128]{1,0:T(8,128)(2,1)} %pack_kernel.1.refs_6_.refs_0_), channel_id=1, source_target_pairs={{0,2},{1,3},{2,0},{3,1},{4,6},{5,7},{6,4},{7,5},{8,10},{9,11},{10,... | collective-permute-start | bytes 1769480 | tf_op jit(solution)/shard_map/ppermute | solution.py:81
  52.4 25.1 %collective-permute-start.8 = (bf16[2304,128]{1,0:T(8,128)(2,1)}, bf16[2304,128]{1,0:T(8,128)(2,1)S(1)}, u32[]{:S(2)}, u32[]{:S(2)}) collective-permute-start(bf16[2304,128]{1,0:T(8,128)(2,1)} %pack_kernel.1.refs_6_.refs_0_), channel_id=1, source_target_pairs={{0,1},{1,0},{2,3},{3,2},{4,5},{5,4},{6,7},{7,6},{8,9},{9,8},{10,11... | collective-permute-start | bytes 1769480 | tf_op jit(solution)/shard_map/ppermute | solution.py:81
  58.8 1.1 copy-start.1
  66.3 0.8 copy-start
  67.1 5.7 %copy-start.18 = (bf16[256,256]{1,0:T(8,128)(2,1)S(1)}, bf16[256,256]{1,0:T(8,128)(2,1)}, u32[]{:S(2)}) copy-start(bf16[256,256]{1,0:T(8,128)(2,1)} %get-tuple-element.30.refs_1_) | copy-start | bytes 393220
  70.1 10.3 %collective-permute-start.9 = (bf16[2304,128]{1,0:T(8,128)(2,1)}, bf16[2304,128]{1,0:T(8,128)(2,1)S(1)}, u32[]{:S(2)}, u32[]{:S(2)}) collective-permute-start(bf16[2304,128]{1,0:T(8,128)(2,1)} %get-tuple-element.34.refs_8_.refs_2_), channel_id=1, source_target_pairs={{0,1},{1,0},{2,3},{3,2},{4,5},{5,4},{6,7},{7,6},{8,9},{9,8},{10,11... | collective-permute-start | bytes 1769480 | tf_op jit(solution)/shard_map/ppermute | solution.py:81
  72.8 7.6 %collective-permute-start.6 = (bf16[256,256]{1,0:T(8,128)(2,1)S(1)}, bf16[256,256]{1,0:T(8,128)(2,1)S(1)}, u32[]{:S(2)}, u32[]{:S(2)}) collective-permute-start(bf16[256,256]{1,0:T(8,128)(2,1)S(1)} %copy-done.18), channel_id=1, source_target_pairs={{0,256},{1,257},{2,258},{3,259},{4,260},{5,261},{6,262},{7,263},{8... | collective-permute-start | bytes 393224 | tf_op jit(solution)/shard_map/ppermute | solution.py:333
  77.5 2.9 %copy-start.4 = (bf16[2304,128]{1,0:T(8,128)(2,1)}, bf16[2304,128]{1,0:T(8,128)(2,1)S(1)}, u32[]{:S(2)}) copy-start(bf16[2304,128]{1,0:T(8,128)(2,1)S(1)} %collective-permute-done.8.refs_7_.refs_1_) | copy-start | bytes 1769476
  80.4 0.7 copy-start.19
  80.4 0.9 copy-start.5
  86.7 12.3 %copy-start.15 = (bf16[576,256]{1,0:T(8,128)(2,1)S(1)}, bf16[576,256]{1,0:T(8,128)(2,1)}, u32[]{:S(2)}) copy-start(bf16[576,256]{1,0:T(8,128)(2,1)} %get-tuple-element.27.refs_1_) | copy-start | bytes 884740
  86.7 15.3 %copy-start.14 = (bf16[576,256]{1,0:T(8,128)(2,1)S(1)}, bf16[576,256]{1,0:T(8,128)(2,1)}, u32[]{:S(2)}) copy-start(bf16[576,256]{1,0:T(8,128)(2,1)} %get-tuple-element.28.refs_2_) | copy-start | bytes 884740
  86.7 17.5 %copy-start.13 = (bf16[576,256]{1,0:T(8,128)(2,1)S(1)}, bf16[576,256]{1,0:T(8,128)(2,1)}, u32[]{:S(2)}) copy-start(bf16[576,256]{1,0:T(8,128)(2,1)} %get-tuple-element.29.refs_3_) | copy-start | bytes 884740
  86.8 41.6 %all-to-all-start.1 = ((bf16[64,72,128]{2,1,0:T(8,128)(2,1)}), bf16[64,72,128]{2,1,0:T(8,128)(2,1)S(1)}, u32[]{:S(2)}, u32[]{:S(2)}) async-start(bf16[64,72,128]{2,1,0:T(8,128)(2,1)} %bitcast.29), calls=%async_computation.1 | async-start | bytes 2359296 | tf_op jit(solution)/shard_map/all_to_all | solution.py:94
  99.1 30.1 %collective-permute-start.3 = (bf16[576,256]{1,0:T(8,128)(2,1)S(1)}, bf16[576,256]{1,0:T(8,128)(2,1)S(1)}, u32[]{:S(2)}, u32[]{:S(2)}) collective-permute-start(bf16[576,256]{1,0:T(8,128)(2,1)S(1)} %copy-done.15), channel_id=1, source_target_pairs={{0,1},{1,0},{2,3},{3,2},{4,5},{5,4},{6,7},{7,6},{8,9},{9,8},{10,11... | collective-permute-start | bytes 884744 | tf_op jit(solution)/shard_map/ppermute | solution.py:81
  102.1 27.1 %collective-permute-start.4 = (bf16[576,256]{1,0:T(8,128)(2,1)S(1)}, bf16[576,256]{1,0:T(8,128)(2,1)S(1)}, u32[]{:S(2)}, u32[]{:S(2)}) collective-permute-start(bf16[576,256]{1,0:T(8,128)(2,1)S(1)} %copy-done.14), channel_id=1, source_target_pairs={{0,2},{1,3},{2,0},{3,1},{4,6},{5,7},{6,4},{7,5},{8,10},{9,11},{10,... | collective-permute-start | bytes 884744 | tf_op jit(solution)/shard_map/ppermute | solution.py:81
  104.3 24.9 %collective-permute-start.5 = (bf16[576,256]{1,0:T(8,128)(2,1)S(1)}, bf16[576,256]{1,0:T(8,128)(2,1)S(1)}, u32[]{:S(2)}, u32[]{:S(2)}) collective-permute-start(bf16[576,256]{1,0:T(8,128)(2,1)S(1)} %copy-done.13), channel_id=1, source_target_pairs={{0,3},{1,2},{2,1},{3,0},{4,7},{5,6},{6,5},{7,4},{8,11},{9,10},{10,... | collective-permute-start | bytes 884744 | tf_op jit(solution)/shard_map/ppermute | solution.py:81
  129.2 0.7 copy-start.6
  129.2 0.8 copy-start.7
  130.0 0.7 copy-start.8
  132.6 9.7 %copy-start.16 = (bf16[512,256]{1,0:T(8,128)(2,1)S(1)}, bf16[512,256]{1,0:T(8,128)(2,1)}, u32[]{:S(2)}) copy-start(bf16[512,256]{1,0:T(8,128)(2,1)} %get-tuple-element.36.refs_2_) | copy-start | bytes 786436
  132.6 38.8 %all-to-all-start.2 = ((bf16[64,72,128]{2,1,0:T(8,128)(2,1)}), bf16[64,72,128]{2,1,0:T(8,128)(2,1)}, u32[]{:S(2)}, u32[]{:S(2)}) async-start(bf16[64,72,128]{2,1,0:T(8,128)(2,1)} %copies_kernel.1), calls=%async_computation.2 | async-start | bytes 2359296 | tf_op jit(solution)/shard_map/all_to_all | solution.py:94
  142.3 8.6 %collective-permute-start.11 = (bf16[512,256]{1,0:T(8,128)(2,1)S(1)}, bf16[512,256]{1,0:T(8,128)(2,1)S(1)}, u32[]{:S(2)}, u32[]{:S(2)}) collective-permute-start(bf16[512,256]{1,0:T(8,128)(2,1)S(1)} %copy-done.16), channel_id=1, source_target_pairs={{0,2},{1,3},{2,0},{3,1},{4,6},{5,7},{6,4},{7,5},{8,10},{9,11},{10,... | collective-permute-start | bytes 786440 | tf_op jit(solution)/shard_map/ppermute | solution.py:81
  144.6 34.5 %collective-permute-start.10 = (bf16[512,256]{1,0:T(8,128)(2,1)S(1)}, bf16[512,256]{1,0:T(8,128)(2,1)S(1)}, u32[]{:S(2)}, u32[]{:S(2)}) collective-permute-start(bf16[512,256]{1,0:T(8,128)(2,1)S(1)} %copy-done.16), channel_id=1, source_target_pairs={{0,1},{1,0},{2,3},{3,2},{4,5},{5,4},{6,7},{7,6},{8,9},{9,8},{10,11... | collective-permute-start | bytes 786440 | tf_op jit(solution)/shard_map/ppermute | solution.py:81
  150.9 20.5 %copy-start.9 = (bf16[512,256]{1,0:T(8,128)(2,1)}, bf16[512,256]{1,0:T(8,128)(2,1)S(1)}, u32[]{:S(2)}) copy-start(bf16[512,256]{1,0:T(8,128)(2,1)S(1)} %collective-permute-done.11.refs_4_) | copy-start | bytes 786436
  150.9 28.1 %collective-permute-start.12 = (bf16[512,256]{1,0:T(8,128)(2,1)S(1)}, bf16[512,256]{1,0:T(8,128)(2,1)S(1)}, u32[]{:S(2)}, u32[]{:S(2)}) collective-permute-start(bf16[512,256]{1,0:T(8,128)(2,1)S(1)} %collective-permute-done.11.refs_4_), channel_id=1, source_target_pairs={{0,1},{1,0},{2,3},{3,2},{4,5},{5,4},{6,7},{7,6},{8,9},{9,8},{10,11... | collective-permute-start | bytes 786440 | tf_op jit(solution)/shard_map/ppermute | solution.py:81
  171.4 43.1 %all-to-all-start.3 = ((bf16[4,2,576,128]{3,2,1,0:T(8,128)(2,1)}), bf16[4,2,576,128]{3,2,1,0:T(8,128)(2,1)S(1)}, u32[]{:S(2)}, u32[]{:S(2)}) async-start(bf16[4,2,576,128]{3,2,1,0:T(8,128)(2,1)} %bitcast.16.refs_1_), calls=%async_computation.3 | async-start | bytes 2359296 | tf_op jit(solution)/shard_map/all_to_all | solution.py:94
  179.0 20.4 %copy-start.17 = (f32[256,256]{1,0:T(8,128)S(1)}, f32[256,256]{1,0:T(8,128)}, u32[]{:S(2)}) copy-start(f32[256,256]{1,0:T(8,128)} %get-tuple-element.39) | copy-start | bytes 786436
  179.0 0.7 copy-start.10
  179.7 0.7 copy-start.11
  184.8 14.6 %collective-permute-start.13 = (bf16[256,256]{1,0:T(8,128)(2,1)}, bf16[256,256]{1,0:T(8,128)(2,1)S(1)}, u32[]{:S(2)}, u32[]{:S(2)}) collective-permute-start(bf16[256,256]{1,0:T(8,128)(2,1)} %get-tuple-element.38), channel_id=1, source_target_pairs={{256,0},{257,1},{258,2},{259,3},{260,4},{261,5},{262,6},{263,7},{2... | collective-permute-start | bytes 393224 | tf_op jit(solution)/shard_map/ppermute | solution.py:367
  200.4 10.7 %copy-start.12 = (bf16[256,256]{1,0:T(8,128)(2,1)}, bf16[256,256]{1,0:T(8,128)(2,1)S(1)}, u32[]{:S(2)}) copy-start(bf16[256,256]{1,0:T(8,128)(2,1)S(1)} %multiply_convert_fusion.refs_4_) | copy-start | bytes 393220
  200.4 6.3 %collective-permute-start.15 = (bf16[256,256]{1,0:T(8,128)(2,1)S(1)}, bf16[256,256]{1,0:T(8,128)(2,1)S(1)}, u32[]{:S(2)}, u32[]{:S(2)}) collective-permute-start(bf16[256,256]{1,0:T(8,128)(2,1)S(1)} %multiply_convert_fusion.refs_4_), channel_id=1, source_target_pairs={{0,2},{1,3},{2,0},{3,1},{4,6},{5,7},{6,4},{7,5},{8,10},{9,11},{10,... | collective-permute-start | bytes 393224 | tf_op jit(solution)/shard_map/ppermute | solution.py:81
  202.8 7.3 %collective-permute-start.14 = (bf16[256,256]{1,0:T(8,128)(2,1)S(1)}, bf16[256,256]{1,0:T(8,128)(2,1)S(1)}, u32[]{:S(2)}, u32[]{:S(2)}) collective-permute-start(bf16[256,256]{1,0:T(8,128)(2,1)S(1)} %multiply_convert_fusion.refs_4_), channel_id=1, source_target_pairs={{0,1},{1,0},{2,3},{3,2},{4,5},{5,4},{6,7},{7,6},{8,9},{9,8},{10,11... | collective-permute-start | bytes 393224 | tf_op jit(solution)/shard_map/ppermute | solution.py:81
  206.8 4.3 %copy-start.20 = (bf16[256,256]{1,0:T(8,128)(2,1)}, bf16[256,256]{1,0:T(8,128)(2,1)S(1)}, u32[]{:S(2)}) copy-start(bf16[256,256]{1,0:T(8,128)(2,1)S(1)} %collective-permute-done.15.refs_6_) | copy-start | bytes 393220
  206.8 4.3 %collective-permute-start.16 = (bf16[256,256]{1,0:T(8,128)(2,1)S(1)}, bf16[256,256]{1,0:T(8,128)(2,1)S(1)}, u32[]{:S(2)}, u32[]{:S(2)}) collective-permute-start(bf16[256,256]{1,0:T(8,128)(2,1)S(1)} %collective-permute-done.15.refs_6_), channel_id=1, source_target_pairs={{0,1},{1,0},{2,3},{3,2},{4,5},{5,4},{6,7},{7,6},{8,9},{9,8},{10,11... | collective-permute-start | bytes 393224 | tf_op jit(solution)/shard_map/ppermute | solution.py:81
  210.1 1.0 copy-start.21
  211.1 0.6 copy-start.22
  214.5 1.1 copy-start.2

commit v4 on v2

--- a/solution.py
+++ b/solution.py
@@ -13,7 +13,7 @@
 BF = jnp.bfloat16
 F32 = jnp.float32
 TOK = ("tok_0", "tok_1")
-PARAMS = pltpu.CompilerParams(vmem_limit_bytes=56 * 1024 * 1024)
+PARAMS = pltpu.CompilerParams(vmem_limit_bytes=24 * 1024 * 1024)
 VM = pl.BlockSpec(memory_space=pltpu.VMEM)
 SM = pl.BlockSpec(memory_space=pltpu.SMEM)
 
@@ -23,22 +23,35 @@
 ROWS = 72
 
 
-def call(kernel, ins, outs, scratch=(), after=()):
-    specs = [SM if a.dtype == jnp.int32 else VM for a in ins] + [ANY] * len(after)
-    count = len(ins)
+def call(kernel, ins, outs, after=(), through=(), scratch=(), leaving=(), plain=False):
+    def held(a):
+        small = plain or a.dtype == jnp.int32 or a.size < 2**15
+        return a if small else pltpu.with_memory_space_constraint(a, pltpu.VMEM)
+
+    n, p, skip = len(outs), len(through), len(ins) + len(after)
+    specs = [SM if a.dtype == jnp.int32 else VM for a in ins]
 
     def body(*refs):
-        kernel(*refs[:count], *refs[count + len(after) :])
+        rest = refs[skip + p :]
+        kernel(*refs[: len(ins)], *rest[:n], *rest[n + p :])
 
     return pl.pallas_call(
         body,
-        out_shape=[jax.ShapeDtypeStruct(s, d) for s, d in outs],
-        in_specs=specs,
-        out_specs=[VM] * len(outs),
+        out_shape=[
+            (pltpu.HBM if i in leaving else pltpu.VMEM)(*o) for i, o in enumerate(outs)
+        ]
+        + [pltpu.VMEM(a.shape, a.dtype) for a in through],
+        in_specs=specs + [VM] * (skip - len(ins) + p),
+        out_specs=[VM] * (n + p),
+        input_output_aliases={skip + i: n + i for i in range(p)},
         scratch_shapes=list(scratch),
         compiler_params=PARAMS,
         name=kernel.__name__,
-    )(*ins, *after)
+    )(*(held(a) for a in (*ins, *after, *through)))
+
+
+def corner(arrays):
+    return sum(lax.slice(a, (0, 0), (8, 128)).astype(F32) for a in arrays)
 
 
 def dot(a, b, ca=1, cb=0):
@@ -89,14 +102,26 @@
     return jnp.concatenate(pieces, axis=1)
 
 
-def pack_kernel(enc, gate, up, own, prev, down, before, first_ref, second_ref, before_ref):
+def pack_kernel(*refs):
+    *ws, o_ref = refs
     at = 0
-    for w in (enc, gate, up):
-        at = put_wide(first_ref, at, w[...])
-    at = 0
-    for w in (own, prev, down):
-        at = put_wide(second_ref, at, w[...])
-    before_ref[...] = before[...].astype(F32).T.astype(BF)
+    for w in ws:
+        at = put_wide(o_ref, at, w[...])
+
+
+def pack_turn_kernel(*refs):
+    *ws, x_ref, o_ref, turned_ref = refs
+    pack_kernel(*ws, o_ref)
+    turned_ref[...] = x_ref[...].astype(F32).T.astype(BF)
+
+
+def pin_kernel(*refs):
+    pass
+
+
+def pregrad_kernel(own_ref, later_ref, slope_ref, o_ref):
+    back = own_ref[...] + later_ref[...].astype(F32)
+    o_ref[...] = (back * slope_ref[...]).astype(BF)
 
 
 def encode_kernel(
@@ -254,57 +279,71 @@
     flip = lambda a: jnp.swapaxes(a[0], 0, 1)
 
     (copies,) = call(
-        spread_kernel, (flip(resid), norm_gain), [((peers, 2 * PITCH, height // 2), BF)]
+        spread_kernel,
+        (flip(resid), norm_gain),
+        [((peers, 2 * PITCH, height // 2), BF)],
+        leaving=(0,),
+        plain=True,
     )
     gathered = exchange(copies)
-    first, second, before = call(
+    (second,) = call(
         pack_kernel,
-        (
-            enc_weight[0], flip(w_gate), flip(w_up),
-            flip(dec_own), flip(dec_prev), w_down[0], prev_codes,
-        ),
-        [
-            ((block * width // 128 + 2 * units * spans, 128), BF),
-            ((2 * block * width // 128 + units * spans, 128), BF),
-            ((width, height), BF),
-        ],
+        (flip(dec_own), flip(dec_prev), w_down[0]),
+        [((2 * block * width // 128 + units * spans, 128), BF)],
+        plain=True,
+    )
+    near, far = toward(second, 1), toward(second, 2)
+    first, before = call(
+        pack_turn_kernel,
+        (enc_weight[0], flip(w_gate), flip(w_up), prev_codes),
+        [((block * width // 128 + 2 * units * spans, 128), BF), ((width, height), BF)],
+        plain=True,
     )
     first = gather4(first)
-    second = gather4(second)
     *normed, codes, slope, hidden = call(
         encode_kernel,
         (place, feature_mask[0], gathered, *first, enc_bias),
         [((block, height), BF)] * 4
         + [((width, height), BF), ((width, height), F32), ((units, height), BF)],
-        [pltpu.VMEM((4 * block, height), F32)],
+        scratch=[pltpu.VMEM((4 * block, height), F32)],
     )
     shifted = lax.ppermute(codes, "layer", [(0, 1)])
+    (far,) = call(pin_kernel, (), [], after=(slope,), through=(far,))
+    second = [second, near, far, toward(far, 1)]
     parts, both = call(
         decode_kernel,
         (place, codes, before, shifted, hidden, *second),
         [((peers, ROWS, height // 2), BF), ((2 * width, height), BF)],
+        leaving=(0,),
     )
     arrived = exchange(parts)
     normed = exchange4(normed)
-    (copies,) = call(total_kernel, (arrived,), [(parts.shape, BF)], after=normed[1:])
+    (copies,) = call(total_kernel, (arrived,), [(parts.shape, BF)], after=(corner(normed[1:]),), leaving=(0,))
     errors = exchange(copies)
     both = gather4(both)
     own_back, prev_back, *err = call(
         back_kernel,
         (place, errors, *second),
         [((width, height), F32), ((width, height), BF)] + [((block, height), BF)] * 4,
-        after=both[1:],
-    )
-    later = lax.ppermute(prev_back, "layer", [(1, 0)]).astype(F32)
+        after=(corner(both[1:]),),
+    )
+    later = lax.ppermute(prev_back, "layer", [(1, 0)])
+    (pregrad,) = call(
+        pregrad_kernel, (own_back, later, slope), [((width, height), BF)]
+    )
+    pregrad = gather4(pregrad)
+    err[1], err[3] = call(
+        pin_kernel, (), [], after=(pregrad[2],), through=(err[1], err[3])
+    )
     err = exchange4(err)
-    pregrad = gather4(((own_back + later) * slope).astype(BF))
     grad_own, grad_prev = call(
-        decoder_grads_kernel, (*err, *both), [((block, width), F32)] * 2
+        decoder_grads_kernel, (*err, *both), [((block, width), F32)] * 2, leaving=(0, 1)
     )
     grad_enc, grad_bias = call(
         encoder_grads_kernel,
         (*normed, *pregrad),
         [((block, width), F32), ((1, width), F32)],
+        leaving=(0, 1),
     )
     return (grad_enc[None], grad_bias, grad_own.T[None], grad_prev.T[None])
 

time: 213 us -> 190 us (0.89)
  waiting for transfers between devices: 77.7 us -> 62.4 us
  Pallas kernels: 26.2 us -> 14.8 us
  starting transfers between devices: 98.4 us -> 103 us
  local copies, waits for them, and re-layouts: 5.51 us -> 7.99 us
    ppermute x18, waiting for transfers between devices: 50 us -> 26.9 us  [toward(): return lax.ppermute(x, TOK, [(i, i ^ k) for i in range(4)])]
    pallas_call x8 -> x12, Pallas kernels: 26.2 us -> 14.8 us  [call(): pl.pallas_call(body, out_shape=[(pltpu.HBM if i in leaving else pltpu.VME...]
    ppermute x18, starting transfers between devices: 53.6 us -> 61.2 us  [toward(): return lax.ppermute(x, TOK, [(i, i ^ k) for i in range(4)])]
    ppermute x1, waiting for transfers between devices: 0.01 us -> 6.03 us  [local(): later = lax.ppermute(prev_back, 'layer', [(1, 0)])]
    all_to_all x3, starting transfers between devices: 38.9 us -> 35.5 us  [exchange(): lax.all_to_all(blocks, 'feat', split_axis=0, concat_axis=0, tiled=True)]
    unnamed x50 -> x68, local copies, waits for them, and re-layouts: 5.51 us -> 7.99 us
  transfers between devices with their start and end apart: 23 -> 23, of which waited for: 9 -> 13; matrix products, arithmetic and copies ran while one was open for 1% -> 0% of each run, Pallas kernels for 5% -> 3%
where the time goes in v4:
time: 190 us; the launch traced here: 189 us
  starting transfers between devices  103 us (54%)
  waiting for transfers between devices  62.4 us (33%)
  Pallas kernels  14.8 us (8%)
  local copies, waits for them, and re-layouts  7.99 us (4%)
    ppermute x18, starting transfers between devices, toward(): return lax.ppermute(x, TOK, [(i, i ^ k) for i in range(4)])  61.2 us
    all_to_all x3, starting transfers between devices, exchange(): lax.all_to_all(blocks, 'feat', split_axis=0, concat_axis=0, tiled=True)  35.5 us
    ppermute x18, waiting for transfers between devices, toward(): return lax.ppermute(x, TOK, [(i, i ^ k) for i in range(4)])  26.9 us
    all_to_all x3, waiting for transfers between devices, exchange(): lax.all_to_all(blocks, 'feat', split_axis=0, concat_axis=0, tiled=True)  26.6 us
    pallas_call x12, Pallas kernels, call(): pl.pallas_call(body, out_shape=[(pltpu.HBM if i in leaving else pltpu.VME...  14.8 us
    unnamed x68, local copies, waits for them, and re-layouts  7.99 us
    ppermute x1, waiting for transfers between devices, local(): later = lax.ppermute(prev_back, 'layer', [(1, 0)])  6.03 us
    ppermute x1, starting transfers between devices, local(): shifted = lax.ppermute(codes, 'layer', [(0, 1)])  4.66 us
  transfers between devices with their start and end apart: 23, of which 13 were waited for; matrix products, arithmetic and copies ran while one was open for 0% of the time, Pallas kernels for 3%

profile of v4, /device:TPU:1, one launch (start us, length us, event | category | flops | bytes accessed | tf_op | source)
XLA Modules:
  0.0 189.3 jit_solution(10102152580732504979)
XLA Ops:
  0.6 0.7 copy-done.27
  2.0 1.2 spread_kernel.1
  3.3 17.3 %all-to-all-start = ((bf16[64,80,128]{2,1,0:T(8,128)(2,1)}), bf16[64,80,128]{2,1,0:T(8,128)(2,1)S(1)}, u32[]{:S(2)}, u32[]{:S(2)}) async-start(bf16[64,80,128]{2,1,0:T(8,128)(2,1)} %spread_kernel.1), calls=%async_computation | async-start | bytes 2621440 | tf_op jit(solution)/shard_map/all_to_all | solution.py:75
  21.4 3.1 %collective-permute-start.1 = (bf16[2592,128]{1,0:T(8,128)(2,1)S(1)}, bf16[2592,128]{1,0:T(8,128)(2,1)}, u32[]{:S(2)}, u32[]{:S(2)}) collective-permute-start(bf16[2592,128]{1,0:T(8,128)(2,1)S(1)} %get-tuple-element.27.refs_3_), channel_id=1, source_target_pairs={{0,2},{1,3},{2,0},{3,1},{4,6},{5,7},{6,4},{7,5},{8,10},{9,11},{10,... | collective-permute-start | bytes 1990664 | tf_op jit(solution)/shard_map/ppermute | solution.py:62
  24.5 0.9 copy-done.21
  25.6 2.2 %collective-permute-start.8 = (bf16[3024,128]{1,0:T(8,128)(2,1)S(1)}, bf16[3024,128]{1,0:T(8,128)(2,1)S(1)}, u32[]{:S(2)}, u32[]{:S(2)}) collective-permute-start(bf16[3024,128]{1,0:T(8,128)(2,1)S(1)} %pack_kernel.1.refs_5_.refs_2_), channel_id=1, source_target_pairs={{0,2},{1,3},{2,0},{3,1},{4,6},{5,7},{6,4},{7,5},{8,10},{9,11},{10,... | collective-permute-start | bytes 2322440 | tf_op jit(solution)/shard_map/ppermute | solution.py:62
  27.7 3.4 %collective-permute-start = (bf16[2592,128]{1,0:T(8,128)(2,1)S(1)}, bf16[2592,128]{1,0:T(8,128)(2,1)}, u32[]{:S(2)}, u32[]{:S(2)}) collective-permute-start(bf16[2592,128]{1,0:T(8,128)(2,1)S(1)} %get-tuple-element.27.refs_3_), channel_id=1, source_target_pairs={{0,1},{1,0},{2,3},{3,2},{4,5},{5,4},{6,7},{7,6},{8,9},{9,8},{10,11... | collective-permute-start | bytes 1990664 | tf_op jit(solution)/shard_map/ppermute | solution.py:62
  31.2 7.7 %collective-permute-done.1.refs_5_ = bf16[2592,128]{1,0:T(8,128)(2,1)} collective-permute-done((bf16[2592,128]{1,0:T(8,128)(2,1)S(1)}, bf16[2592,128]{1,0:T(8,128)(2,1)}, u32[]{:S(2)}, u32[]{:S(2)}) %collective-permute-start.1) | collective-permute-done | bytes 663584 | tf_op jit(solution)/shard_map/ppermute | solution.py:62
  38.8 5.2 %collective-permute-start.2 = (bf16[2592,128]{1,0:T(8,128)(2,1)}, bf16[2592,128]{1,0:T(8,128)(2,1)}, u32[]{:S(2)}, u32[]{:S(2)}) collective-permute-start(bf16[2592,128]{1,0:T(8,128)(2,1)} %collective-permute-done.1.refs_5_), channel_id=1, source_target_pairs={{0,1},{1,0},{2,3},{3,2},{4,5},{5,4},{6,7},{7,6},{8,9},{9,8},{10,11... | collective-permute-start | bytes 1990664 | tf_op jit(solution)/shard_map/ppermute | solution.py:62
  44.1 1.9 %collective-permute-start.7 = (bf16[3024,128]{1,0:T(8,128)(2,1)S(1)}, bf16[3024,128]{1,0:T(8,128)(2,1)}, u32[]{:S(2)}, u32[]{:S(2)}) collective-permute-start(bf16[3024,128]{1,0:T(8,128)(2,1)S(1)} %pack_kernel.1.refs_5_.refs_2_), channel_id=1, source_target_pairs={{0,1},{1,0},{2,3},{3,2},{4,5},{5,4},{6,7},{7,6},{8,9},{9,8},{10,11... | collective-permute-start | bytes 2322440 | tf_op jit(solution)/shard_map/ppermute | solution.py:62
  46.1 6.6 %all-to-all-done.refs_2_ = bf16[64,80,128]{2,1,0:T(8,128)(2,1)S(1)} async-done(((bf16[64,80,128]{2,1,0:T(8,128)(2,1)}), bf16[64,80,128]{2,1,0:T(8,128)(2,1)S(1)}, u32[]{:S(2)}, u32[]{:S(2)}) %all-to-all-start) | async-done | bytes 1310752 | tf_op jit(solution)/shard_map/all_to_all | solution.py:75
  52.7 3.3 %encode_kernel.1 = (bf16[576,256]{1,0:T(8,128)(2,1)S(1)}, bf16[576,256]{1,0:T(8,128)(2,1)S(1)}, bf16[576,256]{1,0:T(8,128)(2,1)S(1)}, bf16[576,256]{1,0:T(8,128)...) custom-call(s32[2]{0:T(128)S(1)} %pad_add_fusion.refs_0_, ...), custom_call_target="tpu_custom_call" | custom-call | tf_op jit(solution)/shard_map/encode_kernel/pallas_call | solution.py:38
  56.2 6.1 %collective-permute-start.9 = (bf16[3024,128]{1,0:T(8,128)(2,1)S(1)}, bf16[3024,128]{1,0:T(8,128)(2,1)S(1)}, u32[]{:S(2)}, u32[]{:S(2)}) collective-permute-start(bf16[3024,128]{1,0:T(8,128)(2,1)S(1)} %pin_kernel.2.refs_7_.refs_4_), channel_id=1, source_target_pairs={{0,1},{1,0},{2,3},{3,2},{4,5},{5,4},{6,7},{7,6},{8,9},{9,8},{10,11... | collective-permute-start | bytes 2322440 | tf_op jit(solution)/shard_map/ppermute | solution.py:62
  62.3 4.7 %collective-permute-start.6 = (bf16[256,256]{1,0:T(8,128)(2,1)S(1)}, bf16[256,256]{1,0:T(8,128)(2,1)S(1)}, u32[]{:S(2)}, u32[]{:S(2)}) collective-permute-start(bf16[256,256]{1,0:T(8,128)(2,1)S(1)} %get-tuple-element.32.refs_1_), channel_id=1, source_target_pairs={{0,256},{1,257},{2,258},{3,259},{4,260},{5,261},{6,262},{7,263},{8... | collective-permute-start | bytes 393224 | tf_op jit(solution)/shard_map/ppermute | solution.py:310
  66.9 2.9 %collective-permute-done.6.refs_3_ = bf16[256,256]{1,0:T(8,128)(2,1)S(1)} collective-permute-done((bf16[256,256]{1,0:T(8,128)(2,1)S(1)}, bf16[256,256]{1,0:T(8,128)(2,1)S(1)}, u32[]{:S(2)}, u32[]{:S(2)}) %collective-permute-start.6) | collective-permute-done | bytes 131104 | tf_op jit(solution)/shard_map/ppermute | solution.py:310
  69.8 3.3 %decode_kernel.1 = (bf16[64,72,128]{2,1,0:T(8,128)(2,1)}, bf16[512,256]{1,0:T(8,128)(2,1)S(1)}) custom-call(s32[2]{0:T(128)S(1)} %pad_add_fusion.refs_0_, bf16[256,256]{1,0:T(8,128)(2,1)S(1)} %get-tuple-element.32.refs_1_, bf16[256,256]{1,0:T(8,128)(2,1)S(1)} %copy-done.26, bf16[256,256]{1,0:T(8,128)(2,1)S(1)} %collective-permute-done.6.refs_3_, ...), custom_call_target="tpu_custom_call" | custom-call | tf_op jit(solution)/shard_map/decode_kernel/pallas_call | solution.py:38
  73.9 9.0 %all-to-all-start.1 = ((bf16[64,72,128]{2,1,0:T(8,128)(2,1)}), bf16[64,72,128]{2,1,0:T(8,128)(2,1)S(1)}, u32[]{:S(2)}, u32[]{:S(2)}) async-start(bf16[64,72,128]{2,1,0:T(8,128)(2,1)} %get-tuple-element.36), calls=%async_computation.1 | async-start | bytes 2359296 | tf_op jit(solution)/shard_map/all_to_all | solution.py:75
  82.9 3.0 %collective-permute-start.3 = (bf16[576,256]{1,0:T(8,128)(2,1)}, bf16[576,256]{1,0:T(8,128)(2,1)S(1)}, u32[]{:S(2)}, u32[]{:S(2)}) collective-permute-start(bf16[576,256]{1,0:T(8,128)(2,1)} %copy-done.33), channel_id=1, source_target_pairs={{0,1},{1,0},{2,3},{3,2},{4,5},{5,4},{6,7},{7,6},{8,9},{9,8},{10,11... | collective-permute-start | bytes 884744 | tf_op jit(solution)/shard_map/ppermute | solution.py:62
  85.9 2.2 %collective-permute-start.4 = (bf16[576,256]{1,0:T(8,128)(2,1)}, bf16[576,256]{1,0:T(8,128)(2,1)S(1)}, u32[]{:S(2)}, u32[]{:S(2)}) collective-permute-start(bf16[576,256]{1,0:T(8,128)(2,1)} %copy-done.32), channel_id=1, source_target_pairs={{0,2},{1,3},{2,0},{3,1},{4,6},{5,7},{6,4},{7,5},{8,10},{9,11},{10,... | collective-permute-start | bytes 884744 | tf_op jit(solution)/shard_map/ppermute | solution.py:62
  88.1 3.2 %collective-permute-start.5 = (bf16[576,256]{1,0:T(8,128)(2,1)}, bf16[576,256]{1,0:T(8,128)(2,1)S(1)}, u32[]{:S(2)}, u32[]{:S(2)}) collective-permute-start(bf16[576,256]{1,0:T(8,128)(2,1)} %copy-done.31), channel_id=1, source_target_pairs={{0,3},{1,2},{2,1},{3,0},{4,7},{5,6},{6,5},{7,4},{8,11},{9,10},{10,... | collective-permute-start | bytes 884744 | tf_op jit(solution)/shard_map/ppermute | solution.py:62
  91.3 5.2 %collective-permute-done.4.refs_2_ = bf16[576,256]{1,0:T(8,128)(2,1)S(1)} collective-permute-done((bf16[576,256]{1,0:T(8,128)(2,1)}, bf16[576,256]{1,0:T(8,128)(2,1)S(1)}, u32[]{:S(2)}, u32[]{:S(2)}) %collective-permute-start.4) | collective-permute-done | bytes 294944 | tf_op jit(solution)/shard_map/ppermute | solution.py:62
  96.6 6.7 %collective-permute-done.5.refs_3_ = bf16[576,256]{1,0:T(8,128)(2,1)S(1)} collective-permute-done((bf16[576,256]{1,0:T(8,128)(2,1)}, bf16[576,256]{1,0:T(8,128)(2,1)S(1)}, u32[]{:S(2)}, u32[]{:S(2)}) %collective-permute-start.5) | collective-permute-done | bytes 294944 | tf_op jit(solution)/shard_map/ppermute | solution.py:62
  103.3 0.7 copy-done.2
  104.0 0.7 copy-done.4
  104.7 0.7 copy-done.6
  105.4 6.8 %all-to-all-done.1.refs_0_ = bf16[64,72,128]{2,1,0:T(8,128)(2,1)S(1)} async-done(((bf16[64,72,128]{2,1,0:T(8,128)(2,1)}), bf16[64,72,128]{2,1,0:T(8,128)(2,1)S(1)}, u32[]{:S(2)}, u32[]{:S(2)}) %all-to-all-start.1) | async-done | bytes 1179680 | tf_op jit(solution)/shard_map/all_to_all | solution.py:75
  112.2 1.3 total_kernel.1
  113.5 9.3 %all-to-all-start.2 = ((bf16[64,72,128]{2,1,0:T(8,128)(2,1)}), bf16[64,72,128]{2,1,0:T(8,128)(2,1)S(1)}, u32[]{:S(2)}, u32[]{:S(2)}) async-start(bf16[64,72,128]{2,1,0:T(8,128)(2,1)} %total_kernel.1), calls=%async_computation.2 | async-start | bytes 2359296 | tf_op jit(solution)/shard_map/all_to_all | solution.py:75
  122.8 2.2 %collective-permute-start.11 = (bf16[512,256]{1,0:T(8,128)(2,1)}, bf16[512,256]{1,0:T(8,128)(2,1)S(1)}, u32[]{:S(2)}, u32[]{:S(2)}) collective-permute-start(bf16[512,256]{1,0:T(8,128)(2,1)} %copy-done.19), channel_id=1, source_target_pairs={{0,2},{1,3},{2,0},{3,1},{4,6},{5,7},{6,4},{7,5},{8,10},{9,11},{10,... | collective-permute-start | bytes 786440 | tf_op jit(solution)/shard_map/ppermute | solution.py:62
  125.0 3.4 %collective-permute-start.10 = (bf16[512,256]{1,0:T(8,128)(2,1)}, bf16[512,256]{1,0:T(8,128)(2,1)S(1)}, u32[]{:S(2)}, u32[]{:S(2)}) collective-permute-start(bf16[512,256]{1,0:T(8,128)(2,1)} %copy-done.19), channel_id=1, source_target_pairs={{0,1},{1,0},{2,3},{3,2},{4,5},{5,4},{6,7},{7,6},{8,9},{9,8},{10,11... | collective-permute-start | bytes 786440 | tf_op jit(solution)/shard_map/ppermute | solution.py:62
  128.4 3.1 %collective-permute-done.11.refs_6_ = bf16[512,256]{1,0:T(8,128)(2,1)S(1)} collective-permute-done((bf16[512,256]{1,0:T(8,128)(2,1)}, bf16[512,256]{1,0:T(8,128)(2,1)S(1)}, u32[]{:S(2)}, u32[]{:S(2)}) %collective-permute-start.11) | collective-permute-done | bytes 262176 | tf_op jit(solution)/shard_map/ppermute | solution.py:62
  131.5 4.0 %collective-permute-start.12 = (bf16[512,256]{1,0:T(8,128)(2,1)S(1)}, bf16[512,256]{1,0:T(8,128)(2,1)S(1)}, u32[]{:S(2)}, u32[]{:S(2)}) collective-permute-start(bf16[512,256]{1,0:T(8,128)(2,1)S(1)} %collective-permute-done.11.refs_6_), channel_id=1, source_target_pairs={{0,1},{1,0},{2,3},{3,2},{4,5},{5,4},{6,7},{7,6},{8,9},{9,8},{10,11... | collective-permute-start | bytes 786440 | tf_op jit(solution)/shard_map/ppermute | solution.py:62
  135.5 1.1 collective-permute-done.12.refs_7_
  136.7 0.7 copy-done.13
  138.8 13.2 %all-to-all-done.2.refs_1_ = bf16[64,72,128]{2,1,0:T(8,128)(2,1)S(1)} async-done(((bf16[64,72,128]{2,1,0:T(8,128)(2,1)}), bf16[64,72,128]{2,1,0:T(8,128)(2,1)S(1)}, u32[]{:S(2)}, u32[]{:S(2)}) %all-to-all-start.2) | async-done | bytes 1179680 | tf_op jit(solution)/shard_map/all_to_all | solution.py:75
  152.0 2.2 %back_kernel.1 = (f32[256,256]{1,0:T(8,128)S(1)}, bf16[256,256]{1,0:T(8,128)(2,1)S(1)}, bf16[576,256]{1,0:T(8,128)(2,1)S(1)}, bf16[576,256]{1,0:T(8,128)(2,1)S(1...) custom-call(s32[2]{0:T(128)S(1)} %pad_add_fusion.refs_0_, ...), custom_call_target="tpu_custom_call" | custom-call | tf_op jit(solution)/shard_map/back_kernel/pallas_call | solution.py:38
  154.2 1.4 collective-permute-start.13
  155.7 6.0 %collective-permute-done.13.refs_1_ = bf16[256,256]{1,0:T(8,128)(2,1)S(1)} collective-permute-done((bf16[256,256]{1,0:T(8,128)(2,1)S(1)}, bf16[256,256]{1,0:T(8,128)(2,1)S(1)}, u32[]{:S(2)}, u32[]{:S(2)}) %collective-permute-start.13) | collective-permute-done | bytes 131104 | tf_op jit(solution)/shard_map/ppermute | solution.py:330
  161.8 2.2 %collective-permute-start.15 = (bf16[256,256]{1,0:T(8,128)(2,1)S(1)}, bf16[256,256]{1,0:T(8,128)(2,1)S(1)}, u32[]{:S(2)}, u32[]{:S(2)}) collective-permute-start(bf16[256,256]{1,0:T(8,128)(2,1)S(1)} %pregrad_kernel.1.refs_4_), channel_id=1, source_target_pairs={{0,2},{1,3},{2,0},{3,1},{4,6},{5,7},{6,4},{7,5},{8,10},{9,11},{10,... | collective-permute-start | bytes 393224 | tf_op jit(solution)/shard_map/ppermute | solution.py:62
  164.0 3.1 %collective-permute-start.18 = (bf16[576,256]{1,0:T(8,128)(2,1)S(1)}, bf16[576,256]{1,0:T(8,128)(2,1)S(1)}, u32[]{:S(2)}, u32[]{:S(2)}) collective-permute-start(bf16[576,256]{1,0:T(8,128)(2,1)S(1)} %get-tuple-element.46), channel_id=1, source_target_pairs={{0,2},{1,3},{2,0},{3,1},{4,6},{5,7},{6,4},{7,5},{8,10},{9,11},{10,... | collective-permute-start | bytes 884744 | tf_op jit(solution)/shard_map/ppermute | solution.py:62
  167.6 9.3 %collective-permute-start.17 = (bf16[576,256]{1,0:T(8,128)(2,1)S(1)}, bf16[576,256]{1,0:T(8,128)(2,1)S(1)}, u32[]{:S(2)}, u32[]{:S(2)}) collective-permute-start(bf16[576,256]{1,0:T(8,128)(2,1)S(1)} %get-tuple-element.45), channel_id=1, source_target_pairs={{0,1},{1,0},{2,3},{3,2},{4,5},{5,4},{6,7},{7,6},{8,9},{9,8},{10,11... | collective-permute-start | bytes 884744 | tf_op jit(solution)/shard_map/ppermute | solution.py:62
  177.0 2.4 %collective-permute-start.19 = (bf16[576,256]{1,0:T(8,128)(2,1)S(1)}, bf16[576,256]{1,0:T(8,128)(2,1)S(1)}, u32[]{:S(2)}, u32[]{:S(2)}) collective-permute-start(bf16[576,256]{1,0:T(8,128)(2,1)S(1)} %get-tuple-element.47), channel_id=1, source_target_pairs={{0,3},{1,2},{2,1},{3,0},{4,7},{5,6},{6,5},{7,4},{8,11},{9,10},{10,... | collective-permute-start | bytes 884744 | tf_op jit(solution)/shard_map/ppermute | solution.py:62
  179.4 2.4 %collective-permute-start.14 = (bf16[256,256]{1,0:T(8,128)(2,1)S(1)}, bf16[256,256]{1,0:T(8,128)(2,1)S(1)}, u32[]{:S(2)}, u32[]{:S(2)}) collective-permute-start(bf16[256,256]{1,0:T(8,128)(2,1)S(1)} %pregrad_kernel.1.refs_4_), channel_id=1, source_target_pairs={{0,1},{1,0},{2,3},{3,2},{4,5},{5,4},{6,7},{7,6},{8,9},{9,8},{10,11... | collective-permute-start | bytes 393224 | tf_op jit(solution)/shard_map/ppermute | solution.py:62
  181.8 1.9 %collective-permute-start.16 = (bf16[256,256]{1,0:T(8,128)(2,1)S(1)}, bf16[256,256]{1,0:T(8,128)(2,1)S(1)}, u32[]{:S(2)}, u32[]{:S(2)}) collective-permute-start(bf16[256,256]{1,0:T(8,128)(2,1)S(1)} %collective-permute-done.15.refs_6_.refs_0_), channel_id=1, source_target_pairs={{0,1},{1,0},{2,3},{3,2},{4,5},{5,4},{6,7},{7,6},{8,9},{9,8},{10,11... | collective-permute-start | bytes 393224 | tf_op jit(solution)/shard_map/ppermute | solution.py:62
  183.7 1.3 collective-permute-done.16.refs_7_
  185.0 1.4 encoder_grads_kernel.1
  186.4 1.1 collective-permute-done.19.refs_3_
  187.5 1.8 decoder_grads_kernel.1
  (81 shorter events, 4.5 us)
Async XLA Ops:
  0.6 0.7 copy-start.27
  3.2 17.3 %copy-start.8 = (bf16[1,576,256]{2,1,0:T(8,128)(2,1)S(1)}, bf16[1,576,256]{2,1,0:T(8,128)(2,1)}, u32[]{:S(2)}) copy-start(bf16[1,576,256]{2,1,0:T(8,128)(2,1)} %param.18) | copy-start | bytes 884740
  3.2 17.3 %copy-start.22 = (bf16[1,576,144]{1,2,0:T(8,128)(2,1)S(1)}, bf16[1,576,144]{1,2,0:T(8,128)(2,1)}, u32[]{:S(2)}) copy-start(bf16[1,576,144]{1,2,0:T(8,128)(2,1)} %param.15) | copy-start | bytes 497668
  3.2 17.3 %copy-start.23 = (bf16[1,576,144]{1,2,0:T(8,128)(2,1)S(1)}, bf16[1,576,144]{1,2,0:T(8,128)(2,1)}, u32[]{:S(2)}) copy-start(bf16[1,576,144]{1,2,0:T(8,128)(2,1)} %param.16) | copy-start | bytes 497668
  3.2 17.3 %copy-start.24 = (bf16[256,256]{1,0:T(8,128)(2,1)S(1)}, bf16[256,256]{1,0:T(8,128)(2,1)}, u32[]{:S(2)}) copy-start(bf16[256,256]{1,0:T(8,128)(2,1)} %refs_3_.1) | copy-start | bytes 393220
  3.2 21.3 %copy-start.9 = (bf16[1,256,576]{1,2,0:T(8,128)(2,1)S(1)}, bf16[1,256,576]{1,2,0:T(8,128)(2,1)}, u32[]{:S(2)}) copy-start(bf16[1,256,576]{1,2,0:T(8,128)(2,1)} %param.20) | copy-start | bytes 884740
  3.3 21.3 %copy-start.10 = (bf16[1,256,576]{1,2,0:T(8,128)(2,1)S(1)}, bf16[1,256,576]{1,2,0:T(8,128)(2,1)}, u32[]{:S(2)}) copy-start(bf16[1,256,576]{1,2,0:T(8,128)(2,1)} %param.21) | copy-start | bytes 884740
  3.3 49.5 %all-to-all-start = ((bf16[64,80,128]{2,1,0:T(8,128)(2,1)}), bf16[64,80,128]{2,1,0:T(8,128)(2,1)S(1)}, u32[]{:S(2)}, u32[]{:S(2)}) async-start(bf16[64,80,128]{2,1,0:T(8,128)(2,1)} %spread_kernel.1), calls=%async_computation | async-start | bytes 2621440 | tf_op jit(solution)/shard_map/all_to_all | solution.py:75
  20.6 32.1 %copy-start.28 = (s32[1,2,2]{2,1,0:T(2,128)S(1)}, s32[1,2,2]{2,1,0:T(2,128)}, u32[]{:S(2)}) copy-start(s32[1,2,2]{2,1,0:T(2,128)} %param.14) | copy-start | bytes 52
  20.6 32.1 %copy-start.29 = (f32[1,256]{1,0:T(1,128)S(1)}, f32[1,256]{1,0:T(1,128)}, u32[]{:S(2)}) copy-start(f32[1,256]{1,0:T(1,128)} %refs_7_.1) | copy-start | bytes 3076
  21.4 17.4 %collective-permute-start.1 = (bf16[2592,128]{1,0:T(8,128)(2,1)S(1)}, bf16[2592,128]{1,0:T(8,128)(2,1)}, u32[]{:S(2)}, u32[]{:S(2)}) collective-permute-start(bf16[2592,128]{1,0:T(8,128)(2,1)S(1)} %get-tuple-element.27.refs_3_), channel_id=1, source_target_pairs={{0,2},{1,3},{2,0},{3,1},{4,6},{5,7},{6,4},{7,5},{8,10},{9,11},{10,... | collective-permute-start | bytes 1990664 | tf_op jit(solution)/shard_map/ppermute | solution.py:62
  24.5 0.9 copy-start.21
  25.6 30.6 %collective-permute-start.8 = (bf16[3024,128]{1,0:T(8,128)(2,1)S(1)}, bf16[3024,128]{1,0:T(8,128)(2,1)S(1)}, u32[]{:S(2)}, u32[]{:S(2)}) collective-permute-start(bf16[3024,128]{1,0:T(8,128)(2,1)S(1)} %pack_kernel.1.refs_5_.refs_2_), channel_id=1, source_target_pairs={{0,2},{1,3},{2,0},{3,1},{4,6},{5,7},{6,4},{7,5},{8,10},{9,11},{10,... | collective-permute-start | bytes 2322440 | tf_op jit(solution)/shard_map/ppermute | solution.py:62
  27.7 18.4 %collective-permute-start = (bf16[2592,128]{1,0:T(8,128)(2,1)S(1)}, bf16[2592,128]{1,0:T(8,128)(2,1)}, u32[]{:S(2)}, u32[]{:S(2)}) collective-permute-start(bf16[2592,128]{1,0:T(8,128)(2,1)S(1)} %get-tuple-element.27.refs_3_), channel_id=1, source_target_pairs={{0,1},{1,0},{2,3},{3,2},{4,5},{5,4},{6,7},{7,6},{8,9},{9,8},{10,11... | collective-permute-start | bytes 1990664 | tf_op jit(solution)/shard_map/ppermute | solution.py:62
  38.8 7.3 %collective-permute-start.2 = (bf16[2592,128]{1,0:T(8,128)(2,1)}, bf16[2592,128]{1,0:T(8,128)(2,1)}, u32[]{:S(2)}, u32[]{:S(2)}) collective-permute-start(bf16[2592,128]{1,0:T(8,128)(2,1)} %collective-permute-done.1.refs_5_), channel_id=1, source_target_pairs={{0,1},{1,0},{2,3},{3,2},{4,5},{5,4},{6,7},{7,6},{8,9},{9,8},{10,11... | collective-permute-start | bytes 1990664 | tf_op jit(solution)/shard_map/ppermute | solution.py:62
  44.1 22.8 %collective-permute-start.7 = (bf16[3024,128]{1,0:T(8,128)(2,1)S(1)}, bf16[3024,128]{1,0:T(8,128)(2,1)}, u32[]{:S(2)}, u32[]{:S(2)}) collective-permute-start(bf16[3024,128]{1,0:T(8,128)(2,1)S(1)} %pack_kernel.1.refs_5_.refs_2_), channel_id=1, source_target_pairs={{0,1},{1,0},{2,3},{3,2},{4,5},{5,4},{6,7},{7,6},{8,9},{9,8},{10,11... | collective-permute-start | bytes 2322440 | tf_op jit(solution)/shard_map/ppermute | solution.py:62
  56.1 17.1 %copy-start = (f32[256,256]{1,0:T(8,128)}, f32[256,256]{1,0:T(8,128)S(1)}, u32[]{:S(2)}) copy-start(f32[256,256]{1,0:T(8,128)S(1)} %get-tuple-element.35.refs_0_.refs_2_) | copy-start | bytes 786436
  56.1 17.1 %copy-start.11 = (bf16[576,256]{1,0:T(8,128)(2,1)}, bf16[576,256]{1,0:T(8,128)(2,1)S(1)}, u32[]{:S(2)}) copy-start(bf16[576,256]{1,0:T(8,128)(2,1)S(1)} %get-tuple-element.28.refs_0_) | copy-start | bytes 884740
  56.1 17.1 %copy-start.31 = (bf16[576,256]{1,0:T(8,128)(2,1)}, bf16[576,256]{1,0:T(8,128)(2,1)S(1)}, u32[]{:S(2)}) copy-start(bf16[576,256]{1,0:T(8,128)(2,1)S(1)} %get-tuple-element.31) | copy-start | bytes 884740
  56.1 17.0 %copy-start.32 = (bf16[576,256]{1,0:T(8,128)(2,1)}, bf16[576,256]{1,0:T(8,128)(2,1)S(1)}, u32[]{:S(2)}) copy-start(bf16[576,256]{1,0:T(8,128)(2,1)S(1)} %get-tuple-element.30) | copy-start | bytes 884740
  56.1 17.0 %copy-start.33 = (bf16[576,256]{1,0:T(8,128)(2,1)}, bf16[576,256]{1,0:T(8,128)(2,1)S(1)}, u32[]{:S(2)}) copy-start(bf16[576,256]{1,0:T(8,128)(2,1)S(1)} %get-tuple-element.29) | copy-start | bytes 884740
  56.1 13.7 %copy-start.26 = (bf16[256,256]{1,0:T(8,128)(2,1)S(1)}, bf16[256,256]{1,0:T(8,128)(2,1)}, u32[]{:S(2)}) copy-start(bf16[256,256]{1,0:T(8,128)(2,1)} %copy-done.25) | copy-start | bytes 393220
  56.2 13.6 %collective-permute-start.9 = (bf16[3024,128]{1,0:T(8,128)(2,1)S(1)}, bf16[3024,128]{1,0:T(8,128)(2,1)S(1)}, u32[]{:S(2)}, u32[]{:S(2)}) collective-permute-start(bf16[3024,128]{1,0:T(8,128)(2,1)S(1)} %pin_kernel.2.refs_7_.refs_4_), channel_id=1, source_target_pairs={{0,1},{1,0},{2,3},{3,2},{4,5},{5,4},{6,7},{7,6},{8,9},{9,8},{10,11... | collective-permute-start | bytes 2322440 | tf_op jit(solution)/shard_map/ppermute | solution.py:62
  62.3 7.6 %collective-permute-start.6 = (bf16[256,256]{1,0:T(8,128)(2,1)S(1)}, bf16[256,256]{1,0:T(8,128)(2,1)S(1)}, u32[]{:S(2)}, u32[]{:S(2)}) collective-permute-start(bf16[256,256]{1,0:T(8,128)(2,1)S(1)} %get-tuple-element.32.refs_1_), channel_id=1, source_target_pairs={{0,256},{1,257},{2,258},{3,259},{4,260},{5,261},{6,262},{7,263},{8... | collective-permute-start | bytes 393224 | tf_op jit(solution)/shard_map/ppermute | solution.py:310
  73.9 38.3 %all-to-all-start.1 = ((bf16[64,72,128]{2,1,0:T(8,128)(2,1)}), bf16[64,72,128]{2,1,0:T(8,128)(2,1)S(1)}, u32[]{:S(2)}, u32[]{:S(2)}) async-start(bf16[64,72,128]{2,1,0:T(8,128)(2,1)} %get-tuple-element.36), calls=%async_computation.1 | async-start | bytes 2359296 | tf_op jit(solution)/shard_map/all_to_all | solution.py:75
  82.9 8.5 %collective-permute-start.3 = (bf16[576,256]{1,0:T(8,128)(2,1)}, bf16[576,256]{1,0:T(8,128)(2,1)S(1)}, u32[]{:S(2)}, u32[]{:S(2)}) collective-permute-start(bf16[576,256]{1,0:T(8,128)(2,1)} %copy-done.33), channel_id=1, source_target_pairs={{0,1},{1,0},{2,3},{3,2},{4,5},{5,4},{6,7},{7,6},{8,9},{9,8},{10,11... | collective-permute-start | bytes 884744 | tf_op jit(solution)/shard_map/ppermute | solution.py:62
  85.9 10.7 %collective-permute-start.4 = (bf16[576,256]{1,0:T(8,128)(2,1)}, bf16[576,256]{1,0:T(8,128)(2,1)S(1)}, u32[]{:S(2)}, u32[]{:S(2)}) collective-permute-start(bf16[576,256]{1,0:T(8,128)(2,1)} %copy-done.32), channel_id=1, source_target_pairs={{0,2},{1,3},{2,0},{3,1},{4,6},{5,7},{6,4},{7,5},{8,10},{9,11},{10,... | collective-permute-start | bytes 884744 | tf_op jit(solution)/shard_map/ppermute | solution.py:62
  88.1 15.2 %collective-permute-start.5 = (bf16[576,256]{1,0:T(8,128)(2,1)}, bf16[576,256]{1,0:T(8,128)(2,1)S(1)}, u32[]{:S(2)}, u32[]{:S(2)}) collective-permute-start(bf16[576,256]{1,0:T(8,128)(2,1)} %copy-done.31), channel_id=1, source_target_pairs={{0,3},{1,2},{2,1},{3,0},{4,7},{5,6},{6,5},{7,4},{8,11},{9,10},{10,... | collective-permute-start | bytes 884744 | tf_op jit(solution)/shard_map/ppermute | solution.py:62
  113.5 38.5 %all-to-all-start.2 = ((bf16[64,72,128]{2,1,0:T(8,128)(2,1)}), bf16[64,72,128]{2,1,0:T(8,128)(2,1)S(1)}, u32[]{:S(2)}, u32[]{:S(2)}) async-start(bf16[64,72,128]{2,1,0:T(8,128)(2,1)} %total_kernel.1), calls=%async_computation.2 | async-start | bytes 2359296 | tf_op jit(solution)/shard_map/all_to_all | solution.py:75
  122.8 8.7 %collective-permute-start.11 = (bf16[512,256]{1,0:T(8,128)(2,1)}, bf16[512,256]{1,0:T(8,128)(2,1)S(1)}, u32[]{:S(2)}, u32[]{:S(2)}) collective-permute-start(bf16[512,256]{1,0:T(8,128)(2,1)} %copy-done.19), channel_id=1, source_target_pairs={{0,2},{1,3},{2,0},{3,1},{4,6},{5,7},{6,4},{7,5},{8,10},{9,11},{10,... | collective-permute-start | bytes 786440 | tf_op jit(solution)/shard_map/ppermute | solution.py:62
  125.0 10.5 %collective-permute-start.10 = (bf16[512,256]{1,0:T(8,128)(2,1)}, bf16[512,256]{1,0:T(8,128)(2,1)S(1)}, u32[]{:S(2)}, u32[]{:S(2)}) collective-permute-start(bf16[512,256]{1,0:T(8,128)(2,1)} %copy-done.19), channel_id=1, source_target_pairs={{0,1},{1,0},{2,3},{3,2},{4,5},{5,4},{6,7},{7,6},{8,9},{9,8},{10,11... | collective-permute-start | bytes 786440 | tf_op jit(solution)/shard_map/ppermute | solution.py:62
  131.5 5.1 %collective-permute-start.12 = (bf16[512,256]{1,0:T(8,128)(2,1)S(1)}, bf16[512,256]{1,0:T(8,128)(2,1)S(1)}, u32[]{:S(2)}, u32[]{:S(2)}) collective-permute-start(bf16[512,256]{1,0:T(8,128)(2,1)S(1)} %collective-permute-done.11.refs_6_), channel_id=1, source_target_pairs={{0,1},{1,0},{2,3},{3,2},{4,5},{5,4},{6,7},{7,6},{8,9},{9,8},{10,11... | collective-permute-start | bytes 786440 | tf_op jit(solution)/shard_map/ppermute | solution.py:62
  152.0 9.7 %copy-start.1 = (f32[256,256]{1,0:T(8,128)S(1)}, f32[256,256]{1,0:T(8,128)}, u32[]{:S(2)}) copy-start(f32[256,256]{1,0:T(8,128)} %copy-done) | copy-start | bytes 786436
  154.2 30.8 %copy-start.3 = (bf16[576,256]{1,0:T(8,128)(2,1)S(1)}, bf16[576,256]{1,0:T(8,128)(2,1)}, u32[]{:S(2)}) copy-start(bf16[576,256]{1,0:T(8,128)(2,1)} %copy-done.2) | copy-start | bytes 884740
  154.2 30.8 %copy-start.5 = (bf16[576,256]{1,0:T(8,128)(2,1)S(1)}, bf16[576,256]{1,0:T(8,128)(2,1)}, u32[]{:S(2)}) copy-start(bf16[576,256]{1,0:T(8,128)(2,1)} %copy-done.4) | copy-start | bytes 884740
  154.2 30.8 %copy-start.7 = (bf16[576,256]{1,0:T(8,128)(2,1)S(1)}, bf16[576,256]{1,0:T(8,128)(2,1)}, u32[]{:S(2)}) copy-start(bf16[576,256]{1,0:T(8,128)(2,1)} %copy-done.6) | copy-start | bytes 884740
  154.2 30.8 %copy-start.12 = (bf16[576,256]{1,0:T(8,128)(2,1)S(1)}, bf16[576,256]{1,0:T(8,128)(2,1)}, u32[]{:S(2)}) copy-start(bf16[576,256]{1,0:T(8,128)(2,1)} %copy-done.11) | copy-start | bytes 884740
  154.2 7.5 %collective-permute-start.13 = (bf16[256,256]{1,0:T(8,128)(2,1)S(1)}, bf16[256,256]{1,0:T(8,128)(2,1)S(1)}, u32[]{:S(2)}, u32[]{:S(2)}) collective-permute-start(bf16[256,256]{1,0:T(8,128)(2,1)S(1)} %get-tuple-element.39), channel_id=1, source_target_pairs={{256,0},{257,1},{258,2},{259,3},{260,4},{261,5},{262,6},{263,7},{2... | collective-permute-start | bytes 393224 | tf_op jit(solution)/shard_map/ppermute | solution.py:330
  161.8 5.8 %collective-permute-start.15 = (bf16[256,256]{1,0:T(8,128)(2,1)S(1)}, bf16[256,256]{1,0:T(8,128)(2,1)S(1)}, u32[]{:S(2)}, u32[]{:S(2)}) collective-permute-start(bf16[256,256]{1,0:T(8,128)(2,1)S(1)} %pregrad_kernel.1.refs_4_), channel_id=1, source_target_pairs={{0,2},{1,3},{2,0},{3,1},{4,6},{5,7},{6,4},{7,5},{8,10},{9,11},{10,... | collective-permute-start | bytes 393224 | tf_op jit(solution)/shard_map/ppermute | solution.py:62
  164.0 22.5 %collective-permute-start.18 = (bf16[576,256]{1,0:T(8,128)(2,1)S(1)}, bf16[576,256]{1,0:T(8,128)(2,1)S(1)}, u32[]{:S(2)}, u32[]{:S(2)}) collective-permute-start(bf16[576,256]{1,0:T(8,128)(2,1)S(1)} %get-tuple-element.46), channel_id=1, source_target_pairs={{0,2},{1,3},{2,0},{3,1},{4,6},{5,7},{6,4},{7,5},{8,10},{9,11},{10,... | collective-permute-start | bytes 884744 | tf_op jit(solution)/shard_map/ppermute | solution.py:62
  167.6 19.9 %copy-start.14 = (bf16[512,256]{1,0:T(8,128)(2,1)S(1)}, bf16[512,256]{1,0:T(8,128)(2,1)}, u32[]{:S(2)}) copy-start(bf16[512,256]{1,0:T(8,128)(2,1)} %copy-done.13) | copy-start | bytes 786436
  167.6 19.9 %copy-start.16 = (bf16[512,256]{1,0:T(8,128)(2,1)S(1)}, bf16[512,256]{1,0:T(8,128)(2,1)}, u32[]{:S(2)}) copy-start(bf16[512,256]{1,0:T(8,128)(2,1)} %copy-done.15) | copy-start | bytes 786436
  167.6 19.9 %copy-start.18 = (bf16[512,256]{1,0:T(8,128)(2,1)S(1)}, bf16[512,256]{1,0:T(8,128)(2,1)}, u32[]{:S(2)}) copy-start(bf16[512,256]{1,0:T(8,128)(2,1)} %copy-done.17) | copy-start | bytes 786436
  167.6 19.9 %copy-start.20 = (bf16[512,256]{1,0:T(8,128)(2,1)S(1)}, bf16[512,256]{1,0:T(8,128)(2,1)}, u32[]{:S(2)}) copy-start(bf16[512,256]{1,0:T(8,128)(2,1)} %copy-done.19) | copy-start | bytes 786436
  167.6 18.8 %collective-permute-start.17 = (bf16[576,256]{1,0:T(8,128)(2,1)S(1)}, bf16[576,256]{1,0:T(8,128)(2,1)S(1)}, u32[]{:S(2)}, u32[]{:S(2)}) collective-permute-start(bf16[576,256]{1,0:T(8,128)(2,1)S(1)} %get-tuple-element.45), channel_id=1, source_target_pairs={{0,1},{1,0},{2,3},{3,2},{4,5},{5,4},{6,7},{7,6},{8,9},{9,8},{10,11... | collective-permute-start | bytes 884744 | tf_op jit(solution)/shard_map/ppermute | solution.py:62
  177.0 10.5 %collective-permute-start.19 = (bf16[576,256]{1,0:T(8,128)(2,1)S(1)}, bf16[576,256]{1,0:T(8,128)(2,1)S(1)}, u32[]{:S(2)}, u32[]{:S(2)}) collective-permute-start(bf16[576,256]{1,0:T(8,128)(2,1)S(1)} %get-tuple-element.47), channel_id=1, source_target_pairs={{0,3},{1,2},{2,1},{3,0},{4,7},{5,6},{6,5},{7,4},{8,11},{9,10},{10,... | collective-permute-start | bytes 884744 | tf_op jit(solution)/shard_map/ppermute | solution.py:62
  179.4 4.3 %collective-permute-start.14 = (bf16[256,256]{1,0:T(8,128)(2,1)S(1)}, bf16[256,256]{1,0:T(8,128)(2,1)S(1)}, u32[]{:S(2)}, u32[]{:S(2)}) collective-permute-start(bf16[256,256]{1,0:T(8,128)(2,1)S(1)} %pregrad_kernel.1.refs_4_), channel_id=1, source_target_pairs={{0,1},{1,0},{2,3},{3,2},{4,5},{5,4},{6,7},{7,6},{8,9},{9,8},{10,11... | collective-permute-start | bytes 393224 | tf_op jit(solution)/shard_map/ppermute | solution.py:62
  181.8 3.2 %collective-permute-start.16 = (bf16[256,256]{1,0:T(8,128)(2,1)S(1)}, bf16[256,256]{1,0:T(8,128)(2,1)S(1)}, u32[]{:S(2)}, u32[]{:S(2)}) collective-permute-start(bf16[256,256]{1,0:T(8,128)(2,1)S(1)} %collective-permute-done.15.refs_6_.refs_0_), channel_id=1, source_target_pairs={{0,1},{1,0},{2,3},{3,2},{4,5},{5,4},{6,7},{7,6},{8,9},{9,8},{10,11... | collective-permute-start | bytes 393224 | tf_op jit(solution)/shard_map/ppermute | solution.py:62
  (9 other events, 6.3 us)

commit v5 on v4

--- a/solution.py
+++ b/solution.py
@@ -13,6 +13,9 @@
 BF = jnp.bfloat16
 F32 = jnp.float32
 TOK = ("tok_0", "tok_1")
+FEAT = ("y_1", "y_0", "z_1", "z_0")
+NEAR = ("y_0", "z_0")
+WIDE = ("y_1", "z_1")
 PARAMS = pltpu.CompilerParams(vmem_limit_bytes=24 * 1024 * 1024)
 VM = pl.BlockSpec(memory_space=pltpu.VMEM)
 SM = pl.BlockSpec(memory_space=pltpu.SMEM)
@@ -58,8 +61,8 @@
     return lax.dot_general(a, b, (((ca,), (cb,)), ((), ())), preferred_element_type=F32)
 
 
-def toward(x, k):
-    return lax.ppermute(x, TOK, [(i, i ^ k) for i in range(4)])
+def toward(x, k, axes=TOK):
+    return lax.ppermute(x, axes, [(i, i ^ k) for i in range(4)])
 
 
 def gather4(x):
@@ -67,12 +70,12 @@
     return [x, toward(x, 1), far, toward(far, 1)]
 
 
-def exchange4(blocks):
-    return [blocks[0]] + [toward(blocks[k], k) for k in (1, 2, 3)]
-
-
-def exchange(blocks):
-    return lax.all_to_all(blocks, "feat", split_axis=0, concat_axis=0, tiled=True)
+def exchange4(blocks, axes=TOK):
+    return [blocks[0]] + [toward(blocks[k], k, axes) for k in (1, 2, 3)]
+
+
+def exchange(blocks, axes=FEAT):
+    return lax.all_to_all(blocks, axes, split_axis=0, concat_axis=0, tiled=True)
 
 
 def spread_kernel(x_ref, gain_ref, o_ref):
@@ -172,12 +175,13 @@
 
 
 def decode_kernel(
-    t_ref, codes_ref, before_ref, shifted_ref, hidden_ref, w0, w1, w2, w3, o_ref, both_ref
+    t_ref, codes_ref, before_ref, shifted_ref, hidden_ref, w0, w1, w2, w3,
+    o0, o1, o2, o3, both_ref, s_ref,
 ):
-    t, layer = t_ref[0], t_ref[1]
+    t, layer, near = t_ref[0], t_ref[1], t_ref[2]
     n = codes_ref.shape[0]
     units = hidden_ref.shape[0]
-    block = o_ref.shape[0] * ROWS // 8
+    _, block, lanes = o0.shape
     both_ref[:n] = codes_ref[...]
 
     @pl.when(layer == 0)
@@ -189,20 +193,21 @@
         both_ref[n:] = shifted_ref[...]
 
     both, hidden = both_ref[...], hidden_ref[...]
-    peers, rows, lanes = o_ref.shape
-    each = block // rows
     for k, w in enumerate((w0, w1, w2, w3)):
         decoder = jnp.concatenate(
             [get_wide(w, 0, block, n), get_wide(w, block * n // 128, block, n)], axis=1
         )
         down = get_wide(w, 2 * block * n // 128, units, block)
         value = dot(decoder, both) - dot(down, hidden, 0, 0)
-        spot = jnp.bitwise_xor(t, k) * each
-        for i in range(each):
-            for h in range(2):
-                o_ref[spot + (h * peers // 2 + i)] = value[
-                    i * rows : (i + 1) * rows, h * lanes : (h + 1) * lanes
-                ].astype(BF)
+        spot = jnp.bitwise_xor(jnp.bitwise_xor(t, near), k)
+        for h in range(2):
+            s_ref[spot, h] = value[:, h * lanes : (h + 1) * lanes].astype(BF)
+    for m, o_ref in enumerate((o0, o1, o2, o3)):
+        o_ref[...] = s_ref[m]
+
+
+def near_total_kernel(x0, x1, x2, x3, o_ref):
+    o_ref[...] = sum(x[...].astype(F32) for x in (x0, x1, x2, x3)).astype(BF)
 
 
 def total_kernel(x_ref, o_ref):
@@ -210,22 +215,18 @@
     o_ref[...] = jnp.broadcast_to(total[None], o_ref.shape)
 
 
-def back_kernel(t_ref, e_ref, w0, w1, w2, w3, own_ref, prev_ref, e0, e1, e2, e3):
-    t = t_ref[0]
-    peers, rows, lanes = e_ref.shape
+def back_kernel(
+    t_ref, x0, x1, x2, x3, w0, w1, w2, w3, own_ref, prev_ref, e0, e1, e2, e3, s_ref
+):
+    t, near = t_ref[0], t_ref[2]
+    for m, x in enumerate((x0, x1, x2, x3)):
+        s_ref[jnp.bitwise_xor(near, m)] = x[...]
     n = own_ref.shape[0]
     block = e0.shape[0]
-    each = block // rows
     total = 0.0
     for k, (err_ref, w) in enumerate(((e0, w0), (e1, w1), (e2, w2), (e3, w3))):
-        spot = jnp.bitwise_xor(t, k) * each
-        half = [
-            jnp.concatenate(
-                [e_ref[spot + (h * peers // 2 + i)].astype(F32) for i in range(each)], axis=0
-            ).astype(BF)
-            for h in range(2)
-        ]
-        err = jnp.concatenate(half, axis=1)
+        spot = jnp.bitwise_xor(t, k)
+        err = jnp.concatenate([s_ref[spot, h] for h in range(2)], axis=1)
         err_ref[...] = err
         decoder = jnp.concatenate(
             [get_wide(w, 0, block, n), get_wide(w, block * n // 128, block, n)], axis=1
@@ -269,13 +270,14 @@
     dec_prev,
 ):
     height, strip = resid.shape[1:]
-    peers = lax.axis_size("feat")
+    peers = lax.axis_size(FEAT)
     width = enc_weight.shape[2]
     units = w_gate.shape[2]
     block = strip * peers // 4
     spans = -(-block // 128)
     t = 2 * lax.axis_index("tok_0") + lax.axis_index("tok_1")
-    place = jnp.stack([t, lax.axis_index("layer")]).astype(jnp.int32)
+    near = 2 * lax.axis_index("y_0") + lax.axis_index("z_0")
+    place = jnp.stack([t, lax.axis_index("layer"), near]).astype(jnp.int32)
     flip = lambda a: jnp.swapaxes(a[0], 0, 1)
 
     (copies,) = call(
@@ -292,7 +294,7 @@
         [((2 * block * width // 128 + units * spans, 128), BF)],
         plain=True,
     )
-    near, far = toward(second, 1), toward(second, 2)
+    beside, far = toward(second, 1), toward(second, 2)
     first, before = call(
         pack_turn_kernel,
         (enc_weight[0], flip(w_gate), flip(w_up), prev_codes),
@@ -309,23 +311,33 @@
     )
     shifted = lax.ppermute(codes, "layer", [(0, 1)])
     (far,) = call(pin_kernel, (), [], after=(slope,), through=(far,))
-    second = [second, near, far, toward(far, 1)]
-    parts, both = call(
+    second = [second, beside, far, toward(far, 1)]
+    slab = (2, block, height // 2)
+    *parts, both = call(
         decode_kernel,
         (place, codes, before, shifted, hidden, *second),
-        [((peers, ROWS, height // 2), BF), ((2 * width, height), BF)],
+        [(slab, BF)] * 4 + [((2 * width, height), BF)],
+        scratch=[pltpu.VMEM((4, *slab), BF)],
+    )
+    (part,) = call(near_total_kernel, exchange4(parts, NEAR), [(slab, BF)], leaving=(0,))
+    arrived = exchange(part.reshape(peers // 4, ROWS, height // 2), WIDE)
+    normed = exchange4(normed)
+    (copies,) = call(
+        total_kernel,
+        (arrived,),
+        [(arrived.shape, BF)],
+        after=(corner(normed[1:]),),
         leaving=(0,),
     )
-    arrived = exchange(parts)
-    normed = exchange4(normed)
-    (copies,) = call(total_kernel, (arrived,), [(parts.shape, BF)], after=(corner(normed[1:]),), leaving=(0,))
-    errors = exchange(copies)
+    errors = exchange(copies, WIDE).reshape(slab)
     both = gather4(both)
+    errors = exchange4([errors] * 4, NEAR)
     own_back, prev_back, *err = call(
         back_kernel,
-        (place, errors, *second),
+        (place, *errors, *second),
         [((width, height), F32), ((width, height), BF)] + [((block, height), BF)] * 4,
         after=(corner(both[1:]),),
+        scratch=[pltpu.VMEM((4, *slab), BF)],
     )
     later = lax.ppermute(prev_back, "layer", [(1, 0)])
     (pregrad,) = call(
@@ -350,31 +362,31 @@
 
 def solution(mesh):
     split = Mesh(
-        mesh.devices.reshape(mesh.shape["layer"], mesh.shape["feat"], 2, 2),
-        ("layer", "feat", "tok_0", "tok_1"),
+        mesh.devices.reshape(mesh.shape["layer"], 4, 2, 4, 2, 2, 2),
+        ("layer", *FEAT, *TOK),
     )
     placed = (
-        P("layer", TOK, "feat"),
-        P("layer", "feat"),
-        P(TOK, "feat"),
-        P("layer", TOK, "feat"),
-        P("layer", TOK, "feat"),
-        P("layer", TOK, "feat"),
-        P("layer", "feat", TOK),
-        P("layer", TOK, "feat"),
-        P("layer", "feat"),
-        P("layer", "feat", TOK),
-        P("layer", "feat", TOK),
+        P("layer", TOK, FEAT),
+        P("layer", FEAT),
+        P(TOK, FEAT),
+        P("layer", TOK, FEAT),
+        P("layer", TOK, FEAT),
+        P("layer", TOK, FEAT),
+        P("layer", FEAT, TOK),
+        P("layer", TOK, FEAT),
+        P("layer", FEAT),
+        P("layer", FEAT, TOK),
+        P("layer", FEAT, TOK),
     )
     return jax.shard_map(
         local,
         mesh=split,
         in_specs=placed,
         out_specs=(
-            P("layer", TOK, "feat"),
-            P("layer", "feat"),
-            P("layer", "feat", TOK),
-            P("layer", "feat", TOK),
+            P("layer", TOK, FEAT),
+            P("layer", FEAT),
+            P("layer", FEAT, TOK),
+            P("layer", FEAT, TOK),
         ),
         check_vma=False,
     )

time: 190 us -> 204 us (1.074)
  starting transfers between devices: 103 us -> 119 us
  local copies, waits for them, and re-layouts: 7.99 us -> 4.89 us
    all_to_all x3, waiting for transfers between devices: 26.6 us -> 7.16 us  [exchange(): return lax.all_to_all(blocks, axes, split_axis=0, concat_axis=0, tiled=True)]
    ppermute x18 -> x24, waiting for transfers between devices: 26.9 us -> 45.8 us  [toward(): return lax.ppermute(x, axes, [(i, i ^ k) for i in range(4)])]
    ppermute x18 -> x24, starting transfers between devices: 61.2 us -> 76.3 us  [toward(): return lax.ppermute(x, axes, [(i, i ^ k) for i in range(4)])]
    unnamed x68 -> x52, local copies, waits for them, and re-layouts: 7.99 us -> 4.89 us
    pallas_call x12 -> x13, Pallas kernels: 14.8 us -> 15.4 us  [call(): pl.pallas_call(body, out_shape=[(pltpu.HBM if i in leaving else pltpu.VME...]
  transfers between devices with their start and end apart: 23 -> 29, of which waited for: 13 -> 16; matrix products, arithmetic and copies ran while one was open for 0% -> 0% of each run, Pallas kernels for 3% -> 2%
where the time goes in v5:
time: 204 us; the launch traced here: 203 us
  starting transfers between devices  119 us (58%)
  waiting for transfers between devices  61.9 us (30%)
  Pallas kernels  15.4 us (8%)
  local copies, waits for them, and re-layouts  4.89 us (2%)
    ppermute x24, starting transfers between devices, toward(): return lax.ppermute(x, axes, [(i, i ^ k) for i in range(4)])  76.3 us
    ppermute x24, waiting for transfers between devices, toward(): return lax.ppermute(x, axes, [(i, i ^ k) for i in range(4)])  45.8 us
    all_to_all x3, starting transfers between devices, exchange(): return lax.all_to_all(blocks, axes, split_axis=0, concat_axis=0, tiled=True)  36.3 us
    pallas_call x13, Pallas kernels, call(): pl.pallas_call(body, out_shape=[(pltpu.HBM if i in leaving else pltpu.VME...  15.4 us
    all_to_all x3, waiting for transfers between devices, exchange(): return lax.all_to_all(blocks, axes, split_axis=0, concat_axis=0, tiled=True)  7.16 us
    ppermute x1, waiting for transfers between devices, local(): later = lax.ppermute(prev_back, 'layer', [(1, 0)])  6.04 us
    unnamed x52, local copies, waits for them, and re-layouts  4.89 us
    ppermute x1, starting transfers between devices, local(): shifted = lax.ppermute(codes, 'layer', [(0, 1)])  4.65 us
  transfers between devices with their start and end apart: 29, of which 16 were waited for; matrix products, arithmetic and copies ran while one was open for 0% of the time, Pallas kernels for 2%

profile of v5, /device:TPU:1, one launch (start us, length us, event | category | flops | bytes accessed | tf_op | source)
XLA Modules:
  0.0 202.8 jit_solution(7716863543838327744)
XLA Ops:
  3.3 17.3 %all-to-all-start = ((bf16[64,80,128]{2,1,0:T(8,128)(2,1)}), bf16[64,80,128]{2,1,0:T(8,128)(2,1)S(1)}, u32[]{:S(2)}, u32[]{:S(2)}) async-start(bf16[64,80,128]{2,1,0:T(8,128)(2,1)} %spread_kernel.1), calls=%async_computation | async-start | bytes 2621440 | tf_op jit(solution)/shard_map/all_to_all | solution.py:78
  21.6 3.1 %collective-permute-start.1 = (bf16[2592,128]{1,0:T(8,128)(2,1)S(1)}, bf16[2592,128]{1,0:T(8,128)(2,1)}, u32[]{:S(2)}, u32[]{:S(2)}) collective-permute-start(bf16[2592,128]{1,0:T(8,128)(2,1)S(1)} %get-tuple-element.30.refs_3_), channel_id=1, source_target_pairs={{0,2},{1,3},{2,0},{3,1},{4,6},{5,7},{6,4},{7,5},{8,10},{9,11},{10,... | collective-permute-start | bytes 1990664 | tf_op jit(solution)/shard_map/ppermute | solution.py:65
  24.9 2.2 %collective-permute-start.8 = (bf16[3024,128]{1,0:T(8,128)(2,1)S(1)}, bf16[3024,128]{1,0:T(8,128)(2,1)S(1)}, u32[]{:S(2)}, u32[]{:S(2)}) collective-permute-start(bf16[3024,128]{1,0:T(8,128)(2,1)S(1)} %pack_kernel.1.refs_5_), channel_id=1, source_target_pairs={{0,2},{1,3},{2,0},{3,1},{4,6},{5,7},{6,4},{7,5},{8,10},{9,11},{10,... | collective-permute-start | bytes 2322440 | tf_op jit(solution)/shard_map/ppermute | solution.py:65
  27.1 3.4 %collective-permute-start = (bf16[2592,128]{1,0:T(8,128)(2,1)S(1)}, bf16[2592,128]{1,0:T(8,128)(2,1)}, u32[]{:S(2)}, u32[]{:S(2)}) collective-permute-start(bf16[2592,128]{1,0:T(8,128)(2,1)S(1)} %get-tuple-element.30.refs_3_), channel_id=1, source_target_pairs={{0,1},{1,0},{2,3},{3,2},{4,5},{5,4},{6,7},{7,6},{8,9},{9,8},{10,11... | collective-permute-start | bytes 1990664 | tf_op jit(solution)/shard_map/ppermute | solution.py:65
  30.5 8.6 %collective-permute-done.1.refs_5_ = bf16[2592,128]{1,0:T(8,128)(2,1)} collective-permute-done((bf16[2592,128]{1,0:T(8,128)(2,1)S(1)}, bf16[2592,128]{1,0:T(8,128)(2,1)}, u32[]{:S(2)}, u32[]{:S(2)}) %collective-permute-start.1) | collective-permute-done | bytes 663584 | tf_op jit(solution)/shard_map/ppermute | solution.py:65
  39.1 5.2 %collective-permute-start.2 = (bf16[2592,128]{1,0:T(8,128)(2,1)}, bf16[2592,128]{1,0:T(8,128)(2,1)}, u32[]{:S(2)}, u32[]{:S(2)}) collective-permute-start(bf16[2592,128]{1,0:T(8,128)(2,1)} %collective-permute-done.1.refs_5_), channel_id=1, source_target_pairs={{0,1},{1,0},{2,3},{3,2},{4,5},{5,4},{6,7},{7,6},{8,9},{9,8},{10,11... | collective-permute-start | bytes 1990664 | tf_op jit(solution)/shard_map/ppermute | solution.py:65
  44.3 1.9 collective-permute-start.7
  46.4 6.3 %all-to-all-done.refs_2_ = bf16[64,80,128]{2,1,0:T(8,128)(2,1)S(1)} async-done(((bf16[64,80,128]{2,1,0:T(8,128)(2,1)}), bf16[64,80,128]{2,1,0:T(8,128)(2,1)S(1)}, u32[]{:S(2)}, u32[]{:S(2)}) %all-to-all-start) | async-done | bytes 1310752 | tf_op jit(solution)/shard_map/all_to_all | solution.py:78
  53.8 3.3 %encode_kernel.1 = (bf16[576,256]{1,0:T(8,128)(2,1)S(1)}, bf16[576,256]{1,0:T(8,128)(2,1)S(1)}, bf16[576,256]{1,0:T(8,128)(2,1)S(1)}, bf16[576,256]{1,0:T(8,128)...) custom-call(s32[3]{0:T(128)S(1)} %pad_add_fusion.refs_0_, ...), custom_call_target="tpu_custom_call" | custom-call | tf_op jit(solution)/shard_map/encode_kernel/pallas_call | solution.py:41
  57.2 6.1 %collective-permute-start.9 = (bf16[3024,128]{1,0:T(8,128)(2,1)S(1)}, bf16[3024,128]{1,0:T(8,128)(2,1)S(1)}, u32[]{:S(2)}, u32[]{:S(2)}) collective-permute-start(bf16[3024,128]{1,0:T(8,128)(2,1)S(1)} %pin_kernel.2.refs_7_), channel_id=1, source_target_pairs={{0,1},{1,0},{2,3},{3,2},{4,5},{5,4},{6,7},{7,6},{8,9},{9,8},{10,11... | collective-permute-start | bytes 2322440 | tf_op jit(solution)/shard_map/ppermute | solution.py:65
  63.3 4.7 %collective-permute-start.6 = (bf16[256,256]{1,0:T(8,128)(2,1)S(1)}, bf16[256,256]{1,0:T(8,128)(2,1)S(1)}, u32[]{:S(2)}, u32[]{:S(2)}) collective-permute-start(bf16[256,256]{1,0:T(8,128)(2,1)S(1)} %get-tuple-element.35.refs_1_), channel_id=1, source_target_pairs={{0,256},{1,257},{2,258},{3,259},{4,260},{5,261},{6,262},{7,263},{8... | collective-permute-start | bytes 393224 | tf_op jit(solution)/shard_map/ppermute | solution.py:312
  68.0 2.9 %collective-permute-done.6.refs_3_ = bf16[256,256]{1,0:T(8,128)(2,1)S(1)} collective-permute-done((bf16[256,256]{1,0:T(8,128)(2,1)S(1)}, bf16[256,256]{1,0:T(8,128)(2,1)S(1)}, u32[]{:S(2)}, u32[]{:S(2)}) %collective-permute-start.6) | collective-permute-done | bytes 131104 | tf_op jit(solution)/shard_map/ppermute | solution.py:312
  70.9 2.4 %decode_kernel.1 = (bf16[2,576,128]{2,1,0:T(8,128)(2,1)S(1)}, bf16[2,576,128]{2,1,0:T(8,128)(2,1)S(1)}, bf16[2,576,128]{2,1,0:T(8,128)(2,1)S(1)}, bf16[2,576,128]{2,1,0:T(8,128)(2,1)S(1)}, bf16[512,256]{1,0:T(8,128)(2,1)S(1)}) custom-call(s32[3]{0:T(128)S(1)} %pad_add_fusion.refs_0_, bf16[256,256]{1,0:T(8,128)(2,1)S(1)} %get-tuple-element.35.refs_1_, ...), custom_call_target="tpu_custom_call" | custom-call | tf_op jit(solution)/shard_map/decode_kernel/pallas_call | solution.py:41
  73.3 2.1 %collective-permute-start.10 = (bf16[2,576,128]{2,1,0:T(8,128)(2,1)S(1)}, bf16[2,576,128]{2,1,0:T(8,128)(2,1)S(1)}, u32[]{:S(2)}, u32[]{:S(2)}) collective-permute-start(bf16[2,576,128]{2,1,0:T(8,128)(2,1)S(1)} %get-tuple-element.40), channel_id=1, source_target_pairs={{0,4},{4,0},{32,36},{36,32},{1,5},{5,1},{33,37},{37,33},{2,6},{6,2... | collective-permute-start | bytes 884744 | tf_op jit(solution)/shard_map/ppermute | solution.py:65
  75.4 2.8 %collective-permute-start.11 = (bf16[2,576,128]{2,1,0:T(8,128)(2,1)S(1)}, bf16[2,576,128]{2,1,0:T(8,128)(2,1)S(1)}, u32[]{:S(2)}, u32[]{:S(2)}) collective-permute-start(bf16[2,576,128]{2,1,0:T(8,128)(2,1)S(1)} %get-tuple-element.41), channel_id=1, source_target_pairs={{0,32},{4,36},{32,0},{36,4},{1,33},{5,37},{33,1},{37,5},{2,34},{6,... | collective-permute-start | bytes 884744 | tf_op jit(solution)/shard_map/ppermute | solution.py:65
  78.2 3.5 %collective-permute-start.12 = (bf16[2,576,128]{2,1,0:T(8,128)(2,1)S(1)}, bf16[2,576,128]{2,1,0:T(8,128)(2,1)S(1)}, u32[]{:S(2)}, u32[]{:S(2)}) collective-permute-start(bf16[2,576,128]{2,1,0:T(8,128)(2,1)S(1)} %get-tuple-element.42), channel_id=1, source_target_pairs={{0,36},{4,32},{32,4},{36,0},{1,37},{5,33},{33,5},{37,1},{2,38},{6,... | collective-permute-start | bytes 884744 | tf_op jit(solution)/shard_map/ppermute | solution.py:65
  81.7 1.2 collective-permute-done.10.refs_1_
  82.9 1.8 collective-permute-done.11.refs_2_
  84.7 7.3 %collective-permute-done.12.refs_3_ = bf16[2,576,128]{2,1,0:T(8,128)(2,1)S(1)} collective-permute-done((bf16[2,576,128]{2,1,0:T(8,128)(2,1)S(1)}, bf16[2,576,128]{2,1,0:T(8,128)(2,1)S(1)}, u32[]{:S(2)}, u32[]{:S(2)}) %collective-permute-start.12) | collective-permute-done | bytes 294944 | tf_op jit(solution)/shard_map/ppermute | solution.py:65
  92.9 7.3 %all-to-all-start.1 = ((bf16[16,72,128]{2,1,0:T(8,128)(2,1)}), bf16[16,72,128]{2,1,0:T(8,128)(2,1)S(1)}, u32[]{:S(2)}, u32[]{:S(2)}) async-start(bf16[16,72,128]{2,1,0:T(8,128)(2,1)} %bitcast.42), calls=%async_computation.1 | async-start | bytes 589824 | tf_op jit(solution)/shard_map/all_to_all | solution.py:78
  100.2 4.2 %collective-permute-start.3 = (bf16[576,256]{1,0:T(8,128)(2,1)}, bf16[576,256]{1,0:T(8,128)(2,1)S(1)}, u32[]{:S(2)}, u32[]{:S(2)}) collective-permute-start(bf16[576,256]{1,0:T(8,128)(2,1)} %copy-done.25), channel_id=1, source_target_pairs={{0,1},{1,0},{2,3},{3,2},{4,5},{5,4},{6,7},{7,6},{8,9},{9,8},{10,11... | collective-permute-start | bytes 884744 | tf_op jit(solution)/shard_map/ppermute | solution.py:65
  104.4 2.2 %collective-permute-start.4 = (bf16[576,256]{1,0:T(8,128)(2,1)}, bf16[576,256]{1,0:T(8,128)(2,1)S(1)}, u32[]{:S(2)}, u32[]{:S(2)}) collective-permute-start(bf16[576,256]{1,0:T(8,128)(2,1)} %copy-done.24), channel_id=1, source_target_pairs={{0,2},{1,3},{2,0},{3,1},{4,6},{5,7},{6,4},{7,5},{8,10},{9,11},{10,... | collective-permute-start | bytes 884744 | tf_op jit(solution)/shard_map/ppermute | solution.py:65
  106.6 3.2 %collective-permute-start.5 = (bf16[576,256]{1,0:T(8,128)(2,1)}, bf16[576,256]{1,0:T(8,128)(2,1)S(1)}, u32[]{:S(2)}, u32[]{:S(2)}) collective-permute-start(bf16[576,256]{1,0:T(8,128)(2,1)} %copy-done.23), channel_id=1, source_target_pairs={{0,3},{1,2},{2,1},{3,0},{4,7},{5,6},{6,5},{7,4},{8,11},{9,10},{10,... | collective-permute-start | bytes 884744 | tf_op jit(solution)/shard_map/ppermute | solution.py:65
  109.9 5.2 %collective-permute-done.4.refs_2_ = bf16[576,256]{1,0:T(8,128)(2,1)S(1)} collective-permute-done((bf16[576,256]{1,0:T(8,128)(2,1)}, bf16[576,256]{1,0:T(8,128)(2,1)S(1)}, u32[]{:S(2)}, u32[]{:S(2)}) %collective-permute-start.4) | collective-permute-done | bytes 294944 | tf_op jit(solution)/shard_map/ppermute | solution.py:65
  115.1 6.4 %collective-permute-done.5.refs_3_ = bf16[576,256]{1,0:T(8,128)(2,1)S(1)} collective-permute-done((bf16[576,256]{1,0:T(8,128)(2,1)}, bf16[576,256]{1,0:T(8,128)(2,1)S(1)}, u32[]{:S(2)}, u32[]{:S(2)}) %collective-permute-start.5) | collective-permute-done | bytes 294944 | tf_op jit(solution)/shard_map/ppermute | solution.py:65
  123.8 11.7 %all-to-all-start.2 = ((bf16[16,72,128]{2,1,0:T(8,128)(2,1)}), bf16[16,72,128]{2,1,0:T(8,128)(2,1)S(1)}, u32[]{:S(2)}, u32[]{:S(2)}) async-start(bf16[16,72,128]{2,1,0:T(8,128)(2,1)} %total_kernel.1), calls=%async_computation.2 | async-start | bytes 589824 | tf_op jit(solution)/shard_map/all_to_all | solution.py:78
  135.5 2.2 %collective-permute-start.17 = (bf16[512,256]{1,0:T(8,128)(2,1)}, bf16[512,256]{1,0:T(8,128)(2,1)}, u32[]{:S(2)}, u32[]{:S(2)}) collective-permute-start(bf16[512,256]{1,0:T(8,128)(2,1)} %copy-done.11), channel_id=1, source_target_pairs={{0,2},{1,3},{2,0},{3,1},{4,6},{5,7},{6,4},{7,5},{8,10},{9,11},{10,... | collective-permute-start | bytes 786440 | tf_op jit(solution)/shard_map/ppermute | solution.py:65
  137.7 2.8 %collective-permute-start.16 = (bf16[512,256]{1,0:T(8,128)(2,1)}, bf16[512,256]{1,0:T(8,128)(2,1)}, u32[]{:S(2)}, u32[]{:S(2)}) collective-permute-start(bf16[512,256]{1,0:T(8,128)(2,1)} %copy-done.11), channel_id=1, source_target_pairs={{0,1},{1,0},{2,3},{3,2},{4,5},{5,4},{6,7},{7,6},{8,9},{9,8},{10,11... | collective-permute-start | bytes 786440 | tf_op jit(solution)/shard_map/ppermute | solution.py:65
  140.5 4.5 %collective-permute-done.17.refs_6_ = bf16[512,256]{1,0:T(8,128)(2,1)} collective-permute-done((bf16[512,256]{1,0:T(8,128)(2,1)}, bf16[512,256]{1,0:T(8,128)(2,1)}, u32[]{:S(2)}, u32[]{:S(2)}) %collective-permute-start.17) | collective-permute-done | bytes 262176 | tf_op jit(solution)/shard_map/ppermute | solution.py:65
  145.0 3.3 %collective-permute-start.18 = (bf16[512,256]{1,0:T(8,128)(2,1)}, bf16[512,256]{1,0:T(8,128)(2,1)}, u32[]{:S(2)}, u32[]{:S(2)}) collective-permute-start(bf16[512,256]{1,0:T(8,128)(2,1)} %collective-permute-done.17.refs_6_), channel_id=1, source_target_pairs={{0,1},{1,0},{2,3},{3,2},{4,5},{5,4},{6,7},{7,6},{8,9},{9,8},{10,11... | collective-permute-start | bytes 786440 | tf_op jit(solution)/shard_map/ppermute | solution.py:65
  149.2 1.9 collective-permute-start.15
  151.1 3.1 %collective-permute-start.14 = (bf16[2,576,128]{2,1,0:T(8,128)(2,1)S(1)}, bf16[2,576,128]{2,1,0:T(8,128)(2,1)S(1)}, u32[]{:S(2)}, u32[]{:S(2)}) collective-permute-start(bf16[2,576,128]{2,1,0:T(8,128)(2,1)S(1)} %bitcast.31), channel_id=1, source_target_pairs={{0,32},{4,36},{32,0},{36,4},{1,33},{5,37},{33,1},{37,5},{2,34},{6,... | collective-permute-start | bytes 884744 | tf_op jit(solution)/shard_map/ppermute | solution.py:65
  154.2 3.4 %collective-permute-start.13 = (bf16[2,576,128]{2,1,0:T(8,128)(2,1)S(1)}, bf16[2,576,128]{2,1,0:T(8,128)(2,1)S(1)}, u32[]{:S(2)}, u32[]{:S(2)}) collective-permute-start(bf16[2,576,128]{2,1,0:T(8,128)(2,1)S(1)} %bitcast.32), channel_id=1, source_target_pairs={{0,4},{4,0},{32,36},{36,32},{1,5},{5,1},{33,37},{37,33},{2,6},{6,2... | collective-permute-start | bytes 884744 | tf_op jit(solution)/shard_map/ppermute | solution.py:65
  158.3 4.5 %collective-permute-done.14.refs_3_ = bf16[2,576,128]{2,1,0:T(8,128)(2,1)S(1)} collective-permute-done((bf16[2,576,128]{2,1,0:T(8,128)(2,1)S(1)}, bf16[2,576,128]{2,1,0:T(8,128)(2,1)S(1)}, u32[]{:S(2)}, u32[]{:S(2)}) %collective-permute-start.14) | collective-permute-done | bytes 294944 | tf_op jit(solution)/shard_map/ppermute | solution.py:65
  162.8 3.0 %collective-permute-done.13.refs_2_ = bf16[2,576,128]{2,1,0:T(8,128)(2,1)S(1)} collective-permute-done((bf16[2,576,128]{2,1,0:T(8,128)(2,1)S(1)}, bf16[2,576,128]{2,1,0:T(8,128)(2,1)S(1)}, u32[]{:S(2)}, u32[]{:S(2)}) %collective-permute-start.13) | collective-permute-done | bytes 294944 | tf_op jit(solution)/shard_map/ppermute | solution.py:65
  165.8 2.2 %back_kernel.1 = (f32[256,256]{1,0:T(8,128)S(1)}, bf16[256,256]{1,0:T(8,128)(2,1)S(1)}, bf16[576,256]{1,0:T(8,128)(2,1)S(1)}, bf16[576,256]{1,0:T(8,128)(2,1)S(1...) custom-call(s32[3]{0:T(128)S(1)} %pad_add_fusion.refs_0_, bf16[2,576,128]{2,1,0:T(8,128)(2,1)S(1)} %bitcast.33, ...), custom_call_target="tpu_custom_call" | custom-call | tf_op jit(solution)/shard_map/back_kernel/pallas_call | solution.py:41
  168.0 1.4 collective-permute-start.19
  169.5 6.0 %collective-permute-done.19.refs_1_ = bf16[256,256]{1,0:T(8,128)(2,1)S(1)} collective-permute-done((bf16[256,256]{1,0:T(8,128)(2,1)S(1)}, bf16[256,256]{1,0:T(8,128)(2,1)S(1)}, u32[]{:S(2)}, u32[]{:S(2)}) %collective-permute-start.19) | collective-permute-done | bytes 131104 | tf_op jit(solution)/shard_map/ppermute | solution.py:342
  175.6 2.4 %collective-permute-start.21 = (bf16[256,256]{1,0:T(8,128)(2,1)S(1)}, bf16[256,256]{1,0:T(8,128)(2,1)S(1)}, u32[]{:S(2)}, u32[]{:S(2)}) collective-permute-start(bf16[256,256]{1,0:T(8,128)(2,1)S(1)} %pregrad_kernel.1.refs_4_), channel_id=1, source_target_pairs={{0,2},{1,3},{2,0},{3,1},{4,6},{5,7},{6,4},{7,5},{8,10},{9,11},{10,... | collective-permute-start | bytes 393224 | tf_op jit(solution)/shard_map/ppermute | solution.py:65
  177.9 3.1 %collective-permute-start.24 = (bf16[576,256]{1,0:T(8,128)(2,1)S(1)}, bf16[576,256]{1,0:T(8,128)(2,1)S(1)}, u32[]{:S(2)}, u32[]{:S(2)}) collective-permute-start(bf16[576,256]{1,0:T(8,128)(2,1)S(1)} %get-tuple-element.52), channel_id=1, source_target_pairs={{0,2},{1,3},{2,0},{3,1},{4,6},{5,7},{6,4},{7,5},{8,10},{9,11},{10,... | collective-permute-start | bytes 884744 | tf_op jit(solution)/shard_map/ppermute | solution.py:65
  181.4 7.9 %collective-permute-start.23 = (bf16[576,256]{1,0:T(8,128)(2,1)S(1)}, bf16[576,256]{1,0:T(8,128)(2,1)S(1)}, u32[]{:S(2)}, u32[]{:S(2)}) collective-permute-start(bf16[576,256]{1,0:T(8,128)(2,1)S(1)} %get-tuple-element.51), channel_id=1, source_target_pairs={{0,1},{1,0},{2,3},{3,2},{4,5},{5,4},{6,7},{7,6},{8,9},{9,8},{10,11... | collective-permute-start | bytes 884744 | tf_op jit(solution)/shard_map/ppermute | solution.py:65
  189.3 2.0 collective-permute-start.25
  191.3 2.4 %collective-permute-start.20 = (bf16[256,256]{1,0:T(8,128)(2,1)S(1)}, bf16[256,256]{1,0:T(8,128)(2,1)S(1)}, u32[]{:S(2)}, u32[]{:S(2)}) collective-permute-start(bf16[256,256]{1,0:T(8,128)(2,1)S(1)} %pregrad_kernel.1.refs_4_), channel_id=1, source_target_pairs={{0,1},{1,0},{2,3},{3,2},{4,5},{5,4},{6,7},{7,6},{8,9},{9,8},{10,11... | collective-permute-start | bytes 393224 | tf_op jit(solution)/shard_map/ppermute | solution.py:65
  193.8 1.9 collective-permute-start.22
  195.7 1.3 collective-permute-done.22.refs_7_
  197.0 1.4 encoder_grads_kernel.1
  198.4 1.4 collective-permute-done.25.refs_3_
  199.8 2.9 %decoder_grads_kernel.1 = (f32[576,256]{1,0:T(8,128)}, f32[576,256]{1,0:T(8,128)}) custom-call(bf16[576,256]{1,0:T(8,128)(2,1)S(1)} %get-tuple-element.48.refs_0_, bf16[576,256]{1,0:T(8,128)(2,1)S(1)} %collective-permute-done.23.refs_1_, bf16[576,256]{1,0:T(8,128)(2,1)S(1)} %collective-permute-done.24.refs_2_, ...), custom_call_target="tpu_custom_call" | custom-call | tf_op jit(solution)/shard_map/decoder_grads_kernel/pallas_call | solution.py:41
  (78 shorter events, 10.1 us)
Async XLA Ops:
  3.2 17.3 %copy-start.6 = (bf16[1,576,256]{2,1,0:T(8,128)(2,1)S(1)}, bf16[1,576,256]{2,1,0:T(8,128)(2,1)}, u32[]{:S(2)}) copy-start(bf16[1,576,256]{2,1,0:T(8,128)(2,1)} %param.18) | copy-start | bytes 884740
  3.2 17.4 %copy-start.14 = (bf16[1,576,144]{1,2,0:T(8,128)(2,1)S(1)}, bf16[1,576,144]{1,2,0:T(8,128)(2,1)}, u32[]{:S(2)}) copy-start(bf16[1,576,144]{1,2,0:T(8,128)(2,1)} %param.15) | copy-start | bytes 497668
  3.2 17.4 %copy-start.15 = (bf16[1,576,144]{1,2,0:T(8,128)(2,1)S(1)}, bf16[1,576,144]{1,2,0:T(8,128)(2,1)}, u32[]{:S(2)}) copy-start(bf16[1,576,144]{1,2,0:T(8,128)(2,1)} %param.16) | copy-start | bytes 497668
  3.2 21.5 %copy-start.7 = (bf16[1,256,576]{1,2,0:T(8,128)(2,1)S(1)}, bf16[1,256,576]{1,2,0:T(8,128)(2,1)}, u32[]{:S(2)}) copy-start(bf16[1,256,576]{1,2,0:T(8,128)(2,1)} %param.20) | copy-start | bytes 884740
  3.2 21.6 %copy-start.8 = (bf16[1,256,576]{1,2,0:T(8,128)(2,1)S(1)}, bf16[1,256,576]{1,2,0:T(8,128)(2,1)}, u32[]{:S(2)}) copy-start(bf16[1,256,576]{1,2,0:T(8,128)(2,1)} %param.21) | copy-start | bytes 884740
  3.2 21.5 %copy-start.13 = (bf16[1,144,576]{2,1,0:T(8,128)(2,1)S(1)}, bf16[1,144,576]{2,1,0:T(8,128)(2,1)}, u32[]{:S(2)}) copy-start(bf16[1,144,576]{2,1,0:T(8,128)(2,1)} %param.17) | copy-start | bytes 497668
  3.3 49.5 %all-to-all-start = ((bf16[64,80,128]{2,1,0:T(8,128)(2,1)}), bf16[64,80,128]{2,1,0:T(8,128)(2,1)S(1)}, u32[]{:S(2)}, u32[]{:S(2)}) async-start(bf16[64,80,128]{2,1,0:T(8,128)(2,1)} %spread_kernel.1), calls=%async_computation | async-start | bytes 2621440 | tf_op jit(solution)/shard_map/all_to_all | solution.py:78
  20.5 32.2 %copy-start.20 = (s32[1,2,2]{2,1,0:T(2,128)S(1)}, s32[1,2,2]{2,1,0:T(2,128)}, u32[]{:S(2)}) copy-start(s32[1,2,2]{2,1,0:T(2,128)} %param.14) | copy-start | bytes 52
  20.6 32.2 %copy-start.21 = (f32[1,256]{1,0:T(1,128)S(1)}, f32[1,256]{1,0:T(1,128)}, u32[]{:S(2)}) copy-start(f32[1,256]{1,0:T(1,128)} %refs_7_.1) | copy-start | bytes 3076
  21.6 17.5 %copy-start.17 = (bf16[256,256]{1,0:T(8,128)(2,1)}, bf16[256,256]{1,0:T(8,128)(2,1)S(1)}, u32[]{:S(2)}) copy-start(bf16[256,256]{1,0:T(8,128)(2,1)S(1)} %get-tuple-element.36.refs_2_) | copy-start | bytes 393220
  21.6 31.1 %copy-start = (bf16[2592,128]{1,0:T(8,128)(2,1)}, bf16[2592,128]{1,0:T(8,128)(2,1)S(1)}, u32[]{:S(2)}) copy-start(bf16[2592,128]{1,0:T(8,128)(2,1)S(1)} %get-tuple-element.30.refs_3_) | copy-start | bytes 1990660
  21.6 17.5 %collective-permute-start.1 = (bf16[2592,128]{1,0:T(8,128)(2,1)S(1)}, bf16[2592,128]{1,0:T(8,128)(2,1)}, u32[]{:S(2)}, u32[]{:S(2)}) collective-permute-start(bf16[2592,128]{1,0:T(8,128)(2,1)S(1)} %get-tuple-element.30.refs_3_), channel_id=1, source_target_pairs={{0,2},{1,3},{2,0},{3,1},{4,6},{5,7},{6,4},{7,5},{8,10},{9,11},{10,... | collective-permute-start | bytes 1990664 | tf_op jit(solution)/shard_map/ppermute | solution.py:65
  24.9 32.3 %collective-permute-start.8 = (bf16[3024,128]{1,0:T(8,128)(2,1)S(1)}, bf16[3024,128]{1,0:T(8,128)(2,1)S(1)}, u32[]{:S(2)}, u32[]{:S(2)}) collective-permute-start(bf16[3024,128]{1,0:T(8,128)(2,1)S(1)} %pack_kernel.1.refs_5_), channel_id=1, source_target_pairs={{0,2},{1,3},{2,0},{3,1},{4,6},{5,7},{6,4},{7,5},{8,10},{9,11},{10,... | collective-permute-start | bytes 2322440 | tf_op jit(solution)/shard_map/ppermute | solution.py:65
  27.1 19.3 %collective-permute-start = (bf16[2592,128]{1,0:T(8,128)(2,1)S(1)}, bf16[2592,128]{1,0:T(8,128)(2,1)}, u32[]{:S(2)}, u32[]{:S(2)}) collective-permute-start(bf16[2592,128]{1,0:T(8,128)(2,1)S(1)} %get-tuple-element.30.refs_3_), channel_id=1, source_target_pairs={{0,1},{1,0},{2,3},{3,2},{4,5},{5,4},{6,7},{7,6},{8,9},{9,8},{10,11... | collective-permute-start | bytes 1990664 | tf_op jit(solution)/shard_map/ppermute | solution.py:65
  39.1 7.3 %collective-permute-start.2 = (bf16[2592,128]{1,0:T(8,128)(2,1)}, bf16[2592,128]{1,0:T(8,128)(2,1)}, u32[]{:S(2)}, u32[]{:S(2)}) collective-permute-start(bf16[2592,128]{1,0:T(8,128)(2,1)} %collective-permute-done.1.refs_5_), channel_id=1, source_target_pairs={{0,1},{1,0},{2,3},{3,2},{4,5},{5,4},{6,7},{7,6},{8,9},{9,8},{10,11... | collective-permute-start | bytes 1990664 | tf_op jit(solution)/shard_map/ppermute | solution.py:65
  44.3 23.6 %collective-permute-start.7 = (bf16[3024,128]{1,0:T(8,128)(2,1)S(1)}, bf16[3024,128]{1,0:T(8,128)(2,1)}, u32[]{:S(2)}, u32[]{:S(2)}) collective-permute-start(bf16[3024,128]{1,0:T(8,128)(2,1)S(1)} %pack_kernel.1.refs_5_), channel_id=1, source_target_pairs={{0,1},{1,0},{2,3},{3,2},{4,5},{5,4},{6,7},{7,6},{8,9},{9,8},{10,11... | collective-permute-start | bytes 2322440 | tf_op jit(solution)/shard_map/ppermute | solution.py:65
  57.2 13.7 %copy-start.9 = (bf16[576,256]{1,0:T(8,128)(2,1)}, bf16[576,256]{1,0:T(8,128)(2,1)S(1)}, u32[]{:S(2)}) copy-start(bf16[576,256]{1,0:T(8,128)(2,1)S(1)} %get-tuple-element.31.refs_0_) | copy-start | bytes 884740
  57.2 13.7 %copy-start.24 = (bf16[576,256]{1,0:T(8,128)(2,1)}, bf16[576,256]{1,0:T(8,128)(2,1)S(1)}, u32[]{:S(2)}) copy-start(bf16[576,256]{1,0:T(8,128)(2,1)S(1)} %get-tuple-element.33) | copy-start | bytes 884740
  57.2 13.7 %copy-start.25 = (bf16[576,256]{1,0:T(8,128)(2,1)}, bf16[576,256]{1,0:T(8,128)(2,1)S(1)}, u32[]{:S(2)}) copy-start(bf16[576,256]{1,0:T(8,128)(2,1)S(1)} %get-tuple-element.32) | copy-start | bytes 884740
  57.2 35.7 %copy-start.23 = (bf16[576,256]{1,0:T(8,128)(2,1)}, bf16[576,256]{1,0:T(8,128)(2,1)S(1)}, u32[]{:S(2)}) copy-start(bf16[576,256]{1,0:T(8,128)(2,1)S(1)} %get-tuple-element.34) | copy-start | bytes 884740
  57.2 13.6 %collective-permute-start.9 = (bf16[3024,128]{1,0:T(8,128)(2,1)S(1)}, bf16[3024,128]{1,0:T(8,128)(2,1)S(1)}, u32[]{:S(2)}, u32[]{:S(2)}) collective-permute-start(bf16[3024,128]{1,0:T(8,128)(2,1)S(1)} %pin_kernel.2.refs_7_), channel_id=1, source_target_pairs={{0,1},{1,0},{2,3},{3,2},{4,5},{5,4},{6,7},{7,6},{8,9},{9,8},{10,11... | collective-permute-start | bytes 2322440 | tf_op jit(solution)/shard_map/ppermute | solution.py:65
  63.3 7.6 %collective-permute-start.6 = (bf16[256,256]{1,0:T(8,128)(2,1)S(1)}, bf16[256,256]{1,0:T(8,128)(2,1)S(1)}, u32[]{:S(2)}, u32[]{:S(2)}) collective-permute-start(bf16[256,256]{1,0:T(8,128)(2,1)S(1)} %get-tuple-element.35.refs_1_), channel_id=1, source_target_pairs={{0,256},{1,257},{2,258},{3,259},{4,260},{5,261},{6,262},{7,263},{8... | collective-permute-start | bytes 393224 | tf_op jit(solution)/shard_map/ppermute | solution.py:312
  73.3 19.6 %copy-start.11 = (bf16[512,256]{1,0:T(8,128)(2,1)}, bf16[512,256]{1,0:T(8,128)(2,1)S(1)}, u32[]{:S(2)}) copy-start(bf16[512,256]{1,0:T(8,128)(2,1)S(1)} %get-tuple-element.43.refs_4_) | copy-start | bytes 786436
  73.3 9.6 %collective-permute-start.10 = (bf16[2,576,128]{2,1,0:T(8,128)(2,1)S(1)}, bf16[2,576,128]{2,1,0:T(8,128)(2,1)S(1)}, u32[]{:S(2)}, u32[]{:S(2)}) collective-permute-start(bf16[2,576,128]{2,1,0:T(8,128)(2,1)S(1)} %get-tuple-element.40), channel_id=1, source_target_pairs={{0,4},{4,0},{32,36},{36,32},{1,5},{5,1},{33,37},{37,33},{2,6},{6,2... | collective-permute-start | bytes 884744 | tf_op jit(solution)/shard_map/ppermute | solution.py:65
  75.4 9.3 %collective-permute-start.11 = (bf16[2,576,128]{2,1,0:T(8,128)(2,1)S(1)}, bf16[2,576,128]{2,1,0:T(8,128)(2,1)S(1)}, u32[]{:S(2)}, u32[]{:S(2)}) collective-permute-start(bf16[2,576,128]{2,1,0:T(8,128)(2,1)S(1)} %get-tuple-element.41), channel_id=1, source_target_pairs={{0,32},{4,36},{32,0},{36,4},{1,33},{5,37},{33,1},{37,5},{2,34},{6,... | collective-permute-start | bytes 884744 | tf_op jit(solution)/shard_map/ppermute | solution.py:65
  78.2 13.8 %collective-permute-start.12 = (bf16[2,576,128]{2,1,0:T(8,128)(2,1)S(1)}, bf16[2,576,128]{2,1,0:T(8,128)(2,1)S(1)}, u32[]{:S(2)}, u32[]{:S(2)}) collective-permute-start(bf16[2,576,128]{2,1,0:T(8,128)(2,1)S(1)} %get-tuple-element.42), channel_id=1, source_target_pairs={{0,36},{4,32},{32,4},{36,0},{1,37},{5,33},{33,5},{37,1},{2,38},{6,... | collective-permute-start | bytes 884744 | tf_op jit(solution)/shard_map/ppermute | solution.py:65
  92.9 30.1 %all-to-all-start.1 = ((bf16[16,72,128]{2,1,0:T(8,128)(2,1)}), bf16[16,72,128]{2,1,0:T(8,128)(2,1)S(1)}, u32[]{:S(2)}, u32[]{:S(2)}) async-start(bf16[16,72,128]{2,1,0:T(8,128)(2,1)} %bitcast.42), calls=%async_computation.1 | async-start | bytes 589824 | tf_op jit(solution)/shard_map/all_to_all | solution.py:78
  100.2 9.7 %collective-permute-start.3 = (bf16[576,256]{1,0:T(8,128)(2,1)}, bf16[576,256]{1,0:T(8,128)(2,1)S(1)}, u32[]{:S(2)}, u32[]{:S(2)}) collective-permute-start(bf16[576,256]{1,0:T(8,128)(2,1)} %copy-done.25), channel_id=1, source_target_pairs={{0,1},{1,0},{2,3},{3,2},{4,5},{5,4},{6,7},{7,6},{8,9},{9,8},{10,11... | collective-permute-start | bytes 884744 | tf_op jit(solution)/shard_map/ppermute | solution.py:65
  104.4 10.7 %collective-permute-start.4 = (bf16[576,256]{1,0:T(8,128)(2,1)}, bf16[576,256]{1,0:T(8,128)(2,1)S(1)}, u32[]{:S(2)}, u32[]{:S(2)}) collective-permute-start(bf16[576,256]{1,0:T(8,128)(2,1)} %copy-done.24), channel_id=1, source_target_pairs={{0,2},{1,3},{2,0},{3,1},{4,6},{5,7},{6,4},{7,5},{8,10},{9,11},{10,... | collective-permute-start | bytes 884744 | tf_op jit(solution)/shard_map/ppermute | solution.py:65
  106.6 14.9 %collective-permute-start.5 = (bf16[576,256]{1,0:T(8,128)(2,1)}, bf16[576,256]{1,0:T(8,128)(2,1)S(1)}, u32[]{:S(2)}, u32[]{:S(2)}) collective-permute-start(bf16[576,256]{1,0:T(8,128)(2,1)} %copy-done.23), channel_id=1, source_target_pairs={{0,3},{1,2},{2,1},{3,0},{4,7},{5,6},{6,5},{7,4},{8,11},{9,10},{10,... | collective-permute-start | bytes 884744 | tf_op jit(solution)/shard_map/ppermute | solution.py:65
  123.8 25.4 %all-to-all-start.2 = ((bf16[16,72,128]{2,1,0:T(8,128)(2,1)}), bf16[16,72,128]{2,1,0:T(8,128)(2,1)S(1)}, u32[]{:S(2)}, u32[]{:S(2)}) async-start(bf16[16,72,128]{2,1,0:T(8,128)(2,1)} %total_kernel.1), calls=%async_computation.2 | async-start | bytes 589824 | tf_op jit(solution)/shard_map/all_to_all | solution.py:78
  135.5 9.5 %collective-permute-start.17 = (bf16[512,256]{1,0:T(8,128)(2,1)}, bf16[512,256]{1,0:T(8,128)(2,1)}, u32[]{:S(2)}, u32[]{:S(2)}) collective-permute-start(bf16[512,256]{1,0:T(8,128)(2,1)} %copy-done.11), channel_id=1, source_target_pairs={{0,2},{1,3},{2,0},{3,1},{4,6},{5,7},{6,4},{7,5},{8,10},{9,11},{10,... | collective-permute-start | bytes 786440 | tf_op jit(solution)/shard_map/ppermute | solution.py:65
  137.7 19.8 %collective-permute-start.16 = (bf16[512,256]{1,0:T(8,128)(2,1)}, bf16[512,256]{1,0:T(8,128)(2,1)}, u32[]{:S(2)}, u32[]{:S(2)}) collective-permute-start(bf16[512,256]{1,0:T(8,128)(2,1)} %copy-done.11), channel_id=1, source_target_pairs={{0,1},{1,0},{2,3},{3,2},{4,5},{5,4},{6,7},{7,6},{8,9},{9,8},{10,11... | collective-permute-start | bytes 786440 | tf_op jit(solution)/shard_map/ppermute | solution.py:65
  145.0 12.6 %collective-permute-start.18 = (bf16[512,256]{1,0:T(8,128)(2,1)}, bf16[512,256]{1,0:T(8,128)(2,1)}, u32[]{:S(2)}, u32[]{:S(2)}) collective-permute-start(bf16[512,256]{1,0:T(8,128)(2,1)} %collective-permute-done.17.refs_6_), channel_id=1, source_target_pairs={{0,1},{1,0},{2,3},{3,2},{4,5},{5,4},{6,7},{7,6},{8,9},{9,8},{10,11... | collective-permute-start | bytes 786440 | tf_op jit(solution)/shard_map/ppermute | solution.py:65
  149.2 9.1 %collective-permute-start.15 = (bf16[2,576,128]{2,1,0:T(8,128)(2,1)S(1)}, bf16[2,576,128]{2,1,0:T(8,128)(2,1)S(1)}, u32[]{:S(2)}, u32[]{:S(2)}) collective-permute-start(bf16[2,576,128]{2,1,0:T(8,128)(2,1)S(1)} %bitcast.30), channel_id=1, source_target_pairs={{0,36},{4,32},{32,4},{36,0},{1,37},{5,33},{33,5},{37,1},{2,38},{6,... | collective-permute-start | bytes 884744 | tf_op jit(solution)/shard_map/ppermute | solution.py:65
  151.1 11.7 %collective-permute-start.14 = (bf16[2,576,128]{2,1,0:T(8,128)(2,1)S(1)}, bf16[2,576,128]{2,1,0:T(8,128)(2,1)S(1)}, u32[]{:S(2)}, u32[]{:S(2)}) collective-permute-start(bf16[2,576,128]{2,1,0:T(8,128)(2,1)S(1)} %bitcast.31), channel_id=1, source_target_pairs={{0,32},{4,36},{32,0},{36,4},{1,33},{5,37},{33,1},{37,5},{2,34},{6,... | collective-permute-start | bytes 884744 | tf_op jit(solution)/shard_map/ppermute | solution.py:65
  154.2 11.6 %collective-permute-start.13 = (bf16[2,576,128]{2,1,0:T(8,128)(2,1)S(1)}, bf16[2,576,128]{2,1,0:T(8,128)(2,1)S(1)}, u32[]{:S(2)}, u32[]{:S(2)}) collective-permute-start(bf16[2,576,128]{2,1,0:T(8,128)(2,1)S(1)} %bitcast.32), channel_id=1, source_target_pairs={{0,4},{4,0},{32,36},{36,32},{1,5},{5,1},{33,37},{37,33},{2,6},{6,2... | collective-permute-start | bytes 884744 | tf_op jit(solution)/shard_map/ppermute | solution.py:65
  168.0 29.0 %copy-start.3 = (bf16[576,256]{1,0:T(8,128)(2,1)S(1)}, bf16[576,256]{1,0:T(8,128)(2,1)}, u32[]{:S(2)}) copy-start(bf16[576,256]{1,0:T(8,128)(2,1)} %copy-done.2) | copy-start | bytes 884740
  168.0 29.0 %copy-start.5 = (bf16[576,256]{1,0:T(8,128)(2,1)S(1)}, bf16[576,256]{1,0:T(8,128)(2,1)}, u32[]{:S(2)}) copy-start(bf16[576,256]{1,0:T(8,128)(2,1)} %copy-done.4) | copy-start | bytes 884740
  168.0 29.0 %copy-start.10 = (bf16[576,256]{1,0:T(8,128)(2,1)S(1)}, bf16[576,256]{1,0:T(8,128)(2,1)}, u32[]{:S(2)}) copy-start(bf16[576,256]{1,0:T(8,128)(2,1)} %copy-done.9) | copy-start | bytes 884740
  168.0 7.5 %collective-permute-start.19 = (bf16[256,256]{1,0:T(8,128)(2,1)S(1)}, bf16[256,256]{1,0:T(8,128)(2,1)S(1)}, u32[]{:S(2)}, u32[]{:S(2)}) collective-permute-start(bf16[256,256]{1,0:T(8,128)(2,1)S(1)} %get-tuple-element.45), channel_id=1, source_target_pairs={{256,0},{257,1},{258,2},{259,3},{260,4},{261,5},{262,6},{263,7},{2... | collective-permute-start | bytes 393224 | tf_op jit(solution)/shard_map/ppermute | solution.py:342
  175.6 24.3 %copy-start.12 = (bf16[512,256]{1,0:T(8,128)(2,1)S(1)}, bf16[512,256]{1,0:T(8,128)(2,1)}, u32[]{:S(2)}) copy-start(bf16[512,256]{1,0:T(8,128)(2,1)} %copy-done.11) | copy-start | bytes 786436
  175.6 5.8 %collective-permute-start.21 = (bf16[256,256]{1,0:T(8,128)(2,1)S(1)}, bf16[256,256]{1,0:T(8,128)(2,1)S(1)}, u32[]{:S(2)}, u32[]{:S(2)}) collective-permute-start(bf16[256,256]{1,0:T(8,128)(2,1)S(1)} %pregrad_kernel.1.refs_4_), channel_id=1, source_target_pairs={{0,2},{1,3},{2,0},{3,1},{4,6},{5,7},{6,4},{7,5},{8,10},{9,11},{10,... | collective-permute-start | bytes 393224 | tf_op jit(solution)/shard_map/ppermute | solution.py:65
  177.9 20.5 %collective-permute-start.24 = (bf16[576,256]{1,0:T(8,128)(2,1)S(1)}, bf16[576,256]{1,0:T(8,128)(2,1)S(1)}, u32[]{:S(2)}, u32[]{:S(2)}) collective-permute-start(bf16[576,256]{1,0:T(8,128)(2,1)S(1)} %get-tuple-element.52), channel_id=1, source_target_pairs={{0,2},{1,3},{2,0},{3,1},{4,6},{5,7},{6,4},{7,5},{8,10},{9,11},{10,... | collective-permute-start | bytes 884744 | tf_op jit(solution)/shard_map/ppermute | solution.py:65
  181.4 17.0 %collective-permute-start.23 = (bf16[576,256]{1,0:T(8,128)(2,1)S(1)}, bf16[576,256]{1,0:T(8,128)(2,1)S(1)}, u32[]{:S(2)}, u32[]{:S(2)}) collective-permute-start(bf16[576,256]{1,0:T(8,128)(2,1)S(1)} %get-tuple-element.51), channel_id=1, source_target_pairs={{0,1},{1,0},{2,3},{3,2},{4,5},{5,4},{6,7},{7,6},{8,9},{9,8},{10,11... | collective-permute-start | bytes 884744 | tf_op jit(solution)/shard_map/ppermute | solution.py:65
  189.3 10.5 %collective-permute-start.25 = (bf16[576,256]{1,0:T(8,128)(2,1)S(1)}, bf16[576,256]{1,0:T(8,128)(2,1)S(1)}, u32[]{:S(2)}, u32[]{:S(2)}) collective-permute-start(bf16[576,256]{1,0:T(8,128)(2,1)S(1)} %get-tuple-element.53), channel_id=1, source_target_pairs={{0,3},{1,2},{2,1},{3,0},{4,7},{5,6},{6,5},{7,4},{8,11},{9,10},{10,... | collective-permute-start | bytes 884744 | tf_op jit(solution)/shard_map/ppermute | solution.py:65
  191.3 4.3 %collective-permute-start.20 = (bf16[256,256]{1,0:T(8,128)(2,1)S(1)}, bf16[256,256]{1,0:T(8,128)(2,1)S(1)}, u32[]{:S(2)}, u32[]{:S(2)}) collective-permute-start(bf16[256,256]{1,0:T(8,128)(2,1)S(1)} %pregrad_kernel.1.refs_4_), channel_id=1, source_target_pairs={{0,1},{1,0},{2,3},{3,2},{4,5},{5,4},{6,7},{7,6},{8,9},{9,8},{10,11... | collective-permute-start | bytes 393224 | tf_op jit(solution)/shard_map/ppermute | solution.py:65
  193.8 3.2 %collective-permute-start.22 = (bf16[256,256]{1,0:T(8,128)(2,1)S(1)}, bf16[256,256]{1,0:T(8,128)(2,1)S(1)}, u32[]{:S(2)}, u32[]{:S(2)}) collective-permute-start(bf16[256,256]{1,0:T(8,128)(2,1)S(1)} %collective-permute-done.21.refs_6_.refs_0_), channel_id=1, source_target_pairs={{0,1},{1,0},{2,3},{3,2},{4,5},{5,4},{6,7},{7,6},{8,9},{9,8},{10,11... | collective-permute-start | bytes 393224 | tf_op jit(solution)/shard_map/ppermute | solution.py:65
  (7 other events, 18.5 us)

commit v6 on v4

--- a/solution.py
+++ b/solution.py
@@ -328,14 +328,18 @@
         after=(corner(both[1:]),),
     )
     later = lax.ppermute(prev_back, "layer", [(1, 0)])
+    err[2] = toward(err[2], 2)
     (pregrad,) = call(
-        pregrad_kernel, (own_back, later, slope), [((width, height), BF)]
+        pregrad_kernel,
+        (own_back, later, slope),
+        [((width, height), BF)],
+        after=(err[2],),
     )
     pregrad = gather4(pregrad)
-    err[1], err[3] = call(
-        pin_kernel, (), [], after=(pregrad[2],), through=(err[1], err[3])
-    )
-    err = exchange4(err)
+    (last,) = call(pin_kernel, (), [], after=(pregrad[2],), through=(err[3],))
+    err[3] = toward(last, 3)
+    (last,) = call(pin_kernel, (), [], after=(pregrad[1],), through=(err[1],))
+    err[1] = toward(last, 1)
     grad_own, grad_prev = call(
         decoder_grads_kernel, (*err, *both), [((block, width), F32)] * 2, leaving=(0, 1)
     )

time: 190 us -> 195 us (1.026)
  waiting for transfers between devices: 62.4 us -> 70.2 us
  starting transfers between devices: 103 us -> 99.7 us
    ppermute x18, waiting for transfers between devices: 26.9 us -> 32.2 us  [toward(): return lax.ppermute(x, TOK, [(i, i ^ k) for i in range(4)])]
    ppermute x18, starting transfers between devices: 61.2 us -> 58.2 us  [toward(): return lax.ppermute(x, TOK, [(i, i ^ k) for i in range(4)])]
    ppermute x1, waiting for transfers between devices: 6.03 us -> 8.5 us  [local(): later = lax.ppermute(prev_back, 'layer', [(1, 0)])]
    pallas_call x12 -> x13, Pallas kernels: 14.8 us -> 14.8 us  [call(): pl.pallas_call(body, out_shape=[(pltpu.HBM if i in leaving else pltpu.VME...]
where the time goes in v6:
time: 195 us; the launch traced here: 194 us
  starting transfers between devices  99.7 us (51%)
  waiting for transfers between devices  70.2 us (36%)
  Pallas kernels  14.8 us (8%)
  local copies, waits for them, and re-layouts  7.98 us (4%)
    ppermute x18, starting transfers between devices, toward(): return lax.ppermute(x, TOK, [(i, i ^ k) for i in range(4)])  58.2 us
    all_to_all x3, starting transfers between devices, exchange(): lax.all_to_all(blocks, 'feat', split_axis=0, concat_axis=0, tiled=True)  35.5 us
    ppermute x18, waiting for transfers between devices, toward(): return lax.ppermute(x, TOK, [(i, i ^ k) for i in range(4)])  32.2 us
    all_to_all x3, waiting for transfers between devices, exchange(): lax.all_to_all(blocks, 'feat', split_axis=0, concat_axis=0, tiled=True)  26.6 us
    pallas_call x13, Pallas kernels, call(): pl.pallas_call(body, out_shape=[(pltpu.HBM if i in leaving else pltpu.VME...  14.8 us
    ppermute x1, waiting for transfers between devices, local(): later = lax.ppermute(prev_back, 'layer', [(1, 0)])  8.5 us
    unnamed x68, local copies, waits for them, and re-layouts  7.98 us
    ppermute x1, starting transfers between devices, local(): shifted = lax.ppermute(codes, 'layer', [(0, 1)])  4.65 us
  transfers between devices with their start and end apart: 23, of which 13 were waited for; matrix products, arithmetic and copies ran while one was open for 0% of the time, Pallas kernels for 3%

profile of v6, /device:TPU:1, one launch (start us, length us, event | category | flops | bytes accessed | tf_op | source)
XLA Modules:
  0.0 194.0 jit_solution(16398057754872005005)
XLA Ops:
  0.6 0.7 copy-done.27
  2.0 1.2 spread_kernel.1
  3.3 17.3 %all-to-all-start = ((bf16[64,80,128]{2,1,0:T(8,128)(2,1)}), bf16[64,80,128]{2,1,0:T(8,128)(2,1)S(1)}, u32[]{:S(2)}, u32[]{:S(2)}) async-start(bf16[64,80,128]{2,1,0:T(8,128)(2,1)} %spread_kernel.1), calls=%async_computation | async-start | bytes 2621440 | tf_op jit(solution)/shard_map/all_to_all | solution.py:75
  21.4 3.1 %collective-permute-start.1 = (bf16[2592,128]{1,0:T(8,128)(2,1)S(1)}, bf16[2592,128]{1,0:T(8,128)(2,1)}, u32[]{:S(2)}, u32[]{:S(2)}) collective-permute-start(bf16[2592,128]{1,0:T(8,128)(2,1)S(1)} %get-tuple-element.25.refs_3_), channel_id=1, source_target_pairs={{0,2},{1,3},{2,0},{3,1},{4,6},{5,7},{6,4},{7,5},{8,10},{9,11},{10,... | collective-permute-start | bytes 1990664 | tf_op jit(solution)/shard_map/ppermute | solution.py:62
  24.5 0.9 copy-done.21
  25.5 2.2 %collective-permute-start.8 = (bf16[3024,128]{1,0:T(8,128)(2,1)S(1)}, bf16[3024,128]{1,0:T(8,128)(2,1)S(1)}, u32[]{:S(2)}, u32[]{:S(2)}) collective-permute-start(bf16[3024,128]{1,0:T(8,128)(2,1)S(1)} %pack_kernel.1.refs_5_.refs_2_), channel_id=1, source_target_pairs={{0,2},{1,3},{2,0},{3,1},{4,6},{5,7},{6,4},{7,5},{8,10},{9,11},{10,... | collective-permute-start | bytes 2322440 | tf_op jit(solution)/shard_map/ppermute | solution.py:62
  27.7 3.4 %collective-permute-start = (bf16[2592,128]{1,0:T(8,128)(2,1)S(1)}, bf16[2592,128]{1,0:T(8,128)(2,1)}, u32[]{:S(2)}, u32[]{:S(2)}) collective-permute-start(bf16[2592,128]{1,0:T(8,128)(2,1)S(1)} %get-tuple-element.25.refs_3_), channel_id=1, source_target_pairs={{0,1},{1,0},{2,3},{3,2},{4,5},{5,4},{6,7},{7,6},{8,9},{9,8},{10,11... | collective-permute-start | bytes 1990664 | tf_op jit(solution)/shard_map/ppermute | solution.py:62
  31.1 7.7 %collective-permute-done.1.refs_5_ = bf16[2592,128]{1,0:T(8,128)(2,1)} collective-permute-done((bf16[2592,128]{1,0:T(8,128)(2,1)S(1)}, bf16[2592,128]{1,0:T(8,128)(2,1)}, u32[]{:S(2)}, u32[]{:S(2)}) %collective-permute-start.1) | collective-permute-done | bytes 663584 | tf_op jit(solution)/shard_map/ppermute | solution.py:62
  38.8 5.2 %collective-permute-start.2 = (bf16[2592,128]{1,0:T(8,128)(2,1)}, bf16[2592,128]{1,0:T(8,128)(2,1)}, u32[]{:S(2)}, u32[]{:S(2)}) collective-permute-start(bf16[2592,128]{1,0:T(8,128)(2,1)} %collective-permute-done.1.refs_5_), channel_id=1, source_target_pairs={{0,1},{1,0},{2,3},{3,2},{4,5},{5,4},{6,7},{7,6},{8,9},{9,8},{10,11... | collective-permute-start | bytes 1990664 | tf_op jit(solution)/shard_map/ppermute | solution.py:62
  44.1 1.9 collective-permute-start.7
  46.1 6.6 %all-to-all-done.refs_2_ = bf16[64,80,128]{2,1,0:T(8,128)(2,1)S(1)} async-done(((bf16[64,80,128]{2,1,0:T(8,128)(2,1)}), bf16[64,80,128]{2,1,0:T(8,128)(2,1)S(1)}, u32[]{:S(2)}, u32[]{:S(2)}) %all-to-all-start) | async-done | bytes 1310752 | tf_op jit(solution)/shard_map/all_to_all | solution.py:75
  52.7 3.3 %encode_kernel.1 = (bf16[576,256]{1,0:T(8,128)(2,1)S(1)}, bf16[576,256]{1,0:T(8,128)(2,1)S(1)}, bf16[576,256]{1,0:T(8,128)(2,1)S(1)}, bf16[576,256]{1,0:T(8,128)...) custom-call(s32[2]{0:T(128)S(1)} %pad_add_fusion.refs_0_, ...), custom_call_target="tpu_custom_call" | custom-call | tf_op jit(solution)/shard_map/encode_kernel/pallas_call | solution.py:38
  56.2 6.1 %collective-permute-start.9 = (bf16[3024,128]{1,0:T(8,128)(2,1)S(1)}, bf16[3024,128]{1,0:T(8,128)(2,1)S(1)}, u32[]{:S(2)}, u32[]{:S(2)}) collective-permute-start(bf16[3024,128]{1,0:T(8,128)(2,1)S(1)} %pin_kernel.3.refs_7_.refs_4_), channel_id=1, source_target_pairs={{0,1},{1,0},{2,3},{3,2},{4,5},{5,4},{6,7},{7,6},{8,9},{9,8},{10,11... | collective-permute-start | bytes 2322440 | tf_op jit(solution)/shard_map/ppermute | solution.py:62
  62.2 4.7 %collective-permute-start.6 = (bf16[256,256]{1,0:T(8,128)(2,1)S(1)}, bf16[256,256]{1,0:T(8,128)(2,1)S(1)}, u32[]{:S(2)}, u32[]{:S(2)}) collective-permute-start(bf16[256,256]{1,0:T(8,128)(2,1)S(1)} %get-tuple-element.30.refs_1_), channel_id=1, source_target_pairs={{0,256},{1,257},{2,258},{3,259},{4,260},{5,261},{6,262},{7,263},{8... | collective-permute-start | bytes 393224 | tf_op jit(solution)/shard_map/ppermute | solution.py:310
  66.9 2.9 %collective-permute-done.6.refs_3_ = bf16[256,256]{1,0:T(8,128)(2,1)S(1)} collective-permute-done((bf16[256,256]{1,0:T(8,128)(2,1)S(1)}, bf16[256,256]{1,0:T(8,128)(2,1)S(1)}, u32[]{:S(2)}, u32[]{:S(2)}) %collective-permute-start.6) | collective-permute-done | bytes 131104 | tf_op jit(solution)/shard_map/ppermute | solution.py:310
  69.8 3.3 %decode_kernel.1 = (bf16[64,72,128]{2,1,0:T(8,128)(2,1)}, bf16[512,256]{1,0:T(8,128)(2,1)S(1)}) custom-call(s32[2]{0:T(128)S(1)} %pad_add_fusion.refs_0_, bf16[256,256]{1,0:T(8,128)(2,1)S(1)} %get-tuple-element.30.refs_1_, bf16[256,256]{1,0:T(8,128)(2,1)S(1)} %copy-done.26, bf16[256,256]{1,0:T(8,128)(2,1)S(1)} %collective-permute-done.6.refs_3_, ...), custom_call_target="tpu_custom_call" | custom-call | tf_op jit(solution)/shard_map/decode_kernel/pallas_call | solution.py:38
  73.9 9.0 %all-to-all-start.1 = ((bf16[64,72,128]{2,1,0:T(8,128)(2,1)}), bf16[64,72,128]{2,1,0:T(8,128)(2,1)S(1)}, u32[]{:S(2)}, u32[]{:S(2)}) async-start(bf16[64,72,128]{2,1,0:T(8,128)(2,1)} %get-tuple-element.34), calls=%async_computation.1 | async-start | bytes 2359296 | tf_op jit(solution)/shard_map/all_to_all | solution.py:75
  82.9 3.0 %collective-permute-start.3 = (bf16[576,256]{1,0:T(8,128)(2,1)}, bf16[576,256]{1,0:T(8,128)(2,1)S(1)}, u32[]{:S(2)}, u32[]{:S(2)}) collective-permute-start(bf16[576,256]{1,0:T(8,128)(2,1)} %copy-done.33), channel_id=1, source_target_pairs={{0,1},{1,0},{2,3},{3,2},{4,5},{5,4},{6,7},{7,6},{8,9},{9,8},{10,11... | collective-permute-start | bytes 884744 | tf_op jit(solution)/shard_map/ppermute | solution.py:62
  85.8 2.2 %collective-permute-start.4 = (bf16[576,256]{1,0:T(8,128)(2,1)}, bf16[576,256]{1,0:T(8,128)(2,1)S(1)}, u32[]{:S(2)}, u32[]{:S(2)}) collective-permute-start(bf16[576,256]{1,0:T(8,128)(2,1)} %copy-done.32), channel_id=1, source_target_pairs={{0,2},{1,3},{2,0},{3,1},{4,6},{5,7},{6,4},{7,5},{8,10},{9,11},{10,... | collective-permute-start | bytes 884744 | tf_op jit(solution)/shard_map/ppermute | solution.py:62
  88.1 3.2 %collective-permute-start.5 = (bf16[576,256]{1,0:T(8,128)(2,1)}, bf16[576,256]{1,0:T(8,128)(2,1)S(1)}, u32[]{:S(2)}, u32[]{:S(2)}) collective-permute-start(bf16[576,256]{1,0:T(8,128)(2,1)} %copy-done.31), channel_id=1, source_target_pairs={{0,3},{1,2},{2,1},{3,0},{4,7},{5,6},{6,5},{7,4},{8,11},{9,10},{10,... | collective-permute-start | bytes 884744 | tf_op jit(solution)/shard_map/ppermute | solution.py:62
  91.3 5.2 %collective-permute-done.4.refs_2_ = bf16[576,256]{1,0:T(8,128)(2,1)S(1)} collective-permute-done((bf16[576,256]{1,0:T(8,128)(2,1)}, bf16[576,256]{1,0:T(8,128)(2,1)S(1)}, u32[]{:S(2)}, u32[]{:S(2)}) %collective-permute-start.4) | collective-permute-done | bytes 294944 | tf_op jit(solution)/shard_map/ppermute | solution.py:62
  96.6 6.7 %collective-permute-done.5.refs_3_ = bf16[576,256]{1,0:T(8,128)(2,1)S(1)} collective-permute-done((bf16[576,256]{1,0:T(8,128)(2,1)}, bf16[576,256]{1,0:T(8,128)(2,1)S(1)}, u32[]{:S(2)}, u32[]{:S(2)}) %collective-permute-start.5) | collective-permute-done | bytes 294944 | tf_op jit(solution)/shard_map/ppermute | solution.py:62
  103.3 0.7 copy-done.2
  104.0 0.7 copy-done.4
  105.4 6.8 %all-to-all-done.1.refs_0_ = bf16[64,72,128]{2,1,0:T(8,128)(2,1)S(1)} async-done(((bf16[64,72,128]{2,1,0:T(8,128)(2,1)}), bf16[64,72,128]{2,1,0:T(8,128)(2,1)S(1)}, u32[]{:S(2)}, u32[]{:S(2)}) %all-to-all-start.1) | async-done | bytes 1179680 | tf_op jit(solution)/shard_map/all_to_all | solution.py:75
  112.2 1.2 total_kernel.1
  113.5 9.3 %all-to-all-start.2 = ((bf16[64,72,128]{2,1,0:T(8,128)(2,1)}), bf16[64,72,128]{2,1,0:T(8,128)(2,1)S(1)}, u32[]{:S(2)}, u32[]{:S(2)}) async-start(bf16[64,72,128]{2,1,0:T(8,128)(2,1)} %total_kernel.1), calls=%async_computation.2 | async-start | bytes 2359296 | tf_op jit(solution)/shard_map/all_to_all | solution.py:75
  122.8 2.2 %collective-permute-start.11 = (bf16[512,256]{1,0:T(8,128)(2,1)}, bf16[512,256]{1,0:T(8,128)(2,1)S(1)}, u32[]{:S(2)}, u32[]{:S(2)}) collective-permute-start(bf16[512,256]{1,0:T(8,128)(2,1)} %copy-done.19), channel_id=1, source_target_pairs={{0,2},{1,3},{2,0},{3,1},{4,6},{5,7},{6,4},{7,5},{8,10},{9,11},{10,... | collective-permute-start | bytes 786440 | tf_op jit(solution)/shard_map/ppermute | solution.py:62
  125.0 3.4 %collective-permute-start.10 = (bf16[512,256]{1,0:T(8,128)(2,1)}, bf16[512,256]{1,0:T(8,128)(2,1)S(1)}, u32[]{:S(2)}, u32[]{:S(2)}) collective-permute-start(bf16[512,256]{1,0:T(8,128)(2,1)} %copy-done.19), channel_id=1, source_target_pairs={{0,1},{1,0},{2,3},{3,2},{4,5},{5,4},{6,7},{7,6},{8,9},{9,8},{10,11... | collective-permute-start | bytes 786440 | tf_op jit(solution)/shard_map/ppermute | solution.py:62
  128.3 3.1 %collective-permute-done.11.refs_6_ = bf16[512,256]{1,0:T(8,128)(2,1)S(1)} collective-permute-done((bf16[512,256]{1,0:T(8,128)(2,1)}, bf16[512,256]{1,0:T(8,128)(2,1)S(1)}, u32[]{:S(2)}, u32[]{:S(2)}) %collective-permute-start.11) | collective-permute-done | bytes 262176 | tf_op jit(solution)/shard_map/ppermute | solution.py:62
  131.5 4.0 %collective-permute-start.12 = (bf16[512,256]{1,0:T(8,128)(2,1)S(1)}, bf16[512,256]{1,0:T(8,128)(2,1)S(1)}, u32[]{:S(2)}, u32[]{:S(2)}) collective-permute-start(bf16[512,256]{1,0:T(8,128)(2,1)S(1)} %collective-permute-done.11.refs_6_), channel_id=1, source_target_pairs={{0,1},{1,0},{2,3},{3,2},{4,5},{5,4},{6,7},{7,6},{8,9},{9,8},{10,11... | collective-permute-start | bytes 786440 | tf_op jit(solution)/shard_map/ppermute | solution.py:62
  135.5 1.1 collective-permute-done.12.refs_7_
  136.6 0.7 copy-done.13
  138.7 13.2 %all-to-all-done.2.refs_1_ = bf16[64,72,128]{2,1,0:T(8,128)(2,1)S(1)} async-done(((bf16[64,72,128]{2,1,0:T(8,128)(2,1)}), bf16[64,72,128]{2,1,0:T(8,128)(2,1)S(1)}, u32[]{:S(2)}, u32[]{:S(2)}) %all-to-all-start.2) | async-done | bytes 1179680 | tf_op jit(solution)/shard_map/all_to_all | solution.py:75
  152.0 2.2 %back_kernel.1 = (f32[256,256]{1,0:T(8,128)S(1)}, bf16[256,256]{1,0:T(8,128)(2,1)S(1)}, bf16[576,256]{1,0:T(8,128)(2,1)S(1)}, bf16[576,256]{1,0:T(8,128)(2,1)S(1...) custom-call(s32[2]{0:T(128)S(1)} %pad_add_fusion.refs_0_, ...), custom_call_target="tpu_custom_call" | custom-call | tf_op jit(solution)/shard_map/back_kernel/pallas_call | solution.py:38
  154.2 2.2 %collective-permute-start.14 = (bf16[576,256]{1,0:T(8,128)(2,1)S(1)}, bf16[576,256]{1,0:T(8,128)(2,1)S(1)}, u32[]{:S(2)}, u32[]{:S(2)}) collective-permute-start(bf16[576,256]{1,0:T(8,128)(2,1)S(1)} %get-tuple-element.38), channel_id=1, source_target_pairs={{0,2},{1,3},{2,0},{3,1},{4,6},{5,7},{6,4},{7,5},{8,10},{9,11},{10,... | collective-permute-start | bytes 884744 | tf_op jit(solution)/shard_map/ppermute | solution.py:62
  156.4 1.3 collective-permute-start.13
  157.7 8.5 %collective-permute-done.13.refs_1_ = bf16[256,256]{1,0:T(8,128)(2,1)S(1)} collective-permute-done((bf16[256,256]{1,0:T(8,128)(2,1)S(1)}, bf16[256,256]{1,0:T(8,128)(2,1)S(1)}, u32[]{:S(2)}, u32[]{:S(2)}) %collective-permute-start.13) | collective-permute-done | bytes 131104 | tf_op jit(solution)/shard_map/ppermute | solution.py:330
  166.3 7.3 %collective-permute-start.15 = (bf16[256,256]{1,0:T(8,128)(2,1)S(1)}, bf16[256,256]{1,0:T(8,128)(2,1)S(1)}, u32[]{:S(2)}, u32[]{:S(2)}) collective-permute-start(bf16[256,256]{1,0:T(8,128)(2,1)S(1)} %pregrad_kernel.1.refs_4_), channel_id=1, source_target_pairs={{0,1},{1,0},{2,3},{3,2},{4,5},{5,4},{6,7},{7,6},{8,9},{9,8},{10,11... | collective-permute-start | bytes 393224 | tf_op jit(solution)/shard_map/ppermute | solution.py:62
  173.6 1.9 collective-permute-start.16
  175.5 2.1 %collective-permute-start.18 = (bf16[576,256]{1,0:T(8,128)(2,1)S(1)}, bf16[576,256]{1,0:T(8,128)(2,1)S(1)}, u32[]{:S(2)}, u32[]{:S(2)}) collective-permute-start(bf16[576,256]{1,0:T(8,128)(2,1)S(1)} %pin_kernel.4), channel_id=1, source_target_pairs={{0,1},{1,0},{2,3},{3,2},{4,5},{5,4},{6,7},{7,6},{8,9},{9,8},{10,11... | collective-permute-start | bytes 884744 | tf_op jit(solution)/shard_map/ppermute | solution.py:62
  177.7 2.9 %collective-permute-done.16.refs_6_.refs_0_ = bf16[256,256]{1,0:T(8,128)(2,1)S(1)} collective-permute-done((bf16[256,256]{1,0:T(8,128)(2,1)S(1)}, bf16[256,256]{1,0:T(8,128)(2,1)S(1)}, u32[]{:S(2)}, u32[]{:S(2)}) %collective-permute-start.16) | collective-permute-done | bytes 131104 | tf_op jit(solution)/shard_map/ppermute | solution.py:62
  180.6 2.7 %collective-permute-start.19 = (bf16[576,256]{1,0:T(8,128)(2,1)S(1)}, bf16[576,256]{1,0:T(8,128)(2,1)S(1)}, u32[]{:S(2)}, u32[]{:S(2)}) collective-permute-start(bf16[576,256]{1,0:T(8,128)(2,1)S(1)} %pin_kernel.5), channel_id=1, source_target_pairs={{0,3},{1,2},{2,1},{3,0},{4,7},{5,6},{6,5},{7,4},{8,11},{9,10},{10,... | collective-permute-start | bytes 884744 | tf_op jit(solution)/shard_map/ppermute | solution.py:62
  183.4 2.0 %collective-permute-start.17 = (bf16[256,256]{1,0:T(8,128)(2,1)S(1)}, bf16[256,256]{1,0:T(8,128)(2,1)S(1)}, u32[]{:S(2)}, u32[]{:S(2)}) collective-permute-start(bf16[256,256]{1,0:T(8,128)(2,1)S(1)} %collective-permute-done.16.refs_6_.refs_0_), channel_id=1, source_target_pairs={{0,1},{1,0},{2,3},{3,2},{4,5},{5,4},{6,7},{7,6},{8,9},{9,8},{10,11... | collective-permute-start | bytes 393224 | tf_op jit(solution)/shard_map/ppermute | solution.py:62
  185.4 1.2 collective-permute-done.17.refs_7_
  186.6 1.4 encoder_grads_kernel.1
  188.0 4.1 %collective-permute-done.19.refs_3_ = bf16[576,256]{1,0:T(8,128)(2,1)S(1)} collective-permute-done((bf16[576,256]{1,0:T(8,128)(2,1)S(1)}, bf16[576,256]{1,0:T(8,128)(2,1)S(1)}, u32[]{:S(2)}, u32[]{:S(2)}) %collective-permute-start.19) | collective-permute-done | bytes 294944 | tf_op jit(solution)/shard_map/ppermute | solution.py:62
  192.2 1.8 decoder_grads_kernel.1
  (82 shorter events, 4.6 us)
Async XLA Ops:
  0.6 0.7 copy-start.27
  3.2 17.3 %copy-start.8 = (bf16[1,576,256]{2,1,0:T(8,128)(2,1)S(1)}, bf16[1,576,256]{2,1,0:T(8,128)(2,1)}, u32[]{:S(2)}) copy-start(bf16[1,576,256]{2,1,0:T(8,128)(2,1)} %param.18) | copy-start | bytes 884740
  3.2 17.3 %copy-start.22 = (bf16[1,576,144]{1,2,0:T(8,128)(2,1)S(1)}, bf16[1,576,144]{1,2,0:T(8,128)(2,1)}, u32[]{:S(2)}) copy-start(bf16[1,576,144]{1,2,0:T(8,128)(2,1)} %param.15) | copy-start | bytes 497668
  3.2 17.3 %copy-start.23 = (bf16[1,576,144]{1,2,0:T(8,128)(2,1)S(1)}, bf16[1,576,144]{1,2,0:T(8,128)(2,1)}, u32[]{:S(2)}) copy-start(bf16[1,576,144]{1,2,0:T(8,128)(2,1)} %param.16) | copy-start | bytes 497668
  3.2 17.3 %copy-start.24 = (bf16[256,256]{1,0:T(8,128)(2,1)S(1)}, bf16[256,256]{1,0:T(8,128)(2,1)}, u32[]{:S(2)}) copy-start(bf16[256,256]{1,0:T(8,128)(2,1)} %refs_3_.1) | copy-start | bytes 393220
  3.2 21.3 %copy-start.9 = (bf16[1,256,576]{1,2,0:T(8,128)(2,1)S(1)}, bf16[1,256,576]{1,2,0:T(8,128)(2,1)}, u32[]{:S(2)}) copy-start(bf16[1,256,576]{1,2,0:T(8,128)(2,1)} %param.20) | copy-start | bytes 884740
  3.2 21.3 %copy-start.10 = (bf16[1,256,576]{1,2,0:T(8,128)(2,1)S(1)}, bf16[1,256,576]{1,2,0:T(8,128)(2,1)}, u32[]{:S(2)}) copy-start(bf16[1,256,576]{1,2,0:T(8,128)(2,1)} %param.21) | copy-start | bytes 884740
  3.3 49.5 %all-to-all-start = ((bf16[64,80,128]{2,1,0:T(8,128)(2,1)}), bf16[64,80,128]{2,1,0:T(8,128)(2,1)S(1)}, u32[]{:S(2)}, u32[]{:S(2)}) async-start(bf16[64,80,128]{2,1,0:T(8,128)(2,1)} %spread_kernel.1), calls=%async_computation | async-start | bytes 2621440 | tf_op jit(solution)/shard_map/all_to_all | solution.py:75
  20.6 32.1 %copy-start.28 = (s32[1,2,2]{2,1,0:T(2,128)S(1)}, s32[1,2,2]{2,1,0:T(2,128)}, u32[]{:S(2)}) copy-start(s32[1,2,2]{2,1,0:T(2,128)} %param.14) | copy-start | bytes 52
  20.6 32.1 %copy-start.29 = (f32[1,256]{1,0:T(1,128)S(1)}, f32[1,256]{1,0:T(1,128)}, u32[]{:S(2)}) copy-start(f32[1,256]{1,0:T(1,128)} %refs_7_.1) | copy-start | bytes 3076
  21.4 17.4 %collective-permute-start.1 = (bf16[2592,128]{1,0:T(8,128)(2,1)S(1)}, bf16[2592,128]{1,0:T(8,128)(2,1)}, u32[]{:S(2)}, u32[]{:S(2)}) collective-permute-start(bf16[2592,128]{1,0:T(8,128)(2,1)S(1)} %get-tuple-element.25.refs_3_), channel_id=1, source_target_pairs={{0,2},{1,3},{2,0},{3,1},{4,6},{5,7},{6,4},{7,5},{8,10},{9,11},{10,... | collective-permute-start | bytes 1990664 | tf_op jit(solution)/shard_map/ppermute | solution.py:62
  24.5 0.9 copy-start.21
  25.5 30.6 %collective-permute-start.8 = (bf16[3024,128]{1,0:T(8,128)(2,1)S(1)}, bf16[3024,128]{1,0:T(8,128)(2,1)S(1)}, u32[]{:S(2)}, u32[]{:S(2)}) collective-permute-start(bf16[3024,128]{1,0:T(8,128)(2,1)S(1)} %pack_kernel.1.refs_5_.refs_2_), channel_id=1, source_target_pairs={{0,2},{1,3},{2,0},{3,1},{4,6},{5,7},{6,4},{7,5},{8,10},{9,11},{10,... | collective-permute-start | bytes 2322440 | tf_op jit(solution)/shard_map/ppermute | solution.py:62
  27.7 18.4 %collective-permute-start = (bf16[2592,128]{1,0:T(8,128)(2,1)S(1)}, bf16[2592,128]{1,0:T(8,128)(2,1)}, u32[]{:S(2)}, u32[]{:S(2)}) collective-permute-start(bf16[2592,128]{1,0:T(8,128)(2,1)S(1)} %get-tuple-element.25.refs_3_), channel_id=1, source_target_pairs={{0,1},{1,0},{2,3},{3,2},{4,5},{5,4},{6,7},{7,6},{8,9},{9,8},{10,11... | collective-permute-start | bytes 1990664 | tf_op jit(solution)/shard_map/ppermute | solution.py:62
  38.8 7.3 %collective-permute-start.2 = (bf16[2592,128]{1,0:T(8,128)(2,1)}, bf16[2592,128]{1,0:T(8,128)(2,1)}, u32[]{:S(2)}, u32[]{:S(2)}) collective-permute-start(bf16[2592,128]{1,0:T(8,128)(2,1)} %collective-permute-done.1.refs_5_), channel_id=1, source_target_pairs={{0,1},{1,0},{2,3},{3,2},{4,5},{5,4},{6,7},{7,6},{8,9},{9,8},{10,11... | collective-permute-start | bytes 1990664 | tf_op jit(solution)/shard_map/ppermute | solution.py:62
  44.1 22.9 %collective-permute-start.7 = (bf16[3024,128]{1,0:T(8,128)(2,1)S(1)}, bf16[3024,128]{1,0:T(8,128)(2,1)}, u32[]{:S(2)}, u32[]{:S(2)}) collective-permute-start(bf16[3024,128]{1,0:T(8,128)(2,1)S(1)} %pack_kernel.1.refs_5_.refs_2_), channel_id=1, source_target_pairs={{0,1},{1,0},{2,3},{3,2},{4,5},{5,4},{6,7},{7,6},{8,9},{9,8},{10,11... | collective-permute-start | bytes 2322440 | tf_op jit(solution)/shard_map/ppermute | solution.py:62
  56.1 17.1 %copy-start = (f32[256,256]{1,0:T(8,128)}, f32[256,256]{1,0:T(8,128)S(1)}, u32[]{:S(2)}) copy-start(f32[256,256]{1,0:T(8,128)S(1)} %get-tuple-element.33.refs_0_.refs_2_) | copy-start | bytes 786436
  56.1 17.1 %copy-start.11 = (bf16[576,256]{1,0:T(8,128)(2,1)}, bf16[576,256]{1,0:T(8,128)(2,1)S(1)}, u32[]{:S(2)}) copy-start(bf16[576,256]{1,0:T(8,128)(2,1)S(1)} %get-tuple-element.26.refs_0_) | copy-start | bytes 884740
  56.1 17.1 %copy-start.31 = (bf16[576,256]{1,0:T(8,128)(2,1)}, bf16[576,256]{1,0:T(8,128)(2,1)S(1)}, u32[]{:S(2)}) copy-start(bf16[576,256]{1,0:T(8,128)(2,1)S(1)} %get-tuple-element.29) | copy-start | bytes 884740
  56.1 17.1 %copy-start.32 = (bf16[576,256]{1,0:T(8,128)(2,1)}, bf16[576,256]{1,0:T(8,128)(2,1)S(1)}, u32[]{:S(2)}) copy-start(bf16[576,256]{1,0:T(8,128)(2,1)S(1)} %get-tuple-element.28) | copy-start | bytes 884740
  56.1 17.0 %copy-start.33 = (bf16[576,256]{1,0:T(8,128)(2,1)}, bf16[576,256]{1,0:T(8,128)(2,1)S(1)}, u32[]{:S(2)}) copy-start(bf16[576,256]{1,0:T(8,128)(2,1)S(1)} %get-tuple-element.27) | copy-start | bytes 884740
  56.1 13.7 %copy-start.26 = (bf16[256,256]{1,0:T(8,128)(2,1)S(1)}, bf16[256,256]{1,0:T(8,128)(2,1)}, u32[]{:S(2)}) copy-start(bf16[256,256]{1,0:T(8,128)(2,1)} %copy-done.25) | copy-start | bytes 393220
  56.2 13.6 %collective-permute-start.9 = (bf16[3024,128]{1,0:T(8,128)(2,1)S(1)}, bf16[3024,128]{1,0:T(8,128)(2,1)S(1)}, u32[]{:S(2)}, u32[]{:S(2)}) collective-permute-start(bf16[3024,128]{1,0:T(8,128)(2,1)S(1)} %pin_kernel.3.refs_7_.refs_4_), channel_id=1, source_target_pairs={{0,1},{1,0},{2,3},{3,2},{4,5},{5,4},{6,7},{7,6},{8,9},{9,8},{10,11... | collective-permute-start | bytes 2322440 | tf_op jit(solution)/shard_map/ppermute | solution.py:62
  62.2 7.6 %collective-permute-start.6 = (bf16[256,256]{1,0:T(8,128)(2,1)S(1)}, bf16[256,256]{1,0:T(8,128)(2,1)S(1)}, u32[]{:S(2)}, u32[]{:S(2)}) collective-permute-start(bf16[256,256]{1,0:T(8,128)(2,1)S(1)} %get-tuple-element.30.refs_1_), channel_id=1, source_target_pairs={{0,256},{1,257},{2,258},{3,259},{4,260},{5,261},{6,262},{7,263},{8... | collective-permute-start | bytes 393224 | tf_op jit(solution)/shard_map/ppermute | solution.py:310
  73.9 38.3 %all-to-all-start.1 = ((bf16[64,72,128]{2,1,0:T(8,128)(2,1)}), bf16[64,72,128]{2,1,0:T(8,128)(2,1)S(1)}, u32[]{:S(2)}, u32[]{:S(2)}) async-start(bf16[64,72,128]{2,1,0:T(8,128)(2,1)} %get-tuple-element.34), calls=%async_computation.1 | async-start | bytes 2359296 | tf_op jit(solution)/shard_map/all_to_all | solution.py:75
  82.9 8.5 %collective-permute-start.3 = (bf16[576,256]{1,0:T(8,128)(2,1)}, bf16[576,256]{1,0:T(8,128)(2,1)S(1)}, u32[]{:S(2)}, u32[]{:S(2)}) collective-permute-start(bf16[576,256]{1,0:T(8,128)(2,1)} %copy-done.33), channel_id=1, source_target_pairs={{0,1},{1,0},{2,3},{3,2},{4,5},{5,4},{6,7},{7,6},{8,9},{9,8},{10,11... | collective-permute-start | bytes 884744 | tf_op jit(solution)/shard_map/ppermute | solution.py:62
  85.8 10.7 %collective-permute-start.4 = (bf16[576,256]{1,0:T(8,128)(2,1)}, bf16[576,256]{1,0:T(8,128)(2,1)S(1)}, u32[]{:S(2)}, u32[]{:S(2)}) collective-permute-start(bf16[576,256]{1,0:T(8,128)(2,1)} %copy-done.32), channel_id=1, source_target_pairs={{0,2},{1,3},{2,0},{3,1},{4,6},{5,7},{6,4},{7,5},{8,10},{9,11},{10,... | collective-permute-start | bytes 884744 | tf_op jit(solution)/shard_map/ppermute | solution.py:62
  88.1 15.2 %collective-permute-start.5 = (bf16[576,256]{1,0:T(8,128)(2,1)}, bf16[576,256]{1,0:T(8,128)(2,1)S(1)}, u32[]{:S(2)}, u32[]{:S(2)}) collective-permute-start(bf16[576,256]{1,0:T(8,128)(2,1)} %copy-done.31), channel_id=1, source_target_pairs={{0,3},{1,2},{2,1},{3,0},{4,7},{5,6},{6,5},{7,4},{8,11},{9,10},{10,... | collective-permute-start | bytes 884744 | tf_op jit(solution)/shard_map/ppermute | solution.py:62
  113.5 38.5 %all-to-all-start.2 = ((bf16[64,72,128]{2,1,0:T(8,128)(2,1)}), bf16[64,72,128]{2,1,0:T(8,128)(2,1)S(1)}, u32[]{:S(2)}, u32[]{:S(2)}) async-start(bf16[64,72,128]{2,1,0:T(8,128)(2,1)} %total_kernel.1), calls=%async_computation.2 | async-start | bytes 2359296 | tf_op jit(solution)/shard_map/all_to_all | solution.py:75
  122.8 8.7 %collective-permute-start.11 = (bf16[512,256]{1,0:T(8,128)(2,1)}, bf16[512,256]{1,0:T(8,128)(2,1)S(1)}, u32[]{:S(2)}, u32[]{:S(2)}) collective-permute-start(bf16[512,256]{1,0:T(8,128)(2,1)} %copy-done.19), channel_id=1, source_target_pairs={{0,2},{1,3},{2,0},{3,1},{4,6},{5,7},{6,4},{7,5},{8,10},{9,11},{10,... | collective-permute-start | bytes 786440 | tf_op jit(solution)/shard_map/ppermute | solution.py:62
  125.0 10.5 %collective-permute-start.10 = (bf16[512,256]{1,0:T(8,128)(2,1)}, bf16[512,256]{1,0:T(8,128)(2,1)S(1)}, u32[]{:S(2)}, u32[]{:S(2)}) collective-permute-start(bf16[512,256]{1,0:T(8,128)(2,1)} %copy-done.19), channel_id=1, source_target_pairs={{0,1},{1,0},{2,3},{3,2},{4,5},{5,4},{6,7},{7,6},{8,9},{9,8},{10,11... | collective-permute-start | bytes 786440 | tf_op jit(solution)/shard_map/ppermute | solution.py:62
  131.5 5.1 %collective-permute-start.12 = (bf16[512,256]{1,0:T(8,128)(2,1)S(1)}, bf16[512,256]{1,0:T(8,128)(2,1)S(1)}, u32[]{:S(2)}, u32[]{:S(2)}) collective-permute-start(bf16[512,256]{1,0:T(8,128)(2,1)S(1)} %collective-permute-done.11.refs_6_), channel_id=1, source_target_pairs={{0,1},{1,0},{2,3},{3,2},{4,5},{5,4},{6,7},{7,6},{8,9},{9,8},{10,11... | collective-permute-start | bytes 786440 | tf_op jit(solution)/shard_map/ppermute | solution.py:62
  152.0 14.2 %copy-start.1 = (f32[256,256]{1,0:T(8,128)S(1)}, f32[256,256]{1,0:T(8,128)}, u32[]{:S(2)}) copy-start(f32[256,256]{1,0:T(8,128)} %copy-done) | copy-start | bytes 786436
  154.2 12.0 %collective-permute-start.14 = (bf16[576,256]{1,0:T(8,128)(2,1)S(1)}, bf16[576,256]{1,0:T(8,128)(2,1)S(1)}, u32[]{:S(2)}, u32[]{:S(2)}) collective-permute-start(bf16[576,256]{1,0:T(8,128)(2,1)S(1)} %get-tuple-element.38), channel_id=1, source_target_pairs={{0,2},{1,3},{2,0},{3,1},{4,6},{5,7},{6,4},{7,5},{8,10},{9,11},{10,... | collective-permute-start | bytes 884744 | tf_op jit(solution)/shard_map/ppermute | solution.py:62
  156.4 9.8 %collective-permute-start.13 = (bf16[256,256]{1,0:T(8,128)(2,1)S(1)}, bf16[256,256]{1,0:T(8,128)(2,1)S(1)}, u32[]{:S(2)}, u32[]{:S(2)}) collective-permute-start(bf16[256,256]{1,0:T(8,128)(2,1)S(1)} %get-tuple-element.37), channel_id=1, source_target_pairs={{256,0},{257,1},{258,2},{259,3},{260,4},{261,5},{262,6},{263,7},{2... | collective-permute-start | bytes 393224 | tf_op jit(solution)/shard_map/ppermute | solution.py:330
  166.2 20.4 %copy-start.3 = (bf16[576,256]{1,0:T(8,128)(2,1)S(1)}, bf16[576,256]{1,0:T(8,128)(2,1)}, u32[]{:S(2)}) copy-start(bf16[576,256]{1,0:T(8,128)(2,1)} %copy-done.2) | copy-start | bytes 884740
  166.2 20.4 %copy-start.5 = (bf16[576,256]{1,0:T(8,128)(2,1)S(1)}, bf16[576,256]{1,0:T(8,128)(2,1)}, u32[]{:S(2)}) copy-start(bf16[576,256]{1,0:T(8,128)(2,1)} %copy-done.4) | copy-start | bytes 884740
  166.2 20.4 %copy-start.7 = (bf16[576,256]{1,0:T(8,128)(2,1)S(1)}, bf16[576,256]{1,0:T(8,128)(2,1)}, u32[]{:S(2)}) copy-start(bf16[576,256]{1,0:T(8,128)(2,1)} %copy-done.6) | copy-start | bytes 884740
  166.2 20.4 %copy-start.12 = (bf16[576,256]{1,0:T(8,128)(2,1)S(1)}, bf16[576,256]{1,0:T(8,128)(2,1)}, u32[]{:S(2)}) copy-start(bf16[576,256]{1,0:T(8,128)(2,1)} %copy-done.11) | copy-start | bytes 884740
  166.3 9.2 %collective-permute-start.15 = (bf16[256,256]{1,0:T(8,128)(2,1)S(1)}, bf16[256,256]{1,0:T(8,128)(2,1)S(1)}, u32[]{:S(2)}, u32[]{:S(2)}) collective-permute-start(bf16[256,256]{1,0:T(8,128)(2,1)S(1)} %pregrad_kernel.1.refs_4_), channel_id=1, source_target_pairs={{0,1},{1,0},{2,3},{3,2},{4,5},{5,4},{6,7},{7,6},{8,9},{9,8},{10,11... | collective-permute-start | bytes 393224 | tf_op jit(solution)/shard_map/ppermute | solution.py:62
  173.6 7.0 %collective-permute-start.16 = (bf16[256,256]{1,0:T(8,128)(2,1)S(1)}, bf16[256,256]{1,0:T(8,128)(2,1)S(1)}, u32[]{:S(2)}, u32[]{:S(2)}) collective-permute-start(bf16[256,256]{1,0:T(8,128)(2,1)S(1)} %pregrad_kernel.1.refs_4_), channel_id=1, source_target_pairs={{0,2},{1,3},{2,0},{3,1},{4,6},{5,7},{6,4},{7,5},{8,10},{9,11},{10,... | collective-permute-start | bytes 393224 | tf_op jit(solution)/shard_map/ppermute | solution.py:62
  175.5 12.5 %collective-permute-start.18 = (bf16[576,256]{1,0:T(8,128)(2,1)S(1)}, bf16[576,256]{1,0:T(8,128)(2,1)S(1)}, u32[]{:S(2)}, u32[]{:S(2)}) collective-permute-start(bf16[576,256]{1,0:T(8,128)(2,1)S(1)} %pin_kernel.4), channel_id=1, source_target_pairs={{0,1},{1,0},{2,3},{3,2},{4,5},{5,4},{6,7},{7,6},{8,9},{9,8},{10,11... | collective-permute-start | bytes 884744 | tf_op jit(solution)/shard_map/ppermute | solution.py:62
  180.6 11.5 %copy-start.14 = (bf16[512,256]{1,0:T(8,128)(2,1)S(1)}, bf16[512,256]{1,0:T(8,128)(2,1)}, u32[]{:S(2)}) copy-start(bf16[512,256]{1,0:T(8,128)(2,1)} %copy-done.13) | copy-start | bytes 786436
  180.6 11.5 %copy-start.16 = (bf16[512,256]{1,0:T(8,128)(2,1)S(1)}, bf16[512,256]{1,0:T(8,128)(2,1)}, u32[]{:S(2)}) copy-start(bf16[512,256]{1,0:T(8,128)(2,1)} %copy-done.15) | copy-start | bytes 786436
  180.6 11.5 %copy-start.18 = (bf16[512,256]{1,0:T(8,128)(2,1)S(1)}, bf16[512,256]{1,0:T(8,128)(2,1)}, u32[]{:S(2)}) copy-start(bf16[512,256]{1,0:T(8,128)(2,1)} %copy-done.17) | copy-start | bytes 786436
  180.6 11.5 %copy-start.20 = (bf16[512,256]{1,0:T(8,128)(2,1)S(1)}, bf16[512,256]{1,0:T(8,128)(2,1)}, u32[]{:S(2)}) copy-start(bf16[512,256]{1,0:T(8,128)(2,1)} %copy-done.19) | copy-start | bytes 786436
  180.6 11.5 %collective-permute-start.19 = (bf16[576,256]{1,0:T(8,128)(2,1)S(1)}, bf16[576,256]{1,0:T(8,128)(2,1)S(1)}, u32[]{:S(2)}, u32[]{:S(2)}) collective-permute-start(bf16[576,256]{1,0:T(8,128)(2,1)S(1)} %pin_kernel.5), channel_id=1, source_target_pairs={{0,3},{1,2},{2,1},{3,0},{4,7},{5,6},{6,5},{7,4},{8,11},{9,10},{10,... | collective-permute-start | bytes 884744 | tf_op jit(solution)/shard_map/ppermute | solution.py:62
  183.4 3.2 %collective-permute-start.17 = (bf16[256,256]{1,0:T(8,128)(2,1)S(1)}, bf16[256,256]{1,0:T(8,128)(2,1)S(1)}, u32[]{:S(2)}, u32[]{:S(2)}) collective-permute-start(bf16[256,256]{1,0:T(8,128)(2,1)S(1)} %collective-permute-done.16.refs_6_.refs_0_), channel_id=1, source_target_pairs={{0,1},{1,0},{2,3},{3,2},{4,5},{5,4},{6,7},{7,6},{8,9},{9,8},{10,11... | collective-permute-start | bytes 393224 | tf_op jit(solution)/shard_map/ppermute | solution.py:62
  (9 other events, 6.3 us)

commit v7 on v5

--- a/solution.py
+++ b/solution.py
@@ -175,13 +175,12 @@
 
 
 def decode_kernel(
-    t_ref, codes_ref, before_ref, shifted_ref, hidden_ref, w0, w1, w2, w3,
-    o0, o1, o2, o3, both_ref, s_ref,
+    t_ref, codes_ref, before_ref, shifted_ref, hidden_ref, w0, w1, w2, w3, o_ref, both_ref
 ):
-    t, layer, near = t_ref[0], t_ref[1], t_ref[2]
+    t, layer = t_ref[0], t_ref[1]
     n = codes_ref.shape[0]
     units = hidden_ref.shape[0]
-    _, block, lanes = o0.shape
+    block = o_ref.shape[0] * ROWS // 8
     both_ref[:n] = codes_ref[...]
 
     @pl.when(layer == 0)
@@ -193,21 +192,20 @@
         both_ref[n:] = shifted_ref[...]
 
     both, hidden = both_ref[...], hidden_ref[...]
+    peers, rows, lanes = o_ref.shape
+    each = block // rows
     for k, w in enumerate((w0, w1, w2, w3)):
         decoder = jnp.concatenate(
             [get_wide(w, 0, block, n), get_wide(w, block * n // 128, block, n)], axis=1
         )
         down = get_wide(w, 2 * block * n // 128, units, block)
         value = dot(decoder, both) - dot(down, hidden, 0, 0)
-        spot = jnp.bitwise_xor(jnp.bitwise_xor(t, near), k)
-        for h in range(2):
-            s_ref[spot, h] = value[:, h * lanes : (h + 1) * lanes].astype(BF)
-    for m, o_ref in enumerate((o0, o1, o2, o3)):
-        o_ref[...] = s_ref[m]
-
-
-def near_total_kernel(x0, x1, x2, x3, o_ref):
-    o_ref[...] = sum(x[...].astype(F32) for x in (x0, x1, x2, x3)).astype(BF)
+        spot = jnp.bitwise_xor(t, k) * (2 * each)
+        for i in range(each):
+            for h in range(2):
+                o_ref[spot + (h * each + i)] = value[
+                    i * rows : (i + 1) * rows, h * lanes : (h + 1) * lanes
+                ].astype(BF)
 
 
 def total_kernel(x_ref, o_ref):
@@ -312,31 +310,28 @@
     shifted = lax.ppermute(codes, "layer", [(0, 1)])
     (far,) = call(pin_kernel, (), [], after=(slope,), through=(far,))
     second = [second, beside, far, toward(far, 1)]
-    slab = (2, block, height // 2)
-    *parts, both = call(
+    parts, both = call(
         decode_kernel,
         (place, codes, before, shifted, hidden, *second),
-        [(slab, BF)] * 4 + [((2 * width, height), BF)],
-        scratch=[pltpu.VMEM((4, *slab), BF)],
-    )
-    (part,) = call(near_total_kernel, exchange4(parts, NEAR), [(slab, BF)], leaving=(0,))
-    arrived = exchange(part.reshape(peers // 4, ROWS, height // 2), WIDE)
+        [((peers, ROWS, height // 2), BF), ((2 * width, height), BF)],
+        leaving=(0,),
+    )
+    arrived = exchange(parts, NEAR + WIDE)
     normed = exchange4(normed)
+    both = gather4(both)
     (copies,) = call(
         total_kernel,
         (arrived,),
-        [(arrived.shape, BF)],
-        after=(corner(normed[1:]),),
+        [((peers // 4, ROWS, height // 2), BF)],
+        after=(corner(normed[1:] + both[1:]),),
         leaving=(0,),
     )
-    errors = exchange(copies, WIDE).reshape(slab)
-    both = gather4(both)
-    errors = exchange4([errors] * 4, NEAR)
+    slab = (2, block, height // 2)
+    errors = exchange4([exchange(copies, WIDE).reshape(slab)] * 4, NEAR)
     own_back, prev_back, *err = call(
         back_kernel,
         (place, *errors, *second),
         [((width, height), F32), ((width, height), BF)] + [((block, height), BF)] * 4,
-        after=(corner(both[1:]),),
         scratch=[pltpu.VMEM((4, *slab), BF)],
     )
     later = lax.ppermute(prev_back, "layer", [(1, 0)])

time: 204 us -> 191 us (0.936)
  starting transfers between devices: 119 us -> 97.3 us
  blocking collectives: 0 us -> 21 us
  waiting for transfers between devices: 61.9 us -> 47.5 us
  local copies, waits for them, and re-layouts: 4.89 us -> 7.99 us
    all_to_all x0 -> x1, blocking collectives: none -> 21 us  [exchange(): return lax.all_to_all(blocks, axes, split_axis=0, concat_axis=0, tiled=True)]
    ppermute x24 -> x21, waiting for transfers between devices: 45.8 us -> 26.3 us  [toward(): return lax.ppermute(x, axes, [(i, i ^ k) for i in range(4)])]
    ppermute x24 -> x21, starting transfers between devices: 76.3 us -> 65 us  [toward(): return lax.ppermute(x, axes, [(i, i ^ k) for i in range(4)])]
    all_to_all x3 -> x2, starting transfers between devices: 36.3 us -> 26.2 us  [exchange(): return lax.all_to_all(blocks, axes, split_axis=0, concat_axis=0, tiled=True)]
    unnamed x52 -> x68, local copies, waits for them, and re-layouts: 4.89 us -> 7.99 us
    all_to_all x3 -> x2, waiting for transfers between devices: 7.16 us -> 10.2 us  [exchange(): return lax.all_to_all(blocks, axes, split_axis=0, concat_axis=0, tiled=True)]
    pallas_call x13 -> x12, Pallas kernels: 15.4 us -> 14.5 us  [call(): pl.pallas_call(body, out_shape=[(pltpu.HBM if i in leaving else pltpu.VME...]
  transfers between devices with their start and end apart: 29 -> 25, of which waited for: 16 -> 12; matrix products, arithmetic and copies ran while one was open for 0% -> 0% of each run, Pallas kernels for 2% -> 3%
where the time goes in v7:
time: 191 us; the launch traced here: 190 us
  starting transfers between devices  97.3 us (51%)
  waiting for transfers between devices  47.5 us (25%)
  blocking collectives  21 us (11%)
  Pallas kernels  14.5 us (8%)
  local copies, waits for them, and re-layouts  7.99 us (4%)
    ppermute x21, starting transfers between devices, toward(): return lax.ppermute(x, axes, [(i, i ^ k) for i in range(4)])  65 us
    ppermute x21, waiting for transfers between devices, toward(): return lax.ppermute(x, axes, [(i, i ^ k) for i in range(4)])  26.3 us
    all_to_all x2, starting transfers between devices, exchange(): return lax.all_to_all(blocks, axes, split_axis=0, concat_axis=0, tiled=True)  26.2 us
    all_to_all x1, blocking collectives, exchange(): return lax.all_to_all(blocks, axes, split_axis=0, concat_axis=0, tiled=True)  21 us
    pallas_call x12, Pallas kernels, call(): pl.pallas_call(body, out_shape=[(pltpu.HBM if i in leaving else pltpu.VME...  14.5 us
    all_to_all x2, waiting for transfers between devices, exchange(): return lax.all_to_all(blocks, axes, split_axis=0, concat_axis=0, tiled=True)  10.2 us
    ppermute x1, waiting for transfers between devices, local(): later = lax.ppermute(prev_back, 'layer', [(1, 0)])  8 us
    unnamed x68, local copies, waits for them, and re-layouts  7.99 us
  transfers between devices with their start and end apart: 25, of which 12 were waited for; matrix products, arithmetic and copies ran while one was open for 0% of the time, Pallas kernels for 3%

profile of v7, /device:TPU:1, one launch (start us, length us, event | category | flops | bytes accessed | tf_op | source)
XLA Modules:
  0.0 189.6 jit_solution(12380462949789805122)
XLA Ops:
  0.6 0.7 copy-done.27
  2.0 1.2 spread_kernel.1
  3.3 17.3 %all-to-all-start = ((bf16[64,80,128]{2,1,0:T(8,128)(2,1)}), bf16[64,80,128]{2,1,0:T(8,128)(2,1)S(1)}, u32[]{:S(2)}, u32[]{:S(2)}) async-start(bf16[64,80,128]{2,1,0:T(8,128)(2,1)} %spread_kernel.1), calls=%async_computation | async-start | bytes 2621440 | tf_op jit(solution)/shard_map/all_to_all | solution.py:78
  21.4 3.1 %collective-permute-start.1 = (bf16[2592,128]{1,0:T(8,128)(2,1)S(1)}, bf16[2592,128]{1,0:T(8,128)(2,1)}, u32[]{:S(2)}, u32[]{:S(2)}) collective-permute-start(bf16[2592,128]{1,0:T(8,128)(2,1)S(1)} %get-tuple-element.27.refs_3_), channel_id=1, source_target_pairs={{0,2},{1,3},{2,0},{3,1},{4,6},{5,7},{6,4},{7,5},{8,10},{9,11},{10,... | collective-permute-start | bytes 1990664 | tf_op jit(solution)/shard_map/ppermute | solution.py:65
  24.5 0.9 copy-done.21
  25.6 2.2 %collective-permute-start.8 = (bf16[3024,128]{1,0:T(8,128)(2,1)S(1)}, bf16[3024,128]{1,0:T(8,128)(2,1)S(1)}, u32[]{:S(2)}, u32[]{:S(2)}) collective-permute-start(bf16[3024,128]{1,0:T(8,128)(2,1)S(1)} %pack_kernel.1.refs_5_), channel_id=1, source_target_pairs={{0,2},{1,3},{2,0},{3,1},{4,6},{5,7},{6,4},{7,5},{8,10},{9,11},{10,... | collective-permute-start | bytes 2322440 | tf_op jit(solution)/shard_map/ppermute | solution.py:65
  27.7 3.4 %collective-permute-start = (bf16[2592,128]{1,0:T(8,128)(2,1)S(1)}, bf16[2592,128]{1,0:T(8,128)(2,1)}, u32[]{:S(2)}, u32[]{:S(2)}) collective-permute-start(bf16[2592,128]{1,0:T(8,128)(2,1)S(1)} %get-tuple-element.27.refs_3_), channel_id=1, source_target_pairs={{0,1},{1,0},{2,3},{3,2},{4,5},{5,4},{6,7},{7,6},{8,9},{9,8},{10,11... | collective-permute-start | bytes 1990664 | tf_op jit(solution)/shard_map/ppermute | solution.py:65
  31.2 7.7 %collective-permute-done.1.refs_5_ = bf16[2592,128]{1,0:T(8,128)(2,1)} collective-permute-done((bf16[2592,128]{1,0:T(8,128)(2,1)S(1)}, bf16[2592,128]{1,0:T(8,128)(2,1)}, u32[]{:S(2)}, u32[]{:S(2)}) %collective-permute-start.1) | collective-permute-done | bytes 663584 | tf_op jit(solution)/shard_map/ppermute | solution.py:65
  38.8 5.2 %collective-permute-start.2 = (bf16[2592,128]{1,0:T(8,128)(2,1)}, bf16[2592,128]{1,0:T(8,128)(2,1)}, u32[]{:S(2)}, u32[]{:S(2)}) collective-permute-start(bf16[2592,128]{1,0:T(8,128)(2,1)} %collective-permute-done.1.refs_5_), channel_id=1, source_target_pairs={{0,1},{1,0},{2,3},{3,2},{4,5},{5,4},{6,7},{7,6},{8,9},{9,8},{10,11... | collective-permute-start | bytes 1990664 | tf_op jit(solution)/shard_map/ppermute | solution.py:65
  44.1 1.9 %collective-permute-start.7 = (bf16[3024,128]{1,0:T(8,128)(2,1)S(1)}, bf16[3024,128]{1,0:T(8,128)(2,1)}, u32[]{:S(2)}, u32[]{:S(2)}) collective-permute-start(bf16[3024,128]{1,0:T(8,128)(2,1)S(1)} %pack_kernel.1.refs_5_), channel_id=1, source_target_pairs={{0,1},{1,0},{2,3},{3,2},{4,5},{5,4},{6,7},{7,6},{8,9},{9,8},{10,11... | collective-permute-start | bytes 2322440 | tf_op jit(solution)/shard_map/ppermute | solution.py:65
  46.1 6.6 %all-to-all-done.refs_2_ = bf16[64,80,128]{2,1,0:T(8,128)(2,1)S(1)} async-done(((bf16[64,80,128]{2,1,0:T(8,128)(2,1)}), bf16[64,80,128]{2,1,0:T(8,128)(2,1)S(1)}, u32[]{:S(2)}, u32[]{:S(2)}) %all-to-all-start) | async-done | bytes 1310752 | tf_op jit(solution)/shard_map/all_to_all | solution.py:78
  52.7 3.4 %encode_kernel.1 = (bf16[576,256]{1,0:T(8,128)(2,1)S(1)}, bf16[576,256]{1,0:T(8,128)(2,1)S(1)}, bf16[576,256]{1,0:T(8,128)(2,1)S(1)}, bf16[576,256]{1,0:T(8,128)...) custom-call(s32[3]{0:T(128)S(1)} %pad_add_fusion.refs_0_, ...), custom_call_target="tpu_custom_call" | custom-call | tf_op jit(solution)/shard_map/encode_kernel/pallas_call | solution.py:41
  56.2 6.1 %collective-permute-start.9 = (bf16[3024,128]{1,0:T(8,128)(2,1)S(1)}, bf16[3024,128]{1,0:T(8,128)(2,1)S(1)}, u32[]{:S(2)}, u32[]{:S(2)}) collective-permute-start(bf16[3024,128]{1,0:T(8,128)(2,1)S(1)} %pin_kernel.2.refs_7_), channel_id=1, source_target_pairs={{0,1},{1,0},{2,3},{3,2},{4,5},{5,4},{6,7},{7,6},{8,9},{9,8},{10,11... | collective-permute-start | bytes 2322440 | tf_op jit(solution)/shard_map/ppermute | solution.py:65
  62.3 4.7 %collective-permute-start.6 = (bf16[256,256]{1,0:T(8,128)(2,1)S(1)}, bf16[256,256]{1,0:T(8,128)(2,1)S(1)}, u32[]{:S(2)}, u32[]{:S(2)}) collective-permute-start(bf16[256,256]{1,0:T(8,128)(2,1)S(1)} %get-tuple-element.32.refs_1_), channel_id=1, source_target_pairs={{0,256},{1,257},{2,258},{3,259},{4,260},{5,261},{6,262},{7,263},{8... | collective-permute-start | bytes 393224 | tf_op jit(solution)/shard_map/ppermute | solution.py:310
  66.9 2.9 %collective-permute-done.6.refs_3_ = bf16[256,256]{1,0:T(8,128)(2,1)S(1)} collective-permute-done((bf16[256,256]{1,0:T(8,128)(2,1)S(1)}, bf16[256,256]{1,0:T(8,128)(2,1)S(1)}, u32[]{:S(2)}, u32[]{:S(2)}) %collective-permute-start.6) | collective-permute-done | bytes 131104 | tf_op jit(solution)/shard_map/ppermute | solution.py:310
  69.8 3.3 %decode_kernel.1 = (bf16[64,72,128]{2,1,0:T(8,128)(2,1)}, bf16[512,256]{1,0:T(8,128)(2,1)S(1)}) custom-call(s32[3]{0:T(128)S(1)} %pad_add_fusion.refs_0_, bf16[256,256]{1,0:T(8,128)(2,1)S(1)} %get-tuple-element.32.refs_1_, bf16[256,256]{1,0:T(8,128)(2,1)S(1)} %copy-done.26, bf16[256,256]{1,0:T(8,128)(2,1)S(1)} %collective-permute-done.6.refs_3_, ...), custom_call_target="tpu_custom_call" | custom-call | tf_op jit(solution)/shard_map/decode_kernel/pallas_call | solution.py:41
  73.9 9.0 %all-to-all-start.1 = ((bf16[64,72,128]{2,1,0:T(8,128)(2,1)}), bf16[64,72,128]{2,1,0:T(8,128)(2,1)S(1)}, u32[]{:S(2)}, u32[]{:S(2)}) async-start(bf16[64,72,128]{2,1,0:T(8,128)(2,1)} %get-tuple-element.36), calls=%async_computation.1 | async-start | bytes 2359296 | tf_op jit(solution)/shard_map/all_to_all | solution.py:78
  82.8 2.2 %collective-permute-start.11 = (bf16[512,256]{1,0:T(8,128)(2,1)}, bf16[512,256]{1,0:T(8,128)(2,1)S(1)}, u32[]{:S(2)}, u32[]{:S(2)}) collective-permute-start(bf16[512,256]{1,0:T(8,128)(2,1)} %copy-done.19), channel_id=1, source_target_pairs={{0,2},{1,3},{2,0},{3,1},{4,6},{5,7},{6,4},{7,5},{8,10},{9,11},{10,... | collective-permute-start | bytes 786440 | tf_op jit(solution)/shard_map/ppermute | solution.py:65
  85.1 3.3 %collective-permute-start.3 = (bf16[576,256]{1,0:T(8,128)(2,1)}, bf16[576,256]{1,0:T(8,128)(2,1)S(1)}, u32[]{:S(2)}, u32[]{:S(2)}) collective-permute-start(bf16[576,256]{1,0:T(8,128)(2,1)} %copy-done.33), channel_id=1, source_target_pairs={{0,1},{1,0},{2,3},{3,2},{4,5},{5,4},{6,7},{7,6},{8,9},{9,8},{10,11... | collective-permute-start | bytes 884744 | tf_op jit(solution)/shard_map/ppermute | solution.py:65
  88.3 3.1 %collective-permute-start.4 = (bf16[576,256]{1,0:T(8,128)(2,1)}, bf16[576,256]{1,0:T(8,128)(2,1)S(1)}, u32[]{:S(2)}, u32[]{:S(2)}) collective-permute-start(bf16[576,256]{1,0:T(8,128)(2,1)} %copy-done.32), channel_id=1, source_target_pairs={{0,2},{1,3},{2,0},{3,1},{4,6},{5,7},{6,4},{7,5},{8,10},{9,11},{10,... | collective-permute-start | bytes 884744 | tf_op jit(solution)/shard_map/ppermute | solution.py:65
  91.4 2.4 %collective-permute-start.5 = (bf16[576,256]{1,0:T(8,128)(2,1)}, bf16[576,256]{1,0:T(8,128)(2,1)S(1)}, u32[]{:S(2)}, u32[]{:S(2)}) collective-permute-start(bf16[576,256]{1,0:T(8,128)(2,1)} %copy-done.31), channel_id=1, source_target_pairs={{0,3},{1,2},{2,1},{3,0},{4,7},{5,6},{6,5},{7,4},{8,11},{9,10},{10,... | collective-permute-start | bytes 884744 | tf_op jit(solution)/shard_map/ppermute | solution.py:65
  93.8 2.1 %collective-permute-start.10 = (bf16[512,256]{1,0:T(8,128)(2,1)}, bf16[512,256]{1,0:T(8,128)(2,1)S(1)}, u32[]{:S(2)}, u32[]{:S(2)}) collective-permute-start(bf16[512,256]{1,0:T(8,128)(2,1)} %copy-done.19), channel_id=1, source_target_pairs={{0,1},{1,0},{2,3},{3,2},{4,5},{5,4},{6,7},{7,6},{8,9},{9,8},{10,11... | collective-permute-start | bytes 786440 | tf_op jit(solution)/shard_map/ppermute | solution.py:65
  96.0 2.2 %collective-permute-start.12 = (bf16[512,256]{1,0:T(8,128)(2,1)S(1)}, bf16[512,256]{1,0:T(8,128)(2,1)S(1)}, u32[]{:S(2)}, u32[]{:S(2)}) collective-permute-start(bf16[512,256]{1,0:T(8,128)(2,1)S(1)} %collective-permute-done.11.refs_6_), channel_id=1, source_target_pairs={{0,1},{1,0},{2,3},{3,2},{4,5},{5,4},{6,7},{7,6},{8,9},{9,8},{10,11... | collective-permute-start | bytes 786440 | tf_op jit(solution)/shard_map/ppermute | solution.py:65
  98.2 1.1 collective-permute-done.4.refs_2_
  99.3 6.6 %collective-permute-done.5.refs_3_ = bf16[576,256]{1,0:T(8,128)(2,1)S(1)} collective-permute-done((bf16[576,256]{1,0:T(8,128)(2,1)}, bf16[576,256]{1,0:T(8,128)(2,1)S(1)}, u32[]{:S(2)}, u32[]{:S(2)}) %collective-permute-start.5) | collective-permute-done | bytes 294944 | tf_op jit(solution)/shard_map/ppermute | solution.py:65
  106.6 0.7 copy-done.4
  107.4 0.7 copy-done.6
  110.2 3.6 %all-to-all-done.1.refs_0_ = bf16[64,72,128]{2,1,0:T(8,128)(2,1)S(1)} async-done(((bf16[64,72,128]{2,1,0:T(8,128)(2,1)}), bf16[64,72,128]{2,1,0:T(8,128)(2,1)S(1)}, u32[]{:S(2)}, u32[]{:S(2)}) %all-to-all-start.1) | async-done | bytes 1179680 | tf_op jit(solution)/shard_map/all_to_all | solution.py:78
  113.8 0.9 total_kernel.1
  114.7 21.0 %all_to_all.15 = bf16[16,72,128]{2,1,0:T(8,128)(2,1)S(1)} all-to-all(bf16[16,72,128]{2,1,0:T(8,128)(2,1)} %total_kernel.1), channel_id=1, replica_groups=mesh['layer'=2,'y_1'=4,'y_0'=2,'z_1'=4,'z_0'=2,'tok_0'=2,'tok_1'=2] {'y_..., dimensions={0} | all-to-all | bytes 589824 | tf_op jit(solution)/shard_map/all_to_all | solution.py:78
  135.8 2.0 %collective-permute-start.15 = (bf16[2,576,128]{2,1,0:T(8,128)(2,1)S(1)}, bf16[2,576,128]{2,1,0:T(8,128)(2,1)S(1)}, u32[]{:S(2)}, u32[]{:S(2)}) collective-permute-start(bf16[2,576,128]{2,1,0:T(8,128)(2,1)S(1)} %bitcast.29), channel_id=1, source_target_pairs={{0,36},{4,32},{32,4},{36,0},{1,37},{5,33},{33,5},{37,1},{2,38},{6,... | collective-permute-start | bytes 884744 | tf_op jit(solution)/shard_map/ppermute | solution.py:65
  137.8 2.5 %collective-permute-start.14 = (bf16[2,576,128]{2,1,0:T(8,128)(2,1)S(1)}, bf16[2,576,128]{2,1,0:T(8,128)(2,1)S(1)}, u32[]{:S(2)}, u32[]{:S(2)}) collective-permute-start(bf16[2,576,128]{2,1,0:T(8,128)(2,1)S(1)} %bitcast.30), channel_id=1, source_target_pairs={{0,32},{4,36},{32,0},{36,4},{1,33},{5,37},{33,1},{37,5},{2,34},{6,... | collective-permute-start | bytes 884744 | tf_op jit(solution)/shard_map/ppermute | solution.py:65
  140.4 3.9 %collective-permute-start.13 = (bf16[2,576,128]{2,1,0:T(8,128)(2,1)S(1)}, bf16[2,576,128]{2,1,0:T(8,128)(2,1)S(1)}, u32[]{:S(2)}, u32[]{:S(2)}) collective-permute-start(bf16[2,576,128]{2,1,0:T(8,128)(2,1)S(1)} %bitcast.31), channel_id=1, source_target_pairs={{0,4},{4,0},{32,36},{36,32},{1,5},{5,1},{33,37},{37,33},{2,6},{6,2... | collective-permute-start | bytes 884744 | tf_op jit(solution)/shard_map/ppermute | solution.py:65
  144.3 4.0 %collective-permute-done.14.refs_3_ = bf16[2,576,128]{2,1,0:T(8,128)(2,1)S(1)} collective-permute-done((bf16[2,576,128]{2,1,0:T(8,128)(2,1)S(1)}, bf16[2,576,128]{2,1,0:T(8,128)(2,1)S(1)}, u32[]{:S(2)}, u32[]{:S(2)}) %collective-permute-start.14) | collective-permute-done | bytes 294944 | tf_op jit(solution)/shard_map/ppermute | solution.py:65
  148.3 4.2 %collective-permute-done.13.refs_2_ = bf16[2,576,128]{2,1,0:T(8,128)(2,1)S(1)} collective-permute-done((bf16[2,576,128]{2,1,0:T(8,128)(2,1)S(1)}, bf16[2,576,128]{2,1,0:T(8,128)(2,1)S(1)}, u32[]{:S(2)}, u32[]{:S(2)}) %collective-permute-start.13) | collective-permute-done | bytes 294944 | tf_op jit(solution)/shard_map/ppermute | solution.py:65
  152.5 2.2 %back_kernel.1 = (f32[256,256]{1,0:T(8,128)S(1)}, bf16[256,256]{1,0:T(8,128)(2,1)S(1)}, bf16[576,256]{1,0:T(8,128)(2,1)S(1)}, bf16[576,256]{1,0:T(8,128)(2,1)S(1...) custom-call(s32[3]{0:T(128)S(1)} %pad_add_fusion.refs_0_, bf16[2,576,128]{2,1,0:T(8,128)(2,1)S(1)} %bitcast.32, ...), custom_call_target="tpu_custom_call" | custom-call | tf_op jit(solution)/shard_map/back_kernel/pallas_call | solution.py:41
  154.8 1.4 collective-permute-start.16
  156.2 8.0 %collective-permute-done.16.refs_1_ = bf16[256,256]{1,0:T(8,128)(2,1)S(1)} collective-permute-done((bf16[256,256]{1,0:T(8,128)(2,1)S(1)}, bf16[256,256]{1,0:T(8,128)(2,1)S(1)}, u32[]{:S(2)}, u32[]{:S(2)}) %collective-permute-start.16) | collective-permute-done | bytes 131104 | tf_op jit(solution)/shard_map/ppermute | solution.py:337
  164.3 2.5 %collective-permute-start.18 = (bf16[256,256]{1,0:T(8,128)(2,1)S(1)}, bf16[256,256]{1,0:T(8,128)(2,1)S(1)}, u32[]{:S(2)}, u32[]{:S(2)}) collective-permute-start(bf16[256,256]{1,0:T(8,128)(2,1)S(1)} %pregrad_kernel.1.refs_4_), channel_id=1, source_target_pairs={{0,2},{1,3},{2,0},{3,1},{4,6},{5,7},{6,4},{7,5},{8,10},{9,11},{10,... | collective-permute-start | bytes 393224 | tf_op jit(solution)/shard_map/ppermute | solution.py:65
  166.8 2.9 %collective-permute-start.21 = (bf16[576,256]{1,0:T(8,128)(2,1)S(1)}, bf16[576,256]{1,0:T(8,128)(2,1)S(1)}, u32[]{:S(2)}, u32[]{:S(2)}) collective-permute-start(bf16[576,256]{1,0:T(8,128)(2,1)S(1)} %get-tuple-element.46), channel_id=1, source_target_pairs={{0,2},{1,3},{2,0},{3,1},{4,6},{5,7},{6,4},{7,5},{8,10},{9,11},{10,... | collective-permute-start | bytes 884744 | tf_op jit(solution)/shard_map/ppermute | solution.py:65
  170.2 7.1 %collective-permute-start.20 = (bf16[576,256]{1,0:T(8,128)(2,1)S(1)}, bf16[576,256]{1,0:T(8,128)(2,1)S(1)}, u32[]{:S(2)}, u32[]{:S(2)}) collective-permute-start(bf16[576,256]{1,0:T(8,128)(2,1)S(1)} %get-tuple-element.45), channel_id=1, source_target_pairs={{0,1},{1,0},{2,3},{3,2},{4,5},{5,4},{6,7},{7,6},{8,9},{9,8},{10,11... | collective-permute-start | bytes 884744 | tf_op jit(solution)/shard_map/ppermute | solution.py:65
  177.3 2.5 %collective-permute-start.22 = (bf16[576,256]{1,0:T(8,128)(2,1)S(1)}, bf16[576,256]{1,0:T(8,128)(2,1)S(1)}, u32[]{:S(2)}, u32[]{:S(2)}) collective-permute-start(bf16[576,256]{1,0:T(8,128)(2,1)S(1)} %get-tuple-element.47), channel_id=1, source_target_pairs={{0,3},{1,2},{2,1},{3,0},{4,7},{5,6},{6,5},{7,4},{8,11},{9,10},{10,... | collective-permute-start | bytes 884744 | tf_op jit(solution)/shard_map/ppermute | solution.py:65
  179.8 2.4 %collective-permute-start.17 = (bf16[256,256]{1,0:T(8,128)(2,1)S(1)}, bf16[256,256]{1,0:T(8,128)(2,1)S(1)}, u32[]{:S(2)}, u32[]{:S(2)}) collective-permute-start(bf16[256,256]{1,0:T(8,128)(2,1)S(1)} %pregrad_kernel.1.refs_4_), channel_id=1, source_target_pairs={{0,1},{1,0},{2,3},{3,2},{4,5},{5,4},{6,7},{7,6},{8,9},{9,8},{10,11... | collective-permute-start | bytes 393224 | tf_op jit(solution)/shard_map/ppermute | solution.py:65
  182.2 1.9 %collective-permute-start.19 = (bf16[256,256]{1,0:T(8,128)(2,1)S(1)}, bf16[256,256]{1,0:T(8,128)(2,1)S(1)}, u32[]{:S(2)}, u32[]{:S(2)}) collective-permute-start(bf16[256,256]{1,0:T(8,128)(2,1)S(1)} %collective-permute-done.18.refs_6_.refs_0_), channel_id=1, source_target_pairs={{0,1},{1,0},{2,3},{3,2},{4,5},{5,4},{6,7},{7,6},{8,9},{9,8},{10,11... | collective-permute-start | bytes 393224 | tf_op jit(solution)/shard_map/ppermute | solution.py:65
  184.1 1.3 collective-permute-done.19.refs_7_
  185.4 1.4 encoder_grads_kernel.1
  186.8 0.9 collective-permute-done.22.refs_3_
  187.8 1.8 decoder_grads_kernel.1
  (85 shorter events, 5.8 us)
Async XLA Ops:
  3.2 17.3 %copy-start.8 = (bf16[1,576,256]{2,1,0:T(8,128)(2,1)S(1)}, bf16[1,576,256]{2,1,0:T(8,128)(2,1)}, u32[]{:S(2)}) copy-start(bf16[1,576,256]{2,1,0:T(8,128)(2,1)} %param.18) | copy-start | bytes 884740
  3.2 17.4 %copy-start.22 = (bf16[1,576,144]{1,2,0:T(8,128)(2,1)S(1)}, bf16[1,576,144]{1,2,0:T(8,128)(2,1)}, u32[]{:S(2)}) copy-start(bf16[1,576,144]{1,2,0:T(8,128)(2,1)} %param.15) | copy-start | bytes 497668
  3.2 17.4 %copy-start.23 = (bf16[1,576,144]{1,2,0:T(8,128)(2,1)S(1)}, bf16[1,576,144]{1,2,0:T(8,128)(2,1)}, u32[]{:S(2)}) copy-start(bf16[1,576,144]{1,2,0:T(8,128)(2,1)} %param.16) | copy-start | bytes 497668
  3.2 17.4 %copy-start.24 = (bf16[256,256]{1,0:T(8,128)(2,1)S(1)}, bf16[256,256]{1,0:T(8,128)(2,1)}, u32[]{:S(2)}) copy-start(bf16[256,256]{1,0:T(8,128)(2,1)} %refs_3_.1) | copy-start | bytes 393220
  3.2 21.3 %copy-start.9 = (bf16[1,256,576]{1,2,0:T(8,128)(2,1)S(1)}, bf16[1,256,576]{1,2,0:T(8,128)(2,1)}, u32[]{:S(2)}) copy-start(bf16[1,256,576]{1,2,0:T(8,128)(2,1)} %param.20) | copy-start | bytes 884740
  3.2 21.3 %copy-start.10 = (bf16[1,256,576]{1,2,0:T(8,128)(2,1)S(1)}, bf16[1,256,576]{1,2,0:T(8,128)(2,1)}, u32[]{:S(2)}) copy-start(bf16[1,256,576]{1,2,0:T(8,128)(2,1)} %param.21) | copy-start | bytes 884740
  3.3 49.5 %all-to-all-start = ((bf16[64,80,128]{2,1,0:T(8,128)(2,1)}), bf16[64,80,128]{2,1,0:T(8,128)(2,1)S(1)}, u32[]{:S(2)}, u32[]{:S(2)}) async-start(bf16[64,80,128]{2,1,0:T(8,128)(2,1)} %spread_kernel.1), calls=%async_computation | async-start | bytes 2621440 | tf_op jit(solution)/shard_map/all_to_all | solution.py:78
  20.5 32.2 %copy-start.28 = (s32[1,2,2]{2,1,0:T(2,128)S(1)}, s32[1,2,2]{2,1,0:T(2,128)}, u32[]{:S(2)}) copy-start(s32[1,2,2]{2,1,0:T(2,128)} %param.14) | copy-start | bytes 52
  20.6 32.2 %copy-start.29 = (f32[1,256]{1,0:T(1,128)S(1)}, f32[1,256]{1,0:T(1,128)}, u32[]{:S(2)}) copy-start(f32[1,256]{1,0:T(1,128)} %refs_7_.1) | copy-start | bytes 3076
  21.4 17.4 %collective-permute-start.1 = (bf16[2592,128]{1,0:T(8,128)(2,1)S(1)}, bf16[2592,128]{1,0:T(8,128)(2,1)}, u32[]{:S(2)}, u32[]{:S(2)}) collective-permute-start(bf16[2592,128]{1,0:T(8,128)(2,1)S(1)} %get-tuple-element.27.refs_3_), channel_id=1, source_target_pairs={{0,2},{1,3},{2,0},{3,1},{4,6},{5,7},{6,4},{7,5},{8,10},{9,11},{10,... | collective-permute-start | bytes 1990664 | tf_op jit(solution)/shard_map/ppermute | solution.py:65
  25.6 30.6 %collective-permute-start.8 = (bf16[3024,128]{1,0:T(8,128)(2,1)S(1)}, bf16[3024,128]{1,0:T(8,128)(2,1)S(1)}, u32[]{:S(2)}, u32[]{:S(2)}) collective-permute-start(bf16[3024,128]{1,0:T(8,128)(2,1)S(1)} %pack_kernel.1.refs_5_), channel_id=1, source_target_pairs={{0,2},{1,3},{2,0},{3,1},{4,6},{5,7},{6,4},{7,5},{8,10},{9,11},{10,... | collective-permute-start | bytes 2322440 | tf_op jit(solution)/shard_map/ppermute | solution.py:65
  27.7 18.4 %collective-permute-start = (bf16[2592,128]{1,0:T(8,128)(2,1)S(1)}, bf16[2592,128]{1,0:T(8,128)(2,1)}, u32[]{:S(2)}, u32[]{:S(2)}) collective-permute-start(bf16[2592,128]{1,0:T(8,128)(2,1)S(1)} %get-tuple-element.27.refs_3_), channel_id=1, source_target_pairs={{0,1},{1,0},{2,3},{3,2},{4,5},{5,4},{6,7},{7,6},{8,9},{9,8},{10,11... | collective-permute-start | bytes 1990664 | tf_op jit(solution)/shard_map/ppermute | solution.py:65
  38.8 7.3 %collective-permute-start.2 = (bf16[2592,128]{1,0:T(8,128)(2,1)}, bf16[2592,128]{1,0:T(8,128)(2,1)}, u32[]{:S(2)}, u32[]{:S(2)}) collective-permute-start(bf16[2592,128]{1,0:T(8,128)(2,1)} %collective-permute-done.1.refs_5_), channel_id=1, source_target_pairs={{0,1},{1,0},{2,3},{3,2},{4,5},{5,4},{6,7},{7,6},{8,9},{9,8},{10,11... | collective-permute-start | bytes 1990664 | tf_op jit(solution)/shard_map/ppermute | solution.py:65
  44.1 22.9 %collective-permute-start.7 = (bf16[3024,128]{1,0:T(8,128)(2,1)S(1)}, bf16[3024,128]{1,0:T(8,128)(2,1)}, u32[]{:S(2)}, u32[]{:S(2)}) collective-permute-start(bf16[3024,128]{1,0:T(8,128)(2,1)S(1)} %pack_kernel.1.refs_5_), channel_id=1, source_target_pairs={{0,1},{1,0},{2,3},{3,2},{4,5},{5,4},{6,7},{7,6},{8,9},{9,8},{10,11... | collective-permute-start | bytes 2322440 | tf_op jit(solution)/shard_map/ppermute | solution.py:65
  56.1 17.0 %copy-start = (f32[256,256]{1,0:T(8,128)}, f32[256,256]{1,0:T(8,128)S(1)}, u32[]{:S(2)}) copy-start(f32[256,256]{1,0:T(8,128)S(1)} %get-tuple-element.35.refs_0_.refs_2_) | copy-start | bytes 786436
  56.1 17.0 %copy-start.11 = (bf16[576,256]{1,0:T(8,128)(2,1)}, bf16[576,256]{1,0:T(8,128)(2,1)S(1)}, u32[]{:S(2)}) copy-start(bf16[576,256]{1,0:T(8,128)(2,1)S(1)} %get-tuple-element.28.refs_0_) | copy-start | bytes 884740
  56.1 17.0 %copy-start.31 = (bf16[576,256]{1,0:T(8,128)(2,1)}, bf16[576,256]{1,0:T(8,128)(2,1)S(1)}, u32[]{:S(2)}) copy-start(bf16[576,256]{1,0:T(8,128)(2,1)S(1)} %get-tuple-element.31) | copy-start | bytes 884740
  56.1 17.0 %copy-start.32 = (bf16[576,256]{1,0:T(8,128)(2,1)}, bf16[576,256]{1,0:T(8,128)(2,1)S(1)}, u32[]{:S(2)}) copy-start(bf16[576,256]{1,0:T(8,128)(2,1)S(1)} %get-tuple-element.30) | copy-start | bytes 884740
  56.1 17.0 %copy-start.33 = (bf16[576,256]{1,0:T(8,128)(2,1)}, bf16[576,256]{1,0:T(8,128)(2,1)S(1)}, u32[]{:S(2)}) copy-start(bf16[576,256]{1,0:T(8,128)(2,1)S(1)} %get-tuple-element.29) | copy-start | bytes 884740
  56.1 13.7 %copy-start.26 = (bf16[256,256]{1,0:T(8,128)(2,1)S(1)}, bf16[256,256]{1,0:T(8,128)(2,1)}, u32[]{:S(2)}) copy-start(bf16[256,256]{1,0:T(8,128)(2,1)} %copy-done.25) | copy-start | bytes 393220
  56.2 13.6 %collective-permute-start.9 = (bf16[3024,128]{1,0:T(8,128)(2,1)S(1)}, bf16[3024,128]{1,0:T(8,128)(2,1)S(1)}, u32[]{:S(2)}, u32[]{:S(2)}) collective-permute-start(bf16[3024,128]{1,0:T(8,128)(2,1)S(1)} %pin_kernel.2.refs_7_), channel_id=1, source_target_pairs={{0,1},{1,0},{2,3},{3,2},{4,5},{5,4},{6,7},{7,6},{8,9},{9,8},{10,11... | collective-permute-start | bytes 2322440 | tf_op jit(solution)/shard_map/ppermute | solution.py:65
  62.3 7.6 %collective-permute-start.6 = (bf16[256,256]{1,0:T(8,128)(2,1)S(1)}, bf16[256,256]{1,0:T(8,128)(2,1)S(1)}, u32[]{:S(2)}, u32[]{:S(2)}) collective-permute-start(bf16[256,256]{1,0:T(8,128)(2,1)S(1)} %get-tuple-element.32.refs_1_), channel_id=1, source_target_pairs={{0,256},{1,257},{2,258},{3,259},{4,260},{5,261},{6,262},{7,263},{8... | collective-permute-start | bytes 393224 | tf_op jit(solution)/shard_map/ppermute | solution.py:310
  73.9 40.0 %all-to-all-start.1 = ((bf16[64,72,128]{2,1,0:T(8,128)(2,1)}), bf16[64,72,128]{2,1,0:T(8,128)(2,1)S(1)}, u32[]{:S(2)}, u32[]{:S(2)}) async-start(bf16[64,72,128]{2,1,0:T(8,128)(2,1)} %get-tuple-element.36), calls=%async_computation.1 | async-start | bytes 2359296 | tf_op jit(solution)/shard_map/all_to_all | solution.py:78
  82.8 13.1 %collective-permute-start.11 = (bf16[512,256]{1,0:T(8,128)(2,1)}, bf16[512,256]{1,0:T(8,128)(2,1)S(1)}, u32[]{:S(2)}, u32[]{:S(2)}) collective-permute-start(bf16[512,256]{1,0:T(8,128)(2,1)} %copy-done.19), channel_id=1, source_target_pairs={{0,2},{1,3},{2,0},{3,1},{4,6},{5,7},{6,4},{7,5},{8,10},{9,11},{10,... | collective-permute-start | bytes 786440 | tf_op jit(solution)/shard_map/ppermute | solution.py:65
  85.1 13.1 %collective-permute-start.3 = (bf16[576,256]{1,0:T(8,128)(2,1)}, bf16[576,256]{1,0:T(8,128)(2,1)S(1)}, u32[]{:S(2)}, u32[]{:S(2)}) collective-permute-start(bf16[576,256]{1,0:T(8,128)(2,1)} %copy-done.33), channel_id=1, source_target_pairs={{0,1},{1,0},{2,3},{3,2},{4,5},{5,4},{6,7},{7,6},{8,9},{9,8},{10,11... | collective-permute-start | bytes 884744 | tf_op jit(solution)/shard_map/ppermute | solution.py:65
  88.3 11.0 %collective-permute-start.4 = (bf16[576,256]{1,0:T(8,128)(2,1)}, bf16[576,256]{1,0:T(8,128)(2,1)S(1)}, u32[]{:S(2)}, u32[]{:S(2)}) collective-permute-start(bf16[576,256]{1,0:T(8,128)(2,1)} %copy-done.32), channel_id=1, source_target_pairs={{0,2},{1,3},{2,0},{3,1},{4,6},{5,7},{6,4},{7,5},{8,10},{9,11},{10,... | collective-permute-start | bytes 884744 | tf_op jit(solution)/shard_map/ppermute | solution.py:65
  91.4 14.5 %collective-permute-start.5 = (bf16[576,256]{1,0:T(8,128)(2,1)}, bf16[576,256]{1,0:T(8,128)(2,1)S(1)}, u32[]{:S(2)}, u32[]{:S(2)}) collective-permute-start(bf16[576,256]{1,0:T(8,128)(2,1)} %copy-done.31), channel_id=1, source_target_pairs={{0,3},{1,2},{2,1},{3,0},{4,7},{5,6},{6,5},{7,4},{8,11},{9,10},{10,... | collective-permute-start | bytes 884744 | tf_op jit(solution)/shard_map/ppermute | solution.py:65
  93.8 12.1 %collective-permute-start.10 = (bf16[512,256]{1,0:T(8,128)(2,1)}, bf16[512,256]{1,0:T(8,128)(2,1)S(1)}, u32[]{:S(2)}, u32[]{:S(2)}) collective-permute-start(bf16[512,256]{1,0:T(8,128)(2,1)} %copy-done.19), channel_id=1, source_target_pairs={{0,1},{1,0},{2,3},{3,2},{4,5},{5,4},{6,7},{7,6},{8,9},{9,8},{10,11... | collective-permute-start | bytes 786440 | tf_op jit(solution)/shard_map/ppermute | solution.py:65
  96.0 10.0 %collective-permute-start.12 = (bf16[512,256]{1,0:T(8,128)(2,1)S(1)}, bf16[512,256]{1,0:T(8,128)(2,1)S(1)}, u32[]{:S(2)}, u32[]{:S(2)}) collective-permute-start(bf16[512,256]{1,0:T(8,128)(2,1)S(1)} %collective-permute-done.11.refs_6_), channel_id=1, source_target_pairs={{0,1},{1,0},{2,3},{3,2},{4,5},{5,4},{6,7},{7,6},{8,9},{9,8},{10,11... | collective-permute-start | bytes 786440 | tf_op jit(solution)/shard_map/ppermute | solution.py:65
  135.8 28.5 %copy-start.1 = (f32[256,256]{1,0:T(8,128)S(1)}, f32[256,256]{1,0:T(8,128)}, u32[]{:S(2)}) copy-start(f32[256,256]{1,0:T(8,128)} %copy-done) | copy-start | bytes 786436
  135.8 8.5 %collective-permute-start.15 = (bf16[2,576,128]{2,1,0:T(8,128)(2,1)S(1)}, bf16[2,576,128]{2,1,0:T(8,128)(2,1)S(1)}, u32[]{:S(2)}, u32[]{:S(2)}) collective-permute-start(bf16[2,576,128]{2,1,0:T(8,128)(2,1)S(1)} %bitcast.29), channel_id=1, source_target_pairs={{0,36},{4,32},{32,4},{36,0},{1,37},{5,33},{33,5},{37,1},{2,38},{6,... | collective-permute-start | bytes 884744 | tf_op jit(solution)/shard_map/ppermute | solution.py:65
  137.8 10.5 %collective-permute-start.14 = (bf16[2,576,128]{2,1,0:T(8,128)(2,1)S(1)}, bf16[2,576,128]{2,1,0:T(8,128)(2,1)S(1)}, u32[]{:S(2)}, u32[]{:S(2)}) collective-permute-start(bf16[2,576,128]{2,1,0:T(8,128)(2,1)S(1)} %bitcast.30), channel_id=1, source_target_pairs={{0,32},{4,36},{32,0},{36,4},{1,33},{5,37},{33,1},{37,5},{2,34},{6,... | collective-permute-start | bytes 884744 | tf_op jit(solution)/shard_map/ppermute | solution.py:65
  140.4 12.2 %collective-permute-start.13 = (bf16[2,576,128]{2,1,0:T(8,128)(2,1)S(1)}, bf16[2,576,128]{2,1,0:T(8,128)(2,1)S(1)}, u32[]{:S(2)}, u32[]{:S(2)}) collective-permute-start(bf16[2,576,128]{2,1,0:T(8,128)(2,1)S(1)} %bitcast.31), channel_id=1, source_target_pairs={{0,4},{4,0},{32,36},{36,32},{1,5},{5,1},{33,37},{37,33},{2,6},{6,2... | collective-permute-start | bytes 884744 | tf_op jit(solution)/shard_map/ppermute | solution.py:65
  154.7 30.7 %copy-start.3 = (bf16[576,256]{1,0:T(8,128)(2,1)S(1)}, bf16[576,256]{1,0:T(8,128)(2,1)}, u32[]{:S(2)}) copy-start(bf16[576,256]{1,0:T(8,128)(2,1)} %copy-done.2) | copy-start | bytes 884740
  154.8 30.7 %copy-start.5 = (bf16[576,256]{1,0:T(8,128)(2,1)S(1)}, bf16[576,256]{1,0:T(8,128)(2,1)}, u32[]{:S(2)}) copy-start(bf16[576,256]{1,0:T(8,128)(2,1)} %copy-done.4) | copy-start | bytes 884740
  154.8 30.7 %copy-start.7 = (bf16[576,256]{1,0:T(8,128)(2,1)S(1)}, bf16[576,256]{1,0:T(8,128)(2,1)}, u32[]{:S(2)}) copy-start(bf16[576,256]{1,0:T(8,128)(2,1)} %copy-done.6) | copy-start | bytes 884740
  154.8 30.7 %copy-start.12 = (bf16[576,256]{1,0:T(8,128)(2,1)S(1)}, bf16[576,256]{1,0:T(8,128)(2,1)}, u32[]{:S(2)}) copy-start(bf16[576,256]{1,0:T(8,128)(2,1)} %copy-done.11) | copy-start | bytes 884740
  154.8 9.4 %collective-permute-start.16 = (bf16[256,256]{1,0:T(8,128)(2,1)S(1)}, bf16[256,256]{1,0:T(8,128)(2,1)S(1)}, u32[]{:S(2)}, u32[]{:S(2)}) collective-permute-start(bf16[256,256]{1,0:T(8,128)(2,1)S(1)} %get-tuple-element.39), channel_id=1, source_target_pairs={{256,0},{257,1},{258,2},{259,3},{260,4},{261,5},{262,6},{263,7},{2... | collective-permute-start | bytes 393224 | tf_op jit(solution)/shard_map/ppermute | solution.py:337
  164.3 23.5 %copy-start.14 = (bf16[512,256]{1,0:T(8,128)(2,1)S(1)}, bf16[512,256]{1,0:T(8,128)(2,1)}, u32[]{:S(2)}) copy-start(bf16[512,256]{1,0:T(8,128)(2,1)} %copy-done.13) | copy-start | bytes 786436
  164.3 23.5 %copy-start.16 = (bf16[512,256]{1,0:T(8,128)(2,1)S(1)}, bf16[512,256]{1,0:T(8,128)(2,1)}, u32[]{:S(2)}) copy-start(bf16[512,256]{1,0:T(8,128)(2,1)} %copy-done.15) | copy-start | bytes 786436
  164.3 23.5 %copy-start.18 = (bf16[512,256]{1,0:T(8,128)(2,1)S(1)}, bf16[512,256]{1,0:T(8,128)(2,1)}, u32[]{:S(2)}) copy-start(bf16[512,256]{1,0:T(8,128)(2,1)} %copy-done.17) | copy-start | bytes 786436
  164.3 23.5 %copy-start.20 = (bf16[512,256]{1,0:T(8,128)(2,1)S(1)}, bf16[512,256]{1,0:T(8,128)(2,1)}, u32[]{:S(2)}) copy-start(bf16[512,256]{1,0:T(8,128)(2,1)} %copy-done.19) | copy-start | bytes 786436
  164.3 5.8 %collective-permute-start.18 = (bf16[256,256]{1,0:T(8,128)(2,1)S(1)}, bf16[256,256]{1,0:T(8,128)(2,1)S(1)}, u32[]{:S(2)}, u32[]{:S(2)}) collective-permute-start(bf16[256,256]{1,0:T(8,128)(2,1)S(1)} %pregrad_kernel.1.refs_4_), channel_id=1, source_target_pairs={{0,2},{1,3},{2,0},{3,1},{4,6},{5,7},{6,4},{7,5},{8,10},{9,11},{10,... | collective-permute-start | bytes 393224 | tf_op jit(solution)/shard_map/ppermute | solution.py:65
  166.8 20.0 %collective-permute-start.21 = (bf16[576,256]{1,0:T(8,128)(2,1)S(1)}, bf16[576,256]{1,0:T(8,128)(2,1)S(1)}, u32[]{:S(2)}, u32[]{:S(2)}) collective-permute-start(bf16[576,256]{1,0:T(8,128)(2,1)S(1)} %get-tuple-element.46), channel_id=1, source_target_pairs={{0,2},{1,3},{2,0},{3,1},{4,6},{5,7},{6,4},{7,5},{8,10},{9,11},{10,... | collective-permute-start | bytes 884744 | tf_op jit(solution)/shard_map/ppermute | solution.py:65
  170.2 16.7 %collective-permute-start.20 = (bf16[576,256]{1,0:T(8,128)(2,1)S(1)}, bf16[576,256]{1,0:T(8,128)(2,1)S(1)}, u32[]{:S(2)}, u32[]{:S(2)}) collective-permute-start(bf16[576,256]{1,0:T(8,128)(2,1)S(1)} %get-tuple-element.45), channel_id=1, source_target_pairs={{0,1},{1,0},{2,3},{3,2},{4,5},{5,4},{6,7},{7,6},{8,9},{9,8},{10,11... | collective-permute-start | bytes 884744 | tf_op jit(solution)/shard_map/ppermute | solution.py:65
  177.3 10.5 %collective-permute-start.22 = (bf16[576,256]{1,0:T(8,128)(2,1)S(1)}, bf16[576,256]{1,0:T(8,128)(2,1)S(1)}, u32[]{:S(2)}, u32[]{:S(2)}) collective-permute-start(bf16[576,256]{1,0:T(8,128)(2,1)S(1)} %get-tuple-element.47), channel_id=1, source_target_pairs={{0,3},{1,2},{2,1},{3,0},{4,7},{5,6},{6,5},{7,4},{8,11},{9,10},{10,... | collective-permute-start | bytes 884744 | tf_op jit(solution)/shard_map/ppermute | solution.py:65
  179.8 4.3 %collective-permute-start.17 = (bf16[256,256]{1,0:T(8,128)(2,1)S(1)}, bf16[256,256]{1,0:T(8,128)(2,1)S(1)}, u32[]{:S(2)}, u32[]{:S(2)}) collective-permute-start(bf16[256,256]{1,0:T(8,128)(2,1)S(1)} %pregrad_kernel.1.refs_4_), channel_id=1, source_target_pairs={{0,1},{1,0},{2,3},{3,2},{4,5},{5,4},{6,7},{7,6},{8,9},{9,8},{10,11... | collective-permute-start | bytes 393224 | tf_op jit(solution)/shard_map/ppermute | solution.py:65
  182.2 3.2 %collective-permute-start.19 = (bf16[256,256]{1,0:T(8,128)(2,1)S(1)}, bf16[256,256]{1,0:T(8,128)(2,1)S(1)}, u32[]{:S(2)}, u32[]{:S(2)}) collective-permute-start(bf16[256,256]{1,0:T(8,128)(2,1)S(1)} %collective-permute-done.18.refs_6_.refs_0_), channel_id=1, source_target_pairs={{0,1},{1,0},{2,3},{3,2},{4,5},{5,4},{6,7},{7,6},{8,9},{9,8},{10,11... | collective-permute-start | bytes 393224 | tf_op jit(solution)/shard_map/ppermute | solution.py:65
  (11 other events, 7.9 us)

commit v8 on v6

--- a/solution.py
+++ b/solution.py
@@ -328,18 +328,15 @@
         after=(corner(both[1:]),),
     )
     later = lax.ppermute(prev_back, "layer", [(1, 0)])
-    err[2] = toward(err[2], 2)
-    (pregrad,) = call(
+    pregrad, err[1], err[3] = call(
         pregrad_kernel,
         (own_back, later, slope),
         [((width, height), BF)],
-        after=(err[2],),
+        through=(err[1], err[3]),
     )
     pregrad = gather4(pregrad)
-    (last,) = call(pin_kernel, (), [], after=(pregrad[2],), through=(err[3],))
-    err[3] = toward(last, 3)
-    (last,) = call(pin_kernel, (), [], after=(pregrad[1],), through=(err[1],))
-    err[1] = toward(last, 1)
+    (err[3],) = call(pin_kernel, (), [], after=(pregrad[2],), through=(err[3],))
+    err = exchange4(err)
     grad_own, grad_prev = call(
         decoder_grads_kernel, (*err, *both), [((block, width), F32)] * 2, leaving=(0, 1)
     )

time: 195 us -> 189 us (0.969)
  waiting for transfers between devices: 70.2 us -> 61.8 us
  starting transfers between devices: 99.7 us -> 102 us
    ppermute x18, waiting for transfers between devices: 32.2 us -> 26.3 us  [toward(): return lax.ppermute(x, TOK, [(i, i ^ k) for i in range(4)])]
    ppermute x18, starting transfers between devices: 58.2 us -> 60.8 us  [toward(): return lax.ppermute(x, TOK, [(i, i ^ k) for i in range(4)])]
    ppermute x1, waiting for transfers between devices: 8.5 us -> 6.03 us  [local(): later = lax.ppermute(prev_back, 'layer', [(1, 0)])]
    pallas_call x13 -> x12, Pallas kernels: 14.8 us -> 14.8 us  [call(): pl.pallas_call(body, out_shape=[(pltpu.HBM if i in leaving else pltpu.VME...]
  transfers between devices with their start and end apart: 23 -> 23, of which waited for: 13 -> 12; matrix products, arithmetic and copies ran while one was open for 0% -> 0% of each run, Pallas kernels for 3% -> 3%
where the time goes in v8:
time: 189 us; the launch traced here: 188 us
  starting transfers between devices  102 us (54%)
  waiting for transfers between devices  61.8 us (33%)
  Pallas kernels  14.8 us (8%)
  local copies, waits for them, and re-layouts  7.99 us (4%)
    ppermute x18, starting transfers between devices, toward(): return lax.ppermute(x, TOK, [(i, i ^ k) for i in range(4)])  60.8 us
    all_to_all x3, starting transfers between devices, exchange(): lax.all_to_all(blocks, 'feat', split_axis=0, concat_axis=0, tiled=True)  35.6 us
    all_to_all x3, waiting for transfers between devices, exchange(): lax.all_to_all(blocks, 'feat', split_axis=0, concat_axis=0, tiled=True)  26.6 us
    ppermute x18, waiting for transfers between devices, toward(): return lax.ppermute(x, TOK, [(i, i ^ k) for i in range(4)])  26.3 us
    pallas_call x12, Pallas kernels, call(): pl.pallas_call(body, out_shape=[(pltpu.HBM if i in leaving else pltpu.VME...  14.8 us
    unnamed x68, local copies, waits for them, and re-layouts  7.99 us
    ppermute x1, waiting for transfers between devices, local(): later = lax.ppermute(prev_back, 'layer', [(1, 0)])  6.03 us
    ppermute x1, starting transfers between devices, local(): shifted = lax.ppermute(codes, 'layer', [(0, 1)])  4.66 us
  transfers between devices with their start and end apart: 23, of which 12 were waited for; matrix products, arithmetic and copies ran while one was open for 0% of the time, Pallas kernels for 3%

profile of v8, /device:TPU:1, one launch (start us, length us, event | category | flops | bytes accessed | tf_op | source)
XLA Modules:
  0.0 188.3 jit_solution(7659682397593775094)
XLA Ops:
  0.6 0.7 copy-done.27
  2.0 1.2 spread_kernel.1
  3.3 17.3 %all-to-all-start = ((bf16[64,80,128]{2,1,0:T(8,128)(2,1)}), bf16[64,80,128]{2,1,0:T(8,128)(2,1)S(1)}, u32[]{:S(2)}, u32[]{:S(2)}) async-start(bf16[64,80,128]{2,1,0:T(8,128)(2,1)} %spread_kernel.1), calls=%async_computation | async-start | bytes 2621440 | tf_op jit(solution)/shard_map/all_to_all | solution.py:75
  21.4 3.1 %collective-permute-start.1 = (bf16[2592,128]{1,0:T(8,128)(2,1)S(1)}, bf16[2592,128]{1,0:T(8,128)(2,1)}, u32[]{:S(2)}, u32[]{:S(2)}) collective-permute-start(bf16[2592,128]{1,0:T(8,128)(2,1)S(1)} %get-tuple-element.28.refs_3_), channel_id=1, source_target_pairs={{0,2},{1,3},{2,0},{3,1},{4,6},{5,7},{6,4},{7,5},{8,10},{9,11},{10,... | collective-permute-start | bytes 1990664 | tf_op jit(solution)/shard_map/ppermute | solution.py:62
  24.5 0.9 copy-done.21
  25.6 2.2 %collective-permute-start.8 = (bf16[3024,128]{1,0:T(8,128)(2,1)S(1)}, bf16[3024,128]{1,0:T(8,128)(2,1)S(1)}, u32[]{:S(2)}, u32[]{:S(2)}) collective-permute-start(bf16[3024,128]{1,0:T(8,128)(2,1)S(1)} %pack_kernel.1.refs_5_.refs_2_), channel_id=1, source_target_pairs={{0,2},{1,3},{2,0},{3,1},{4,6},{5,7},{6,4},{7,5},{8,10},{9,11},{10,... | collective-permute-start | bytes 2322440 | tf_op jit(solution)/shard_map/ppermute | solution.py:62
  27.7 3.4 %collective-permute-start = (bf16[2592,128]{1,0:T(8,128)(2,1)S(1)}, bf16[2592,128]{1,0:T(8,128)(2,1)}, u32[]{:S(2)}, u32[]{:S(2)}) collective-permute-start(bf16[2592,128]{1,0:T(8,128)(2,1)S(1)} %get-tuple-element.28.refs_3_), channel_id=1, source_target_pairs={{0,1},{1,0},{2,3},{3,2},{4,5},{5,4},{6,7},{7,6},{8,9},{9,8},{10,11... | collective-permute-start | bytes 1990664 | tf_op jit(solution)/shard_map/ppermute | solution.py:62
  31.2 7.7 %collective-permute-done.1.refs_5_ = bf16[2592,128]{1,0:T(8,128)(2,1)} collective-permute-done((bf16[2592,128]{1,0:T(8,128)(2,1)S(1)}, bf16[2592,128]{1,0:T(8,128)(2,1)}, u32[]{:S(2)}, u32[]{:S(2)}) %collective-permute-start.1) | collective-permute-done | bytes 663584 | tf_op jit(solution)/shard_map/ppermute | solution.py:62
  38.8 5.2 %collective-permute-start.2 = (bf16[2592,128]{1,0:T(8,128)(2,1)}, bf16[2592,128]{1,0:T(8,128)(2,1)}, u32[]{:S(2)}, u32[]{:S(2)}) collective-permute-start(bf16[2592,128]{1,0:T(8,128)(2,1)} %collective-permute-done.1.refs_5_), channel_id=1, source_target_pairs={{0,1},{1,0},{2,3},{3,2},{4,5},{5,4},{6,7},{7,6},{8,9},{9,8},{10,11... | collective-permute-start | bytes 1990664 | tf_op jit(solution)/shard_map/ppermute | solution.py:62
  44.1 1.9 %collective-permute-start.7 = (bf16[3024,128]{1,0:T(8,128)(2,1)S(1)}, bf16[3024,128]{1,0:T(8,128)(2,1)}, u32[]{:S(2)}, u32[]{:S(2)}) collective-permute-start(bf16[3024,128]{1,0:T(8,128)(2,1)S(1)} %pack_kernel.1.refs_5_.refs_2_), channel_id=1, source_target_pairs={{0,1},{1,0},{2,3},{3,2},{4,5},{5,4},{6,7},{7,6},{8,9},{9,8},{10,11... | collective-permute-start | bytes 2322440 | tf_op jit(solution)/shard_map/ppermute | solution.py:62
  46.1 6.6 %all-to-all-done.refs_2_ = bf16[64,80,128]{2,1,0:T(8,128)(2,1)S(1)} async-done(((bf16[64,80,128]{2,1,0:T(8,128)(2,1)}), bf16[64,80,128]{2,1,0:T(8,128)(2,1)S(1)}, u32[]{:S(2)}, u32[]{:S(2)}) %all-to-all-start) | async-done | bytes 1310752 | tf_op jit(solution)/shard_map/all_to_all | solution.py:75
  52.7 3.3 %encode_kernel.1 = (bf16[576,256]{1,0:T(8,128)(2,1)S(1)}, bf16[576,256]{1,0:T(8,128)(2,1)S(1)}, bf16[576,256]{1,0:T(8,128)(2,1)S(1)}, bf16[576,256]{1,0:T(8,128)...) custom-call(s32[2]{0:T(128)S(1)} %pad_add_fusion.refs_0_, ...), custom_call_target="tpu_custom_call" | custom-call | tf_op jit(solution)/shard_map/encode_kernel/pallas_call | solution.py:38
  56.2 6.1 %collective-permute-start.9 = (bf16[3024,128]{1,0:T(8,128)(2,1)S(1)}, bf16[3024,128]{1,0:T(8,128)(2,1)S(1)}, u32[]{:S(2)}, u32[]{:S(2)}) collective-permute-start(bf16[3024,128]{1,0:T(8,128)(2,1)S(1)} %pin_kernel.2.refs_7_.refs_4_), channel_id=1, source_target_pairs={{0,1},{1,0},{2,3},{3,2},{4,5},{5,4},{6,7},{7,6},{8,9},{9,8},{10,11... | collective-permute-start | bytes 2322440 | tf_op jit(solution)/shard_map/ppermute | solution.py:62
  62.2 4.7 %collective-permute-start.6 = (bf16[256,256]{1,0:T(8,128)(2,1)S(1)}, bf16[256,256]{1,0:T(8,128)(2,1)S(1)}, u32[]{:S(2)}, u32[]{:S(2)}) collective-permute-start(bf16[256,256]{1,0:T(8,128)(2,1)S(1)} %get-tuple-element.33.refs_1_), channel_id=1, source_target_pairs={{0,256},{1,257},{2,258},{3,259},{4,260},{5,261},{6,262},{7,263},{8... | collective-permute-start | bytes 393224 | tf_op jit(solution)/shard_map/ppermute | solution.py:310
  66.9 2.9 %collective-permute-done.6.refs_3_ = bf16[256,256]{1,0:T(8,128)(2,1)S(1)} collective-permute-done((bf16[256,256]{1,0:T(8,128)(2,1)S(1)}, bf16[256,256]{1,0:T(8,128)(2,1)S(1)}, u32[]{:S(2)}, u32[]{:S(2)}) %collective-permute-start.6) | collective-permute-done | bytes 131104 | tf_op jit(solution)/shard_map/ppermute | solution.py:310
  69.8 3.3 %decode_kernel.1 = (bf16[64,72,128]{2,1,0:T(8,128)(2,1)}, bf16[512,256]{1,0:T(8,128)(2,1)S(1)}) custom-call(s32[2]{0:T(128)S(1)} %pad_add_fusion.refs_0_, bf16[256,256]{1,0:T(8,128)(2,1)S(1)} %get-tuple-element.33.refs_1_, bf16[256,256]{1,0:T(8,128)(2,1)S(1)} %copy-done.26, bf16[256,256]{1,0:T(8,128)(2,1)S(1)} %collective-permute-done.6.refs_3_, ...), custom_call_target="tpu_custom_call" | custom-call | tf_op jit(solution)/shard_map/decode_kernel/pallas_call | solution.py:38
  73.9 9.0 %all-to-all-start.1 = ((bf16[64,72,128]{2,1,0:T(8,128)(2,1)}), bf16[64,72,128]{2,1,0:T(8,128)(2,1)S(1)}, u32[]{:S(2)}, u32[]{:S(2)}) async-start(bf16[64,72,128]{2,1,0:T(8,128)(2,1)} %get-tuple-element.37), calls=%async_computation.1 | async-start | bytes 2359296 | tf_op jit(solution)/shard_map/all_to_all | solution.py:75
  82.9 3.0 %collective-permute-start.3 = (bf16[576,256]{1,0:T(8,128)(2,1)}, bf16[576,256]{1,0:T(8,128)(2,1)S(1)}, u32[]{:S(2)}, u32[]{:S(2)}) collective-permute-start(bf16[576,256]{1,0:T(8,128)(2,1)} %copy-done.33), channel_id=1, source_target_pairs={{0,1},{1,0},{2,3},{3,2},{4,5},{5,4},{6,7},{7,6},{8,9},{9,8},{10,11... | collective-permute-start | bytes 884744 | tf_op jit(solution)/shard_map/ppermute | solution.py:62
  85.9 2.2 %collective-permute-start.4 = (bf16[576,256]{1,0:T(8,128)(2,1)}, bf16[576,256]{1,0:T(8,128)(2,1)S(1)}, u32[]{:S(2)}, u32[]{:S(2)}) collective-permute-start(bf16[576,256]{1,0:T(8,128)(2,1)} %copy-done.32), channel_id=1, source_target_pairs={{0,2},{1,3},{2,0},{3,1},{4,6},{5,7},{6,4},{7,5},{8,10},{9,11},{10,... | collective-permute-start | bytes 884744 | tf_op jit(solution)/shard_map/ppermute | solution.py:62
  88.1 3.2 %collective-permute-start.5 = (bf16[576,256]{1,0:T(8,128)(2,1)}, bf16[576,256]{1,0:T(8,128)(2,1)S(1)}, u32[]{:S(2)}, u32[]{:S(2)}) collective-permute-start(bf16[576,256]{1,0:T(8,128)(2,1)} %copy-done.31), channel_id=1, source_target_pairs={{0,3},{1,2},{2,1},{3,0},{4,7},{5,6},{6,5},{7,4},{8,11},{9,10},{10,... | collective-permute-start | bytes 884744 | tf_op jit(solution)/shard_map/ppermute | solution.py:62
  91.3 5.2 %collective-permute-done.4.refs_2_ = bf16[576,256]{1,0:T(8,128)(2,1)S(1)} collective-permute-done((bf16[576,256]{1,0:T(8,128)(2,1)}, bf16[576,256]{1,0:T(8,128)(2,1)S(1)}, u32[]{:S(2)}, u32[]{:S(2)}) %collective-permute-start.4) | collective-permute-done | bytes 294944 | tf_op jit(solution)/shard_map/ppermute | solution.py:62
  96.6 6.7 %collective-permute-done.5.refs_3_ = bf16[576,256]{1,0:T(8,128)(2,1)S(1)} collective-permute-done((bf16[576,256]{1,0:T(8,128)(2,1)}, bf16[576,256]{1,0:T(8,128)(2,1)S(1)}, u32[]{:S(2)}, u32[]{:S(2)}) %collective-permute-start.5) | collective-permute-done | bytes 294944 | tf_op jit(solution)/shard_map/ppermute | solution.py:62
  103.3 0.7 copy-done.2
  104.0 0.7 copy-done.4
  104.7 0.7 copy-done.6
  105.5 6.8 %all-to-all-done.1.refs_0_ = bf16[64,72,128]{2,1,0:T(8,128)(2,1)S(1)} async-done(((bf16[64,72,128]{2,1,0:T(8,128)(2,1)}), bf16[64,72,128]{2,1,0:T(8,128)(2,1)S(1)}, u32[]{:S(2)}, u32[]{:S(2)}) %all-to-all-start.1) | async-done | bytes 1179680 | tf_op jit(solution)/shard_map/all_to_all | solution.py:75
  112.2 1.3 total_kernel.1
  113.5 9.3 %all-to-all-start.2 = ((bf16[64,72,128]{2,1,0:T(8,128)(2,1)}), bf16[64,72,128]{2,1,0:T(8,128)(2,1)S(1)}, u32[]{:S(2)}, u32[]{:S(2)}) async-start(bf16[64,72,128]{2,1,0:T(8,128)(2,1)} %total_kernel.1), calls=%async_computation.2 | async-start | bytes 2359296 | tf_op jit(solution)/shard_map/all_to_all | solution.py:75
  122.8 2.2 %collective-permute-start.11 = (bf16[512,256]{1,0:T(8,128)(2,1)}, bf16[512,256]{1,0:T(8,128)(2,1)S(1)}, u32[]{:S(2)}, u32[]{:S(2)}) collective-permute-start(bf16[512,256]{1,0:T(8,128)(2,1)} %copy-done.19), channel_id=1, source_target_pairs={{0,2},{1,3},{2,0},{3,1},{4,6},{5,7},{6,4},{7,5},{8,10},{9,11},{10,... | collective-permute-start | bytes 786440 | tf_op jit(solution)/shard_map/ppermute | solution.py:62
  125.0 3.4 %collective-permute-start.10 = (bf16[512,256]{1,0:T(8,128)(2,1)}, bf16[512,256]{1,0:T(8,128)(2,1)S(1)}, u32[]{:S(2)}, u32[]{:S(2)}) collective-permute-start(bf16[512,256]{1,0:T(8,128)(2,1)} %copy-done.19), channel_id=1, source_target_pairs={{0,1},{1,0},{2,3},{3,2},{4,5},{5,4},{6,7},{7,6},{8,9},{9,8},{10,11... | collective-permute-start | bytes 786440 | tf_op jit(solution)/shard_map/ppermute | solution.py:62
  128.4 3.1 %collective-permute-done.11.refs_6_ = bf16[512,256]{1,0:T(8,128)(2,1)S(1)} collective-permute-done((bf16[512,256]{1,0:T(8,128)(2,1)}, bf16[512,256]{1,0:T(8,128)(2,1)S(1)}, u32[]{:S(2)}, u32[]{:S(2)}) %collective-permute-start.11) | collective-permute-done | bytes 262176 | tf_op jit(solution)/shard_map/ppermute | solution.py:62
  131.5 4.0 %collective-permute-start.12 = (bf16[512,256]{1,0:T(8,128)(2,1)S(1)}, bf16[512,256]{1,0:T(8,128)(2,1)S(1)}, u32[]{:S(2)}, u32[]{:S(2)}) collective-permute-start(bf16[512,256]{1,0:T(8,128)(2,1)S(1)} %collective-permute-done.11.refs_6_), channel_id=1, source_target_pairs={{0,1},{1,0},{2,3},{3,2},{4,5},{5,4},{6,7},{7,6},{8,9},{9,8},{10,11... | collective-permute-start | bytes 786440 | tf_op jit(solution)/shard_map/ppermute | solution.py:62
  135.5 1.1 collective-permute-done.12.refs_7_
  136.7 0.7 copy-done.13
  138.8 13.2 %all-to-all-done.2.refs_1_ = bf16[64,72,128]{2,1,0:T(8,128)(2,1)S(1)} async-done(((bf16[64,72,128]{2,1,0:T(8,128)(2,1)}), bf16[64,72,128]{2,1,0:T(8,128)(2,1)S(1)}, u32[]{:S(2)}, u32[]{:S(2)}) %all-to-all-start.2) | async-done | bytes 1179680 | tf_op jit(solution)/shard_map/all_to_all | solution.py:75
  152.0 2.2 %back_kernel.1 = (f32[256,256]{1,0:T(8,128)S(1)}, bf16[256,256]{1,0:T(8,128)(2,1)S(1)}, bf16[576,256]{1,0:T(8,128)(2,1)S(1)}, bf16[576,256]{1,0:T(8,128)(2,1)S(1...) custom-call(s32[2]{0:T(128)S(1)} %pad_add_fusion.refs_0_, ...), custom_call_target="tpu_custom_call" | custom-call | tf_op jit(solution)/shard_map/back_kernel/pallas_call | solution.py:38
  154.3 1.4 collective-permute-start.13
  155.7 6.0 %collective-permute-done.13.refs_1_ = bf16[256,256]{1,0:T(8,128)(2,1)S(1)} collective-permute-done((bf16[256,256]{1,0:T(8,128)(2,1)S(1)}, bf16[256,256]{1,0:T(8,128)(2,1)S(1)}, u32[]{:S(2)}, u32[]{:S(2)}) %collective-permute-start.13) | collective-permute-done | bytes 131104 | tf_op jit(solution)/shard_map/ppermute | solution.py:330
  161.8 2.2 %collective-permute-start.15 = (bf16[256,256]{1,0:T(8,128)(2,1)S(1)}, bf16[256,256]{1,0:T(8,128)(2,1)S(1)}, u32[]{:S(2)}, u32[]{:S(2)}) collective-permute-start(bf16[256,256]{1,0:T(8,128)(2,1)S(1)} %get-tuple-element.43.refs_4_), channel_id=1, source_target_pairs={{0,2},{1,3},{2,0},{3,1},{4,6},{5,7},{6,4},{7,5},{8,10},{9,11},{10,... | collective-permute-start | bytes 393224 | tf_op jit(solution)/shard_map/ppermute | solution.py:62
  164.0 3.1 %collective-permute-start.18 = (bf16[576,256]{1,0:T(8,128)(2,1)S(1)}, bf16[576,256]{1,0:T(8,128)(2,1)S(1)}, u32[]{:S(2)}, u32[]{:S(2)}) collective-permute-start(bf16[576,256]{1,0:T(8,128)(2,1)S(1)} %get-tuple-element.48), channel_id=1, source_target_pairs={{0,2},{1,3},{2,0},{3,1},{4,6},{5,7},{6,4},{7,5},{8,10},{9,11},{10,... | collective-permute-start | bytes 884744 | tf_op jit(solution)/shard_map/ppermute | solution.py:62
  167.1 8.7 %collective-permute-start.17 = (bf16[576,256]{1,0:T(8,128)(2,1)S(1)}, bf16[576,256]{1,0:T(8,128)(2,1)S(1)}, u32[]{:S(2)}, u32[]{:S(2)}) collective-permute-start(bf16[576,256]{1,0:T(8,128)(2,1)S(1)} %get-tuple-element.47), channel_id=1, source_target_pairs={{0,1},{1,0},{2,3},{3,2},{4,5},{5,4},{6,7},{7,6},{8,9},{9,8},{10,11... | collective-permute-start | bytes 884744 | tf_op jit(solution)/shard_map/ppermute | solution.py:62
  175.8 2.6 %collective-permute-start.19 = (bf16[576,256]{1,0:T(8,128)(2,1)S(1)}, bf16[576,256]{1,0:T(8,128)(2,1)S(1)}, u32[]{:S(2)}, u32[]{:S(2)}) collective-permute-start(bf16[576,256]{1,0:T(8,128)(2,1)S(1)} %pin_kernel.3), channel_id=1, source_target_pairs={{0,3},{1,2},{2,1},{3,0},{4,7},{5,6},{6,5},{7,4},{8,11},{9,10},{10,... | collective-permute-start | bytes 884744 | tf_op jit(solution)/shard_map/ppermute | solution.py:62
  178.4 2.4 %collective-permute-start.14 = (bf16[256,256]{1,0:T(8,128)(2,1)S(1)}, bf16[256,256]{1,0:T(8,128)(2,1)S(1)}, u32[]{:S(2)}, u32[]{:S(2)}) collective-permute-start(bf16[256,256]{1,0:T(8,128)(2,1)S(1)} %get-tuple-element.43.refs_4_), channel_id=1, source_target_pairs={{0,1},{1,0},{2,3},{3,2},{4,5},{5,4},{6,7},{7,6},{8,9},{9,8},{10,11... | collective-permute-start | bytes 393224 | tf_op jit(solution)/shard_map/ppermute | solution.py:62
  180.8 1.9 %collective-permute-start.16 = (bf16[256,256]{1,0:T(8,128)(2,1)S(1)}, bf16[256,256]{1,0:T(8,128)(2,1)S(1)}, u32[]{:S(2)}, u32[]{:S(2)}) collective-permute-start(bf16[256,256]{1,0:T(8,128)(2,1)S(1)} %collective-permute-done.15.refs_6_.refs_0_), channel_id=1, source_target_pairs={{0,1},{1,0},{2,3},{3,2},{4,5},{5,4},{6,7},{7,6},{8,9},{9,8},{10,11... | collective-permute-start | bytes 393224 | tf_op jit(solution)/shard_map/ppermute | solution.py:62
  182.7 1.3 collective-permute-done.16.refs_7_
  184.1 1.4 encoder_grads_kernel.1
  185.4 1.0 collective-permute-done.19.refs_3_
  186.5 1.8 decoder_grads_kernel.1
  (81 shorter events, 3.9 us)
Async XLA Ops:
  0.6 0.7 copy-start.27
  3.2 17.3 %copy-start.8 = (bf16[1,576,256]{2,1,0:T(8,128)(2,1)S(1)}, bf16[1,576,256]{2,1,0:T(8,128)(2,1)}, u32[]{:S(2)}) copy-start(bf16[1,576,256]{2,1,0:T(8,128)(2,1)} %param.18) | copy-start | bytes 884740
  3.2 17.3 %copy-start.22 = (bf16[1,576,144]{1,2,0:T(8,128)(2,1)S(1)}, bf16[1,576,144]{1,2,0:T(8,128)(2,1)}, u32[]{:S(2)}) copy-start(bf16[1,576,144]{1,2,0:T(8,128)(2,1)} %param.15) | copy-start | bytes 497668
  3.2 17.3 %copy-start.23 = (bf16[1,576,144]{1,2,0:T(8,128)(2,1)S(1)}, bf16[1,576,144]{1,2,0:T(8,128)(2,1)}, u32[]{:S(2)}) copy-start(bf16[1,576,144]{1,2,0:T(8,128)(2,1)} %param.16) | copy-start | bytes 497668
  3.2 17.3 %copy-start.24 = (bf16[256,256]{1,0:T(8,128)(2,1)S(1)}, bf16[256,256]{1,0:T(8,128)(2,1)}, u32[]{:S(2)}) copy-start(bf16[256,256]{1,0:T(8,128)(2,1)} %refs_3_.1) | copy-start | bytes 393220
  3.2 21.3 %copy-start.9 = (bf16[1,256,576]{1,2,0:T(8,128)(2,1)S(1)}, bf16[1,256,576]{1,2,0:T(8,128)(2,1)}, u32[]{:S(2)}) copy-start(bf16[1,256,576]{1,2,0:T(8,128)(2,1)} %param.20) | copy-start | bytes 884740
  3.3 21.3 %copy-start.10 = (bf16[1,256,576]{1,2,0:T(8,128)(2,1)S(1)}, bf16[1,256,576]{1,2,0:T(8,128)(2,1)}, u32[]{:S(2)}) copy-start(bf16[1,256,576]{1,2,0:T(8,128)(2,1)} %param.21) | copy-start | bytes 884740
  3.3 49.5 %all-to-all-start = ((bf16[64,80,128]{2,1,0:T(8,128)(2,1)}), bf16[64,80,128]{2,1,0:T(8,128)(2,1)S(1)}, u32[]{:S(2)}, u32[]{:S(2)}) async-start(bf16[64,80,128]{2,1,0:T(8,128)(2,1)} %spread_kernel.1), calls=%async_computation | async-start | bytes 2621440 | tf_op jit(solution)/shard_map/all_to_all | solution.py:75
  20.6 32.1 %copy-start.28 = (s32[1,2,2]{2,1,0:T(2,128)S(1)}, s32[1,2,2]{2,1,0:T(2,128)}, u32[]{:S(2)}) copy-start(s32[1,2,2]{2,1,0:T(2,128)} %param.14) | copy-start | bytes 52
  20.6 32.1 %copy-start.29 = (f32[1,256]{1,0:T(1,128)S(1)}, f32[1,256]{1,0:T(1,128)}, u32[]{:S(2)}) copy-start(f32[1,256]{1,0:T(1,128)} %refs_7_.1) | copy-start | bytes 3076
  21.4 17.4 %collective-permute-start.1 = (bf16[2592,128]{1,0:T(8,128)(2,1)S(1)}, bf16[2592,128]{1,0:T(8,128)(2,1)}, u32[]{:S(2)}, u32[]{:S(2)}) collective-permute-start(bf16[2592,128]{1,0:T(8,128)(2,1)S(1)} %get-tuple-element.28.refs_3_), channel_id=1, source_target_pairs={{0,2},{1,3},{2,0},{3,1},{4,6},{5,7},{6,4},{7,5},{8,10},{9,11},{10,... | collective-permute-start | bytes 1990664 | tf_op jit(solution)/shard_map/ppermute | solution.py:62
  24.5 0.9 copy-start.21
  25.6 30.6 %collective-permute-start.8 = (bf16[3024,128]{1,0:T(8,128)(2,1)S(1)}, bf16[3024,128]{1,0:T(8,128)(2,1)S(1)}, u32[]{:S(2)}, u32[]{:S(2)}) collective-permute-start(bf16[3024,128]{1,0:T(8,128)(2,1)S(1)} %pack_kernel.1.refs_5_.refs_2_), channel_id=1, source_target_pairs={{0,2},{1,3},{2,0},{3,1},{4,6},{5,7},{6,4},{7,5},{8,10},{9,11},{10,... | collective-permute-start | bytes 2322440 | tf_op jit(solution)/shard_map/ppermute | solution.py:62
  27.7 18.4 %collective-permute-start = (bf16[2592,128]{1,0:T(8,128)(2,1)S(1)}, bf16[2592,128]{1,0:T(8,128)(2,1)}, u32[]{:S(2)}, u32[]{:S(2)}) collective-permute-start(bf16[2592,128]{1,0:T(8,128)(2,1)S(1)} %get-tuple-element.28.refs_3_), channel_id=1, source_target_pairs={{0,1},{1,0},{2,3},{3,2},{4,5},{5,4},{6,7},{7,6},{8,9},{9,8},{10,11... | collective-permute-start | bytes 1990664 | tf_op jit(solution)/shard_map/ppermute | solution.py:62
  38.8 7.3 %collective-permute-start.2 = (bf16[2592,128]{1,0:T(8,128)(2,1)}, bf16[2592,128]{1,0:T(8,128)(2,1)}, u32[]{:S(2)}, u32[]{:S(2)}) collective-permute-start(bf16[2592,128]{1,0:T(8,128)(2,1)} %collective-permute-done.1.refs_5_), channel_id=1, source_target_pairs={{0,1},{1,0},{2,3},{3,2},{4,5},{5,4},{6,7},{7,6},{8,9},{9,8},{10,11... | collective-permute-start | bytes 1990664 | tf_op jit(solution)/shard_map/ppermute | solution.py:62
  44.1 22.8 %collective-permute-start.7 = (bf16[3024,128]{1,0:T(8,128)(2,1)S(1)}, bf16[3024,128]{1,0:T(8,128)(2,1)}, u32[]{:S(2)}, u32[]{:S(2)}) collective-permute-start(bf16[3024,128]{1,0:T(8,128)(2,1)S(1)} %pack_kernel.1.refs_5_.refs_2_), channel_id=1, source_target_pairs={{0,1},{1,0},{2,3},{3,2},{4,5},{5,4},{6,7},{7,6},{8,9},{9,8},{10,11... | collective-permute-start | bytes 2322440 | tf_op jit(solution)/shard_map/ppermute | solution.py:62
  56.1 17.1 %copy-start = (f32[256,256]{1,0:T(8,128)}, f32[256,256]{1,0:T(8,128)S(1)}, u32[]{:S(2)}) copy-start(f32[256,256]{1,0:T(8,128)S(1)} %get-tuple-element.36.refs_0_.refs_2_) | copy-start | bytes 786436
  56.1 17.1 %copy-start.11 = (bf16[576,256]{1,0:T(8,128)(2,1)}, bf16[576,256]{1,0:T(8,128)(2,1)S(1)}, u32[]{:S(2)}) copy-start(bf16[576,256]{1,0:T(8,128)(2,1)S(1)} %get-tuple-element.29.refs_0_) | copy-start | bytes 884740
  56.1 17.1 %copy-start.31 = (bf16[576,256]{1,0:T(8,128)(2,1)}, bf16[576,256]{1,0:T(8,128)(2,1)S(1)}, u32[]{:S(2)}) copy-start(bf16[576,256]{1,0:T(8,128)(2,1)S(1)} %get-tuple-element.32) | copy-start | bytes 884740
  56.1 17.0 %copy-start.32 = (bf16[576,256]{1,0:T(8,128)(2,1)}, bf16[576,256]{1,0:T(8,128)(2,1)S(1)}, u32[]{:S(2)}) copy-start(bf16[576,256]{1,0:T(8,128)(2,1)S(1)} %get-tuple-element.31) | copy-start | bytes 884740
  56.1 17.0 %copy-start.33 = (bf16[576,256]{1,0:T(8,128)(2,1)}, bf16[576,256]{1,0:T(8,128)(2,1)S(1)}, u32[]{:S(2)}) copy-start(bf16[576,256]{1,0:T(8,128)(2,1)S(1)} %get-tuple-element.30) | copy-start | bytes 884740
  56.1 13.7 %copy-start.26 = (bf16[256,256]{1,0:T(8,128)(2,1)S(1)}, bf16[256,256]{1,0:T(8,128)(2,1)}, u32[]{:S(2)}) copy-start(bf16[256,256]{1,0:T(8,128)(2,1)} %copy-done.25) | copy-start | bytes 393220
  56.2 13.6 %collective-permute-start.9 = (bf16[3024,128]{1,0:T(8,128)(2,1)S(1)}, bf16[3024,128]{1,0:T(8,128)(2,1)S(1)}, u32[]{:S(2)}, u32[]{:S(2)}) collective-permute-start(bf16[3024,128]{1,0:T(8,128)(2,1)S(1)} %pin_kernel.2.refs_7_.refs_4_), channel_id=1, source_target_pairs={{0,1},{1,0},{2,3},{3,2},{4,5},{5,4},{6,7},{7,6},{8,9},{9,8},{10,11... | collective-permute-start | bytes 2322440 | tf_op jit(solution)/shard_map/ppermute | solution.py:62
  62.2 7.6 %collective-permute-start.6 = (bf16[256,256]{1,0:T(8,128)(2,1)S(1)}, bf16[256,256]{1,0:T(8,128)(2,1)S(1)}, u32[]{:S(2)}, u32[]{:S(2)}) collective-permute-start(bf16[256,256]{1,0:T(8,128)(2,1)S(1)} %get-tuple-element.33.refs_1_), channel_id=1, source_target_pairs={{0,256},{1,257},{2,258},{3,259},{4,260},{5,261},{6,262},{7,263},{8... | collective-permute-start | bytes 393224 | tf_op jit(solution)/shard_map/ppermute | solution.py:310
  73.9 38.3 %all-to-all-start.1 = ((bf16[64,72,128]{2,1,0:T(8,128)(2,1)}), bf16[64,72,128]{2,1,0:T(8,128)(2,1)S(1)}, u32[]{:S(2)}, u32[]{:S(2)}) async-start(bf16[64,72,128]{2,1,0:T(8,128)(2,1)} %get-tuple-element.37), calls=%async_computation.1 | async-start | bytes 2359296 | tf_op jit(solution)/shard_map/all_to_all | solution.py:75
  82.9 8.5 %collective-permute-start.3 = (bf16[576,256]{1,0:T(8,128)(2,1)}, bf16[576,256]{1,0:T(8,128)(2,1)S(1)}, u32[]{:S(2)}, u32[]{:S(2)}) collective-permute-start(bf16[576,256]{1,0:T(8,128)(2,1)} %copy-done.33), channel_id=1, source_target_pairs={{0,1},{1,0},{2,3},{3,2},{4,5},{5,4},{6,7},{7,6},{8,9},{9,8},{10,11... | collective-permute-start | bytes 884744 | tf_op jit(solution)/shard_map/ppermute | solution.py:62
  85.9 10.7 %collective-permute-start.4 = (bf16[576,256]{1,0:T(8,128)(2,1)}, bf16[576,256]{1,0:T(8,128)(2,1)S(1)}, u32[]{:S(2)}, u32[]{:S(2)}) collective-permute-start(bf16[576,256]{1,0:T(8,128)(2,1)} %copy-done.32), channel_id=1, source_target_pairs={{0,2},{1,3},{2,0},{3,1},{4,6},{5,7},{6,4},{7,5},{8,10},{9,11},{10,... | collective-permute-start | bytes 884744 | tf_op jit(solution)/shard_map/ppermute | solution.py:62
  88.1 15.2 %collective-permute-start.5 = (bf16[576,256]{1,0:T(8,128)(2,1)}, bf16[576,256]{1,0:T(8,128)(2,1)S(1)}, u32[]{:S(2)}, u32[]{:S(2)}) collective-permute-start(bf16[576,256]{1,0:T(8,128)(2,1)} %copy-done.31), channel_id=1, source_target_pairs={{0,3},{1,2},{2,1},{3,0},{4,7},{5,6},{6,5},{7,4},{8,11},{9,10},{10,... | collective-permute-start | bytes 884744 | tf_op jit(solution)/shard_map/ppermute | solution.py:62
  113.5 38.5 %all-to-all-start.2 = ((bf16[64,72,128]{2,1,0:T(8,128)(2,1)}), bf16[64,72,128]{2,1,0:T(8,128)(2,1)S(1)}, u32[]{:S(2)}, u32[]{:S(2)}) async-start(bf16[64,72,128]{2,1,0:T(8,128)(2,1)} %total_kernel.1), calls=%async_computation.2 | async-start | bytes 2359296 | tf_op jit(solution)/shard_map/all_to_all | solution.py:75
  122.8 8.7 %collective-permute-start.11 = (bf16[512,256]{1,0:T(8,128)(2,1)}, bf16[512,256]{1,0:T(8,128)(2,1)S(1)}, u32[]{:S(2)}, u32[]{:S(2)}) collective-permute-start(bf16[512,256]{1,0:T(8,128)(2,1)} %copy-done.19), channel_id=1, source_target_pairs={{0,2},{1,3},{2,0},{3,1},{4,6},{5,7},{6,4},{7,5},{8,10},{9,11},{10,... | collective-permute-start | bytes 786440 | tf_op jit(solution)/shard_map/ppermute | solution.py:62
  125.0 10.5 %collective-permute-start.10 = (bf16[512,256]{1,0:T(8,128)(2,1)}, bf16[512,256]{1,0:T(8,128)(2,1)S(1)}, u32[]{:S(2)}, u32[]{:S(2)}) collective-permute-start(bf16[512,256]{1,0:T(8,128)(2,1)} %copy-done.19), channel_id=1, source_target_pairs={{0,1},{1,0},{2,3},{3,2},{4,5},{5,4},{6,7},{7,6},{8,9},{9,8},{10,11... | collective-permute-start | bytes 786440 | tf_op jit(solution)/shard_map/ppermute | solution.py:62
  131.5 5.1 %collective-permute-start.12 = (bf16[512,256]{1,0:T(8,128)(2,1)S(1)}, bf16[512,256]{1,0:T(8,128)(2,1)S(1)}, u32[]{:S(2)}, u32[]{:S(2)}) collective-permute-start(bf16[512,256]{1,0:T(8,128)(2,1)S(1)} %collective-permute-done.11.refs_6_), channel_id=1, source_target_pairs={{0,1},{1,0},{2,3},{3,2},{4,5},{5,4},{6,7},{7,6},{8,9},{9,8},{10,11... | collective-permute-start | bytes 786440 | tf_op jit(solution)/shard_map/ppermute | solution.py:62
  152.0 9.7 %copy-start.1 = (f32[256,256]{1,0:T(8,128)S(1)}, f32[256,256]{1,0:T(8,128)}, u32[]{:S(2)}) copy-start(f32[256,256]{1,0:T(8,128)} %copy-done) | copy-start | bytes 786436
  154.2 29.8 %copy-start.3 = (bf16[576,256]{1,0:T(8,128)(2,1)S(1)}, bf16[576,256]{1,0:T(8,128)(2,1)}, u32[]{:S(2)}) copy-start(bf16[576,256]{1,0:T(8,128)(2,1)} %copy-done.2) | copy-start | bytes 884740
  154.2 29.8 %copy-start.5 = (bf16[576,256]{1,0:T(8,128)(2,1)S(1)}, bf16[576,256]{1,0:T(8,128)(2,1)}, u32[]{:S(2)}) copy-start(bf16[576,256]{1,0:T(8,128)(2,1)} %copy-done.4) | copy-start | bytes 884740
  154.2 29.8 %copy-start.7 = (bf16[576,256]{1,0:T(8,128)(2,1)S(1)}, bf16[576,256]{1,0:T(8,128)(2,1)}, u32[]{:S(2)}) copy-start(bf16[576,256]{1,0:T(8,128)(2,1)} %copy-done.6) | copy-start | bytes 884740
  154.2 29.8 %copy-start.12 = (bf16[576,256]{1,0:T(8,128)(2,1)S(1)}, bf16[576,256]{1,0:T(8,128)(2,1)}, u32[]{:S(2)}) copy-start(bf16[576,256]{1,0:T(8,128)(2,1)} %copy-done.11) | copy-start | bytes 884740
  154.3 7.5 %collective-permute-start.13 = (bf16[256,256]{1,0:T(8,128)(2,1)S(1)}, bf16[256,256]{1,0:T(8,128)(2,1)S(1)}, u32[]{:S(2)}, u32[]{:S(2)}) collective-permute-start(bf16[256,256]{1,0:T(8,128)(2,1)S(1)} %get-tuple-element.40), channel_id=1, source_target_pairs={{256,0},{257,1},{258,2},{259,3},{260,4},{261,5},{262,6},{263,7},{2... | collective-permute-start | bytes 393224 | tf_op jit(solution)/shard_map/ppermute | solution.py:330
  161.8 14.0 %collective-permute-start.15 = (bf16[256,256]{1,0:T(8,128)(2,1)S(1)}, bf16[256,256]{1,0:T(8,128)(2,1)S(1)}, u32[]{:S(2)}, u32[]{:S(2)}) collective-permute-start(bf16[256,256]{1,0:T(8,128)(2,1)S(1)} %get-tuple-element.43.refs_4_), channel_id=1, source_target_pairs={{0,2},{1,3},{2,0},{3,1},{4,6},{5,7},{6,4},{7,5},{8,10},{9,11},{10,... | collective-permute-start | bytes 393224 | tf_op jit(solution)/shard_map/ppermute | solution.py:62
  164.0 21.5 %collective-permute-start.18 = (bf16[576,256]{1,0:T(8,128)(2,1)S(1)}, bf16[576,256]{1,0:T(8,128)(2,1)S(1)}, u32[]{:S(2)}, u32[]{:S(2)}) collective-permute-start(bf16[576,256]{1,0:T(8,128)(2,1)S(1)} %get-tuple-element.48), channel_id=1, source_target_pairs={{0,2},{1,3},{2,0},{3,1},{4,6},{5,7},{6,4},{7,5},{8,10},{9,11},{10,... | collective-permute-start | bytes 884744 | tf_op jit(solution)/shard_map/ppermute | solution.py:62
  167.1 18.4 %collective-permute-start.17 = (bf16[576,256]{1,0:T(8,128)(2,1)S(1)}, bf16[576,256]{1,0:T(8,128)(2,1)S(1)}, u32[]{:S(2)}, u32[]{:S(2)}) collective-permute-start(bf16[576,256]{1,0:T(8,128)(2,1)S(1)} %get-tuple-element.47), channel_id=1, source_target_pairs={{0,1},{1,0},{2,3},{3,2},{4,5},{5,4},{6,7},{7,6},{8,9},{9,8},{10,11... | collective-permute-start | bytes 884744 | tf_op jit(solution)/shard_map/ppermute | solution.py:62
  175.7 10.7 %copy-start.14 = (bf16[512,256]{1,0:T(8,128)(2,1)S(1)}, bf16[512,256]{1,0:T(8,128)(2,1)}, u32[]{:S(2)}) copy-start(bf16[512,256]{1,0:T(8,128)(2,1)} %copy-done.13) | copy-start | bytes 786436
  175.8 10.7 %copy-start.16 = (bf16[512,256]{1,0:T(8,128)(2,1)S(1)}, bf16[512,256]{1,0:T(8,128)(2,1)}, u32[]{:S(2)}) copy-start(bf16[512,256]{1,0:T(8,128)(2,1)} %copy-done.15) | copy-start | bytes 786436
  175.8 10.7 %copy-start.18 = (bf16[512,256]{1,0:T(8,128)(2,1)S(1)}, bf16[512,256]{1,0:T(8,128)(2,1)}, u32[]{:S(2)}) copy-start(bf16[512,256]{1,0:T(8,128)(2,1)} %copy-done.17) | copy-start | bytes 786436
  175.8 10.7 %copy-start.20 = (bf16[512,256]{1,0:T(8,128)(2,1)S(1)}, bf16[512,256]{1,0:T(8,128)(2,1)}, u32[]{:S(2)}) copy-start(bf16[512,256]{1,0:T(8,128)(2,1)} %copy-done.19) | copy-start | bytes 786436
  175.8 10.7 %collective-permute-start.19 = (bf16[576,256]{1,0:T(8,128)(2,1)S(1)}, bf16[576,256]{1,0:T(8,128)(2,1)S(1)}, u32[]{:S(2)}, u32[]{:S(2)}) collective-permute-start(bf16[576,256]{1,0:T(8,128)(2,1)S(1)} %pin_kernel.3), channel_id=1, source_target_pairs={{0,3},{1,2},{2,1},{3,0},{4,7},{5,6},{6,5},{7,4},{8,11},{9,10},{10,... | collective-permute-start | bytes 884744 | tf_op jit(solution)/shard_map/ppermute | solution.py:62
  178.4 4.3 %collective-permute-start.14 = (bf16[256,256]{1,0:T(8,128)(2,1)S(1)}, bf16[256,256]{1,0:T(8,128)(2,1)S(1)}, u32[]{:S(2)}, u32[]{:S(2)}) collective-permute-start(bf16[256,256]{1,0:T(8,128)(2,1)S(1)} %get-tuple-element.43.refs_4_), channel_id=1, source_target_pairs={{0,1},{1,0},{2,3},{3,2},{4,5},{5,4},{6,7},{7,6},{8,9},{9,8},{10,11... | collective-permute-start | bytes 393224 | tf_op jit(solution)/shard_map/ppermute | solution.py:62
  180.8 3.2 %collective-permute-start.16 = (bf16[256,256]{1,0:T(8,128)(2,1)S(1)}, bf16[256,256]{1,0:T(8,128)(2,1)S(1)}, u32[]{:S(2)}, u32[]{:S(2)}) collective-permute-start(bf16[256,256]{1,0:T(8,128)(2,1)S(1)} %collective-permute-done.15.refs_6_.refs_0_), channel_id=1, source_target_pairs={{0,1},{1,0},{2,3},{3,2},{4,5},{5,4},{6,7},{7,6},{8,9},{9,8},{10,11... | collective-permute-start | bytes 393224 | tf_op jit(solution)/shard_map/ppermute | solution.py:62
  (9 other events, 6.3 us)
